TPU v7x, 32 devices: a whole 2x2x4 slice. The times are simulated.
32 devices in a mesh: ctx: 8 (over y, x, core), tp: 4 (over z).
Axes of the slice: x: 2, y: 2, z: 4, core: 2. Of those that a mesh axis runs over, the one named last changes fastest.
Arguments:
- residual_in: bfloat16 [2, 2048, 4096], P(None, 'ctx', 'tp'), may hold values from -6 to 6
- mr_qkv: bfloat16 [2, 2048, 3, 4096], P(None, 'ctx', None, 'tp'), may hold values from -6 to 6
- mr_short_w: float32 [3, 3, 4096], P(None, None, 'tp'), may hold values from -3.5 to 3.5
- mr_filter: bfloat16 [128, 4096], P(None, 'tp'), may hold values from -0.5 to 0.5
- mr_skip: float32 [4096], P('tp'), may hold values from -4 to 4
- mr_out_w: bfloat16 [4096, 4096], P('tp', 'ctx'), may hold values from -0.09375 to 0.09375
- lr_gain: float32 [4096], replicated, may hold values from 0.1 to 1.9
- lr_in_w: bfloat16 [4096, 3, 4096], P(None, None, 'tp'), may hold values from -0.09375 to 0.09375
- lr_short_w: float32 [3, 3, 4096], P(None, None, 'tp'), may hold values from -3.5 to 3.5
- lr_rate: float32 [16, 4096], P(None, 'tp'), may hold values from 0 to 1, as said below
- lr_res: float32 [16, 4096], P(None, 'tp'), may hold values from -3 to 3
- lr_skip: float32 [4096], P('tp'), may hold values from -4 to 4
- lr_out_w: bfloat16 [4096, 4096], P('tp', 'ctx'), may hold values from -0.09375 to 0.09375
Outputs:
- residual_out: bfloat16 [2, 2048, 4096], P(None, 'ctx', 'tp')
Inputs may be any that keep to these rules, and one draw needn't show every extreme that they name: `lr_rate`: each rate lies between 0.1 / 2048 and 1 / 20.
All inputs are finite; a program needn't handle non-finite values.
Results may differ from a plain program's by a relative error of at most 0.034.
Values may be sent and summed in bfloat16 or wider, within the bound.
No kernel may reach another device: no remote copies, remote signals or barrier semaphores. Data moves between devices by JAX's collectives and lax.ppermute only.
A program may use at most 192 MiB of HBM per device.

v0:
```python
import jax
import jax.numpy as jnp
from jax import lax
from jax.sharding import PartitionSpec as P


def from_behind(value, axis, steps):
    count = lax.axis_size(axis)
    first, last = (max(0, -steps), min(count, count - steps))
    return lax.ppermute(value, axis, [(source, source + steps) for source in range(first, last)])


def short_filter(inputs, earlier, weights):
    span = earlier.shape[1]
    count = inputs.shape[1]
    joined = jnp.concatenate([earlier, inputs], axis=1)
    total = jnp.zeros(inputs.shape, jnp.float32)
    for lag in range(weights.shape[0]):
        total = total + weights[lag] * joined[:, span - lag : span - lag + count]
    return total


def toeplitz_taps(extended, taps):
    sequences, span, width = extended.shape
    length = taps.shape[0]
    count = (span + 1) // length
    padded = jnp.concatenate([jnp.zeros((sequences, 1, width), extended.dtype), extended], axis=1)
    blocks = padded.reshape(sequences, count, length, width)
    offsets = jnp.arange(length)[:, None] - jnp.arange(length)[None, :]
    nothing = jnp.zeros((), taps.dtype)
    lower = jnp.where(
        (offsets >= 0)[:, :, None],
        jnp.take(taps, jnp.clip(offsets, 0, length - 1), axis=0),
        nothing,
    )
    upper = jnp.where(
        (offsets < 0)[:, :, None],
        jnp.take(taps, jnp.clip(offsets + length, 0, length - 1), axis=0),
        nothing,
    )
    result = jnp.einsum("ijc,sbjc->sbic", lower, blocks[:, 1:], preferred_element_type=jnp.float32)
    result = result + jnp.einsum(
        "ijc,sbjc->sbic", upper, blocks[:, :-1], preferred_element_type=jnp.float32
    )
    return result.reshape(sequences, (count - 1) * length, width)


def local(
    residual_in,
    mr_qkv,
    mr_short_w,
    mr_filter,
    mr_skip,
    mr_out_w,
    lr_gain,
    lr_in_w,
    lr_short_w,
    lr_rate,
    lr_res,
    lr_skip,
    lr_out_w,
):
    sequences, tokens, _, width = mr_qkv.shape
    length = mr_filter.shape[0]
    prior = mr_short_w.shape[0] - 1
    highest = lax.Precision.HIGHEST
    arrived = from_behind(mr_qkv[:, tokens - length + 1 - prior :], "ctx", 1)
    joined = jnp.concatenate([arrived, mr_qkv], axis=1)
    mixed = short_filter(joined[:, prior:], joined[:, :prior], mr_short_w)
    extended = (mixed[:, :, 1] * mixed[:, :, 2]).astype(jnp.bfloat16)
    queries = mixed[:, length - 1 :, 0]
    own_product = extended[:, length - 1 :]
    mr_conv = toeplitz_taps(extended, mr_filter)
    mr_z = (queries * (mr_conv + mr_skip * own_product.astype(jnp.float32))).astype(jnp.bfloat16)
    mr_flat = mr_z.reshape(sequences * tokens, width)
    mr_terms = jnp.dot(
        mr_flat,
        lax.all_gather(mr_out_w, "ctx", axis=1, tiled=True),
        preferred_element_type=jnp.float32,
    )
    model = mr_terms.shape[1]
    mr_share = lax.psum_scatter(
        mr_terms.reshape(sequences, tokens, model).astype(jnp.bfloat16),
        "tp",
        scatter_dimension=2,
        tiled=True,
    ).astype(jnp.float32)
    residual_mid = (residual_in.astype(jnp.float32) + mr_share).astype(jnp.bfloat16)
    whole_mid = lax.all_gather(residual_mid, "tp", axis=2, tiled=True)
    widened = whole_mid.astype(jnp.float32)
    meansq = jnp.mean(widened * widened, axis=-1, keepdims=True)
    normed = (widened * lax.rsqrt(meansq + 1e-06) * lr_gain).astype(jnp.bfloat16)
    lr_qkv = jnp.dot(
        normed.reshape(sequences * tokens, model),
        lr_in_w.reshape(model, 3 * width),
        preferred_element_type=jnp.float32,
    )
    lr_qkv = lr_qkv.astype(jnp.bfloat16).reshape(sequences, tokens, 3, width)
    lr_edge_rows = from_behind(lr_qkv[:, tokens - prior :], "ctx", 1)
    lr_mixed = short_filter(lr_qkv, lr_edge_rows, lr_short_w)
    lr_u = lr_mixed[:, :, 1] * lr_mixed[:, :, 2]
    span = min(32, length)
    count = tokens // span
    poles = lr_rate.shape[0]
    steps_f = jnp.arange(span, dtype=jnp.float32)
    weight = lr_res * jnp.sqrt(1.0 - jnp.exp(-2.0 * lr_rate))
    powers = jnp.exp(-lr_rate[None] * steps_f[:, None, None])
    kernel = jnp.sum(weight[None] * powers, axis=1)
    offsets = jnp.arange(span)[:, None] - jnp.arange(span)[None, :]
    inner = jnp.where(
        (offsets >= 0)[:, :, None], jnp.take(kernel, jnp.clip(offsets, 0, span - 1), axis=0), 0.0
    )
    lr_blocks = lr_u.reshape(sequences, count, span, width)
    intra = jnp.einsum("ijc,sbjc->sbic", inner, lr_blocks, precision=highest)
    closing = jnp.exp(-lr_rate[None] * (span - 1 - steps_f)[:, None, None])
    block_ends = jnp.einsum("jnc,sbjc->sbnc", closing, lr_blocks, precision=highest)
    opening = weight[None] * jnp.exp(-lr_rate[None] * (steps_f + 1.0)[:, None, None])
    block_decay = jnp.exp(-lr_rate * span)

    def advance(state, block_end):
        return (block_decay * state + block_end, state)

    final, starts = lax.scan(
        advance, jnp.zeros((sequences, poles, width), jnp.float32), jnp.moveaxis(block_ends, 1, 0)
    )
    position = lax.axis_index("ctx")
    piece = lax.all_gather(final[None].astype(jnp.bfloat16), "ctx", axis=0, tiled=True).astype(
        jnp.float32
    )
    index = jnp.arange(piece.shape[0], dtype=jnp.int32)
    distance = jnp.maximum(position - 1 - index, 0).astype(jnp.float32)
    factor = jnp.exp(-lr_rate[None] * tokens * distance[:, None, None])
    factor = jnp.where((index < position)[:, None, None], factor, 0.0)
    entering = jnp.zeros_like(final) + jnp.sum(factor[:, None] * piece, axis=0)
    block_steps = jnp.arange(count, dtype=jnp.float32) * span
    lifted = jnp.exp(-lr_rate[None] * block_steps[:, None, None])
    states = starts + lifted[:, None] * entering[None]
    inflow = jnp.einsum("inc,bsnc->sbic", opening, states, precision=highest)
    lr_conv = (intra + inflow).reshape(sequences, tokens, width)
    lr_z = (lr_mixed[:, :, 0] * (lr_conv + lr_skip * lr_u)).astype(jnp.bfloat16)
    lr_flat = lr_z.reshape(sequences * tokens, width)
    lr_terms = jnp.dot(
        lr_flat,
        lax.all_gather(lr_out_w, "ctx", axis=1, tiled=True),
        preferred_element_type=jnp.float32,
    )
    lr_share = lax.psum_scatter(
        lr_terms.reshape(sequences, tokens, model).astype(jnp.bfloat16),
        "tp",
        scatter_dimension=2,
        tiled=True,
    ).astype(jnp.float32)
    return (residual_mid.astype(jnp.float32) + lr_share).astype(jnp.bfloat16)


def solution(mesh):
    in_specs = (
        P(None, "ctx", "tp"),
        P(None, "ctx", None, "tp"),
        P(None, None, "tp"),
        P(None, "tp"),
        P("tp"),
        P("tp", "ctx"),
        P(),
        P(None, None, "tp"),
        P(None, None, "tp"),
        P(None, "tp"),
        P(None, "tp"),
        P("tp"),
        P("tp", "ctx"),
    )
    out_specs = P(None, "ctx", "tp")
    return jax.shard_map(local, mesh=mesh, in_specs=in_specs, out_specs=out_specs, check_vma=False)
```

profile of v0, /device:TPU:0, one launch (start us, length us, event | category | flops | bytes accessed | tf_op | source)
XLA Modules:
  0.0 776.0 jit_solution(343745663504819711)
XLA Ops:
  7.3 1.9 slice.70
  9.2 2.8 copy.122
  12.0 3.7 collective-permute-start
  15.7 69.9 %gather_fusion.2 = bf16[16384,1024]{1,0:T(8,128)(2,1)} fusion(bf16[128,1024]{1,0:T(8,128)(2,1)S(1)} %copy-done, s32[16384]{0:T(1024)S(1)} %bitcast_clamp_fusion), kind=kCustom, calls=%fused_computation.1.clone | custom fusion | bytes 67174400 | tf_op jit(solution)/shard_map/jit(_take)/gather | solution.py:38
  85.6 46.0 %copy.99 = bf16[128,128,1024]{1,0,2:T(8,128)(2,1)} copy(bf16[128,128,1024]{2,1,0:T(8,128)(2,1)} %bitcast.121) | data formatting | bytes 67108864 | tf_op jit(solution)/shard_map/jit(_take)/gather | solution.py:38
  131.7 69.9 %gather_fusion.1 = bf16[16384,1024]{1,0:T(8,128)(2,1)} fusion(bf16[128,1024]{1,0:T(8,128)(2,1)S(1)} %copy-done, s32[16384]{0:T(1024)S(1)} %bitcast_clamp_fusion.1), kind=kCustom, calls=%fused_computation.clone | custom fusion | bytes 67174400 | tf_op jit(solution)/shard_map/jit(_take)/gather | solution.py:33
  201.6 46.2 %copy.97 = bf16[128,128,1024]{1,0,2:T(8,128)(2,1)} copy(bf16[128,128,1024]{2,1,0:T(8,128)(2,1)} %bitcast.122) | data formatting | bytes 67108864 | tf_op jit(solution)/shard_map/jit(_take)/gather | solution.py:33
  247.9 1.8 copy.93
  251.3 3.5 multiply_add_fusion
  254.8 3.6 copy-done.4
  260.6 3.6 copy.124
  264.3 2.0 copy.123
  266.3 22.9 %fusion = f32[1024,2,2,128]{3,2,1,0:T(2,128)} fusion(bf16[2,2,128,1024]{2,1,0,3:T(2,128)(2,1)} %copy.124, bf16[128,128,1024]{1,0,2:T(8,128)(2,1)} %copy.99, pred[128,128]{1,0:T(8,128)(4,1)S(1)} %get-tuple-element.102, pred[128,128]{1,0:T(8,128)(4,1)S(1)} %get-tuple-element.101), kind=kOutput, calls=%fused_computation.5 | convolution fusion | flops 167772160 | bytes 36732928 | tf_op jit(solution)/shard_map/ijc,sbjc->sbic/dot_general | solution.py:42
  289.2 22.9 %add_bitcast_fusion = f32[2,2,128,1024]{2,1,0,3:T(2,128)} fusion(f32[1024,2,2,128]{3,2,1,0:T(2,128)} %fusion, bf16[2,2,128,1024]{2,1,0,3:T(2,128)(2,1)S(1)} %copy-done.14, bf16[128,128,1024]{1,0,2:T(8,128)(2,1)} %copy.97, pred[128,128]{1,0:T(8,128)(4,1)S(1)} %get-tuple-element.104, pred[128,128]{1,0:T(8,128)(4,1)S(1)} %get-tuple-element.103), kind=kOutput, calls=%fused_computation.81 | convolution fusion | flops 168296448 | bytes 38830080 | tf_op jit(solution)/shard_map/ijc,sbjc->sbic/dot_general | solution.py:41
  312.1 4.5 copy.121
  316.7 2.9 fusion.58
  319.6 9.5 %fusion.36 = bf16[2,256,4096]{2,1,0:T(8,128)(2,1)} fusion(bf16[2,256,1024]{2,1,0:T(8,128)(2,1)S(1)} %fusion.58, bf16[1024,4096]{1,0:T(8,128)(2,1)} %all-gather.5.cloned.1.call-done), kind=kOutput, calls=%fused_computation.49 | convolution fusion | flops 4297064448 | bytes 13631488 | tf_op jit(solution)/shard_map/dot_general | solution.py:76
  329.1 78.3 %reduce-scatter.3.cloned.1.call-done = bf16[2,256,1024]{2,1,0:T(8,128)(2,1)} async-done(((bf16[2,256,4096]{2,1,0:T(8,128)(2,1)}), bf16[2,256,1024]{2,1,0:T(8,128)(2,1)}) %reduce-scatter.3.cloned.1.call-update) | async-done | bytes 1048592 | tf_op jit(solution)/shard_map/reduce_scatter | solution.py:82
  407.4 2.6 add_convert_fusion.1
  410.8 33.6 %copy.101 = bf16[4096,3,1024]{0,2,1:T(8,128)(2,1)} copy(bf16[4096,3,1024]{2,0,1:T(8,128)(2,1)} %param.24) | data formatting | bytes 50331648 | tf_op args[7]
  446.2 12.5 %multiply_reduce_fusion = f32[32,1024]{0,1:T(8,128)} fusion(f32[16,1024]{0,1:T(8,128)S(1)} %copy.108, f32[16,1024]{0,1:T(8,128)S(1)} %copy.107), kind=kLoop, calls=%fused_computation.45 | loop fusion | flops 1540096 | bytes 262144 | tf_op jit(solution)/shard_map/reduce_sum | solution.py:108
  458.7 32.8 %all-gather.7.cloned.1.call-done = bf16[2,256,4096]{2,1,0:T(8,128)(2,1)} async-done(((bf16[2,256,1024]{2,1,0:T(8,128)(2,1)}), bf16[2,256,4096]{2,1,0:T(8,128)(2,1)}) %all-gather.7.cloned.1.call-update) | async-done | bytes 4194320 | tf_op jit(solution)/shard_map/all_gather | solution.py:89
  491.5 3.1 fusion.16
  494.6 5.8 fusion.18
  500.4 20.6 %convolution_convert_fusion = bf16[512,3072]{1,0:T(8,128)(2,1)} fusion(bf16[512,4096]{1,0:T(8,128)(2,1)} %bitcast.127, bf16[4096,3072]{0,1:T(8,128)(2,1)} %bitcast.123), kind=kOutput, calls=%fused_computation.56 | convolution fusion | flops 12886474752 | bytes 32505856 | tf_op jit(solution)/shard_map/dot_general | solution.py:93
  521.0 4.7 copy.102
  525.8 3.8 reshape.181
  529.5 2.9 slice.107
  532.4 4.7 copy.104
  537.2 2.4 collective-permute-start.1
  540.8 5.6 gather_fusion
  546.3 14.3 %copy.110 = f32[32,32,1024]{1,0,2:T(8,128)} copy(f32[32,32,1024]{2,1,0:T(8,128)} %bitcast.124) | data formatting | bytes 8388608 | tf_op jit(solution)/shard_map/jit(_take)/gather | solution.py:111
  560.7 6.8 copy.103
  567.5 5.5 multiply_add_fusion.1
  573.0 2.7 copy-done.3
  576.2 6.3 copy.111
  582.5 18.3 %fusion.48 = f32[8,2,16,1024]{2,0,1,3:T(8,128)} fusion(f32[2,8,32,1024]{2,1,0,3:T(8,128)} %copy.111, f32[32]{0:T(128)S(1)} %iota_subtract_fusion.2, f32[16,1024]{0,1:T(8,128)S(1)} %copy-done.6), kind=kOutput, calls=%fused_computation.64 | convolution fusion | flops 101187584 | bytes 3211392 | tf_op jit(solution)/shard_map/jnc,sbjc->sbnc/dot_general | solution.py:116
  600.8 5.2 copy.113
  606.0 5.9 while.13
  611.9 9.9 %all-gather = bf16[16,16,1024]{2,1,0:T(8,128)(2,1)S(1)} all-gather(bf16[2,16,1024]{2,1,0:T(8,128)(2,1)S(1)} %convert_element_type.103), channel_id=2, replica_groups=mesh['ctx'=8,'tp'=4] {'ctx'}, dimensions={0}, use_global_device_ids=true | all-gather | bytes 589824 | tf_op jit(solution)/shard_map/all_gather | solution.py:127
  623.2 6.4 copy.114
  629.6 29.4 %fusion.8 = f32[1024,2,8,32]{3,2,1,0:T(8,128)S(1)} fusion(f32[2,8,32,1024]{2,1,0,3:T(8,128)} %copy.111, f32[32,32,1024]{1,0,2:T(8,128)} %copy.110, pred[32,32]{1,0:T(8,128)(4,1)S(1)} %get-tuple-element.108, pred[32,32]{1,0:T(8,128)(4,1)S(1)} %get-tuple-element.107), kind=kOutput, calls=%fused_computation.15 | convolution fusion | flops 203423744 | bytes 8390656 | tf_op jit(solution)/shard_map/ijc,sbjc->sbic/dot_general | solution.py:114
  659.0 13.8 %bitcast_add_fusion.1 = f32[2,8,32,1024]{2,1,0,3:T(8,128)} fusion(f32[1024,2,8,32]{3,2,1,0:T(8,128)S(1)} %fusion.8, f32[8,2,16,1024]{2,0,1,3:T(8,128)S(1)} %copy-done.2, f32[32]{0:T(128)S(1)} %iota_add_fusion, f32[16,1024]{0,1:T(8,128)S(1)} %copy-done.6, f32[16,1024]{0,1:T(8,128)S(1)} %copy-done.10), kind=kOutput, calls=%fused_computation.35 | convolution fusion | flops 102236160 | bytes 5374080 | tf_op jit(solution)/shard_map/inc,bsnc->sbic/dot_general | solution.py:138
  672.9 5.1 copy.115
  678.0 3.7 fusion.56
  681.7 9.5 %fusion.39 = bf16[2,256,4096]{2,1,0:T(8,128)(2,1)} fusion(bf16[2,256,1024]{2,1,0:T(8,128)(2,1)S(1)} %fusion.56, bf16[1024,4096]{1,0:T(8,128)(2,1)} %all-gather.9.cloned.1.call-done), kind=kOutput, calls=%fused_computation.50 | convolution fusion | flops 4297064448 | bytes 13631488 | tf_op jit(solution)/shard_map/dot_general | solution.py:142
  691.3 75.4 %reduce-scatter.5.cloned.1.call-done = bf16[2,256,1024]{2,1,0:T(8,128)(2,1)} async-done(((bf16[2,256,4096]{2,1,0:T(8,128)(2,1)}), bf16[2,256,1024]{2,1,0:T(8,128)(2,1)}) %reduce-scatter.5.cloned.1.call-update) | async-done | bytes 1048592 | tf_op jit(solution)/shard_map/reduce_scatter | solution.py:147
  766.6 2.6 add_convert_fusion
  (104 shorter events, 16.2 us)
Async XLA Ops:
  6.5 9.2 %copy-start = (bf16[128,1024]{1,0:T(8,128)(2,1)S(1)}, bf16[128,1024]{1,0:T(8,128)(2,1)}, u32[]{:S(2)}) copy-start(bf16[128,1024]{1,0:T(8,128)(2,1)} %param.20) | copy-start | bytes 786436
  6.5 313.0 %all-gather.5.cloned.1.call-start = ((), (), s32[]{:S(2)}) async-start(), calls=%async_computation.2 | async-start | bytes 9437184 | tf_op jit(solution)/shard_map/all_gather | solution.py:78
  7.3 400.2 %reduce-scatter.3.cloned.1.call-start = ((), (), s32[]{:S(2)}) async-start(), calls=%async_computation.3 | async-start | bytes 5242880 | tf_op jit(solution)/shard_map/reduce_scatter | solution.py:82
  12.0 235.9 %collective-permute-start = (bf16[2,129,3,1024]{3,0,2,1:T(2,128)(2,1)}, bf16[2,129,3,1024]{3,0,2,1:T(2,128)(2,1)}, u32[]{:S(2)}, u32[]{:S(2)}) collective-permute-start(bf16[2,129,3,1024]{3,0,2,1:T(2,128)(2,1)} %copy.122), channel_id=1, source_target_pairs={{0,4},{4,8},{8,12},{12,16},{16,20},{20,24},{24,28},{1,5},{5,9},{9,... | collective-permute-start | bytes 4755464 | tf_op jit(solution)/shard_map/ppermute | solution.py:10
  201.6 46.3 %copy-start.17 = (f32[3,3,1024]{2,1,0:T(4,128)S(1)}, f32[3,3,1024]{2,1,0:T(4,128)}, u32[]{:S(2)}) copy-start(f32[3,3,1024]{2,1,0:T(4,128)} %param.19) | copy-start | bytes 110596
  201.6 48.2 %copy-start.8 = (bf16[2,256,3,1024]{3,1,2,0:T(8,128)(2,1)S(1)}, bf16[2,256,3,1024]{3,1,2,0:T(8,128)(2,1)}, u32[]{:S(2)}) copy-start(bf16[2,256,3,1024]{3,1,2,0:T(8,128)(2,1)} %param.18) | copy-start | bytes 9437188
  254.8 3.7 copy-start.4
  266.3 22.9 %copy-start.14 = (bf16[2,2,128,1024]{2,1,0,3:T(2,128)(2,1)S(1)}, bf16[2,2,128,1024]{2,1,0,3:T(2,128)(2,1)}, u32[]{:S(2)}) copy-start(bf16[2,2,128,1024]{2,1,0,3:T(2,128)(2,1)} %copy.123) | copy-start | bytes 3145732
  289.2 27.4 %copy-start.21 = (f32[1024]{0:T(1024)S(1)}, f32[1024]{0:T(1024)}, u32[]{:S(2)}) copy-start(f32[1024]{0:T(1024)} %param.21) | copy-start | bytes 12292
  319.5 87.9 %copy-start.13 = (bf16[2,256,1024]{2,1,0:T(8,128)(2,1)S(1)}, bf16[2,256,1024]{2,1,0:T(8,128)(2,1)}, u32[]{:S(2)}) copy-start(bf16[2,256,1024]{2,1,0:T(8,128)(2,1)} %param.17) | copy-start | bytes 3145732
  329.1 162.4 %all-gather.7.cloned.1.call-start = ((), (), s32[]{:S(2)}) async-start(), calls=%async_computation.4 | async-start | bytes 5242880 | tf_op jit(solution)/shard_map/all_gather | solution.py:89
  410.1 271.7 %all-gather.9.cloned.1.call-start = ((), (), s32[]{:S(2)}) async-start(), calls=%async_computation.5 | async-start | bytes 9437184 | tf_op jit(solution)/shard_map/all_gather | solution.py:144
  410.6 356.0 %reduce-scatter.5.cloned.1.call-start = ((), (), s32[]{:S(2)}) async-start(), calls=%async_computation.6 | async-start | bytes 5242880 | tf_op jit(solution)/shard_map/reduce_scatter | solution.py:147
  410.7 33.7 %copy-start.15 = (f32[16,1024]{1,0:T(8,128)S(1)}, f32[16,1024]{1,0:T(8,128)}, u32[]{:S(2)}) copy-start(f32[16,1024]{1,0:T(8,128)} %param.26) | copy-start | bytes 196612
  410.7 33.7 %copy-start.16 = (f32[16,1024]{1,0:T(8,128)S(1)}, f32[16,1024]{1,0:T(8,128)}, u32[]{:S(2)}) copy-start(f32[16,1024]{1,0:T(8,128)} %param.27) | copy-start | bytes 196612
  410.8 34.3 %copy-start.18 = (f32[3,3,1024]{2,1,0:T(4,128)S(1)}, f32[3,3,1024]{2,1,0:T(4,128)}, u32[]{:S(2)}) copy-start(f32[3,3,1024]{2,1,0:T(4,128)} %param.25) | copy-start | bytes 110596
  444.4 50.2 %copy-start.19 = (f32[4096]{0:T(1024)S(1)}, f32[4096]{0:T(1024)}, u32[]{:S(2)}) copy-start(f32[4096]{0:T(1024)} %param.23) | copy-start | bytes 49156
  444.7 76.4 %copy-start.5 = (f32[16,1024]{0,1:T(8,128)}, f32[16,1024]{0,1:T(8,128)S(1)}, u32[]{:S(2)}) copy-start(f32[16,1024]{0,1:T(8,128)S(1)} %copy.108) | copy-start | bytes 196612
  444.9 76.2 %copy-start.9 = (f32[16,1024]{0,1:T(8,128)}, f32[16,1024]{0,1:T(8,128)S(1)}, u32[]{:S(2)}) copy-start(f32[16,1024]{0,1:T(8,128)S(1)} %copy.107) | copy-start | bytes 196612
  537.2 30.3 %collective-permute-start.1 = (bf16[2,2,3,1024]{3,1,2,0:T(2,128)(2,1)}, bf16[2,2,3,1024]{3,1,2,0:T(2,128)(2,1)}, u32[]{:S(2)}, u32[]{:S(2)}) collective-permute-start(bf16[2,2,3,1024]{3,1,2,0:T(2,128)(2,1)} %copy.104), channel_id=1, source_target_pairs={{0,4},{4,8},{8,12},{12,16},{16,20},{20,24},{24,28},{1,5},{5,9},{9,... | collective-permute-start | bytes 73736 | tf_op jit(solution)/shard_map/ppermute | solution.py:10
  573.0 2.7 copy-start.3
  575.7 6.9 copy-start.6
  600.8 21.0 %copy-start.11 = (f32[8,16,1024]{2,1,0:T(8,128)S(1)}, f32[8,16,1024]{2,1,0:T(8,128)}, u32[]{:S(2)}) copy-start(f32[8,16,1024]{2,1,0:T(8,128)} %get-tuple-element.105) | copy-start | bytes 1572868
  600.8 21.1 %copy-start.12 = (f32[8,16,1024]{2,1,0:T(8,128)S(1)}, f32[8,16,1024]{2,1,0:T(8,128)}, u32[]{:S(2)}) copy-start(f32[8,16,1024]{2,1,0:T(8,128)} %get-tuple-element.106) | copy-start | bytes 1572868
  629.6 29.4 %copy-start.2 = (f32[8,2,16,1024]{2,0,1,3:T(8,128)S(1)}, f32[8,2,16,1024]{2,0,1,3:T(8,128)}, u32[]{:S(2)}) copy-start(f32[8,2,16,1024]{2,0,1,3:T(8,128)} %copy.114) | copy-start | bytes 3145732
  629.6 29.4 %copy-start.10 = (f32[16,1024]{0,1:T(8,128)S(1)}, f32[16,1024]{0,1:T(8,128)}, u32[]{:S(2)}) copy-start(f32[16,1024]{0,1:T(8,128)} %copy-done.9) | copy-start | bytes 196612
  672.8 5.2 copy-start.20
  681.7 85.0 %copy-start.7 = (bf16[2,256,1024]{2,1,0:T(8,128)(2,1)S(1)}, bf16[2,256,1024]{2,1,0:T(8,128)(2,1)}, u32[]{:S(2)}) copy-start(bf16[2,256,1024]{2,1,0:T(8,128)(2,1)} %add_convert_fusion.1) | copy-start | bytes 3145732
  681.7 87.5 %copy-start.1 = (bf16[128,1024]{1,0:T(8,128)(2,1)S(1)}, bf16[128,1024]{1,0:T(8,128)(2,1)}, u32[]{:S(2)}) copy-start(bf16[128,1024]{1,0:T(8,128)(2,1)} %param.20) | copy-start | bytes 786436
Sparse Core Ops, SparseCore 0:
  9.2 63.7 all-gather.4
  329.2 78.1 reduce-scatter.2
  410.2 81.2 all-gather.6
  493.4 54.4 all-gather.8
  691.4 75.2 reduce-scatter.4
where the time goes:
time: 782 us; the launch traced here: 776 us
  local copies, waits for them, and re-layouts  358 us (46%)
  waiting for transfers between devices  188 us (24%)
  matrix products  147 us (19%)
  other arithmetic  53.4 us (7%)
  between operations  13.8 us (2%)
  blocking collectives  9.85 us (1%)
    gather x2, local copies, waits for them, and re-layouts, toeplitz_taps(): jnp.take(taps, jnp.clip(offsets, 0, length - 1), axis=0)  116 us
    gather x2, local copies, waits for them, and re-layouts, toeplitz_taps(): jnp.take(taps, jnp.clip(offsets + length, 0, length - 1), axis=0)  116 us
    reduce_scatter x1, waiting for transfers between devices, local(): lax.psum_scatter(mr_terms.reshape(sequences, tokens, model).astype(jnp.bf...  78.3 us
    reduce_scatter x1, waiting for transfers between devices, local(): lax.psum_scatter(lr_terms.reshape(sequences, tokens, model).astype(jnp.bf...  75.4 us
    unnamed x49, local copies, waits for them, and re-layouts  53.7 us
    all_gather x1, waiting for transfers between devices, local(): whole_mid = lax.all_gather(residual_mid, 'tp', axis=2, tiled=True)  32.8 us
    dot_general x1, matrix products, local(): intra = jnp.einsum('ijc,sbjc->sbic', inner, lr_blocks, precision=highest)  29.4 us
    dot_general x1, matrix products, toeplitz_taps(): jnp.einsum('ijc,sbjc->sbic', upper, blocks[:, :-1], preferred_element_typ...  22.9 us
  transfers between devices with their start and end apart: 7, of which 3 were waited for; matrix products, arithmetic and copies ran while one was open for 68% of the time, Pallas kernels for 0%

commit v1 on v0

v1 whole, which is shorter than its diff:
```python
import functools

import jax
import jax.numpy as jnp
from jax import lax
from jax.experimental import pallas as pl
from jax.experimental.pallas import tpu as pltpu
from jax.sharding import PartitionSpec as P

F32 = jnp.float32
BF16 = jnp.bfloat16
LANES = 128
SUB = 8
HALO = 16
STEP = 8


def params(mebibytes, **more):
    return pltpu.CompilerParams(vmem_limit_bytes=mebibytes * 2**20, **more)


def vmem(count):
    return [pl.BlockSpec(memory_space=pltpu.VMEM)] * count


def cost(flops, moved):
    return pl.CostEstimate(flops=int(flops), bytes_accessed=int(moved), transcendentals=0)


def tiles(value):
    width = value.shape[-1]
    room = SUB * LANES
    if width < room:
        value = jnp.pad(value, [(0, 0)] * (value.ndim - 1) + [(0, room - width)])
    return value.reshape(value.shape[:-1] + (SUB, LANES)).astype(F32)


def put_rows(flat_ref, first, rows, lane_tile, value):
    flat_ref[pl.ds(first * SUB + lane_tile, rows, stride=SUB), :] = value


def get_rows(flat_ref, first, rows, lane_tile):
    return flat_ref[pl.ds(first * SUB + lane_tile, rows, stride=SUB), :]


def mr_kernel(x_ref, halo_ref, short_ref, filter_ref, skip_ref, z_ref, raw, u, zs):
    _, _, tokens, width = x_ref.shape
    taps = filter_ref.shape[0]
    lags = short_ref.shape[0]
    prior = lags - 1
    for tile in range(width // LANES):
        lanes = slice(tile * LANES, (tile + 1) * LANES)
        put_rows(u, 0, taps, tile, halo_ref[0, :taps, lanes].astype(F32))
        tail = halo_ref[0, taps : taps + HALO, lanes].astype(F32)
        for p in range(3):
            put_rows(raw.at[p], 0, prior, tile, tail[prior * p : prior * (p + 1)])
            put_rows(raw.at[p], prior, tokens, tile, x_ref[0, p, :, lanes].astype(F32))
    raw3 = raw.reshape(3, tokens + prior, SUB, LANES)
    u3 = u.reshape(taps + tokens, SUB, LANES)
    zs3 = zs.reshape(tokens, SUB, LANES)

    def mix(p, first, rows):
        total = short_ref[0, p] * raw3[p, pl.ds(first + prior, rows)]
        for lag in range(1, lags):
            total = total + short_ref[lag, p] * raw3[p, pl.ds(first + prior - lag, rows)]
        return total

    @pl.loop(0, tokens // STEP)
    def _(block):
        first = block * STEP
        product = mix(1, first, STEP) * mix(2, first, STEP)
        u3[pl.ds(taps + first, STEP)] = product.astype(BF16).astype(F32)

    @pl.loop(0, tokens // STEP)
    def _(block):
        first = block * STEP

        def chunk(index, totals):
            tap = index * STEP
            base = first + taps - tap - (STEP - 1)
            window = [u3[base + j] for j in range(2 * STEP - 1)]
            totals = list(totals)
            for k in range(STEP):
                weight = filter_ref[tap + k]
                for t in range(STEP):
                    totals[t] = totals[t] + weight * window[t - k + STEP - 1]
            return tuple(totals)

        nothing = jnp.zeros((SUB, LANES), F32)
        totals = lax.fori_loop(0, taps // STEP, chunk, (nothing,) * STEP)
        queries = mix(0, first, STEP)
        for t in range(STEP):
            zs3[first + t] = queries[t] * (totals[t] + skip_ref[...] * u3[taps + first + t])

    for tile in range(width // LANES):
        lanes = slice(tile * LANES, (tile + 1) * LANES)
        z_ref[:, lanes] = get_rows(zs, 0, tokens, tile).astype(BF16)


def mr_filtered(x, halo, short_w, taps_w, skip, seq):
    _, _, tokens, width = x.shape
    taps = taps_w.shape[0]
    prior = short_w.shape[0] - 1
    rows = halo.shape[1]
    return pl.pallas_call(
        mr_kernel,
        grid=(1,),
        out_shape=jax.ShapeDtypeStruct((tokens, width), BF16),
        in_specs=[
            pl.BlockSpec((1, 3, tokens, width), lambda i: (seq, 0, 0, 0)),
            pl.BlockSpec((1, rows, width), lambda i: (seq, 0, 0)),
            *vmem(3),
        ],
        out_specs=pl.BlockSpec((tokens, width), lambda i: (0, 0)),
        scratch_shapes=[
            pltpu.VMEM((3, (tokens + prior) * SUB, LANES), F32),
            pltpu.VMEM(((taps + tokens) * SUB, LANES), F32),
            pltpu.VMEM((tokens * SUB, LANES), F32),
        ],
        compiler_params=params(32),
        cost_estimate=cost(2.0e10, 4e6),
        name="mr_filtered",
    )(x, halo, short_w, taps_w, skip)


def project_kernel(places, scalar_ref, z_ref, *refs):
    weights, out_ref = refs[:-1], refs[-1]
    width = out_ref.shape[2]
    z = z_ref[...]
    for (offset, piece, whole), weight in zip(places, weights, strict=True):
        columns = weight.shape[1]
        owner = lax.bitwise_xor(scalar_ref[0], offset)
        start = owner * whole + piece * columns
        share = lax.div(start, width)
        lanes = pl.ds(pl.multiple_of(lax.rem(start, width), columns), columns)
        out_ref[share, :, lanes] = jnp.dot(z, weight[...], preferred_element_type=F32).astype(BF16)


def project(z, position, places, weights, shares):
    tokens, width = z.shape
    total = sum(w.shape[1] for w in weights)
    return pl.pallas_call(
        functools.partial(project_kernel, places),
        out_shape=jax.ShapeDtypeStruct((shares, tokens, total // shares), BF16),
        in_specs=[pl.BlockSpec(memory_space=pltpu.SMEM), *vmem(1 + len(weights))],
        out_specs=pl.BlockSpec(memory_space=pltpu.VMEM),
        compiler_params=params(40),
        cost_estimate=cost(2 * tokens * width * total, 2 * total * (width + tokens)),
        name="project",
    )(position, z, *weights)


def swap_gather(block, axis, pieces):
    count = lax.axis_size(axis)
    bits = [1 << k for k in range(count.bit_length() - 1)]
    whole = block.shape[1]
    columns = whole // pieces
    places, arrays = [], []
    for piece in range(pieces):
        far = bits[:0:-1]
        turn = piece % max(1, len(far))
        held = [(0, block[:, piece * columns : (piece + 1) * columns])]
        for bit in far[turn:] + far[:turn] + bits[:1]:
            pairs = [(i, i ^ bit) for i in range(count)]
            held = held + [(offset ^ bit, lax.ppermute(v, axis, pairs)) for offset, v in held]
        places += [(offset, piece, whole) for offset, _ in held]
        arrays += [v for _, v in held]
    return tuple(places), arrays


def add(a, b):
    return (a.astype(F32) + b.astype(F32)).astype(BF16)


def line_scatter(parts, axis):
    count = lax.axis_size(axis)
    place = lax.axis_index(axis)

    def part(share):
        return lax.dynamic_index_in_dim(parts, jnp.clip(share, 0, count - 1), 0, False)

    from_low = from_high = None
    for step in range(1, count):
        up = [(p, p + 1) for p in range(step)]
        down = [(p, p - 1) for p in range(count - step, count)]
        up_share = count - step + place
        down_share = step - count + place
        if step < count - 1 - step:
            value = part(jnp.where(place < step, up_share, down_share))
            if from_low is not None:
                value = add(value, from_low)
            from_low = from_high = lax.ppermute(value, axis, up + down)
        else:
            low, high = part(up_share), part(down_share)
            if from_low is not None:
                low, high = add(low, from_low), add(high, from_high)
            from_low = lax.ppermute(low, axis, up)
            from_high = lax.ppermute(high, axis, down)
    return part(place), from_low, from_high


def line_gather(value, axis):
    count = lax.axis_size(axis)
    place = lax.axis_index(axis)
    low, high = [], []
    up_value = down_value = value
    for step in range(1, count):
        up = [(p, p + 1) for p in range(step - 1, count - 1)]
        down = [(p, p - 1) for p in range(1, count - step + 1)]
        if step - 1 > count - step:
            both = lax.ppermute(jnp.where(place >= step - 1, up_value, down_value), axis, up + down)
            up_value = down_value = both
        else:
            up_value = lax.ppermute(up_value, axis, up)
            down_value = lax.ppermute(down_value, axis, down)
        low.append(up_value)
        high.append(down_value)
    return [value, *low, *high]


def lr_in_kernel(count, scalar_ref, halo_ref, gain_ref, *refs):
    blocks, (w_ref, out_ref, mid, normed) = refs[: 2 * count - 1], refs[2 * count - 1 :]
    tokens, width = blocks[0].shape
    own, low, high = blocks[0], blocks[1:count], blocks[count:]

    @pl.when((pl.program_id(0) == 0) & (pl.program_id(1) == 0))
    def _():
        for share in range(count):
            lanes = pl.ds(share * width, width)
            mid[:HALO, lanes] = halo_ref[share]
            for place in range(count):
                source = own if place == share else (low[place - share - 1] if share < place else high[share - place - 1])

                @pl.when(scalar_ref[0] == place)
                def _(source=source, lanes=lanes):
                    mid[HALO:, lanes] = source[...]

        rows = HALO

        @pl.loop(0, (tokens + HALO) // rows)
        def _(block):
            where = pl.ds(pl.multiple_of(block * rows, rows), rows)
            wide = mid[where, :].astype(F32)
            scale = lax.rsqrt(jnp.mean(wide * wide, axis=-1, keepdims=True) + 1e-6)
            normed[where, :] = (wide * scale * gain_ref[...]).astype(BF16)

    out_ref[0] = jnp.dot(normed[...], w_ref[0], preferred_element_type=F32).astype(BF16)


def lr_in(place, halo, gain, blocks, weight):
    count = halo.shape[0]
    tokens, width = blocks[0].shape
    _, model, out_width = weight.shape
    columns = min(512, out_width)
    rows = tokens + HALO
    return pl.pallas_call(
        functools.partial(lr_in_kernel, count),
        grid=(3, out_width // columns),
        out_shape=jax.ShapeDtypeStruct((3, rows, out_width), BF16),
        in_specs=[
            pl.BlockSpec(memory_space=pltpu.SMEM),
            *vmem(2 + len(blocks)),
            pl.BlockSpec((1, model, columns), lambda p, j: (p, 0, j)),
        ],
        out_specs=pl.BlockSpec((1, rows, columns), lambda p, j: (p, 0, j)),
        scratch_shapes=[pltpu.VMEM((rows, model), BF16), pltpu.VMEM((rows, model), BF16)],
        compiler_params=params(48),
        cost_estimate=cost(6 * rows * model * out_width, 6 * model * out_width),
        name="lr_in",
    )(place, halo, gain, *blocks, weight)


def lr_mix_kernel(x_ref, short_ref, rate_ref, q_ref, u_ref, end_ref, raw):
    _, rows, width = x_ref.shape
    tokens = rows - HALO
    lags = short_ref.shape[0]
    prior = lags - 1
    poles = rate_ref.shape[0]
    for tile in range(width // LANES):
        lanes = slice(tile * LANES, (tile + 1) * LANES)
        for p in range(3):
            wide = x_ref[p, :, lanes].astype(F32)
            put_rows(raw.at[p], 0, rows, tile, wide)
    raw3 = raw.reshape(3, rows, SUB, LANES)
    decay = [jnp.exp(-rate_ref[n]) for n in range(poles)]

    def mix(p, first):
        total = short_ref[0, p] * raw3[p, pl.ds(first + HALO, STEP)]
        for lag in range(1, lags):
            total = total + short_ref[lag, p] * raw3[p, pl.ds(first + HALO - lag, STEP)]
        return total

    def block(index, states):
        first = index * STEP
        q_ref[pl.ds(first, STEP)] = mix(0, first)
        product = mix(1, first) * mix(2, first)
        u_ref[pl.ds(first, STEP)] = product
        states = list(states)
        for t in range(STEP):
            for n in range(poles):
                states[n] = decay[n] * states[n] + product[t]
        return tuple(states)

    nothing = jnp.zeros((SUB, LANES), F32)
    states = lax.fori_loop(0, tokens // STEP, block, (nothing,) * poles)
    for n in range(poles):
        end_ref[n] = states[n].astype(BF16)


def lr_mix(x, short_w, rate):
    _, rows, width = x.shape
    tokens = rows - HALO
    poles = rate.shape[0]
    return pl.pallas_call(
        lr_mix_kernel,
        out_shape=(
            jax.ShapeDtypeStruct((tokens, SUB, LANES), F32),
            jax.ShapeDtypeStruct((tokens, SUB, LANES), F32),
            jax.ShapeDtypeStruct((poles, SUB, LANES), BF16),
        ),
        in_specs=vmem(3),
        out_specs=tuple(vmem(3)),
        scratch_shapes=[pltpu.VMEM((3, rows * SUB, LANES), F32)],
        compiler_params=params(32),
        cost_estimate=cost(4e9, 5e6),
        name="lr_mix",
    )(x, short_w, rate)


def lr_modal_kernel(scalar_ref, q_ref, u_ref, ends_ref, rate_ref, res_ref, skip_ref, z_ref, zs):
    tokens = q_ref.shape[0]
    width = z_ref.shape[1]
    count, poles = ends_ref.shape[:2]
    position = scalar_ref[0]
    decay, weight, enter = [], [], []
    for n in range(poles):
        rate = rate_ref[n]
        decay.append(jnp.exp(-rate))
        weight.append(res_ref[n] * jnp.sqrt(1.0 - jnp.exp(-2.0 * rate)))

        def arrive(index, total, n=n, rate=rate):
            distance = (position - 1 - index).astype(F32)
            return total + jnp.exp(-rate * tokens * distance) * ends_ref[index, n].astype(F32)

        enter.append(lax.fori_loop(0, position, arrive, jnp.zeros((SUB, LANES), F32)))
    zs3 = zs.reshape(tokens, SUB, LANES)

    def block(index, states):
        first = index * STEP
        states = list(states)
        for t in range(STEP):
            value = u_ref[first + t]
            total = skip_ref[...] * value
            for n in range(poles):
                states[n] = decay[n] * states[n] + value
                total = total + weight[n] * states[n]
            zs3[first + t] = q_ref[first + t] * total
        return tuple(states)

    lax.fori_loop(0, tokens // STEP, block, tuple(enter))
    for tile in range(width // LANES):
        lanes = slice(tile * LANES, (tile + 1) * LANES)
        z_ref[:, lanes] = get_rows(zs, 0, tokens, tile).astype(BF16)


def lr_modal(position, q, u, ends, rate, res, skip, width):
    tokens = q.shape[0]
    return pl.pallas_call(
        lr_modal_kernel,
        out_shape=jax.ShapeDtypeStruct((tokens, width), BF16),
        in_specs=[pl.BlockSpec(memory_space=pltpu.SMEM), *vmem(6)],
        out_specs=pl.BlockSpec(memory_space=pltpu.VMEM),
        scratch_shapes=[pltpu.VMEM((tokens * SUB, LANES), F32)],
        compiler_params=params(32),
        cost_estimate=cost(8e9, 4e6),
        name="lr_modal",
    )(position, q, u, ends, rate, res, skip)


def local(
    residual_in,
    mr_qkv,
    mr_short_w,
    mr_filter,
    mr_skip,
    mr_out_w,
    lr_gain,
    lr_in_w,
    lr_short_w,
    lr_rate,
    lr_res,
    lr_skip,
    lr_out_w,
):
    sequences, tokens, _, width = mr_qkv.shape
    taps = mr_filter.shape[0]
    prior = mr_short_w.shape[0] - 1
    ctx, tp = lax.axis_size("ctx"), lax.axis_size("tp")
    position = lax.axis_index("ctx").astype(jnp.int32).reshape(1)
    place = lax.axis_index("tp").astype(jnp.int32).reshape(1)
    onward = [(i, i + 1) for i in range(ctx - 1)]

    tail = mr_qkv[:, tokens - taps - prior :].astype(F32)
    mixed = sum(mr_short_w[lag, 1:] * tail[:, prior - lag : prior - lag + taps, 1:] for lag in range(prior + 1))
    tail_u = (mixed[:, :, 0] * mixed[:, :, 1]).astype(BF16)
    last = jnp.swapaxes(mr_qkv[:, tokens - prior :], 1, 2).reshape(sequences, 3 * prior, width)
    last = jnp.pad(last, ((0, 0), (0, HALO - 3 * prior), (0, 0)))
    halo = lax.ppermute(jnp.concatenate([tail_u, last], axis=1), "ctx", onward)

    places, mr_weights = swap_gather(mr_out_w, "ctx", 2)
    x = jnp.swapaxes(mr_qkv, 1, 2)
    mr_short, lr_short = tiles(mr_short_w), tiles(lr_short_w)
    mr_taps, mr_direct = tiles(mr_filter), tiles(mr_skip)
    rate, res, lr_direct = tiles(lr_rate), tiles(lr_res), tiles(lr_skip)
    in_w = jnp.swapaxes(lr_in_w, 0, 1)
    gain = lr_gain.reshape(1, -1)

    lr_weights = lax.all_gather(lr_out_w, "ctx", axis=0)
    lr_weights = [lr_weights[i] for i in range(ctx)]
    lr_places = tuple((i, 0, lr_out_w.shape[1]) for i in range(ctx))
    zero = jnp.zeros((1,), jnp.int32)

    mids, outs = [], []
    zs = [mr_filtered(x, halo, mr_short, mr_taps, mr_direct, s) for s in range(sequences)]
    for s in range(sequences):
        parts = project(zs[s], position, places, mr_weights, tp)
        own, low, high = line_scatter(parts, "tp")
        total = own.astype(F32) + low.astype(F32) + high.astype(F32)
        mids.append((residual_in[s].astype(F32) + total).astype(BF16))
    xs = []
    for s in range(sequences):
        edge = lax.ppermute(mids[s][tokens - HALO :], "ctx", onward)
        edge = lax.all_gather(edge, "tp", axis=0)
        blocks = line_gather(mids[s], "tp")
        xs.append(lr_in(place, edge, gain, blocks, in_w))
    for s in range(sequences):
        q, u, end = lr_mix(xs[s], lr_short, rate)
        ends = lax.all_gather(end, "ctx", axis=0)
        z = lr_modal(position, q, u, ends, rate, res, lr_direct, width)
        parts = project(z, zero, lr_places, lr_weights, tp)
        own, low, high = line_scatter(parts, "tp")
        total = own.astype(F32) + low.astype(F32) + high.astype(F32)
        outs.append((mids[s].astype(F32) + total).astype(BF16))
    return jnp.stack(outs)


def solution(mesh):
    in_specs = (
        P(None, "ctx", "tp"),
        P(None, "ctx", None, "tp"),
        P(None, None, "tp"),
        P(None, "tp"),
        P("tp"),
        P("tp", "ctx"),
        P(),
        P(None, None, "tp"),
        P(None, None, "tp"),
        P(None, "tp"),
        P(None, "tp"),
        P("tp"),
        P("tp", "ctx"),
    )
    out_specs = P(None, "ctx", "tp")
    return jax.shard_map(local, mesh=mesh, in_specs=in_specs, out_specs=out_specs, check_vma=False)
```

time: 782 us -> 423 us (0.54)
  local copies, waits for them, and re-layouts: 358 us -> 12.8 us
  matrix products: 147 us -> 0 us
  starting transfers between devices: 6.2 us -> 111 us
  Pallas kernels: 0 us -> 81.8 us
  waiting for transfers between devices: 188 us -> 130 us
  blocking collectives: 9.85 us -> 52.3 us
  other arithmetic: 53.4 us -> 18.5 us
    gather x6 -> x0, local copies, waits for them, and re-layouts: 252 us -> none  [the longest x2 116 us: toeplitz_taps(): jnp.take(taps, jnp.clip(offsets, 0, length - 1), axis=0)]
    reduce_scatter x2 -> x0, waiting for transfers between devices: 154 us -> none  [the longest x1 78.3 us: local(): lax.psum_scatter(mr_terms.reshape(sequences, tokens, model).astype(jnp.bf...]
    dot_general x8 -> x0, matrix products: 147 us -> none  [the longest x1 29.4 us: local(): intra = jnp.einsum('ijc,sbjc->sbic', inner, lr_blocks, precision=highest)]
    ppermute x2 -> x47, waiting for transfers between devices: 0.01 us -> 129 us  [the longest x8 44.6 us: line_scatter(): from_low = lax.ppermute(low, axis, up)]
    ppermute x2 -> x47, starting transfers between devices: 6.04 us -> 111 us  [the longest x8 38.7 us: line_scatter(): from_low = lax.ppermute(low, axis, up)]
    pallas_call x0 -> x12, Pallas kernels: none -> 81.8 us  [the longest x2 30.7 us: lr_in(): pl.pallas_call(functools.partial(lr_in_kernel, count), grid=(3, out_width...]
    unnamed x49 -> x53, local copies, waits for them, and re-layouts: 53.7 us -> 6.11 us
    all_gather x1 -> x4, blocking collectives: 9.85 us -> 52.3 us  [the longest x2 34.7 us: local(): edge = lax.all_gather(edge, 'tp', axis=0)]
  transfers between devices with their start and end apart: 7 -> 48, of which waited for: 3 -> 23; matrix products, arithmetic and copies ran while one was open for 68% -> 5% of each run, Pallas kernels for 0% -> 19%
where the time goes in v1:
time: 423 us; the launch traced here: 420 us
  waiting for transfers between devices  130 us (31%)
  starting transfers between devices  111 us (26%)
  Pallas kernels  81.8 us (19%)
  blocking collectives  52.3 us (12%)
  other arithmetic  18.5 us (4%)
  between operations  14.2 us (3%)
  local copies, waits for them, and re-layouts  12.8 us (3%)
    ppermute x8, waiting for transfers between devices, line_scatter(): from_low = lax.ppermute(low, axis, up)  44.6 us
    ppermute x8, starting transfers between devices, line_scatter(): from_low = lax.ppermute(low, axis, up)  38.7 us
    all_gather x2, blocking collectives, local(): edge = lax.all_gather(edge, 'tp', axis=0)  34.7 us
    ppermute x14, waiting for transfers between devices, swap_gather(): lax.ppermute(v, axis, pairs)  34.6 us
    pallas_call x2, Pallas kernels, lr_in(): pl.pallas_call(functools.partial(lr_in_kernel, count), grid=(3, out_width...  30.7 us
    pallas_call x2, Pallas kernels, mr_filtered(): pl.pallas_call(mr_kernel, grid=(1,), out_shape=jax.ShapeDtypeStruct((toke...  29.8 us
    ppermute x14, starting transfers between devices, swap_gather(): lax.ppermute(v, axis, pairs)  22.8 us
    ppermute x4, waiting for transfers between devices, line_scatter(): from_low = from_high = lax.ppermute(value, axis, up + down)  22.1 us
  transfers between devices with their start and end apart: 48, of which 23 were waited for; matrix products, arithmetic and copies ran while one was open for 5% of the time, Pallas kernels for 19%

profile of v1, /device:TPU:0, one launch (start us, length us, event | category | flops | bytes accessed | tf_op | source)
XLA Modules:
  0.0 420.3 jit_solution(2919718476152778638)
XLA Ops:
  12.6 3.3 collective-permute-start
  21.1 18.5 %collective-permute-done.8.refs_9_ = bf16[1024,256]{1,0:T(8,128)(2,1)S(1)} collective-permute-done((bf16[1024,256]{1,0:T(8,128)(2,1)S(1)}, bf16[1024,256]{1,0:T(8,128)(2,1)S(1)}, u32[]{:S(2)}, u32[]{:S(2)}) %collective-permute-start.8) | collective-permute-done | bytes 524320 | tf_op jit(solution)/shard_map/ppermute | solution.py:165
  39.6 14.5 %collective-permute-start.11 = (bf16[1024,256]{1,0:T(8,128)(2,1)S(1)}, bf16[1024,256]{1,0:T(8,128)(2,1)S(1)}, u32[]{:S(2)}, u32[]{:S(2)}) collective-permute-start(bf16[1024,256]{1,0:T(8,128)(2,1)S(1)} %get-tuple-element.43.refs_8_), channel_id=1, source_target_pairs={{0,4},{4,0},{8,12},{12,8},{16,20},{20,16},{24,28},{28,24},{1,5},{5... | collective-permute-start | bytes 1572872 | tf_op jit(solution)/shard_map/ppermute | solution.py:165
  54.2 9.3 %collective-permute-done.9.refs_10_ = bf16[1024,256]{1,0:T(8,128)(2,1)S(1)} collective-permute-done((bf16[1024,256]{1,0:T(8,128)(2,1)S(1)}, bf16[1024,256]{1,0:T(8,128)(2,1)S(1)}, u32[]{:S(2)}, u32[]{:S(2)}) %collective-permute-start.9) | collective-permute-done | bytes 524320 | tf_op jit(solution)/shard_map/ppermute | solution.py:165
  69.5 14.9 %mr_filtered.3.z_ref = bf16[256,1024]{1,0:T(8,128)(2,1)S(1)} custom-call(bf16[2,3,256,1024]{3,2,1,0:T(8,128)(2,1)S(1)} %bitcast.107, bf16[2,144,1024]{2,1,0:T(8,128)(2,1)} %collective-permute-done.halo_ref, f32[3,3,8,128]{3,2,1,0:T(8,128)S(1)} %reshape.84.short_ref, f32[128,8,128]{2,1,0:T(8,128)S(1)} %bitcast.111, f32[8,128]{1,0:T(8,128)S(1)} %bitcast.123), custom_call_target="tpu_custom_call" | custom-call | flops 20000000000 | bytes 4000000 | tf_op jit(solution)/shard_map/mr_filtered/pallas_call | solution.py:105
  85.2 4.3 %collective-permute-done.10.refs_11_ = bf16[1024,256]{1,0:T(8,128)(2,1)S(1)} collective-permute-done((bf16[1024,256]{1,0:T(8,128)(2,1)S(1)}, bf16[1024,256]{1,0:T(8,128)(2,1)S(1)}, u32[]{:S(2)}, u32[]{:S(2)}) %collective-permute-start.10) | collective-permute-done | bytes 524320 | tf_op jit(solution)/shard_map/ppermute | solution.py:165
  92.5 14.9 %mr_filtered.2.z_ref = bf16[256,1024]{1,0:T(8,128)(2,1)S(1)} custom-call(bf16[2,3,256,1024]{3,2,1,0:T(8,128)(2,1)S(1)} %bitcast.108, bf16[2,144,1024]{2,1,0:T(8,128)(2,1)} %collective-permute-done.halo_ref, f32[3,3,8,128]{3,2,1,0:T(8,128)S(1)} %reshape.84.short_ref, f32[128,8,128]{2,1,0:T(8,128)S(1)} %bitcast.112, f32[8,128]{1,0:T(8,128)S(1)} %bitcast.124), custom_call_target="tpu_custom_call" | custom-call | flops 20000000000 | bytes 4000000 | tf_op jit(solution)/shard_map/mr_filtered/pallas_call | solution.py:105
  110.8 4.0 collective-permute-start.31
  120.7 5.8 %collective-permute-done.31 = bf16[256,1024]{1,0:T(8,128)(2,1)} collective-permute-done((bf16[256,1024]{1,0:T(8,128)(2,1)}, bf16[256,1024]{1,0:T(8,128)(2,1)}, u32[]{:S(2)}, u32[]{:S(2)}) %collective-permute-start.31) | collective-permute-done | bytes 524320 | tf_op jit(solution)/shard_map/ppermute | solution.py:192
  128.9 5.2 %collective-permute-start.32 = (bf16[256,1024]{1,0:T(8,128)(2,1)}, bf16[256,1024]{1,0:T(8,128)(2,1)}, u32[]{:S(2)}, u32[]{:S(2)}) collective-permute-start(bf16[256,1024]{1,0:T(8,128)(2,1)} %get-tuple-element.31), channel_id=1, source_target_pairs={{0,1},{1,2},{4,5},{5,6},{8,9},{9,10},{12,13},{13,14},{16,17},{17,1... | collective-permute-start | bytes 1572872 | tf_op jit(solution)/shard_map/ppermute | solution.py:197
  139.1 5.3 %collective-permute-start.16 = (bf16[256,1024]{1,0:T(8,128)(2,1)S(1)}, bf16[256,1024]{1,0:T(8,128)(2,1)}, u32[]{:S(2)}, u32[]{:S(2)}) collective-permute-start(bf16[256,1024]{1,0:T(8,128)(2,1)S(1)} %get-tuple-element.27), channel_id=1, source_target_pairs={{0,1},{1,2},{4,5},{5,6},{8,9},{9,10},{12,13},{13,14},{16,17},{17,1... | collective-permute-start | bytes 1572872 | tf_op jit(solution)/shard_map/ppermute | solution.py:197
  145.9 3.2 collective-permute-done.32
  149.0 2.6 fusion.18
  151.6 5.2 %collective-permute-start.33 = (bf16[256,1024]{1,0:T(8,128)(2,1)}, bf16[256,1024]{1,0:T(8,128)(2,1)}, u32[]{:S(2)}, u32[]{:S(2)}) collective-permute-start(bf16[256,1024]{1,0:T(8,128)(2,1)} %get-tuple-element.39), channel_id=1, source_target_pairs={{0,1},{1,2},{2,3},{4,5},{5,6},{6,7},{8,9},{9,10},{10,11},{12,13},{... | collective-permute-start | bytes 1572872 | tf_op jit(solution)/shard_map/ppermute | solution.py:197
  161.8 5.3 %collective-permute-start.17 = (bf16[256,1024]{1,0:T(8,128)(2,1)S(1)}, bf16[256,1024]{1,0:T(8,128)(2,1)}, u32[]{:S(2)}, u32[]{:S(2)}) collective-permute-start(bf16[256,1024]{1,0:T(8,128)(2,1)S(1)} %get-tuple-element.35), channel_id=1, source_target_pairs={{0,1},{1,2},{2,3},{4,5},{5,6},{6,7},{8,9},{9,10},{10,11},{12,13},{... | collective-permute-start | bytes 1572872 | tf_op jit(solution)/shard_map/ppermute | solution.py:197
  168.6 2.9 collective-permute-done.33
  171.8 9.9 %collective-permute-done.17 = bf16[256,1024]{1,0:T(8,128)(2,1)} collective-permute-done((bf16[256,1024]{1,0:T(8,128)(2,1)S(1)}, bf16[256,1024]{1,0:T(8,128)(2,1)}, u32[]{:S(2)}, u32[]{:S(2)}) %collective-permute-start.17) | collective-permute-done | bytes 524320 | tf_op jit(solution)/shard_map/ppermute | solution.py:197
  182.0 2.9 fusion.31
  184.9 5.0 %collective-permute-start.21 = (bf16[256,1024]{1,0:T(8,128)(2,1)S(1)}, bf16[256,1024]{1,0:T(8,128)(2,1)}, u32[]{:S(2)}, u32[]{:S(2)}) collective-permute-start(bf16[256,1024]{1,0:T(8,128)(2,1)S(1)} %get-tuple-element.41.refs_0_), channel_id=1, source_target_pairs={{0,1},{1,2},{2,3},{4,5},{5,6},{6,7},{8,9},{9,10},{10,11},{12,13},{... | collective-permute-start | bytes 1572872 | tf_op jit(solution)/shard_map/ppermute | solution.py:214
  191.2 5.4 %collective-permute-start.37 = (bf16[256,1024]{1,0:T(8,128)(2,1)S(1)}, bf16[256,1024]{1,0:T(8,128)(2,1)}, u32[]{:S(2)}, u32[]{:S(2)}) collective-permute-start(bf16[256,1024]{1,0:T(8,128)(2,1)S(1)} %get-tuple-element.42.refs_0_), channel_id=1, source_target_pairs={{0,1},{1,2},{2,3},{4,5},{5,6},{6,7},{8,9},{9,10},{10,11},{12,13},{... | collective-permute-start | bytes 1572872 | tf_op jit(solution)/shard_map/ppermute | solution.py:214
  197.8 3.6 collective-permute-done.21.refs_1_
  202.1 4.6 %collective-permute-done.23.refs_4_ = bf16[256,1024]{1,0:T(8,128)(2,1)} collective-permute-done((bf16[256,1024]{1,0:T(8,128)(2,1)S(1)}, bf16[256,1024]{1,0:T(8,128)(2,1)}, u32[]{:S(2)}, u32[]{:S(2)}) %collective-permute-start.23) | collective-permute-done | bytes 524320 | tf_op jit(solution)/shard_map/ppermute | solution.py:215
  208.0 2.8 collective-permute-done.37.refs_1_
  211.5 6.5 %collective-permute-done.39.refs_4_ = bf16[256,1024]{1,0:T(8,128)(2,1)} collective-permute-done((bf16[256,1024]{1,0:T(8,128)(2,1)S(1)}, bf16[256,1024]{1,0:T(8,128)(2,1)}, u32[]{:S(2)}, u32[]{:S(2)}) %collective-permute-start.39) | collective-permute-done | bytes 524320 | tf_op jit(solution)/shard_map/ppermute | solution.py:215
  219.3 9.8 %collective-permute-done.24.refs_5_ = bf16[256,1024]{1,0:T(8,128)(2,1)S(1)} collective-permute-done((bf16[256,1024]{1,0:T(8,128)(2,1)}, bf16[256,1024]{1,0:T(8,128)(2,1)S(1)}, u32[]{:S(2)}, u32[]{:S(2)}) %collective-permute-start.24) | collective-permute-done | bytes 524320 | tf_op jit(solution)/shard_map/ppermute | solution.py:215
  233.5 3.2 collective-permute-start.36
  236.7 21.1 %all-gather = bf16[64,1024]{1,0:T(8,128)(2,1)S(1)} all-gather(bf16[16,1024]{1,0:T(8,128)(2,1)S(1)} %collective-permute-done.20), channel_id=2, replica_groups=mesh['ctx'=8,'tp'=4] {'tp'}, dimensions={0}, use_global_device_ids=true | all-gather | bytes 163840 | tf_op jit(solution)/shard_map/all_gather | solution.py:433
  257.8 13.6 %all-gather.3 = bf16[64,1024]{1,0:T(8,128)(2,1)S(1)} all-gather(bf16[16,1024]{1,0:T(8,128)(2,1)S(1)} %collective-permute-done.36), channel_id=5, replica_groups=mesh['ctx'=8,'tp'=4] {'tp'}, dimensions={0}, use_global_device_ids=true | all-gather | bytes 163840 | tf_op jit(solution)/shard_map/all_gather | solution.py:433
  272.8 15.4 %lr_in.2.x_ref = bf16[3,272,1024]{2,1,0:T(8,128)(2,1)S(1)} custom-call(s32[1]{0:T(128)} %bitcast.16.scalar_ref, bf16[4,16,1024]{2,1,0:T(8,128)(2,1)S(1)} %bitcast.110, f32[1,4096]{1,0:T(1,128)S(1)} %bitcast.115, bf16[256,1024]{1,0:T(8,128)(2,1)S(1)} %get-tuple-element.41.refs_0_, bf16[256,1024]{1,0:T(8,128)(2,1)} %collective-permute-done.21.refs_1_, ...), custom_call_target="tpu_custom_call" | custom-call | flops 6845104128 | bytes 25165824 | tf_op jit(solution)/shard_map/lr_in/pallas_call | solution.py:256
  288.2 2.7 lr_mix.2
  290.9 8.2 %all-gather.1 = bf16[128,8,128]{2,1,0:T(8,128)(2,1)S(1)} all-gather(bf16[16,8,128]{2,1,0:T(8,128)(2,1)S(1)} %get-tuple-element.13), channel_id=3, replica_groups=mesh['ctx'=8,'tp'=4] {'ctx'}, dimensions={0}, use_global_device_ids=true | all-gather | bytes 294912 | tf_op jit(solution)/shard_map/all_gather | solution.py:438
  299.1 15.3 %lr_in.3.x_ref = bf16[3,272,1024]{2,1,0:T(8,128)(2,1)S(1)} custom-call(s32[1]{0:T(128)} %bitcast.16.scalar_ref, bf16[4,16,1024]{2,1,0:T(8,128)(2,1)S(1)} %bitcast.109, f32[1,4096]{1,0:T(1,128)S(1)} %bitcast.116, bf16[256,1024]{1,0:T(8,128)(2,1)S(1)} %get-tuple-element.42.refs_0_, bf16[256,1024]{1,0:T(8,128)(2,1)} %collective-permute-done.37.refs_1_, ...), custom_call_target="tpu_custom_call" | custom-call | flops 6845104128 | bytes 25165824 | tf_op jit(solution)/shard_map/lr_in/pallas_call | solution.py:256
  314.5 2.7 lr_mix.3
  317.2 9.4 %all-gather.4 = bf16[128,8,128]{2,1,0:T(8,128)(2,1)S(1)} all-gather(bf16[16,8,128]{2,1,0:T(8,128)(2,1)S(1)} %get-tuple-element.16), channel_id=6, replica_groups=mesh['ctx'=8,'tp'=4] {'ctx'}, dimensions={0}, use_global_device_ids=true | all-gather | bytes 294912 | tf_op jit(solution)/shard_map/all_gather | solution.py:438
  326.6 3.1 lr_modal.2.z_ref
  329.7 3.1 lr_modal.3.z_ref
  332.9 3.9 fusion.36
  339.2 4.8 %collective-permute-start.26 = (bf16[256,1024]{1,0:T(8,128)(2,1)S(1)}, bf16[256,1024]{1,0:T(8,128)(2,1)S(1)}, u32[]{:S(2)}, u32[]{:S(2)}) collective-permute-start(bf16[256,1024]{1,0:T(8,128)(2,1)S(1)} %dynamic-slice_bitcast_fusion.2), channel_id=1, source_target_pairs={{0,1},{3,2},{4,5},{7,6},{8,9},{11,10},{12,13},{15,14},{16,17},{19,... | collective-permute-start | bytes 1572872 | tf_op jit(solution)/shard_map/ppermute | solution.py:192
  347.7 8.3 %collective-permute-done.26 = bf16[256,1024]{1,0:T(8,128)(2,1)S(1)} collective-permute-done((bf16[256,1024]{1,0:T(8,128)(2,1)S(1)}, bf16[256,1024]{1,0:T(8,128)(2,1)S(1)}, u32[]{:S(2)}, u32[]{:S(2)}) %collective-permute-start.26) | collective-permute-done | bytes 524320 | tf_op jit(solution)/shard_map/ppermute | solution.py:192
  356.4 4.4 %collective-permute-start.27 = (bf16[256,1024]{1,0:T(8,128)(2,1)S(1)}, bf16[256,1024]{1,0:T(8,128)(2,1)S(1)}, u32[]{:S(2)}, u32[]{:S(2)}) collective-permute-start(bf16[256,1024]{1,0:T(8,128)(2,1)S(1)} %get-tuple-element.25), channel_id=1, source_target_pairs={{0,1},{1,2},{4,5},{5,6},{8,9},{9,10},{12,13},{13,14},{16,17},{17,1... | collective-permute-start | bytes 1572872 | tf_op jit(solution)/shard_map/ppermute | solution.py:197
  361.5 5.8 %collective-permute-done.42 = bf16[256,1024]{1,0:T(8,128)(2,1)S(1)} collective-permute-done((bf16[256,1024]{1,0:T(8,128)(2,1)S(1)}, bf16[256,1024]{1,0:T(8,128)(2,1)S(1)}, u32[]{:S(2)}, u32[]{:S(2)}) %collective-permute-start.42) | collective-permute-done | bytes 524320 | tf_op jit(solution)/shard_map/ppermute | solution.py:192
  367.6 4.4 %collective-permute-start.43 = (bf16[256,1024]{1,0:T(8,128)(2,1)S(1)}, bf16[256,1024]{1,0:T(8,128)(2,1)S(1)}, u32[]{:S(2)}, u32[]{:S(2)}) collective-permute-start(bf16[256,1024]{1,0:T(8,128)(2,1)S(1)} %get-tuple-element.29), channel_id=1, source_target_pairs={{0,1},{1,2},{4,5},{5,6},{8,9},{9,10},{12,13},{13,14},{16,17},{17,1... | collective-permute-start | bytes 1572872 | tf_op jit(solution)/shard_map/ppermute | solution.py:197
  372.8 5.8 %collective-permute-done.27 = bf16[256,1024]{1,0:T(8,128)(2,1)S(1)} collective-permute-done((bf16[256,1024]{1,0:T(8,128)(2,1)S(1)}, bf16[256,1024]{1,0:T(8,128)(2,1)S(1)}, u32[]{:S(2)}, u32[]{:S(2)}) %collective-permute-start.27) | collective-permute-done | bytes 524320 | tf_op jit(solution)/shard_map/ppermute | solution.py:197
  378.9 4.4 %collective-permute-start.28 = (bf16[256,1024]{1,0:T(8,128)(2,1)S(1)}, bf16[256,1024]{1,0:T(8,128)(2,1)S(1)}, u32[]{:S(2)}, u32[]{:S(2)}) collective-permute-start(bf16[256,1024]{1,0:T(8,128)(2,1)S(1)} %get-tuple-element.33), channel_id=1, source_target_pairs={{0,1},{1,2},{2,3},{4,5},{5,6},{6,7},{8,9},{9,10},{10,11},{12,13},{... | collective-permute-start | bytes 1572872 | tf_op jit(solution)/shard_map/ppermute | solution.py:197
  384.7 5.1 %collective-permute-done.43 = bf16[256,1024]{1,0:T(8,128)(2,1)S(1)} collective-permute-done((bf16[256,1024]{1,0:T(8,128)(2,1)S(1)}, bf16[256,1024]{1,0:T(8,128)(2,1)S(1)}, u32[]{:S(2)}, u32[]{:S(2)}) %collective-permute-start.43) | collective-permute-done | bytes 524320 | tf_op jit(solution)/shard_map/ppermute | solution.py:197
  390.2 4.4 %collective-permute-start.44 = (bf16[256,1024]{1,0:T(8,128)(2,1)S(1)}, bf16[256,1024]{1,0:T(8,128)(2,1)S(1)}, u32[]{:S(2)}, u32[]{:S(2)}) collective-permute-start(bf16[256,1024]{1,0:T(8,128)(2,1)S(1)} %get-tuple-element.37), channel_id=1, source_target_pairs={{0,1},{1,2},{2,3},{4,5},{5,6},{6,7},{8,9},{9,10},{10,11},{12,13},{... | collective-permute-start | bytes 1572872 | tf_op jit(solution)/shard_map/ppermute | solution.py:197
  395.9 5.1 %collective-permute-done.28 = bf16[256,1024]{1,0:T(8,128)(2,1)S(1)} collective-permute-done((bf16[256,1024]{1,0:T(8,128)(2,1)S(1)}, bf16[256,1024]{1,0:T(8,128)(2,1)S(1)}, u32[]{:S(2)}, u32[]{:S(2)}) %collective-permute-start.28) | collective-permute-done | bytes 524320 | tf_op jit(solution)/shard_map/ppermute | solution.py:197
  401.4 10.6 %collective-permute-done.44 = bf16[256,1024]{1,0:T(8,128)(2,1)S(1)} collective-permute-done((bf16[256,1024]{1,0:T(8,128)(2,1)S(1)}, bf16[256,1024]{1,0:T(8,128)(2,1)S(1)}, u32[]{:S(2)}, u32[]{:S(2)}) %collective-permute-start.44) | collective-permute-done | bytes 524320 | tf_op jit(solution)/shard_map/ppermute | solution.py:197
  (151 shorter events, 71.5 us)
Async XLA Ops:
  6.5 326.4 %all-gather.7.cloned.1.call-start = ((), (), s32[]{:S(2)}) async-start(), calls=%async_computation | async-start | bytes 9437184 | tf_op jit(solution)/shard_map/all_gather | solution.py:418
  12.6 53.4 %collective-permute-start = (bf16[2,144,1024]{2,1,0:T(8,128)(2,1)}, bf16[2,144,1024]{2,1,0:T(8,128)(2,1)}, u32[]{:S(2)}, u32[]{:S(2)}) collective-permute-start(bf16[2,144,1024]{2,1,0:T(8,128)(2,1)} %fusion.32), channel_id=1, source_target_pairs={{0,4},{4,8},{8,12},{12,16},{16,20},{20,24},{24,28},{1,5},{5,9},{9,... | collective-permute-start | bytes 1769480 | tf_op jit(solution)/shard_map/ppermute | solution.py:408
  16.0 23.6 %collective-permute-start.8 = (bf16[1024,256]{1,0:T(8,128)(2,1)S(1)}, bf16[1024,256]{1,0:T(8,128)(2,1)S(1)}, u32[]{:S(2)}, u32[]{:S(2)}) collective-permute-start(bf16[1024,256]{1,0:T(8,128)(2,1)S(1)} %get-tuple-element.43.refs_8_), channel_id=1, source_target_pairs={{0,8},{4,12},{8,0},{12,4},{16,24},{20,28},{24,16},{28,20},{1,9},{5... | collective-permute-start | bytes 1572872 | tf_op jit(solution)/shard_map/ppermute | solution.py:165
  17.8 36.4 %collective-permute-start.1 = (bf16[1024,256]{1,0:T(8,128)(2,1)S(1)}, bf16[1024,256]{1,0:T(8,128)(2,1)S(1)}, u32[]{:S(2)}, u32[]{:S(2)}) collective-permute-start(bf16[1024,256]{1,0:T(8,128)(2,1)S(1)} %get-tuple-element.44.refs_0_), channel_id=1, source_target_pairs={{0,16},{4,20},{8,24},{12,28},{16,0},{20,4},{24,8},{28,12},{1,17},{... | collective-permute-start | bytes 1572872 | tf_op jit(solution)/shard_map/ppermute | solution.py:165
  19.3 44.3 %collective-permute-start.9 = (bf16[1024,256]{1,0:T(8,128)(2,1)S(1)}, bf16[1024,256]{1,0:T(8,128)(2,1)S(1)}, u32[]{:S(2)}, u32[]{:S(2)}) collective-permute-start(bf16[1024,256]{1,0:T(8,128)(2,1)S(1)} %get-tuple-element.43.refs_8_), channel_id=1, source_target_pairs={{0,16},{4,20},{8,24},{12,28},{16,0},{20,4},{24,8},{28,12},{1,17},{... | collective-permute-start | bytes 1572872 | tf_op jit(solution)/shard_map/ppermute | solution.py:165
  19.8 46.3 %collective-permute-start.2 = (bf16[1024,256]{1,0:T(8,128)(2,1)S(1)}, bf16[1024,256]{1,0:T(8,128)(2,1)S(1)}, u32[]{:S(2)}, u32[]{:S(2)}) collective-permute-start(bf16[1024,256]{1,0:T(8,128)(2,1)S(1)} %get-tuple-element.44.refs_0_), channel_id=1, source_target_pairs={{0,8},{4,12},{8,0},{12,4},{16,24},{20,28},{24,16},{28,20},{1,9},{5... | collective-permute-start | bytes 1572872 | tf_op jit(solution)/shard_map/ppermute | solution.py:165
  39.6 44.9 %collective-permute-start.11 = (bf16[1024,256]{1,0:T(8,128)(2,1)S(1)}, bf16[1024,256]{1,0:T(8,128)(2,1)S(1)}, u32[]{:S(2)}, u32[]{:S(2)}) collective-permute-start(bf16[1024,256]{1,0:T(8,128)(2,1)S(1)} %get-tuple-element.43.refs_8_), channel_id=1, source_target_pairs={{0,4},{4,0},{8,12},{12,8},{16,20},{20,16},{24,28},{28,24},{1,5},{5... | collective-permute-start | bytes 1572872 | tf_op jit(solution)/shard_map/ppermute | solution.py:165
  54.2 30.5 %collective-permute-start.4 = (bf16[1024,256]{1,0:T(8,128)(2,1)S(1)}, bf16[1024,256]{1,0:T(8,128)(2,1)S(1)}, u32[]{:S(2)}, u32[]{:S(2)}) collective-permute-start(bf16[1024,256]{1,0:T(8,128)(2,1)S(1)} %get-tuple-element.44.refs_0_), channel_id=1, source_target_pairs={{0,4},{4,0},{8,12},{12,8},{16,20},{20,16},{24,28},{28,24},{1,5},{5... | collective-permute-start | bytes 1572872 | tf_op jit(solution)/shard_map/ppermute | solution.py:165
  63.6 25.9 %collective-permute-start.10 = (bf16[1024,256]{1,0:T(8,128)(2,1)S(1)}, bf16[1024,256]{1,0:T(8,128)(2,1)S(1)}, u32[]{:S(2)}, u32[]{:S(2)}) collective-permute-start(bf16[1024,256]{1,0:T(8,128)(2,1)S(1)} %collective-permute-done.8.refs_9_), channel_id=1, source_target_pairs={{0,16},{4,20},{8,24},{12,28},{16,0},{20,4},{24,8},{28,12},{1,17},{... | collective-permute-start | bytes 1572872 | tf_op jit(solution)/shard_map/ppermute | solution.py:165
  66.0 25.9 %collective-permute-start.12 = (bf16[1024,256]{1,0:T(8,128)(2,1)S(1)}, bf16[1024,256]{1,0:T(8,128)(2,1)S(1)}, u32[]{:S(2)}, u32[]{:S(2)}) collective-permute-start(bf16[1024,256]{1,0:T(8,128)(2,1)S(1)} %collective-permute-done.8.refs_9_), channel_id=1, source_target_pairs={{0,4},{4,0},{8,12},{12,8},{16,20},{20,16},{24,28},{28,24},{1,5},{5... | collective-permute-start | bytes 1572872 | tf_op jit(solution)/shard_map/ppermute | solution.py:165
  66.1 25.9 %collective-permute-start.3 = (bf16[1024,256]{1,0:T(8,128)(2,1)S(1)}, bf16[1024,256]{1,0:T(8,128)(2,1)S(1)}, u32[]{:S(2)}, u32[]{:S(2)}) collective-permute-start(bf16[1024,256]{1,0:T(8,128)(2,1)S(1)} %collective-permute-done.1.refs_1_), channel_id=1, source_target_pairs={{0,8},{4,12},{8,0},{12,4},{16,24},{20,28},{24,16},{28,20},{1,9},{5... | collective-permute-start | bytes 1572872 | tf_op jit(solution)/shard_map/ppermute | solution.py:165
  84.5 22.8 %collective-permute-start.5 = (bf16[1024,256]{1,0:T(8,128)(2,1)S(1)}, bf16[1024,256]{1,0:T(8,128)(2,1)S(1)}, u32[]{:S(2)}, u32[]{:S(2)}) collective-permute-start(bf16[1024,256]{1,0:T(8,128)(2,1)S(1)} %collective-permute-done.1.refs_1_), channel_id=1, source_target_pairs={{0,4},{4,0},{8,12},{12,8},{16,20},{20,16},{24,28},{28,24},{1,5},{5... | collective-permute-start | bytes 1572872 | tf_op jit(solution)/shard_map/ppermute | solution.py:165
  84.6 22.7 %collective-permute-start.13 = (bf16[1024,256]{1,0:T(8,128)(2,1)S(1)}, bf16[1024,256]{1,0:T(8,128)(2,1)S(1)}, u32[]{:S(2)}, u32[]{:S(2)}) collective-permute-start(bf16[1024,256]{1,0:T(8,128)(2,1)S(1)} %collective-permute-done.9.refs_10_), channel_id=1, source_target_pairs={{0,4},{4,0},{8,12},{12,8},{16,20},{20,16},{24,28},{28,24},{1,5},{5... | collective-permute-start | bytes 1572872 | tf_op jit(solution)/shard_map/ppermute | solution.py:165
  89.5 17.9 %collective-permute-start.6 = (bf16[1024,256]{1,0:T(8,128)(2,1)S(1)}, bf16[1024,256]{1,0:T(8,128)(2,1)S(1)}, u32[]{:S(2)}, u32[]{:S(2)}) collective-permute-start(bf16[1024,256]{1,0:T(8,128)(2,1)S(1)} %collective-permute-done.2.refs_2_), channel_id=1, source_target_pairs={{0,4},{4,0},{8,12},{12,8},{16,20},{20,16},{24,28},{28,24},{1,5},{5... | collective-permute-start | bytes 1572872 | tf_op jit(solution)/shard_map/ppermute | solution.py:165
  91.9 15.4 %collective-permute-start.14 = (bf16[1024,256]{1,0:T(8,128)(2,1)S(1)}, bf16[1024,256]{1,0:T(8,128)(2,1)S(1)}, u32[]{:S(2)}, u32[]{:S(2)}) collective-permute-start(bf16[1024,256]{1,0:T(8,128)(2,1)S(1)} %collective-permute-done.10.refs_11_), channel_id=1, source_target_pairs={{0,4},{4,0},{8,12},{12,8},{16,20},{20,16},{24,28},{28,24},{1,5},{5... | collective-permute-start | bytes 1572872 | tf_op jit(solution)/shard_map/ppermute | solution.py:165
  92.0 15.4 %collective-permute-start.7 = (bf16[1024,256]{1,0:T(8,128)(2,1)S(1)}, bf16[1024,256]{1,0:T(8,128)(2,1)S(1)}, u32[]{:S(2)}, u32[]{:S(2)}) collective-permute-start(bf16[1024,256]{1,0:T(8,128)(2,1)S(1)} %collective-permute-done.3.refs_3_), channel_id=1, source_target_pairs={{0,4},{4,0},{8,12},{12,8},{16,20},{20,16},{24,28},{28,24},{1,5},{5... | collective-permute-start | bytes 1572872 | tf_op jit(solution)/shard_map/ppermute | solution.py:165
  110.8 15.8 %collective-permute-start.31 = (bf16[256,1024]{1,0:T(8,128)(2,1)}, bf16[256,1024]{1,0:T(8,128)(2,1)}, u32[]{:S(2)}, u32[]{:S(2)}) collective-permute-start(bf16[256,1024]{1,0:T(8,128)(2,1)} %dynamic-slice_bitcast_fusion.1), channel_id=1, source_target_pairs={{0,1},{3,2},{4,5},{7,6},{8,9},{11,10},{12,13},{15,14},{16,17},{19,... | collective-permute-start | bytes 1572872 | tf_op jit(solution)/shard_map/ppermute | solution.py:192
  118.6 19.0 %collective-permute-start.15 = (bf16[256,1024]{1,0:T(8,128)(2,1)S(1)}, bf16[256,1024]{1,0:T(8,128)(2,1)}, u32[]{:S(2)}, u32[]{:S(2)}) collective-permute-start(bf16[256,1024]{1,0:T(8,128)(2,1)S(1)} %dynamic-slice_bitcast_fusion.3), channel_id=1, source_target_pairs={{0,1},{3,2},{4,5},{7,6},{8,9},{11,10},{12,13},{15,14},{16,17},{19,... | collective-permute-start | bytes 1572872 | tf_op jit(solution)/shard_map/ppermute | solution.py:192
  128.9 20.1 %collective-permute-start.32 = (bf16[256,1024]{1,0:T(8,128)(2,1)}, bf16[256,1024]{1,0:T(8,128)(2,1)}, u32[]{:S(2)}, u32[]{:S(2)}) collective-permute-start(bf16[256,1024]{1,0:T(8,128)(2,1)} %get-tuple-element.31), channel_id=1, source_target_pairs={{0,1},{1,2},{4,5},{5,6},{8,9},{9,10},{12,13},{13,14},{16,17},{17,1... | collective-permute-start | bytes 1572872 | tf_op jit(solution)/shard_map/ppermute | solution.py:197
  134.0 15.0 %collective-permute-start.34 = (bf16[256,1024]{1,0:T(8,128)(2,1)}, bf16[256,1024]{1,0:T(8,128)(2,1)}, u32[]{:S(2)}, u32[]{:S(2)}) collective-permute-start(bf16[256,1024]{1,0:T(8,128)(2,1)} %get-tuple-element.32), channel_id=1, source_target_pairs={{2,1},{3,2},{6,5},{7,6},{10,9},{11,10},{14,13},{15,14},{18,17},{19... | collective-permute-start | bytes 1572872 | tf_op jit(solution)/shard_map/ppermute | solution.py:198
  139.1 21.1 %collective-permute-start.16 = (bf16[256,1024]{1,0:T(8,128)(2,1)S(1)}, bf16[256,1024]{1,0:T(8,128)(2,1)}, u32[]{:S(2)}, u32[]{:S(2)}) collective-permute-start(bf16[256,1024]{1,0:T(8,128)(2,1)S(1)} %get-tuple-element.27), channel_id=1, source_target_pairs={{0,1},{1,2},{4,5},{5,6},{8,9},{9,10},{12,13},{13,14},{16,17},{17,1... | collective-permute-start | bytes 1572872 | tf_op jit(solution)/shard_map/ppermute | solution.py:197
  144.4 15.8 %collective-permute-start.18 = (bf16[256,1024]{1,0:T(8,128)(2,1)S(1)}, bf16[256,1024]{1,0:T(8,128)(2,1)}, u32[]{:S(2)}, u32[]{:S(2)}) collective-permute-start(bf16[256,1024]{1,0:T(8,128)(2,1)S(1)} %get-tuple-element.28), channel_id=1, source_target_pairs={{2,1},{3,2},{6,5},{7,6},{10,9},{11,10},{14,13},{15,14},{18,17},{19... | collective-permute-start | bytes 1572872 | tf_op jit(solution)/shard_map/ppermute | solution.py:198
  151.6 19.9 %collective-permute-start.33 = (bf16[256,1024]{1,0:T(8,128)(2,1)}, bf16[256,1024]{1,0:T(8,128)(2,1)}, u32[]{:S(2)}, u32[]{:S(2)}) collective-permute-start(bf16[256,1024]{1,0:T(8,128)(2,1)} %get-tuple-element.39), channel_id=1, source_target_pairs={{0,1},{1,2},{2,3},{4,5},{5,6},{6,7},{8,9},{9,10},{10,11},{12,13},{... | collective-permute-start | bytes 1572872 | tf_op jit(solution)/shard_map/ppermute | solution.py:197
  156.8 15.0 %collective-permute-start.35 = (bf16[256,1024]{1,0:T(8,128)(2,1)}, bf16[256,1024]{1,0:T(8,128)(2,1)}, u32[]{:S(2)}, u32[]{:S(2)}) collective-permute-start(bf16[256,1024]{1,0:T(8,128)(2,1)} %get-tuple-element.40), channel_id=1, source_target_pairs={{1,0},{2,1},{3,2},{5,4},{6,5},{7,6},{9,8},{10,9},{11,10},{13,12},{... | collective-permute-start | bytes 1572872 | tf_op jit(solution)/shard_map/ppermute | solution.py:198
  161.8 19.9 %collective-permute-start.17 = (bf16[256,1024]{1,0:T(8,128)(2,1)S(1)}, bf16[256,1024]{1,0:T(8,128)(2,1)}, u32[]{:S(2)}, u32[]{:S(2)}) collective-permute-start(bf16[256,1024]{1,0:T(8,128)(2,1)S(1)} %get-tuple-element.35), channel_id=1, source_target_pairs={{0,1},{1,2},{2,3},{4,5},{5,6},{6,7},{8,9},{9,10},{10,11},{12,13},{... | collective-permute-start | bytes 1572872 | tf_op jit(solution)/shard_map/ppermute | solution.py:197
  167.1 14.9 %collective-permute-start.19 = (bf16[256,1024]{1,0:T(8,128)(2,1)S(1)}, bf16[256,1024]{1,0:T(8,128)(2,1)}, u32[]{:S(2)}, u32[]{:S(2)}) collective-permute-start(bf16[256,1024]{1,0:T(8,128)(2,1)S(1)} %get-tuple-element.36), channel_id=1, source_target_pairs={{1,0},{2,1},{3,2},{5,4},{6,5},{7,6},{9,8},{10,9},{11,10},{13,12},{... | collective-permute-start | bytes 1572872 | tf_op jit(solution)/shard_map/ppermute | solution.py:198
  184.9 16.5 %collective-permute-start.21 = (bf16[256,1024]{1,0:T(8,128)(2,1)S(1)}, bf16[256,1024]{1,0:T(8,128)(2,1)}, u32[]{:S(2)}, u32[]{:S(2)}) collective-permute-start(bf16[256,1024]{1,0:T(8,128)(2,1)S(1)} %get-tuple-element.41.refs_0_), channel_id=1, source_target_pairs={{0,1},{1,2},{2,3},{4,5},{5,6},{6,7},{8,9},{9,10},{10,11},{12,13},{... | collective-permute-start | bytes 1572872 | tf_op jit(solution)/shard_map/ppermute | solution.py:214
  189.9 16.8 %collective-permute-start.23 = (bf16[256,1024]{1,0:T(8,128)(2,1)S(1)}, bf16[256,1024]{1,0:T(8,128)(2,1)}, u32[]{:S(2)}, u32[]{:S(2)}) collective-permute-start(bf16[256,1024]{1,0:T(8,128)(2,1)S(1)} %get-tuple-element.41.refs_0_), channel_id=1, source_target_pairs={{1,0},{2,1},{3,2},{5,4},{6,5},{7,6},{9,8},{10,9},{11,10},{13,12},{... | collective-permute-start | bytes 1572872 | tf_op jit(solution)/shard_map/ppermute | solution.py:215
  191.2 19.7 %collective-permute-start.37 = (bf16[256,1024]{1,0:T(8,128)(2,1)S(1)}, bf16[256,1024]{1,0:T(8,128)(2,1)}, u32[]{:S(2)}, u32[]{:S(2)}) collective-permute-start(bf16[256,1024]{1,0:T(8,128)(2,1)S(1)} %get-tuple-element.42.refs_0_), channel_id=1, source_target_pairs={{0,1},{1,2},{2,3},{4,5},{5,6},{6,7},{8,9},{9,10},{10,11},{12,13},{... | collective-permute-start | bytes 1572872 | tf_op jit(solution)/shard_map/ppermute | solution.py:214
  196.5 21.4 %collective-permute-start.39 = (bf16[256,1024]{1,0:T(8,128)(2,1)S(1)}, bf16[256,1024]{1,0:T(8,128)(2,1)}, u32[]{:S(2)}, u32[]{:S(2)}) collective-permute-start(bf16[256,1024]{1,0:T(8,128)(2,1)S(1)} %get-tuple-element.42.refs_0_), channel_id=1, source_target_pairs={{1,0},{2,1},{3,2},{5,4},{6,5},{7,6},{9,8},{10,9},{11,10},{13,12},{... | collective-permute-start | bytes 1572872 | tf_op jit(solution)/shard_map/ppermute | solution.py:215
  201.4 17.8 %collective-permute-start.22 = (bf16[256,1024]{1,0:T(8,128)(2,1)}, bf16[256,1024]{1,0:T(8,128)(2,1)S(1)}, u32[]{:S(2)}, u32[]{:S(2)}) collective-permute-start(bf16[256,1024]{1,0:T(8,128)(2,1)} %collective-permute-done.21.refs_1_), channel_id=1, source_target_pairs={{1,2},{2,3},{5,6},{6,7},{9,10},{10,11},{13,14},{14,15},{17,18},{18... | collective-permute-start | bytes 1572872 | tf_op jit(solution)/shard_map/ppermute | solution.py:214
  206.7 22.4 %collective-permute-start.24 = (bf16[256,1024]{1,0:T(8,128)(2,1)}, bf16[256,1024]{1,0:T(8,128)(2,1)S(1)}, u32[]{:S(2)}, u32[]{:S(2)}) collective-permute-start(bf16[256,1024]{1,0:T(8,128)(2,1)} %collective-permute-done.23.refs_4_), channel_id=1, source_target_pairs={{1,0},{2,1},{5,4},{6,5},{9,8},{10,9},{13,12},{14,13},{17,16},{18,1... | collective-permute-start | bytes 1572872 | tf_op jit(solution)/shard_map/ppermute | solution.py:215
  210.8 60.6 %collective-permute-start.38 = (bf16[256,1024]{1,0:T(8,128)(2,1)}, bf16[256,1024]{1,0:T(8,128)(2,1)S(1)}, u32[]{:S(2)}, u32[]{:S(2)}) collective-permute-start(bf16[256,1024]{1,0:T(8,128)(2,1)} %collective-permute-done.37.refs_1_), channel_id=1, source_target_pairs={{1,2},{2,3},{5,6},{6,7},{9,10},{10,11},{13,14},{14,15},{17,18},{18... | collective-permute-start | bytes 1572872 | tf_op jit(solution)/shard_map/ppermute | solution.py:214
  218.0 53.4 %collective-permute-start.40 = (bf16[256,1024]{1,0:T(8,128)(2,1)}, bf16[256,1024]{1,0:T(8,128)(2,1)S(1)}, u32[]{:S(2)}, u32[]{:S(2)}) collective-permute-start(bf16[256,1024]{1,0:T(8,128)(2,1)} %collective-permute-done.39.refs_4_), channel_id=1, source_target_pairs={{1,0},{2,1},{5,4},{6,5},{9,8},{10,9},{13,12},{14,13},{17,16},{18,1... | collective-permute-start | bytes 1572872 | tf_op jit(solution)/shard_map/ppermute | solution.py:215
  230.7 42.0 %collective-permute-start.25 = (bf16[256,1024]{1,0:T(8,128)(2,1)}, bf16[256,1024]{1,0:T(8,128)(2,1)S(1)}, u32[]{:S(2)}, u32[]{:S(2)}) collective-permute-start(bf16[256,1024]{1,0:T(8,128)(2,1)} %broadcast_select_fusion.1), channel_id=1, source_target_pairs={{2,3},{1,0},{6,7},{5,4},{10,11},{9,8},{14,15},{13,12},{18,19},{17,... | collective-permute-start | bytes 1572872 | tf_op jit(solution)/shard_map/ppermute | solution.py:211
  232.0 4.6 %collective-permute-start.20 = (bf16[16,1024]{1,0:T(8,128)(2,1)S(1)}, bf16[16,1024]{1,0:T(8,128)(2,1)S(1)}, u32[]{:S(2)}, u32[]{:S(2)}) collective-permute-start(bf16[16,1024]{1,0:T(8,128)(2,1)S(1)} %slice.109), channel_id=1, source_target_pairs={{0,4},{4,8},{8,12},{12,16},{16,20},{20,24},{24,28},{1,5},{5,9},{9,... | collective-permute-start | bytes 98312 | tf_op jit(solution)/shard_map/ppermute | solution.py:432
  233.5 24.4 %collective-permute-start.36 = (bf16[16,1024]{1,0:T(8,128)(2,1)S(1)}, bf16[16,1024]{1,0:T(8,128)(2,1)S(1)}, u32[]{:S(2)}, u32[]{:S(2)}) collective-permute-start(bf16[16,1024]{1,0:T(8,128)(2,1)S(1)} %slice.118), channel_id=1, source_target_pairs={{0,4},{4,8},{8,12},{12,16},{16,20},{20,24},{24,28},{1,5},{5,9},{9,... | collective-permute-start | bytes 98312 | tf_op jit(solution)/shard_map/ppermute | solution.py:432
  271.5 27.7 %collective-permute-start.41 = (bf16[256,1024]{1,0:T(8,128)(2,1)S(1)}, bf16[256,1024]{1,0:T(8,128)(2,1)S(1)}, u32[]{:S(2)}, u32[]{:S(2)}) collective-permute-start(bf16[256,1024]{1,0:T(8,128)(2,1)S(1)} %broadcast_select_fusion), channel_id=1, source_target_pairs={{2,3},{1,0},{6,7},{5,4},{10,11},{9,8},{14,15},{13,12},{18,19},{17,... | collective-permute-start | bytes 1572872 | tf_op jit(solution)/shard_map/ppermute | solution.py:211
  339.2 16.9 %collective-permute-start.26 = (bf16[256,1024]{1,0:T(8,128)(2,1)S(1)}, bf16[256,1024]{1,0:T(8,128)(2,1)S(1)}, u32[]{:S(2)}, u32[]{:S(2)}) collective-permute-start(bf16[256,1024]{1,0:T(8,128)(2,1)S(1)} %dynamic-slice_bitcast_fusion.2), channel_id=1, source_target_pairs={{0,1},{3,2},{4,5},{7,6},{8,9},{11,10},{12,13},{15,14},{16,17},{19,... | collective-permute-start | bytes 1572872 | tf_op jit(solution)/shard_map/ppermute | solution.py:192
  346.4 20.9 %collective-permute-start.42 = (bf16[256,1024]{1,0:T(8,128)(2,1)S(1)}, bf16[256,1024]{1,0:T(8,128)(2,1)S(1)}, u32[]{:S(2)}, u32[]{:S(2)}) collective-permute-start(bf16[256,1024]{1,0:T(8,128)(2,1)S(1)} %dynamic-slice_bitcast_fusion), channel_id=1, source_target_pairs={{0,1},{3,2},{4,5},{7,6},{8,9},{11,10},{12,13},{15,14},{16,17},{19,... | collective-permute-start | bytes 1572872 | tf_op jit(solution)/shard_map/ppermute | solution.py:192
  356.4 22.1 %collective-permute-start.27 = (bf16[256,1024]{1,0:T(8,128)(2,1)S(1)}, bf16[256,1024]{1,0:T(8,128)(2,1)S(1)}, u32[]{:S(2)}, u32[]{:S(2)}) collective-permute-start(bf16[256,1024]{1,0:T(8,128)(2,1)S(1)} %get-tuple-element.25), channel_id=1, source_target_pairs={{0,1},{1,2},{4,5},{5,6},{8,9},{9,10},{12,13},{13,14},{16,17},{17,1... | collective-permute-start | bytes 1572872 | tf_op jit(solution)/shard_map/ppermute | solution.py:197
  360.8 17.7 %collective-permute-start.29 = (bf16[256,1024]{1,0:T(8,128)(2,1)S(1)}, bf16[256,1024]{1,0:T(8,128)(2,1)S(1)}, u32[]{:S(2)}, u32[]{:S(2)}) collective-permute-start(bf16[256,1024]{1,0:T(8,128)(2,1)S(1)} %get-tuple-element.26), channel_id=1, source_target_pairs={{2,1},{3,2},{6,5},{7,6},{10,9},{11,10},{14,13},{15,14},{18,17},{19... | collective-permute-start | bytes 1572872 | tf_op jit(solution)/shard_map/ppermute | solution.py:198
  367.6 22.1 %collective-permute-start.43 = (bf16[256,1024]{1,0:T(8,128)(2,1)S(1)}, bf16[256,1024]{1,0:T(8,128)(2,1)S(1)}, u32[]{:S(2)}, u32[]{:S(2)}) collective-permute-start(bf16[256,1024]{1,0:T(8,128)(2,1)S(1)} %get-tuple-element.29), channel_id=1, source_target_pairs={{0,1},{1,2},{4,5},{5,6},{8,9},{9,10},{12,13},{13,14},{16,17},{17,1... | collective-permute-start | bytes 1572872 | tf_op jit(solution)/shard_map/ppermute | solution.py:197
  372.1 17.7 %collective-permute-start.45 = (bf16[256,1024]{1,0:T(8,128)(2,1)S(1)}, bf16[256,1024]{1,0:T(8,128)(2,1)S(1)}, u32[]{:S(2)}, u32[]{:S(2)}) collective-permute-start(bf16[256,1024]{1,0:T(8,128)(2,1)S(1)} %get-tuple-element.30), channel_id=1, source_target_pairs={{2,1},{3,2},{6,5},{7,6},{10,9},{11,10},{14,13},{15,14},{18,17},{19... | collective-permute-start | bytes 1572872 | tf_op jit(solution)/shard_map/ppermute | solution.py:198
  378.9 22.1 %collective-permute-start.28 = (bf16[256,1024]{1,0:T(8,128)(2,1)S(1)}, bf16[256,1024]{1,0:T(8,128)(2,1)S(1)}, u32[]{:S(2)}, u32[]{:S(2)}) collective-permute-start(bf16[256,1024]{1,0:T(8,128)(2,1)S(1)} %get-tuple-element.33), channel_id=1, source_target_pairs={{0,1},{1,2},{2,3},{4,5},{5,6},{6,7},{8,9},{9,10},{10,11},{12,13},{... | collective-permute-start | bytes 1572872 | tf_op jit(solution)/shard_map/ppermute | solution.py:197
  383.4 17.6 %collective-permute-start.30 = (bf16[256,1024]{1,0:T(8,128)(2,1)S(1)}, bf16[256,1024]{1,0:T(8,128)(2,1)S(1)}, u32[]{:S(2)}, u32[]{:S(2)}) collective-permute-start(bf16[256,1024]{1,0:T(8,128)(2,1)S(1)} %get-tuple-element.34), channel_id=1, source_target_pairs={{1,0},{2,1},{3,2},{5,4},{6,5},{7,6},{9,8},{10,9},{11,10},{13,12},{... | collective-permute-start | bytes 1572872 | tf_op jit(solution)/shard_map/ppermute | solution.py:198
  390.2 21.8 %collective-permute-start.44 = (bf16[256,1024]{1,0:T(8,128)(2,1)S(1)}, bf16[256,1024]{1,0:T(8,128)(2,1)S(1)}, u32[]{:S(2)}, u32[]{:S(2)}) collective-permute-start(bf16[256,1024]{1,0:T(8,128)(2,1)S(1)} %get-tuple-element.37), channel_id=1, source_target_pairs={{0,1},{1,2},{2,3},{4,5},{5,6},{6,7},{8,9},{9,10},{10,11},{12,13},{... | collective-permute-start | bytes 1572872 | tf_op jit(solution)/shard_map/ppermute | solution.py:197
  394.6 17.4 %collective-permute-start.46 = (bf16[256,1024]{1,0:T(8,128)(2,1)S(1)}, bf16[256,1024]{1,0:T(8,128)(2,1)S(1)}, u32[]{:S(2)}, u32[]{:S(2)}) collective-permute-start(bf16[256,1024]{1,0:T(8,128)(2,1)S(1)} %get-tuple-element.38), channel_id=1, source_target_pairs={{1,0},{2,1},{3,2},{5,4},{6,5},{7,6},{9,8},{10,9},{11,10},{13,12},{... | collective-permute-start | bytes 1572872 | tf_op jit(solution)/shard_map/ppermute | solution.py:198
  (25 other events, 673.7 us)
Sparse Core Ops, SparseCore 0:
  9.2 85.7 all-gather.6

commit v2 on v1

v2 whole, which is shorter than its diff:
```python
import functools

import jax
import jax.numpy as jnp
from jax import lax
from jax.experimental import pallas as pl
from jax.experimental.pallas import tpu as pltpu
from jax.sharding import PartitionSpec as P

F32 = jnp.float32
BF16 = jnp.bfloat16
LANES = 128
SUB = 8
HALO = 16
STEP = 8


def params(mebibytes, **more):
    return pltpu.CompilerParams(vmem_limit_bytes=mebibytes * 2**20, **more)


def vmem(count):
    return [pl.BlockSpec(memory_space=pltpu.VMEM)] * count


def cost(flops, moved):
    return pl.CostEstimate(flops=int(flops), bytes_accessed=int(moved), transcendentals=0)


def tiles(value):
    width = value.shape[-1]
    room = SUB * LANES
    if width < room:
        value = jnp.pad(value, [(0, 0)] * (value.ndim - 1) + [(0, room - width)])
    return value.reshape(value.shape[:-1] + (SUB, LANES)).astype(F32)


def put_rows(flat_ref, first, rows, lane_tile, value):
    flat_ref[pl.ds(first * SUB + lane_tile, rows, stride=SUB), :] = value


def get_rows(flat_ref, first, rows, lane_tile):
    return flat_ref[pl.ds(first * SUB + lane_tile, rows, stride=SUB), :]


def window_sum(filter_ref, source3, base, chunks, totals):
    def chunk(index, totals):
        tap = index * STEP
        window = [source3[base - tap - (STEP - 1) + j] for j in range(2 * STEP - 1)]
        totals = list(totals)
        for k in range(STEP):
            weight = filter_ref[tap + k]
            for t in range(STEP):
                totals[t] = totals[t] + weight * window[t - k + STEP - 1]
        return tuple(totals)

    return lax.fori_loop(*chunks, chunk, tuple(totals))


def mr_local_kernel(x_ref, short_ref, filter_ref, skip_ref, q_ref, conv_ref, raw, u):
    _, _, tokens, width = x_ref.shape
    taps = filter_ref.shape[0]
    lags = short_ref.shape[0]
    prior = lags - 1
    for tile in range(width // LANES):
        lanes = slice(tile * LANES, (tile + 1) * LANES)
        for p in range(3):
            put_rows(raw.at[p], prior, tokens, tile, x_ref[0, p, :, lanes].astype(F32))
    raw3 = raw.reshape(3, tokens + prior, SUB, LANES)
    u3 = u.reshape(taps + tokens, SUB, LANES)
    for p in range(3):
        raw3[p, :prior] = jnp.zeros((prior, SUB, LANES), F32)

    @pl.loop(0, taps // STEP)
    def _(block):
        u3[pl.ds(block * STEP, STEP)] = jnp.zeros((STEP, SUB, LANES), F32)

    def mix(p, first, rows):
        total = short_ref[0, p] * raw3[p, pl.ds(first + prior, rows)]
        for lag in range(1, lags):
            total = total + short_ref[lag, p] * raw3[p, pl.ds(first + prior - lag, rows)]
        return total

    @pl.loop(0, tokens // STEP)
    def _(block):
        first = block * STEP
        q_ref[pl.ds(first, STEP)] = mix(0, first, STEP)
        product = mix(1, first, STEP) * mix(2, first, STEP)
        u3[pl.ds(taps + first, STEP)] = product.astype(BF16).astype(F32)

    @pl.loop(0, tokens // STEP)
    def _(block):
        first = block * STEP
        totals = [skip_ref[...] * u3[taps + first + t] for t in range(STEP)]
        chunks = (0, lax.min(block + 1, taps // STEP))
        totals = window_sum(filter_ref, u3, taps + first, chunks, totals)
        for t in range(STEP):
            conv_ref[first + t] = totals[t]


def mr_local(x, short_w, taps_w, skip, seq):
    _, _, tokens, width = x.shape
    taps = taps_w.shape[0]
    prior = short_w.shape[0] - 1
    rows = jax.ShapeDtypeStruct((tokens, SUB, LANES), F32)
    return pl.pallas_call(
        mr_local_kernel,
        grid=(1,),
        out_shape=(rows, rows),
        in_specs=[pl.BlockSpec((1, 3, tokens, width), lambda i: (seq, 0, 0, 0)), *vmem(3)],
        out_specs=(pl.BlockSpec((tokens, SUB, LANES), lambda i: (0, 0, 0)),) * 2,
        scratch_shapes=[
            pltpu.VMEM((3, (tokens + prior) * SUB, LANES), F32),
            pltpu.VMEM(((taps + tokens) * SUB, LANES), F32),
        ],
        compiler_params=params(20),
        cost_estimate=cost(1e9, 1e6),
        name="mr_local",
    )(x, short_w, taps_w, skip)


def mr_finish_kernel(x_ref, halo_ref, q_ref, conv_ref, short_ref, filter_ref, skip_ref, z_ref, raw, extra, zs):
    tokens, _, _ = q_ref.shape
    width = z_ref.shape[1]
    taps = filter_ref.shape[0]
    lags = short_ref.shape[0]
    prior = lags - 1
    for tile in range(width // LANES):
        lanes = slice(tile * LANES, (tile + 1) * LANES)
        put_rows(extra, 0, taps, tile, halo_ref[0, :taps, lanes].astype(F32))
        tail = halo_ref[0, taps : taps + HALO, lanes].astype(F32)
        for p in range(3):
            put_rows(raw.at[p], 0, prior, tile, tail[prior * p : prior * (p + 1)])
            put_rows(raw.at[p], prior, prior, tile, x_ref[0, p, :, lanes].astype(F32)[:prior])
    raw3 = raw.reshape(3, 2 * prior, SUB, LANES)
    extra3 = extra.reshape(taps + 2 * STEP, SUB, LANES)
    zs3 = zs.reshape(tokens, SUB, LANES)

    def mix(p, t, lowest):
        total = short_ref[0, p] * raw3[p, prior + t]
        for lag in range(1, lags):
            if prior + t - lag >= lowest:
                total = total + short_ref[lag, p] * raw3[p, prior + t - lag]
        return total

    extra3[taps:] = jnp.zeros((2 * STEP, SUB, LANES), F32)
    for t in range(prior):
        whole = (mix(1, t, 0) * mix(2, t, 0)).astype(BF16).astype(F32)
        alone = (mix(1, t, prior) * mix(2, t, prior)).astype(BF16).astype(F32)
        extra3[taps + t] = whole - alone

    def sums(block):
        first = block * STEP
        chunks = (lax.max(block - 1, 0), taps // STEP)
        totals = [conv_ref[first + t] for t in range(STEP)]
        return first, window_sum(filter_ref, extra3, taps + first, chunks, totals)

    first, totals = sums(0)
    for t in range(STEP):
        if t < prior:
            zs3[t] = mix(0, t, 0) * (totals[t] + skip_ref[...] * extra3[taps + t])
        else:
            zs3[t] = q_ref[t] * totals[t]

    @pl.loop(1, taps // STEP + 1)
    def _(block):
        first, totals = sums(block)
        for t in range(STEP):
            zs3[first + t] = q_ref[first + t] * totals[t]

    @pl.loop(taps // STEP + 1, tokens // STEP)
    def _(block):
        where = pl.ds(block * STEP, STEP)
        zs3[where] = q_ref[where] * conv_ref[where]

    for tile in range(width // LANES):
        lanes = slice(tile * LANES, (tile + 1) * LANES)
        z_ref[:, lanes] = get_rows(zs, 0, tokens, tile).astype(BF16)


def mr_finish(x, halo, q, conv, short_w, taps_w, skip, seq):
    _, _, tokens, width = x.shape
    taps = taps_w.shape[0]
    prior = short_w.shape[0] - 1
    rows = pl.BlockSpec((tokens, SUB, LANES), lambda i: (0, 0, 0))
    return pl.pallas_call(
        mr_finish_kernel,
        grid=(1,),
        out_shape=jax.ShapeDtypeStruct((tokens, width), BF16),
        in_specs=[
            pl.BlockSpec((1, 3, HALO, width), lambda i: (seq, 0, 0, 0)),
            pl.BlockSpec((1, halo.shape[1], width), lambda i: (seq, 0, 0)),
            rows,
            rows,
            *vmem(3),
        ],
        out_specs=pl.BlockSpec((tokens, width), lambda i: (0, 0)),
        scratch_shapes=[
            pltpu.VMEM((3, 2 * prior * SUB, LANES), F32),
            pltpu.VMEM(((taps + 2 * STEP) * SUB, LANES), F32),
            pltpu.VMEM((tokens * SUB, LANES), F32),
        ],
        compiler_params=params(20),
        cost_estimate=cost(1e9, 1e6),
        name="mr_finish",
    )(x, halo, q, conv, short_w, taps_w, skip)


def project_kernel(places, scalar_ref, z_ref, *refs):
    count = len(places)
    weights = refs[:count]
    out_ref, result = refs[-4 - count], refs[-3 - count]
    held, in_sems, out_sems = refs[-2 - count : -2], refs[-2], refs[-1]
    width = out_ref.shape[2]
    copies = [pltpu.make_async_copy(weights[k], held[k], in_sems.at[k]) for k in range(count)]
    for copy in copies:
        copy.start()
    z = z_ref[...]
    sent = []
    begun = 0
    for k, (offset, begin, whole) in enumerate(places):
        columns = held[k].shape[1]
        start = lax.bitwise_xor(scalar_ref[0], offset) * whole + begin
        share = lax.div(start, width)
        lanes = pl.ds(pl.multiple_of(lax.rem(start, width), columns), columns)
        mine = slice(begun, begun + columns)
        begun += columns
        copies[k].wait()
        result[:, mine] = jnp.dot(z, held[k][...], preferred_element_type=F32).astype(BF16)
        sent.append(pltpu.make_async_copy(result.at[:, mine], out_ref.at[share, :, lanes], out_sems.at[k]))
        sent[-1].start()
    for copy in sent:
        copy.wait()


def project(z, position, places, weights, shares, given=None):
    tokens, width = z.shape
    total = sum(w.shape[1] for w in weights)
    model = places[0][2] * lax.axis_size("ctx")
    extra = [] if given is None else [given]
    anywhere = pl.BlockSpec(memory_space=pl.ANY)
    return pl.pallas_call(
        functools.partial(project_kernel, places),
        out_shape=jax.ShapeDtypeStruct((shares, tokens, model // shares), BF16),
        in_specs=[
            pl.BlockSpec(memory_space=pltpu.SMEM),
            *vmem(1),
            *[anywhere] * (len(weights) + len(extra)),
        ],
        out_specs=anywhere,
        scratch_shapes=[
            pltpu.VMEM((tokens, total), BF16),
            *[pltpu.VMEM(w.shape, w.dtype) for w in weights],
            pltpu.SemaphoreType.DMA((len(weights),)),
            pltpu.SemaphoreType.DMA((len(weights),)),
        ],
        input_output_aliases={2 + len(weights): 0} if extra else {},
        compiler_params=params(16),
        cost_estimate=cost(2 * tokens * width * total, 2 * total * (width + tokens)),
        name="project",
    )(position, z, *weights, *extra)


def after(value, *others):
    return lax.optimization_barrier((value, *others))[0]


def swap_pairs(axis, bit):
    return [(i, i ^ bit) for i in range(lax.axis_size(axis))]


def swap_gather(block, axis, middle=None, late=None):
    count = lax.axis_size(axis)
    far = [1 << k for k in range(count.bit_length() - 1, 0, -1) if 1 << k < count]
    whole = block.shape[1]
    have = {(0, 0): block}
    for bit in far:
        have[bit, 0] = lax.ppermute(block, axis, swap_pairs(axis, bit))
    near = dict(have)
    pieces = 1 << max(1, len(far)).bit_length() - 1
    columns = whole // pieces
    for piece in range(pieces if far else 0):
        begin = piece * columns
        part = {bit: have[bit, 0][:, begin : begin + columns] for bit in far}
        order = far[piece:] + far[:piece]
        known = [order[0]]
        for bit in order[1:]:
            for offset in list(known):
                value = part[offset] if middle is None else after(part[offset], middle)
                part[offset ^ bit] = lax.ppermute(value, axis, swap_pairs(axis, bit))
                have[offset ^ bit, begin] = part[offset ^ bit]
                known.append(offset ^ bit)
            known.append(bit)
    for key in list(have):
        value = have[key]
        if key in near:
            value = value if middle is None else after(value, middle)
        else:
            value = value if late is None else after(value, late)
        have[key[0] ^ 1, key[1]] = lax.ppermute(value, axis, swap_pairs(axis, 1))
    return tuple((offset, begin, whole) for offset, begin in have), list(have.values())


def add(a, b):
    return (a.astype(F32) + b.astype(F32)).astype(BF16)


def line_scatter(parts, axis):
    count = lax.axis_size(axis)
    place = lax.axis_index(axis)

    def part(share):
        return lax.dynamic_index_in_dim(parts, jnp.clip(share, 0, count - 1), 0, False)

    from_low = from_high = None
    for step in range(1, count):
        up = [(p, p + 1) for p in range(step)]
        down = [(p, p - 1) for p in range(count - step, count)]
        up_share = count - step + place
        down_share = step - count + place
        if step < count - 1 - step:
            value = part(jnp.where(place < step, up_share, down_share))
            if from_low is not None:
                value = add(value, from_low)
            from_low = from_high = lax.ppermute(value, axis, up + down)
        else:
            low, high = part(up_share), part(down_share)
            if from_low is not None:
                low, high = add(low, from_low), add(high, from_high)
            from_low = lax.ppermute(low, axis, up)
            from_high = lax.ppermute(high, axis, down)
    return part(place), from_low, from_high


def line_gather(value, axis):
    count = lax.axis_size(axis)

    def move(what, *pairs):
        return lax.ppermute(what, axis, pairs)

    if count == 4:
        outer = move(value, (0, 1), (1, 0), (2, 3), (3, 2))
        inner = move(value, (1, 2), (2, 1))
        crossed = move(outer, (1, 2), (2, 1))
        outward = move(inner, (1, 0), (2, 3))
        last = move(crossed, (1, 0), (2, 3))
        table = ((0, 1, 4, 5), (1, 0, 2, 3), (3, 2, 0, 1), (5, 4, 1, 0))
        return [value, outer, inner, crossed, outward, last], table
    low, high = [value], [value]
    for step in range(1, count):
        low.append(move(low[-1], *[(p, p + 1) for p in range(step - 1, count - 1)]))
        high.append(move(high[-1], *[(p, p - 1) for p in range(1, count - step + 1)]))
    table = tuple(
        tuple(place - share if share <= place else count - 1 + share - place for share in range(count))
        for place in range(count)
    )
    return low + high[1:], table


def lr_in_kernel(table, scalar_ref, gain_ref, *refs):
    count = len(table)
    *blocks, w_ref, out_ref, mid, normed, held, sems = refs
    tokens, width = blocks[0].shape
    parts, _, _, columns = held.shape
    copies = []
    for k in range(parts):
        p, begin = divmod(k * columns, width)
        copies.append(pltpu.make_async_copy(w_ref.at[p, :, pl.ds(begin, columns)], held.at[k, 0], sems.at[k]))
        copies[-1].start()
    for share in range(count):
        lanes = pl.ds(share * width, width)
        for place in range(count):

            @pl.when(scalar_ref[0] == place)
            def _(source=blocks[table[place][share]], lanes=lanes):
                mid[:, lanes] = source[...]

    @pl.loop(0, tokens // HALO)
    def _(block):
        where = pl.ds(pl.multiple_of(block * HALO, HALO), HALO)
        wide = mid[where, :].astype(F32)
        scale = lax.rsqrt(jnp.mean(wide * wide, axis=-1, keepdims=True) + 1e-6)
        normed[where, :] = (wide * scale * gain_ref[...]).astype(BF16)

    for k in range(parts):
        p, begin = divmod(k * columns, width)
        copies[k].wait()
        total = jnp.dot(normed[...], held[k, 0], preferred_element_type=F32)
        out_ref[p, :, begin : begin + columns] = total.astype(BF16)


def lr_in(place, gain, blocks, table, weight):
    tokens, width = blocks[0].shape
    _, model, _ = weight.shape
    columns = min(512, width)
    parts = 3 * width // columns
    return pl.pallas_call(
        functools.partial(lr_in_kernel, table),
        out_shape=jax.ShapeDtypeStruct((3, tokens, width), BF16),
        in_specs=[
            pl.BlockSpec(memory_space=pltpu.SMEM),
            *vmem(1 + len(blocks)),
            pl.BlockSpec(memory_space=pl.ANY),
        ],
        out_specs=pl.BlockSpec(memory_space=pltpu.VMEM),
        scratch_shapes=[
            pltpu.VMEM((tokens, model), BF16),
            pltpu.VMEM((tokens, model), BF16),
            pltpu.VMEM((parts, 1, model, columns), BF16),
            pltpu.SemaphoreType.DMA((parts,)),
        ],
        compiler_params=params(40),
        cost_estimate=cost(6 * tokens * model * width, 6 * model * width),
        name="lr_in",
    )(place, gain, *blocks, weight)


def lr_mix_kernel(x_ref, short_ref, rate_ref, q_ref, u_ref, send_ref, raw):
    _, tokens, width = x_ref.shape
    lags = short_ref.shape[0]
    prior = lags - 1
    poles = rate_ref.shape[0]
    for tile in range(width // LANES):
        lanes = slice(tile * LANES, (tile + 1) * LANES)
        for p in range(3):
            put_rows(raw.at[p], prior, tokens, tile, x_ref[p, :, lanes].astype(F32))
    raw3 = raw.reshape(3, tokens + prior, SUB, LANES)
    for p in range(3):
        raw3[p, :prior] = jnp.zeros((prior, SUB, LANES), F32)
    decay = [jnp.exp(-rate_ref[n]) for n in range(poles)]

    def mix(p, first):
        total = short_ref[0, p] * raw3[p, pl.ds(first + prior, STEP)]
        for lag in range(1, lags):
            total = total + short_ref[lag, p] * raw3[p, pl.ds(first + prior - lag, STEP)]
        return total

    def block(index, states):
        first = index * STEP
        q_ref[pl.ds(first, STEP)] = mix(0, first)
        product = mix(1, first) * mix(2, first)
        u_ref[pl.ds(first, STEP)] = product
        states = list(states)
        for t in range(STEP):
            for n in range(poles):
                states[n] = decay[n] * states[n] + product[t]
        return tuple(states)

    nothing = jnp.zeros((SUB, LANES), F32)
    states = lax.fori_loop(0, tokens // STEP, block, (nothing,) * poles)
    rows = [*states]
    rows += [raw3[p, prior + j] for p in (1, 2) for j in range(prior)]
    rows += [raw3[p, tokens + j] for p in range(3) for j in range(prior)]
    for n, row in enumerate(rows):
        send_ref[n] = row.astype(BF16)
    for n in range(len(rows), send_ref.shape[0]):
        send_ref[n] = jnp.zeros((SUB, LANES), BF16)


def lr_mix(x, short_w, rate):
    _, tokens, width = x.shape
    poles = rate.shape[0]
    prior = short_w.shape[0] - 1
    sent = -(-(poles + 5 * prior) // HALO) * HALO
    return pl.pallas_call(
        lr_mix_kernel,
        out_shape=(
            jax.ShapeDtypeStruct((tokens, SUB, LANES), F32),
            jax.ShapeDtypeStruct((tokens, SUB, LANES), F32),
            jax.ShapeDtypeStruct((sent, SUB, LANES), BF16),
        ),
        in_specs=vmem(3),
        out_specs=tuple(vmem(3)),
        scratch_shapes=[pltpu.VMEM((3, (tokens + prior) * SUB, LANES), F32)],
        compiler_params=params(16),
        cost_estimate=cost(1e9, 1e6),
        name="lr_mix",
    )(x, short_w, rate)


def lr_modal_kernel(scalar_ref, q_ref, u_ref, sent_ref, short_ref, rate_ref, res_ref, skip_ref, z_ref, zs, change):
    tokens = q_ref.shape[0]
    width = z_ref.shape[1]
    lags = short_ref.shape[0]
    prior = lags - 1
    poles = rate_ref.shape[0]
    position = scalar_ref[0]
    zs3 = zs.reshape(tokens, SUB, LANES)

    def head(index, p, j):
        return sent_ref[index, poles + (p - 1) * prior + j].astype(F32)

    def tail(index, p, j):
        return sent_ref[index, poles + 2 * prior + p * prior + j].astype(F32)

    def missed(index, p, t):
        total = short_ref[t + 1, p] * tail(index - 1, p, prior - 1)
        for lag in range(t + 2, lags):
            total = total + short_ref[lag, p] * tail(index - 1, p, prior + t - lag)
        return total

    def had(index, p, t):
        total = short_ref[0, p] * head(index, p, t)
        for lag in range(1, t + 1):
            total = total + short_ref[lag, p] * head(index, p, t - lag)
        return total

    def change_of_u(index, t):
        key, value = had(index, 1, t), had(index, 2, t)
        more_key, more_value = missed(index, 1, t), missed(index, 2, t)
        return key * more_value + more_key * value + more_key * more_value

    nothing = jnp.zeros((SUB, LANES), F32)
    change[0] = jnp.zeros((prior, SUB, LANES), F32)

    @pl.loop(1, position + 1)
    def _(index):
        for t in range(prior):
            change[index, t] = change_of_u(index, t)

    decay, weight, enter = [], [], []
    for n in range(poles):
        rate = rate_ref[n]
        decay.append(jnp.exp(-rate))
        weight.append(res_ref[n] * jnp.sqrt(1.0 - jnp.exp(-2.0 * rate)))

        def arrive(index, total, n=n, rate=rate):
            distance = (position - 1 - index).astype(F32)
            end = sent_ref[index, n].astype(F32)
            for t in range(prior):
                end = end + jnp.exp(-rate * (tokens - 1 - t)) * change[index, t]
            return total + jnp.exp(-rate * tokens * distance) * end

        enter.append(lax.fori_loop(0, position, arrive, nothing))

    first_u, first_q = [], []
    for t in range(prior):
        first_u.append(u_ref[t] + change[position, t])
        before = lax.max(position, 1)
        first_q.append(q_ref[t] + jnp.where(position > 0, missed(before, 0, t), 0.0))

    def row(states, value, query):
        total = skip_ref[...] * value
        for n in range(poles):
            states[n] = decay[n] * states[n] + value
            total = total + weight[n] * states[n]
        return query * total

    states = list(enter)
    for t in range(STEP):
        value, query = (first_u[t], first_q[t]) if t < prior else (u_ref[t], q_ref[t])
        zs3[t] = row(states, value, query)

    def block(index, states):
        first = index * STEP
        states = list(states)
        for t in range(STEP):
            zs3[first + t] = row(states, u_ref[first + t], q_ref[first + t])
        return tuple(states)

    lax.fori_loop(1, tokens // STEP, block, tuple(states))
    for tile in range(width // LANES):
        lanes = slice(tile * LANES, (tile + 1) * LANES)
        z_ref[:, lanes] = get_rows(zs, 0, tokens, tile).astype(BF16)


def lr_modal(position, q, u, sent, short_w, rate, res, skip, width):
    tokens = q.shape[0]
    prior = short_w.shape[0] - 1
    return pl.pallas_call(
        lr_modal_kernel,
        out_shape=jax.ShapeDtypeStruct((tokens, width), BF16),
        in_specs=[pl.BlockSpec(memory_space=pltpu.SMEM), *vmem(7)],
        out_specs=pl.BlockSpec(memory_space=pltpu.VMEM),
        scratch_shapes=[
            pltpu.VMEM((tokens * SUB, LANES), F32),
            pltpu.VMEM((sent.shape[0], prior, SUB, LANES), F32),
        ],
        compiler_params=params(16),
        cost_estimate=cost(1e9, 1e6),
        name="lr_modal",
    )(position, q, u, sent, short_w, rate, res, skip)


def local(
    residual_in,
    mr_qkv,
    mr_short_w,
    mr_filter,
    mr_skip,
    mr_out_w,
    lr_gain,
    lr_in_w,
    lr_short_w,
    lr_rate,
    lr_res,
    lr_skip,
    lr_out_w,
):
    sequences, tokens, _, width = mr_qkv.shape
    taps = mr_filter.shape[0]
    prior = mr_short_w.shape[0] - 1
    ctx, tp = lax.axis_size("ctx"), lax.axis_size("tp")
    position = lax.axis_index("ctx").astype(jnp.int32).reshape(1)
    place = lax.axis_index("tp").astype(jnp.int32).reshape(1)
    onward = [(i, i + 1) for i in range(ctx - 1)]

    tail = mr_qkv[:, tokens - taps - prior :].astype(F32)
    mixed = sum(mr_short_w[lag, 1:] * tail[:, prior - lag : prior - lag + taps, 1:] for lag in range(prior + 1))
    tail_u = (mixed[:, :, 0] * mixed[:, :, 1]).astype(BF16)
    last = jnp.swapaxes(mr_qkv[:, tokens - prior :], 1, 2).reshape(sequences, 3 * prior, width)
    last = jnp.pad(last, ((0, 0), (0, HALO - 3 * prior), (0, 0)))
    halo = lax.ppermute(jnp.concatenate([tail_u, last], axis=1), "ctx", onward)

    x = jnp.swapaxes(mr_qkv, 1, 2)
    mr_short, lr_short = tiles(mr_short_w), tiles(lr_short_w)
    mr_taps, mr_direct = tiles(mr_filter), tiles(mr_skip)
    rate, res, lr_direct = tiles(lr_rate), tiles(lr_res), tiles(lr_skip)
    in_w = jnp.swapaxes(lr_in_w, 0, 1)
    gain = lr_gain.reshape(1, -1)

    own = [mr_local(x, mr_short, mr_taps, mr_direct, s) for s in range(sequences)]
    zs = [mr_finish(x, halo, *own[s], mr_short, mr_taps, mr_direct, s) for s in range(sequences)]
    places, mr_weights = swap_gather(mr_out_w, "ctx", own[-1][0], zs[-1])
    early = [k for k, (offset, _, whole) in enumerate(places) if mr_weights[k].shape[1] == whole]
    late = [k for k in range(len(places)) if k not in early]

    def project_pieces(z):
        terms = None
        for ks in (early, late):
            if ks:
                terms = project(z, position, tuple(places[k] for k in ks), [mr_weights[k] for k in ks], tp, terms)
        return terms

    parts = [project_pieces(z) for z in zs]
    lr_places, lr_weights = swap_gather(after(lr_out_w, parts[-1]), "ctx")

    mids, blocks, outs = [], [], []
    before = lr_weights[: -len(late) // 2]
    for s in range(sequences):
        share = lax.psum_scatter(after(parts[s], *parts[:s]), "tp", scatter_dimension=0)
        mid = (residual_in[s].astype(F32) + after(share, *before).astype(F32)).astype(BF16)
        mid = lax.optimization_barrier(mid)
        mids.append(mid)
        arrays, table = line_gather(mid, "tp")
        blocks.append(arrays)
        before = [*lr_weights, *arrays]
    for s in range(sequences):
        more = blocks[s + 1] if s + 1 < sequences else None
        x = lr_in(place, gain, blocks[s], table, in_w)
        if more:
            x = after(x, *more[1:3])
        q, u, send = lr_mix(x, lr_short, rate)
        sent = lax.all_gather(send, "ctx", axis=0)
        if more:
            sent = after(sent, *more[3:5])
        z = lr_modal(position, q, u, sent, lr_short, rate, res, lr_direct, width)
        share = lax.psum_scatter(project(z, position, lr_places, lr_weights, tp), "tp", scatter_dimension=0)
        outs.append((mids[s].astype(F32) + share.astype(F32)).astype(BF16))
    return jnp.stack(outs)


def solution(mesh):
    in_specs = (
        P(None, "ctx", "tp"),
        P(None, "ctx", None, "tp"),
        P(None, None, "tp"),
        P(None, "tp"),
        P("tp"),
        P("tp", "ctx"),
        P(),
        P(None, None, "tp"),
        P(None, None, "tp"),
        P(None, "tp"),
        P(None, "tp"),
        P("tp"),
        P("tp", "ctx"),
    )
    out_specs = P(None, "ctx", "tp")
    return jax.shard_map(local, mesh=mesh, in_specs=in_specs, out_specs=out_specs, check_vma=False)
```

time: 423 us -> 384 us (0.908)
  starting transfers between devices: 111 us -> 28.3 us
  waiting for transfers between devices: 130 us -> 196 us
  blocking collectives: 52.3 us -> 24 us
  Pallas kernels: 81.8 us -> 93.6 us
  other arithmetic: 18.5 us -> 9.9 us
  local copies, waits for them, and re-layouts: 12.8 us -> 17.4 us
    ppermute x46 -> x28, starting transfers between devices: 107 us -> 26 us  [the longest x10 11.9 us: move(): return lax.ppermute(what, axis, pairs)]
    reduce_scatter x0 -> x4, waiting for transfers between devices: none -> 42.6 us  [the longest x2 41.6 us: local(): lax.psum_scatter(project(z, position, lr_places, lr_weights, tp), 'tp', s...]
    all_gather x4 -> x2, blocking collectives: 52.3 us -> 24 us  [local(): sent = lax.all_gather(send, 'ctx', axis=0)]
    ppermute x46 -> x28, waiting for transfers between devices: 129 us -> 154 us  [the longest x10 104 us: move(): return lax.ppermute(what, axis, pairs)]
    pallas_call x4 -> x6, Pallas kernels: 9.66 us -> 27.9 us  [project(): pl.pallas_call(functools.partial(project_kernel, places), out_shape=jax.S...]
    convert_element_type x9 -> x2, other arithmetic: 12.2 us -> 2.78 us  [local(): (residual_in[s].astype(F32) + after(share, *before).astype(F32)).astype(B...]
    unnamed x53 -> x89, local copies, waits for them, and re-layouts: 6.11 us -> 15.1 us
    pallas_call x4 -> x6, Pallas kernels: 60.5 us -> 54.2 us  [the longest x2 23.4 us: lr_in(): pl.pallas_call(functools.partial(lr_in_kernel, table), out_shape=jax.Shap...]
  transfers between devices with their start and end apart: 48 -> 33, of which waited for: 23 -> 15; matrix products, arithmetic and copies ran while one was open for 5% -> 2% of each run, Pallas kernels for 19% -> 21%
where the time goes in v2:
time: 384 us; the launch traced here: 383 us
  waiting for transfers between devices  196 us (51%)
  Pallas kernels  93.6 us (24%)
  starting transfers between devices  28.3 us (7%)
  blocking collectives  24 us (6%)
  local copies, waits for them, and re-layouts  17.4 us (5%)
  between operations  14 us (4%)
  other arithmetic  9.9 us (3%)
    ppermute x10, waiting for transfers between devices, move(): return lax.ppermute(what, axis, pairs)  104 us
    reduce_scatter x2, waiting for transfers between devices, local(): lax.psum_scatter(project(z, position, lr_places, lr_weights, tp), 'tp', s...  41.6 us
    ppermute x4, waiting for transfers between devices, swap_gather(): have[bit, 0] = lax.ppermute(block, axis, swap_pairs(axis, bit))  31.7 us
    pallas_call x6, Pallas kernels, project(): pl.pallas_call(functools.partial(project_kernel, places), out_shape=jax.S...  27.9 us
    all_gather x2, blocking collectives, local(): sent = lax.all_gather(send, 'ctx', axis=0)  24 us
    pallas_call x2, Pallas kernels, lr_in(): pl.pallas_call(functools.partial(lr_in_kernel, table), out_shape=jax.Shap...  23.4 us
    pallas_call x2, Pallas kernels, mr_local(): pl.pallas_call(mr_local_kernel, grid=(1,), out_shape=(rows, rows), in_spe...  20.9 us
    ppermute x4, waiting for transfers between devices, swap_gather(): part[offset ^ bit] = lax.ppermute(value, axis, swap_pairs(axis, bit))  18.1 us
  transfers between devices with their start and end apart: 33, of which 15 were waited for; matrix products, arithmetic and copies ran while one was open for 2% of the time, Pallas kernels for 21%

profile of v2, /device:TPU:0, one launch (start us, length us, event | category | flops | bytes accessed | tf_op | source)
XLA Modules:
  0.0 383.3 jit_solution(7791894628931142833)
XLA Ops:
  6.5 3.0 collective-permute-start.1
  9.5 1.5 collective-permute-start.3
  11.0 1.9 copy_convert_fusion
  14.7 2.1 collective-permute-start
  17.1 10.5 %mr_local.3 = (f32[256,8,128]{2,1,0:T(8,128)S(1)}, f32[256,8,128]{2,1,0:T(8,128)S(1)}) custom-call(bf16[2,3,256,1024]{3,2,1,0:T(8,128)(2,1)S(1)} %bitcast.45, f32[3,3,8,128]{3,2,1,0:T(8,128)S(1)} %reshape.48.short_ref, f32[128,8,128]{2,1,0:T(8,128)S(1)} %bitcast.49, f32[8,128]{1,0:T(8,128)S(1)} %bitcast.63), custom_call_target="tpu_custom_call" | custom-call | flops 1000000000 | bytes 1000000 | tf_op jit(solution)/shard_map/mr_local/pallas_call | solution.py:106
  28.0 5.0 %collective-permute-done.1.refs_1_ = bf16[1024,512]{1,0:T(8,128)(2,1)} collective-permute-done((bf16[1024,512]{1,0:T(8,128)(2,1)}, bf16[1024,512]{1,0:T(8,128)(2,1)}, u32[]{:S(2)}, u32[]{:S(2)}) %collective-permute-start.1) | collective-permute-done | bytes 1048608 | tf_op jit(solution)/shard_map/ppermute | solution.py:278
  33.0 2.9 collective-permute-done.3.refs_2_
  38.2 4.1 %collective-permute-start.2 = (bf16[1024,256]{1,0:T(8,128)(2,1)S(1)}, bf16[1024,256]{1,0:T(8,128)(2,1)}, u32[]{:S(2)}, u32[]{:S(2)}) collective-permute-start(bf16[1024,256]{1,0:T(8,128)(2,1)S(1)} %slice.69), channel_id=1, source_target_pairs={{0,8},{4,12},{8,0},{12,4},{16,24},{20,28},{24,16},{28,20},{1,9},{5... | collective-permute-start | bytes 1572872 | tf_op jit(solution)/shard_map/ppermute | solution.py:290
  42.3 4.9 %mr_finish.3.z_ref = bf16[256,1024]{1,0:T(8,128)(2,1)S(1)} custom-call(bf16[2,3,256,1024]{3,2,1,0:T(8,128)(2,1)S(1)} %bitcast.46, bf16[2,144,1024]{2,1,0:T(8,128)(2,1)} %collective-permute-done.halo_ref, f32[256,8,128]{2,1,0:T(8,128)S(1)} %get-tuple-element.30.q_ref, f32[256,8,128]{2,1,0:T(8,128)S(1)} %get-tuple-element.33.conv_ref, ...), custom_call_target="tpu_custom_call" | custom-call | flops 1000000000 | bytes 1000000 | tf_op jit(solution)/shard_map/mr_finish/pallas_call | solution.py:186
  48.0 3.5 collective-permute-done.4.refs_1_
  51.5 2.3 collective-permute-done.2.refs_0_
  54.9 10.5 %mr_local.2 = (f32[256,8,128]{2,1,0:T(8,128)S(1)}, f32[256,8,128]{2,1,0:T(8,128)S(1)}) custom-call(bf16[2,3,256,1024]{3,2,1,0:T(8,128)(2,1)S(1)} %bitcast.47, f32[3,3,8,128]{3,2,1,0:T(8,128)S(1)} %reshape.48.short_ref, f32[128,8,128]{2,1,0:T(8,128)S(1)} %bitcast.51, f32[8,128]{1,0:T(8,128)S(1)} %bitcast.65), custom_call_target="tpu_custom_call" | custom-call | flops 1000000000 | bytes 1000000 | tf_op jit(solution)/shard_map/mr_local/pallas_call | solution.py:106
  65.3 5.0 %mr_finish.2.z_ref = bf16[256,1024]{1,0:T(8,128)(2,1)S(1)} custom-call(bf16[2,3,256,1024]{3,2,1,0:T(8,128)(2,1)S(1)} %bitcast.48, bf16[2,144,1024]{2,1,0:T(8,128)(2,1)} %collective-permute-done.halo_ref, f32[256,8,128]{2,1,0:T(8,128)S(1)} %get-tuple-element.28.q_ref, f32[256,8,128]{2,1,0:T(8,128)S(1)} %get-tuple-element.29.conv_ref, ...), custom_call_target="tpu_custom_call" | custom-call | flops 1000000000 | bytes 1000000 | tf_op jit(solution)/shard_map/mr_finish/pallas_call | solution.py:186
  70.3 4.7 %project.6.refs_4_ = bf16[4,256,1024]{2,1,0:T(8,128)(2,1)} custom-call(s32[1]{0:T(128)} %bitcast.1.scalar_ref, bf16[256,1024]{1,0:T(8,128)(2,1)S(1)} %mr_finish.2.z_ref, bf16[1024,512]{1,0:T(8,128)(2,1)} %refs_0_.3, bf16[1024,512]{1,0:T(8,128)(2,1)} %collective-permute-done.1.refs_1_, bf16[1024,512]{1,0:T(8,128)(2,1)} %collective-permute-done.3.refs_2_, ...), custom_call_target="tpu_custom_call" | custom-call | flops 1610612736 | bytes 7864320 | tf_op jit(solution)/shard_map/project/pallas_call | solution.py:242
  75.0 3.4 project.7
  79.5 4.7 %project.8.refs_4_ = bf16[4,256,1024]{2,1,0:T(8,128)(2,1)} custom-call(s32[1]{0:T(128)} %bitcast.1.scalar_ref, bf16[256,1024]{1,0:T(8,128)(2,1)S(1)} %copy-done.4, bf16[1024,512]{1,0:T(8,128)(2,1)} %refs_0_.3, bf16[1024,512]{1,0:T(8,128)(2,1)} %collective-permute-done.1.refs_1_, bf16[1024,512]{1,0:T(8,128)(2,1)} %collective-permute-done.3.refs_2_, ...), custom_call_target="tpu_custom_call" | custom-call | flops 1610612736 | bytes 7864320 | tf_op jit(solution)/shard_map/project/pallas_call | solution.py:242
  84.2 3.5 project.9
  89.5 1.5 collective-permute-start.11
  91.0 23.5 %collective-permute-done.10.refs_1_ = bf16[1024,512]{1,0:T(8,128)(2,1)S(1)} collective-permute-done((bf16[1024,512]{1,0:T(8,128)(2,1)S(1)}, bf16[1024,512]{1,0:T(8,128)(2,1)S(1)}, u32[]{:S(2)}, u32[]{:S(2)}) %collective-permute-start.10) | collective-permute-done | bytes 1048608 | tf_op jit(solution)/shard_map/ppermute | solution.py:278
  115.2 1.3 collective-permute-start.12
  118.3 11.0 %collective-permute-done.12.refs_3_ = bf16[1024,256]{1,0:T(8,128)(2,1)S(1)} collective-permute-done((bf16[1024,256]{1,0:T(8,128)(2,1)S(1)}, bf16[1024,256]{1,0:T(8,128)(2,1)S(1)}, u32[]{:S(2)}, u32[]{:S(2)}) %collective-permute-start.12) | collective-permute-done | bytes 524320 | tf_op jit(solution)/shard_map/ppermute | solution.py:290
  129.3 1.3 collective-permute-done.13.refs_4_
  133.5 1.4 fusion.7.refs_0_
  134.9 1.6 collective-permute-start.17
  137.2 33.8 %collective-permute-done.17.refs_1_ = bf16[256,1024]{1,0:T(8,128)(2,1)S(1)} collective-permute-done((bf16[256,1024]{1,0:T(8,128)(2,1)S(1)}, bf16[256,1024]{1,0:T(8,128)(2,1)S(1)}, u32[]{:S(2)}, u32[]{:S(2)}) %collective-permute-start.17) | collective-permute-done | bytes 524320 | tf_op jit(solution)/shard_map/ppermute | solution.py:339
  171.0 1.4 collective-permute-start.19
  173.8 1.3 collective-permute-start.20
  175.9 1.3 collective-permute-start.21
  179.7 10.6 %collective-permute-done.20.refs_4_ = bf16[256,1024]{1,0:T(8,128)(2,1)} collective-permute-done((bf16[256,1024]{1,0:T(8,128)(2,1)S(1)}, bf16[256,1024]{1,0:T(8,128)(2,1)}, u32[]{:S(2)}, u32[]{:S(2)}) %collective-permute-start.20) | collective-permute-done | bytes 524320 | tf_op jit(solution)/shard_map/ppermute | solution.py:339
  190.3 13.5 %collective-permute-done.21.refs_5_ = bf16[256,1024]{1,0:T(8,128)(2,1)} collective-permute-done((bf16[256,1024]{1,0:T(8,128)(2,1)}, bf16[256,1024]{1,0:T(8,128)(2,1)}, u32[]{:S(2)}, u32[]{:S(2)}) %collective-permute-start.21) | collective-permute-done | bytes 524320 | tf_op jit(solution)/shard_map/ppermute | solution.py:339
  203.8 1.4 fusion.6.refs_0_
  205.3 1.5 collective-permute-start.25
  206.8 11.4 %collective-permute-done.24.refs_1_ = bf16[256,1024]{1,0:T(8,128)(2,1)} collective-permute-done((bf16[256,1024]{1,0:T(8,128)(2,1)S(1)}, bf16[256,1024]{1,0:T(8,128)(2,1)}, u32[]{:S(2)}, u32[]{:S(2)}) %collective-permute-start.24) | collective-permute-done | bytes 524320 | tf_op jit(solution)/shard_map/ppermute | solution.py:339
  218.2 1.5 collective-permute-start.26
  219.7 1.3 collective-permute-start.27
  223.1 11.7 %lr_in.2.x_ref = bf16[3,256,1024]{2,1,0:T(8,128)(2,1)S(1)} custom-call(s32[1]{0:T(128)} %bitcast.11.scalar_ref, f32[1,4096]{1,0:T(1,128)S(1)} %bitcast.55, bf16[256,1024]{1,0:T(8,128)(2,1)S(1)} %fusion.7.refs_0_, bf16[256,1024]{1,0:T(8,128)(2,1)S(1)} %copy-done.30, bf16[256,1024]{1,0:T(8,128)(2,1)S(1)} %copy-done.32, ...), custom_call_target="tpu_custom_call" | custom-call | flops 6442450944 | bytes 25165824 | tf_op jit(solution)/shard_map/lr_in/pallas_call | solution.py:397
  234.8 2.7 lr_mix.2
  237.5 10.8 %all-gather = bf16[256,8,128]{2,1,0:T(8,128)(2,1)S(1)} all-gather(bf16[32,8,128]{2,1,0:T(8,128)(2,1)S(1)} %get-tuple-element.46), channel_id=2, replica_groups=mesh['ctx'=8,'tp'=4] {'ctx'}, dimensions={0}, use_global_device_ids=true | all-gather | bytes 589824 | tf_op jit(solution)/shard_map/all_gather | solution.py:654
  249.1 3.1 lr_modal.2.z_ref
  252.3 5.8 %project.10 = bf16[4,256,1024]{2,1,0:T(8,128)(2,1)} custom-call(s32[1]{0:T(128)} %bitcast.1.scalar_ref, bf16[256,1024]{1,0:T(8,128)(2,1)S(1)} %lr_modal.2.z_ref, bf16[1024,512]{1,0:T(8,128)(2,1)S(1)} %copy-done.6, bf16[1024,512]{1,0:T(8,128)(2,1)S(1)} %collective-permute-done.10.refs_1_, bf16[1024,512]{1,0:T(8,128)(2,1)S(1)} %collective-permute-done.11.refs_2_, ...), custom_call_target="tpu_custom_call" | custom-call | flops 2147483648 | bytes 10485760 | tf_op jit(solution)/shard_map/project/pallas_call | solution.py:242
  258.1 1.3 collective-permute-start.28
  259.4 34.5 %collective-permute-done.28.refs_5_ = bf16[256,1024]{1,0:T(8,128)(2,1)S(1)} collective-permute-done((bf16[256,1024]{1,0:T(8,128)(2,1)}, bf16[256,1024]{1,0:T(8,128)(2,1)S(1)}, u32[]{:S(2)}, u32[]{:S(2)}) %collective-permute-start.28) | collective-permute-done | bytes 524320 | tf_op jit(solution)/shard_map/ppermute | solution.py:339
  295.0 11.7 %lr_in.3.x_ref = bf16[3,256,1024]{2,1,0:T(8,128)(2,1)S(1)} custom-call(s32[1]{0:T(128)} %bitcast.11.scalar_ref, f32[1,4096]{1,0:T(1,128)S(1)} %bitcast.56, bf16[256,1024]{1,0:T(8,128)(2,1)S(1)} %fusion.6.refs_0_, bf16[256,1024]{1,0:T(8,128)(2,1)} %collective-permute-done.24.refs_1_, bf16[256,1024]{1,0:T(8,128)(2,1)} %collective-permute-done.25.refs_2_, ...), custom_call_target="tpu_custom_call" | custom-call | flops 6442450944 | bytes 25165824 | tf_op jit(solution)/shard_map/lr_in/pallas_call | solution.py:397
  306.7 2.7 lr_mix.3
  309.5 13.2 %all-gather.1 = bf16[256,8,128]{2,1,0:T(8,128)(2,1)S(1)} all-gather(bf16[32,8,128]{2,1,0:T(8,128)(2,1)S(1)} %get-tuple-element.50), channel_id=3, replica_groups=mesh['ctx'=8,'tp'=4] {'ctx'}, dimensions={0}, use_global_device_ids=true | all-gather | bytes 589824 | tf_op jit(solution)/shard_map/all_gather | solution.py:654
  322.7 3.1 lr_modal.3.z_ref
  325.8 5.8 %project.11 = bf16[4,256,1024]{2,1,0:T(8,128)(2,1)} custom-call(s32[1]{0:T(128)} %bitcast.1.scalar_ref, bf16[256,1024]{1,0:T(8,128)(2,1)S(1)} %lr_modal.3.z_ref, bf16[1024,512]{1,0:T(8,128)(2,1)S(1)} %copy-done.7, bf16[1024,512]{1,0:T(8,128)(2,1)S(1)} %collective-permute-done.10.refs_1_, bf16[1024,512]{1,0:T(8,128)(2,1)S(1)} %collective-permute-done.11.refs_2_, ...), custom_call_target="tpu_custom_call" | custom-call | flops 2147483648 | bytes 10485760 | tf_op jit(solution)/shard_map/project/pallas_call | solution.py:242
  332.9 41.6 %reduce-scatter.11.cloned.1.call-done = bf16[1,256,1024]{2,1,0:T(8,128)(2,1)} async-done(((bf16[4,256,1024]{2,1,0:T(8,128)(2,1)}), bf16[1,256,1024]{2,1,0:T(8,128)(2,1)}) %reduce-scatter.11.cloned.1.call-update) | async-done | bytes 524304 | tf_op jit(solution)/shard_map/reduce_scatter | solution.py:658
  (149 shorter events, 27.5 us)
Async XLA Ops:
  6.5 126.9 %reduce-scatter.5.cloned.1.call-start = ((), (), s32[]{:S(2)}) async-start(), calls=%async_computation.4 | async-start | bytes 2621440 | tf_op jit(solution)/shard_map/reduce_scatter | solution.py:641
  6.5 26.4 %collective-permute-start.1 = (bf16[1024,512]{1,0:T(8,128)(2,1)}, bf16[1024,512]{1,0:T(8,128)(2,1)}, u32[]{:S(2)}, u32[]{:S(2)}) collective-permute-start(bf16[1024,512]{1,0:T(8,128)(2,1)} %refs_0_.3), channel_id=1, source_target_pairs={{0,16},{4,20},{8,24},{12,28},{16,0},{20,4},{24,8},{28,12},{1,17},{... | collective-permute-start | bytes 3145736 | tf_op jit(solution)/shard_map/ppermute | solution.py:278
  9.5 26.4 %collective-permute-start.3 = (bf16[1024,512]{1,0:T(8,128)(2,1)}, bf16[1024,512]{1,0:T(8,128)(2,1)}, u32[]{:S(2)}, u32[]{:S(2)}) collective-permute-start(bf16[1024,512]{1,0:T(8,128)(2,1)} %refs_0_.3), channel_id=1, source_target_pairs={{0,8},{4,12},{8,0},{12,4},{16,24},{20,28},{24,16},{28,20},{1,9},{5... | collective-permute-start | bytes 3145736 | tf_op jit(solution)/shard_map/ppermute | solution.py:278
  14.7 23.4 %collective-permute-start = (bf16[2,144,1024]{2,1,0:T(8,128)(2,1)}, bf16[2,144,1024]{2,1,0:T(8,128)(2,1)}, u32[]{:S(2)}, u32[]{:S(2)}) collective-permute-start(bf16[2,144,1024]{2,1,0:T(8,128)(2,1)} %fusion.8), channel_id=1, source_target_pairs={{0,4},{4,8},{8,12},{12,16},{16,20},{20,24},{24,28},{1,5},{5,9},{9,... | collective-permute-start | bytes 1769480 | tf_op jit(solution)/shard_map/ppermute | solution.py:613
  17.0 25.2 %copy-start.1 = (f32[16,8,8,128]{3,2,1,0:T(8,128)}, f32[16,8,8,128]{3,2,1,0:T(8,128)S(1)}, u32[]{:S(2)}) copy-start(f32[16,8,8,128]{3,2,1,0:T(8,128)S(1)} %copy.24) | copy-start | bytes 1572868
  27.5 42.8 %collective-permute-start.7 = (bf16[1024,512]{1,0:T(8,128)(2,1)}, bf16[1024,512]{1,0:T(8,128)(2,1)}, u32[]{:S(2)}, u32[]{:S(2)}) collective-permute-start(bf16[1024,512]{1,0:T(8,128)(2,1)} %refs_0_.3), channel_id=1, source_target_pairs={{0,4},{4,0},{8,12},{12,8},{16,20},{20,16},{24,28},{28,24},{1,5},{5... | collective-permute-start | bytes 3145736 | tf_op jit(solution)/shard_map/ppermute | solution.py:300
  33.0 37.3 %collective-permute-start.8 = (bf16[1024,512]{1,0:T(8,128)(2,1)}, bf16[1024,512]{1,0:T(8,128)(2,1)}, u32[]{:S(2)}, u32[]{:S(2)}) collective-permute-start(bf16[1024,512]{1,0:T(8,128)(2,1)} %collective-permute-done.1.refs_1_), channel_id=1, source_target_pairs={{0,4},{4,0},{8,12},{12,8},{16,20},{20,16},{24,28},{28,24},{1,5},{5... | collective-permute-start | bytes 3145736 | tf_op jit(solution)/shard_map/ppermute | solution.py:300
  35.9 34.4 %collective-permute-start.9 = (bf16[1024,512]{1,0:T(8,128)(2,1)}, bf16[1024,512]{1,0:T(8,128)(2,1)}, u32[]{:S(2)}, u32[]{:S(2)}) collective-permute-start(bf16[1024,512]{1,0:T(8,128)(2,1)} %collective-permute-done.3.refs_2_), channel_id=1, source_target_pairs={{0,4},{4,0},{8,12},{12,8},{16,20},{20,16},{24,28},{28,24},{1,5},{5... | collective-permute-start | bytes 3145736 | tf_op jit(solution)/shard_map/ppermute | solution.py:300
  37.0 14.5 %collective-permute-start.4 = (bf16[1024,256]{1,0:T(8,128)(2,1)S(1)}, bf16[1024,256]{1,0:T(8,128)(2,1)}, u32[]{:S(2)}, u32[]{:S(2)}) collective-permute-start(bf16[1024,256]{1,0:T(8,128)(2,1)S(1)} %slice.70), channel_id=1, source_target_pairs={{0,16},{4,20},{8,24},{12,28},{16,0},{20,4},{24,8},{28,12},{1,17},{... | collective-permute-start | bytes 1572872 | tf_op jit(solution)/shard_map/ppermute | solution.py:290
  38.2 15.7 %collective-permute-start.2 = (bf16[1024,256]{1,0:T(8,128)(2,1)S(1)}, bf16[1024,256]{1,0:T(8,128)(2,1)}, u32[]{:S(2)}, u32[]{:S(2)}) collective-permute-start(bf16[1024,256]{1,0:T(8,128)(2,1)S(1)} %slice.69), channel_id=1, source_target_pairs={{0,8},{4,12},{8,0},{12,4},{16,24},{20,28},{24,16},{28,20},{1,9},{5... | collective-permute-start | bytes 1572872 | tf_op jit(solution)/shard_map/ppermute | solution.py:290
  51.5 23.5 %collective-permute-start.6 = (bf16[1024,256]{1,0:T(8,128)(2,1)}, bf16[1024,256]{1,0:T(8,128)(2,1)}, u32[]{:S(2)}, u32[]{:S(2)}) collective-permute-start(bf16[1024,256]{1,0:T(8,128)(2,1)} %collective-permute-done.4.refs_1_), channel_id=1, source_target_pairs={{0,4},{4,0},{8,12},{12,8},{16,20},{20,16},{24,28},{28,24},{1,5},{5... | collective-permute-start | bytes 1572872 | tf_op jit(solution)/shard_map/ppermute | solution.py:300
  53.8 21.2 %collective-permute-start.5 = (bf16[1024,256]{1,0:T(8,128)(2,1)}, bf16[1024,256]{1,0:T(8,128)(2,1)}, u32[]{:S(2)}, u32[]{:S(2)}) collective-permute-start(bf16[1024,256]{1,0:T(8,128)(2,1)} %collective-permute-done.2.refs_0_), channel_id=1, source_target_pairs={{0,4},{4,0},{8,12},{12,8},{16,20},{20,16},{24,28},{28,24},{1,5},{5... | collective-permute-start | bytes 1572872 | tf_op jit(solution)/shard_map/ppermute | solution.py:300
  78.5 101.2 %reduce-scatter.7.cloned.1.call-start = ((), (), s32[]{:S(2)}) async-start(), calls=%async_computation.5 | async-start | bytes 2621440 | tf_op jit(solution)/shard_map/reduce_scatter | solution.py:641
  87.8 243.8 %reduce-scatter.9.cloned.1.call-start = ((), (), s32[]{:S(2)}) async-start(), calls=%async_computation.6 | async-start | bytes 2621440 | tf_op jit(solution)/shard_map/reduce_scatter | solution.py:658
  89.0 25.6 %collective-permute-start.10 = (bf16[1024,512]{1,0:T(8,128)(2,1)S(1)}, bf16[1024,512]{1,0:T(8,128)(2,1)S(1)}, u32[]{:S(2)}, u32[]{:S(2)}) collective-permute-start(bf16[1024,512]{1,0:T(8,128)(2,1)S(1)} %copy-done.5), channel_id=1, source_target_pairs={{0,16},{4,20},{8,24},{12,28},{16,0},{20,4},{24,8},{28,12},{1,17},{... | collective-permute-start | bytes 3145736 | tf_op jit(solution)/shard_map/ppermute | solution.py:278
  89.5 25.3 %collective-permute-start.11 = (bf16[1024,512]{1,0:T(8,128)(2,1)S(1)}, bf16[1024,512]{1,0:T(8,128)(2,1)S(1)}, u32[]{:S(2)}, u32[]{:S(2)}) collective-permute-start(bf16[1024,512]{1,0:T(8,128)(2,1)S(1)} %copy-done.5), channel_id=1, source_target_pairs={{0,8},{4,12},{8,0},{12,4},{16,24},{20,28},{24,16},{28,20},{1,9},{5... | collective-permute-start | bytes 3145736 | tf_op jit(solution)/shard_map/ppermute | solution.py:278
  91.0 26.3 %collective-permute-start.14 = (bf16[1024,512]{1,0:T(8,128)(2,1)S(1)}, bf16[1024,512]{1,0:T(8,128)(2,1)S(1)}, u32[]{:S(2)}, u32[]{:S(2)}) collective-permute-start(bf16[1024,512]{1,0:T(8,128)(2,1)S(1)} %copy-done.5), channel_id=1, source_target_pairs={{0,4},{4,0},{8,12},{12,8},{16,20},{20,16},{24,28},{28,24},{1,5},{5... | collective-permute-start | bytes 3145736 | tf_op jit(solution)/shard_map/ppermute | solution.py:300
  114.6 16.1 %collective-permute-start.15 = (bf16[1024,512]{1,0:T(8,128)(2,1)S(1)}, bf16[1024,512]{1,0:T(8,128)(2,1)S(1)}, u32[]{:S(2)}, u32[]{:S(2)}) collective-permute-start(bf16[1024,512]{1,0:T(8,128)(2,1)S(1)} %collective-permute-done.10.refs_1_), channel_id=1, source_target_pairs={{0,4},{4,0},{8,12},{12,8},{16,20},{20,16},{24,28},{28,24},{1,5},{5... | collective-permute-start | bytes 3145736 | tf_op jit(solution)/shard_map/ppermute | solution.py:300
  114.8 17.6 %collective-permute-start.16 = (bf16[1024,512]{1,0:T(8,128)(2,1)S(1)}, bf16[1024,512]{1,0:T(8,128)(2,1)S(1)}, u32[]{:S(2)}, u32[]{:S(2)}) collective-permute-start(bf16[1024,512]{1,0:T(8,128)(2,1)S(1)} %collective-permute-done.11.refs_2_), channel_id=1, source_target_pairs={{0,4},{4,0},{8,12},{12,8},{16,20},{20,16},{24,28},{28,24},{1,5},{5... | collective-permute-start | bytes 3145736 | tf_op jit(solution)/shard_map/ppermute | solution.py:300
  115.1 91.6 %copy-start.40 = (f32[16,1024]{1,0:T(8,128)S(1)}, f32[16,1024]{1,0:T(8,128)}, u32[]{:S(2)}) copy-start(f32[16,1024]{1,0:T(8,128)} %param.22) | copy-start | bytes 196612
  115.2 91.6 %copy-start.42 = (f32[3,3,1024]{2,1,0:T(4,128)S(1)}, f32[3,3,1024]{2,1,0:T(4,128)}, u32[]{:S(2)}) copy-start(f32[3,3,1024]{2,1,0:T(4,128)} %param.21) | copy-start | bytes 110596
  115.2 91.6 %copy-start.41 = (f32[16,1024]{1,0:T(8,128)S(1)}, f32[16,1024]{1,0:T(8,128)}, u32[]{:S(2)}) copy-start(f32[16,1024]{1,0:T(8,128)} %param.23) | copy-start | bytes 196612
  115.2 105.8 %copy-start.35 = (f32[4096]{0:T(1024)S(1)}, f32[4096]{0:T(1024)}, u32[]{:S(2)}) copy-start(f32[4096]{0:T(1024)} %param.19) | copy-start | bytes 49156
  115.2 14.1 %collective-permute-start.12 = (bf16[1024,256]{1,0:T(8,128)(2,1)S(1)}, bf16[1024,256]{1,0:T(8,128)(2,1)S(1)}, u32[]{:S(2)}, u32[]{:S(2)}) collective-permute-start(bf16[1024,256]{1,0:T(8,128)(2,1)S(1)} %slice.71), channel_id=1, source_target_pairs={{0,8},{4,12},{8,0},{12,4},{16,24},{20,28},{24,16},{28,20},{1,9},{5... | collective-permute-start | bytes 1572872 | tf_op jit(solution)/shard_map/ppermute | solution.py:290
  116.5 14.1 %collective-permute-start.13 = (bf16[1024,256]{1,0:T(8,128)(2,1)S(1)}, bf16[1024,256]{1,0:T(8,128)(2,1)S(1)}, u32[]{:S(2)}, u32[]{:S(2)}) collective-permute-start(bf16[1024,256]{1,0:T(8,128)(2,1)S(1)} %slice.72), channel_id=1, source_target_pairs={{0,16},{4,20},{8,24},{12,28},{16,0},{20,4},{24,8},{28,12},{1,17},{... | collective-permute-start | bytes 1572872 | tf_op jit(solution)/shard_map/ppermute | solution.py:290
  134.9 36.2 %collective-permute-start.17 = (bf16[256,1024]{1,0:T(8,128)(2,1)S(1)}, bf16[256,1024]{1,0:T(8,128)(2,1)S(1)}, u32[]{:S(2)}, u32[]{:S(2)}) collective-permute-start(bf16[256,1024]{1,0:T(8,128)(2,1)S(1)} %fusion.7.refs_0_), channel_id=1, source_target_pairs={{0,1},{1,0},{2,3},{3,2},{4,5},{5,4},{6,7},{7,6},{8,9},{9,8},{10,11... | collective-permute-start | bytes 1572872 | tf_op jit(solution)/shard_map/ppermute | solution.py:339
  136.5 37.3 %collective-permute-start.18 = (bf16[256,1024]{1,0:T(8,128)(2,1)S(1)}, bf16[256,1024]{1,0:T(8,128)(2,1)S(1)}, u32[]{:S(2)}, u32[]{:S(2)}) collective-permute-start(bf16[256,1024]{1,0:T(8,128)(2,1)S(1)} %fusion.7.refs_0_), channel_id=1, source_target_pairs={{1,2},{2,1},{5,6},{6,5},{9,10},{10,9},{13,14},{14,13},{17,18},{18,... | collective-permute-start | bytes 1572872 | tf_op jit(solution)/shard_map/ppermute | solution.py:339
  171.0 4.9 %collective-permute-start.19 = (bf16[256,1024]{1,0:T(8,128)(2,1)S(1)}, bf16[256,1024]{1,0:T(8,128)(2,1)}, u32[]{:S(2)}, u32[]{:S(2)}) collective-permute-start(bf16[256,1024]{1,0:T(8,128)(2,1)S(1)} %collective-permute-done.17.refs_1_), channel_id=1, source_target_pairs={{1,2},{2,1},{5,6},{6,5},{9,10},{10,9},{13,14},{14,13},{17,18},{18,... | collective-permute-start | bytes 1572872 | tf_op jit(solution)/shard_map/ppermute | solution.py:339
  173.3 3.9 %collective-permute-start.22 = (bf16[1024,256]{1,0:T(8,128)(2,1)}, bf16[1024,256]{1,0:T(8,128)(2,1)S(1)}, u32[]{:S(2)}, u32[]{:S(2)}) collective-permute-start(bf16[1024,256]{1,0:T(8,128)(2,1)} %copy-done.17), channel_id=1, source_target_pairs={{0,4},{4,0},{8,12},{12,8},{16,20},{20,16},{24,28},{28,24},{1,5},{5... | collective-permute-start | bytes 1572872 | tf_op jit(solution)/shard_map/ppermute | solution.py:300
  173.3 4.7 %collective-permute-start.23 = (bf16[1024,256]{1,0:T(8,128)(2,1)}, bf16[1024,256]{1,0:T(8,128)(2,1)S(1)}, u32[]{:S(2)}, u32[]{:S(2)}) collective-permute-start(bf16[1024,256]{1,0:T(8,128)(2,1)} %copy-done.20), channel_id=1, source_target_pairs={{0,4},{4,0},{8,12},{12,8},{16,20},{20,16},{24,28},{28,24},{1,5},{5... | collective-permute-start | bytes 1572872 | tf_op jit(solution)/shard_map/ppermute | solution.py:300
  173.8 16.5 %collective-permute-start.20 = (bf16[256,1024]{1,0:T(8,128)(2,1)S(1)}, bf16[256,1024]{1,0:T(8,128)(2,1)}, u32[]{:S(2)}, u32[]{:S(2)}) collective-permute-start(bf16[256,1024]{1,0:T(8,128)(2,1)S(1)} %collective-permute-done.18.refs_2_), channel_id=1, source_target_pairs={{1,0},{2,3},{5,4},{6,7},{9,8},{10,11},{13,12},{14,15},{17,16},{18,... | collective-permute-start | bytes 1572872 | tf_op jit(solution)/shard_map/ppermute | solution.py:339
  175.9 27.9 %collective-permute-start.21 = (bf16[256,1024]{1,0:T(8,128)(2,1)}, bf16[256,1024]{1,0:T(8,128)(2,1)}, u32[]{:S(2)}, u32[]{:S(2)}) collective-permute-start(bf16[256,1024]{1,0:T(8,128)(2,1)} %collective-permute-done.19.refs_3_), channel_id=1, source_target_pairs={{1,0},{2,3},{5,4},{6,7},{9,8},{10,11},{13,12},{14,15},{17,16},{18,... | collective-permute-start | bytes 1572872 | tf_op jit(solution)/shard_map/ppermute | solution.py:339
  205.2 13.0 %collective-permute-start.24 = (bf16[256,1024]{1,0:T(8,128)(2,1)S(1)}, bf16[256,1024]{1,0:T(8,128)(2,1)}, u32[]{:S(2)}, u32[]{:S(2)}) collective-permute-start(bf16[256,1024]{1,0:T(8,128)(2,1)S(1)} %fusion.6.refs_0_), channel_id=1, source_target_pairs={{0,1},{1,0},{2,3},{3,2},{4,5},{5,4},{6,7},{7,6},{8,9},{9,8},{10,11... | collective-permute-start | bytes 1572872 | tf_op jit(solution)/shard_map/ppermute | solution.py:339
  205.3 14.4 %collective-permute-start.25 = (bf16[256,1024]{1,0:T(8,128)(2,1)S(1)}, bf16[256,1024]{1,0:T(8,128)(2,1)}, u32[]{:S(2)}, u32[]{:S(2)}) collective-permute-start(bf16[256,1024]{1,0:T(8,128)(2,1)S(1)} %fusion.6.refs_0_), channel_id=1, source_target_pairs={{1,2},{2,1},{5,6},{6,5},{9,10},{10,9},{13,14},{14,13},{17,18},{18,... | collective-permute-start | bytes 1572872 | tf_op jit(solution)/shard_map/ppermute | solution.py:339
  218.2 30.1 %collective-permute-start.26 = (bf16[256,1024]{1,0:T(8,128)(2,1)}, bf16[256,1024]{1,0:T(8,128)(2,1)}, u32[]{:S(2)}, u32[]{:S(2)}) collective-permute-start(bf16[256,1024]{1,0:T(8,128)(2,1)} %collective-permute-done.24.refs_1_), channel_id=1, source_target_pairs={{1,2},{2,1},{5,6},{6,5},{9,10},{10,9},{13,14},{14,13},{17,18},{18,... | collective-permute-start | bytes 1572872 | tf_op jit(solution)/shard_map/ppermute | solution.py:339
  219.7 28.6 %collective-permute-start.27 = (bf16[256,1024]{1,0:T(8,128)(2,1)}, bf16[256,1024]{1,0:T(8,128)(2,1)S(1)}, u32[]{:S(2)}, u32[]{:S(2)}) collective-permute-start(bf16[256,1024]{1,0:T(8,128)(2,1)} %collective-permute-done.25.refs_2_), channel_id=1, source_target_pairs={{1,0},{2,3},{5,4},{6,7},{9,8},{10,11},{13,12},{14,15},{17,16},{18,... | collective-permute-start | bytes 1572872 | tf_op jit(solution)/shard_map/ppermute | solution.py:339
  234.8 17.4 %copy-start.18 = (bf16[1024,256]{1,0:T(8,128)(2,1)S(1)}, bf16[1024,256]{1,0:T(8,128)(2,1)}, u32[]{:S(2)}) copy-start(bf16[1024,256]{1,0:T(8,128)(2,1)} %copy-done.17) | copy-start | bytes 1572868
  234.8 17.4 %copy-start.21 = (bf16[1024,256]{1,0:T(8,128)(2,1)S(1)}, bf16[1024,256]{1,0:T(8,128)(2,1)}, u32[]{:S(2)}) copy-start(bf16[1024,256]{1,0:T(8,128)(2,1)} %copy-done.20) | copy-start | bytes 1572868
  234.8 17.4 %copy-start.24 = (bf16[1024,256]{1,0:T(8,128)(2,1)S(1)}, bf16[1024,256]{1,0:T(8,128)(2,1)}, u32[]{:S(2)}) copy-start(bf16[1024,256]{1,0:T(8,128)(2,1)} %copy-done.23) | copy-start | bytes 1572868
  234.8 17.4 %copy-start.27 = (bf16[1024,256]{1,0:T(8,128)(2,1)S(1)}, bf16[1024,256]{1,0:T(8,128)(2,1)}, u32[]{:S(2)}) copy-start(bf16[1024,256]{1,0:T(8,128)(2,1)} %copy-done.26) | copy-start | bytes 1572868
  258.1 116.4 %reduce-scatter.11.cloned.1.call-start = ((), (), s32[]{:S(2)}) async-start(), calls=%async_computation.7 | async-start | bytes 2621440 | tf_op jit(solution)/shard_map/reduce_scatter | solution.py:658
  258.1 35.8 %collective-permute-start.28 = (bf16[256,1024]{1,0:T(8,128)(2,1)}, bf16[256,1024]{1,0:T(8,128)(2,1)S(1)}, u32[]{:S(2)}, u32[]{:S(2)}) collective-permute-start(bf16[256,1024]{1,0:T(8,128)(2,1)} %collective-permute-done.26.refs_3_), channel_id=1, source_target_pairs={{1,0},{2,3},{5,4},{6,7},{9,8},{10,11},{13,12},{14,15},{17,16},{18,... | collective-permute-start | bytes 1572872 | tf_op jit(solution)/shard_map/ppermute | solution.py:339
  306.7 19.1 %copy-start.19 = (bf16[1024,256]{1,0:T(8,128)(2,1)S(1)}, bf16[1024,256]{1,0:T(8,128)(2,1)}, u32[]{:S(2)}) copy-start(bf16[1024,256]{1,0:T(8,128)(2,1)} %copy-done.17) | copy-start | bytes 1572868
  306.7 19.1 %copy-start.22 = (bf16[1024,256]{1,0:T(8,128)(2,1)S(1)}, bf16[1024,256]{1,0:T(8,128)(2,1)}, u32[]{:S(2)}) copy-start(bf16[1024,256]{1,0:T(8,128)(2,1)} %copy-done.20) | copy-start | bytes 1572868
  306.7 19.1 %copy-start.25 = (bf16[1024,256]{1,0:T(8,128)(2,1)S(1)}, bf16[1024,256]{1,0:T(8,128)(2,1)}, u32[]{:S(2)}) copy-start(bf16[1024,256]{1,0:T(8,128)(2,1)} %copy-done.23) | copy-start | bytes 1572868
  306.7 19.1 %copy-start.28 = (bf16[1024,256]{1,0:T(8,128)(2,1)S(1)}, bf16[1024,256]{1,0:T(8,128)(2,1)}, u32[]{:S(2)}) copy-start(bf16[1024,256]{1,0:T(8,128)(2,1)} %copy-done.26) | copy-start | bytes 1572868
  309.4 16.4 %copy-start.7 = (bf16[1024,512]{1,0:T(8,128)(2,1)S(1)}, bf16[1024,512]{1,0:T(8,128)(2,1)}, u32[]{:S(2)}) copy-start(bf16[1024,512]{1,0:T(8,128)(2,1)} %refs_0_.5) | copy-start | bytes 3145732
  309.4 16.4 %copy-start.10 = (bf16[1024,512]{1,0:T(8,128)(2,1)S(1)}, bf16[1024,512]{1,0:T(8,128)(2,1)}, u32[]{:S(2)}) copy-start(bf16[1024,512]{1,0:T(8,128)(2,1)} %copy-done.8) | copy-start | bytes 3145732
  (28 other events, 141.7 us)
Sparse Core Ops, SparseCore 0:
  78.6 44.3 reduce-scatter.4
  125.4 54.2 reduce-scatter.6
  258.2 51.4 reduce-scatter.8
  331.7 42.7 reduce-scatter.10

commit v3 on v2

v3 whole, which is shorter than its diff:
```python
import functools

import jax
import jax.numpy as jnp
from jax import lax
from jax.experimental import pallas as pl
from jax.experimental.pallas import tpu as pltpu
from jax.sharding import PartitionSpec as P

F32 = jnp.float32
BF16 = jnp.bfloat16
LANES = 128
SUB = 8
HALO = 16
STEP = 8
VMEM_MIB = 56


def params(mebibytes, **more):
    return pltpu.CompilerParams(vmem_limit_bytes=mebibytes * 2**20, **more)


def vmem(count):
    return [pl.BlockSpec(memory_space=pltpu.VMEM)] * count


def in_hbm(count):
    return [pl.BlockSpec(memory_space=pltpu.HBM)] * count


def cost(flops, moved):
    return pl.CostEstimate(flops=int(flops), bytes_accessed=int(moved), transcendentals=0)


def tiles(value):
    width = value.shape[-1]
    room = SUB * LANES
    if width < room:
        value = jnp.pad(value, [(0, 0)] * (value.ndim - 1) + [(0, room - width)])
    return value.reshape(value.shape[:-1] + (SUB, LANES)).astype(F32)


def put_rows(flat_ref, first, rows, lane_tile, value):
    flat_ref[pl.ds(first * SUB + lane_tile, rows, stride=SUB), :] = value


def get_rows(flat_ref, first, rows, lane_tile):
    return flat_ref[pl.ds(first * SUB + lane_tile, rows, stride=SUB), :]


def window_sum(filter_ref, source3, base, chunks, totals):
    def chunk(index, totals):
        tap = index * STEP
        window = [source3[base - tap - (STEP - 1) + j] for j in range(2 * STEP - 1)]
        totals = list(totals)
        for k in range(STEP):
            weight = filter_ref[tap + k]
            for t in range(STEP):
                totals[t] = totals[t] + weight * window[t - k + STEP - 1]
        return tuple(totals)

    return lax.fori_loop(*chunks, chunk, tuple(totals))


def mr_local_kernel(x_ref, short_ref, filter_ref, skip_ref, z_ref, q_ref, conv_ref, raw, u, zs):
    _, _, tokens, width = x_ref.shape
    head = q_ref.shape[1]
    taps = filter_ref.shape[0]
    lags = short_ref.shape[0]
    prior = lags - 1
    for tile in range(width // LANES):
        lanes = slice(tile * LANES, (tile + 1) * LANES)
        for p in range(3):
            put_rows(raw.at[p], prior, tokens, tile, x_ref[0, p, :, lanes].astype(F32))
    raw3 = raw.reshape(3, tokens + prior, SUB, LANES)
    u3 = u.reshape(taps + tokens, SUB, LANES)
    zs3 = zs.reshape(tokens, SUB, LANES)
    for p in range(3):
        raw3[p, :prior] = jnp.zeros((prior, SUB, LANES), F32)

    @pl.loop(0, taps // STEP)
    def _(block):
        u3[pl.ds(block * STEP, STEP)] = jnp.zeros((STEP, SUB, LANES), F32)

    def mix(p, first, rows):
        total = short_ref[0, p] * raw3[p, pl.ds(first + prior, rows)]
        for lag in range(1, lags):
            total = total + short_ref[lag, p] * raw3[p, pl.ds(first + prior - lag, rows)]
        return total

    @pl.loop(0, tokens // STEP)
    def _(block):
        first = block * STEP
        product = mix(1, first, STEP) * mix(2, first, STEP)
        u3[pl.ds(taps + first, STEP)] = product.astype(BF16).astype(F32)

    def sums(block):
        first = block * STEP
        totals = [skip_ref[...] * u3[taps + first + t] for t in range(STEP)]
        chunks = (0, lax.min(block + 1, taps // STEP))
        return first, mix(0, first, STEP), window_sum(filter_ref, u3, taps + first, chunks, totals)

    @pl.loop(0, head // STEP)
    def _(block):
        first, queries, totals = sums(block)
        q_ref[0, pl.ds(first, STEP)] = queries
        for t in range(STEP):
            conv_ref[0, first + t] = totals[t]

    @pl.loop(head // STEP, tokens // STEP)
    def _(block):
        first, queries, totals = sums(block)
        for t in range(STEP):
            zs3[first + t] = queries[t] * totals[t]

    for tile in range(width // LANES):
        lanes = slice(tile * LANES, (tile + 1) * LANES)
        z_ref[0, head:, lanes] = get_rows(zs, head, tokens - head, tile).astype(BF16)


def mr_local(x, short_w, taps_w, skip):
    sequences, _, tokens, width = x.shape
    taps = taps_w.shape[0]
    prior = short_w.shape[0] - 1
    head = taps + HALO
    rows = jax.ShapeDtypeStruct((sequences, head, SUB, LANES), F32)
    return pl.pallas_call(
        mr_local_kernel,
        grid=(sequences,),
        out_shape=(jax.ShapeDtypeStruct((sequences, tokens, width), BF16), rows, rows),
        in_specs=[pl.BlockSpec((1, 3, tokens, width), lambda i: (i, 0, 0, 0)), *vmem(3)],
        out_specs=(
            pl.BlockSpec((1, tokens, width), lambda i: (i, 0, 0)),
            *(pl.BlockSpec((1, head, SUB, LANES), lambda i: (i, 0, 0, 0)),) * 2,
        ),
        scratch_shapes=[
            pltpu.VMEM((3, (tokens + prior) * SUB, LANES), F32),
            pltpu.VMEM(((taps + tokens) * SUB, LANES), F32),
            pltpu.VMEM((tokens * SUB, LANES), F32),
        ],
        compiler_params=params(VMEM_MIB),
        cost_estimate=cost(1e9, 1e6),
        name="mr_local",
    )(x, short_w, taps_w, skip)


def mr_finish_kernel(x_ref, halo_ref, q_ref, conv_ref, short_ref, filter_ref, skip_ref, gate_ref, z_ref, raw, extra, zs):
    tokens = q_ref.shape[1]
    width = z_ref.shape[1]
    taps = filter_ref.shape[0]
    lags = short_ref.shape[0]
    prior = lags - 1
    for tile in range(width // LANES):
        lanes = slice(tile * LANES, (tile + 1) * LANES)
        put_rows(extra, 0, taps, tile, halo_ref[0, :taps, lanes].astype(F32))
        tail = halo_ref[0, taps : taps + HALO, lanes].astype(F32)
        for p in range(3):
            put_rows(raw.at[p], 0, prior, tile, tail[prior * p : prior * (p + 1)])
            put_rows(raw.at[p], prior, prior, tile, x_ref[0, p, :, lanes].astype(F32)[:prior])
    raw3 = raw.reshape(3, 2 * prior, SUB, LANES)
    extra3 = extra.reshape(taps + 2 * STEP, SUB, LANES)
    zs3 = zs.reshape(tokens, SUB, LANES)

    def mix(p, t, lowest):
        total = short_ref[0, p] * raw3[p, prior + t]
        for lag in range(1, lags):
            if prior + t - lag >= lowest:
                total = total + short_ref[lag, p] * raw3[p, prior + t - lag]
        return total

    extra3[taps:] = jnp.zeros((2 * STEP, SUB, LANES), F32)
    for t in range(prior):
        whole = (mix(1, t, 0) * mix(2, t, 0)).astype(BF16).astype(F32)
        alone = (mix(1, t, prior) * mix(2, t, prior)).astype(BF16).astype(F32)
        extra3[taps + t] = whole - alone

    def sums(block):
        first = block * STEP
        chunks = (lax.max(block - 1, 0), taps // STEP)
        totals = [conv_ref[0, first + t] for t in range(STEP)]
        return first, window_sum(filter_ref, extra3, taps + first, chunks, totals)

    first, totals = sums(0)
    for t in range(STEP):
        if t < prior:
            zs3[t] = mix(0, t, 0) * (totals[t] + skip_ref[...] * extra3[taps + t])
        else:
            zs3[t] = q_ref[0, t] * totals[t]

    @pl.loop(1, taps // STEP + 1)
    def _(block):
        first, totals = sums(block)
        for t in range(STEP):
            zs3[first + t] = q_ref[0, first + t] * totals[t]

    @pl.loop(taps // STEP + 1, tokens // STEP)
    def _(block):
        where = pl.ds(block * STEP, STEP)
        zs3[where] = q_ref[0, where] * conv_ref[0, where]

    for tile in range(width // LANES):
        lanes = slice(tile * LANES, (tile + 1) * LANES)
        z_ref[:, lanes] = get_rows(zs, 0, tokens, tile).astype(BF16)


def mr_finish(x, halo, q, conv, short_w, taps_w, skip, seq, gate):
    width = x.shape[3]
    head = q.shape[1]
    taps = taps_w.shape[0]
    prior = short_w.shape[0] - 1
    rows = pl.BlockSpec((1, head, SUB, LANES), lambda i: (seq, 0, 0, 0))
    return pl.pallas_call(
        mr_finish_kernel,
        grid=(1,),
        out_shape=jax.ShapeDtypeStruct((head, width), BF16),
        in_specs=[
            pl.BlockSpec((1, 3, HALO, width), lambda i: (seq, 0, 0, 0)),
            pl.BlockSpec((1, halo.shape[1], width), lambda i: (seq, 0, 0)),
            rows,
            rows,
            *vmem(3),
            *in_hbm(1),
        ],
        out_specs=pl.BlockSpec((head, width), lambda i: (0, 0)),
        scratch_shapes=[
            pltpu.VMEM((3, 2 * prior * SUB, LANES), F32),
            pltpu.VMEM(((taps + 2 * STEP) * SUB, LANES), F32),
            pltpu.VMEM((head * SUB, LANES), F32),
        ],
        compiler_params=params(VMEM_MIB),
        cost_estimate=cost(4e10, 1e6),
        name="mr_finish",
    )(x, halo, q, conv, short_w, taps_w, skip, gate)


def place_blocks(places, position, z, copies, held, result, out_ref, out_sems):
    width = out_ref.shape[2]
    sent = []
    begun = 0
    for k, (offset, begin, whole) in enumerate(places):
        columns = held[k].shape[1]
        start = lax.bitwise_xor(position, offset) * whole + begin
        share = lax.div(start, width)
        lanes = pl.ds(pl.multiple_of(lax.rem(start, width), columns), columns)
        mine = slice(begun, begun + columns)
        begun += columns
        copies.get(k)
        result[:, mine] = jnp.dot(z, held[k][...], preferred_element_type=F32).astype(BF16)
        sent.append(pltpu.make_async_copy(result.at[:, mine], out_ref.at[share, :, lanes], out_sems.at[k]))
        sent[-1].start()
    for copy in sent:
        copy.wait()


class Fetch:
    def __init__(self, copies, ahead=3):
        self.copies, self.ahead = copies, ahead

    def begin(self):
        for copies in self.copies[: self.ahead]:
            for copy in copies:
                copy.start()

    def get(self, k):
        for copy in self.copies[k]:
            copy.wait()
        if k + self.ahead < len(self.copies):
            for copy in self.copies[k + self.ahead]:
                copy.start()


def fetch(sources, held, sems):
    return Fetch([(pltpu.make_async_copy(sources[k], held[k], sems.at[k]),) for k in range(len(held))])


def project_kernel(places, seq, scalar_ref, head_ref, body_ref, *refs):
    count = len(places)
    weights = refs[:count]
    out_ref, z_ref, z_sems, result = refs[-6 - count], refs[-5 - count], refs[-4 - count], refs[-3 - count]
    held, in_sems, out_sems = refs[-2 - count : -2], refs[-2], refs[-1]
    head = head_ref.shape[0]
    rest = z_ref.shape[0] - head
    first = pltpu.make_async_copy(head_ref, z_ref.at[pl.ds(0, head)], z_sems.at[0])
    second = pltpu.make_async_copy(body_ref.at[seq, pl.ds(head, rest)], z_ref.at[pl.ds(head, rest)], z_sems.at[1])
    first.start()
    second.start()
    copies = fetch(weights, held, in_sems)
    copies.begin()
    first.wait()
    second.wait()
    place_blocks(places, scalar_ref[0], z_ref[...], copies, held, result, out_ref, out_sems)


def project(z, position, places, weights, shares, given=None):
    head, body, seq = z
    _, tokens, width = body.shape
    total = sum(w.shape[1] for w in weights)
    model = places[0][2] * lax.axis_size("ctx")
    extra = [] if given is None else [given]
    return pl.pallas_call(
        functools.partial(project_kernel, places, seq),
        out_shape=jax.ShapeDtypeStruct((shares, tokens, model // shares), BF16),
        in_specs=[pl.BlockSpec(memory_space=pltpu.SMEM), *in_hbm(2 + len(weights) + len(extra))],
        out_specs=in_hbm(1)[0],
        scratch_shapes=[
            pltpu.VMEM((tokens, width), BF16),
            pltpu.SemaphoreType.DMA((2,)),
            pltpu.VMEM((tokens, total), BF16),
            *[pltpu.VMEM(w.shape, w.dtype) for w in weights],
            pltpu.SemaphoreType.DMA((len(weights),)),
            pltpu.SemaphoreType.DMA((len(weights),)),
        ],
        input_output_aliases={3 + len(weights): 0} if extra else {},
        compiler_params=params(VMEM_MIB),
        cost_estimate=cost(2 * tokens * width * total, 2 * total * (width + tokens)),
        name="project",
    )(position, head, body, *weights, *extra)


def after(value, *others):
    return lax.optimization_barrier((value, *others))[0]


def swap_pairs(axis, bit):
    return [(i, i ^ bit) for i in range(lax.axis_size(axis))]


def together(*values):
    return lax.optimization_barrier(values)


class SwapGather:
    def __init__(self, block, axis):
        count = lax.axis_size(axis)
        self.axis, self.whole = axis, block.shape[1]
        self.far = [1 << k for k in range(count.bit_length() - 1, 0, -1) if 1 << k < count]
        self.arrays = {(0, 0): block}

    def swap(self, value, bit):
        return lax.ppermute(value, self.axis, swap_pairs(self.axis, bit))

    def near(self, keys):
        for offset, begin in keys:
            self.arrays[offset ^ 1, begin] = self.swap(self.arrays[offset, begin], 1)

    def first(self):
        block = self.arrays[0, 0]
        for bit in self.far:
            self.arrays[bit, 0] = self.swap(block, bit)
        self.near([(0, 0)])

    def second(self):
        pieces = 1 << max(1, len(self.far)).bit_length() - 1
        columns = self.whole // pieces
        for piece in range(pieces if len(self.far) > 1 else 0):
            begin = piece * columns
            part = {bit: self.arrays[bit, 0][:, begin : begin + columns] for bit in self.far}
            order = self.far[piece:] + self.far[:piece]
            known = [order[0]]
            for bit in order[1:]:
                for offset in list(known):
                    part[offset ^ bit] = self.swap(part[offset], bit)
                    self.arrays[offset ^ bit, begin] = part[offset ^ bit]
                    known.append(offset ^ bit)
                known.append(bit)
        self.near([(bit, 0) for bit in self.far])

    def third(self):
        self.near([key for key in self.arrays if (key[0] ^ 1, key[1]) not in self.arrays])

    def places(self, keys):
        return tuple((offset, begin, self.whole) for offset, begin in keys)


def add(a, b):
    return (a.astype(F32) + b.astype(F32)).astype(BF16)


def line_part(parts, axis, share):
    return lax.dynamic_index_in_dim(parts, jnp.clip(share, 0, lax.axis_size(axis) - 1), 0, False)


def line_scatter(parts, axis, step, arrived):
    count = lax.axis_size(axis)
    place = lax.axis_index(axis)
    up = [(p, p + 1) for p in range(step)]
    down = [(p, p - 1) for p in range(count - step, count)]
    up_share = count - step + place
    down_share = step - count + place
    if step < count - 1 - step:
        value = line_part(parts, axis, jnp.where(place < step, up_share, down_share))
        if arrived:
            value = add(value, arrived[0])
        return [lax.ppermute(value, axis, up + down)] * 2
    low, high = line_part(parts, axis, up_share), line_part(parts, axis, down_share)
    if arrived:
        low, high = add(low, arrived[0]), add(high, arrived[1])
    return [lax.ppermute(low, axis, up), lax.ppermute(high, axis, down)]


def line_gather(value, axis, step, arrays):
    count = lax.axis_size(axis)

    def move(what, *pairs):
        return lax.ppermute(what, axis, pairs)

    if count == 4:
        if step == 1:
            return [value, move(value, (0, 1), (1, 0), (2, 3), (3, 2)), move(value, (1, 2), (2, 1))]
        if step == 2:
            return arrays + [move(arrays[1], (1, 2), (2, 1)), move(arrays[2], (1, 0), (2, 3))]
        return arrays + [move(arrays[3], (1, 0), (2, 3))]
    if step > 1:
        return arrays
    low, high = [value], [value]
    for hop in range(1, count):
        low.append(move(low[-1], *[(p, p + 1) for p in range(hop - 1, count - 1)]))
        high.append(move(high[-1], *[(p, p - 1) for p in range(1, count - hop + 1)]))
    return low + high[1:]


def line_table(count):
    if count == 4:
        return ((0, 1, 4, 5), (1, 0, 2, 3), (3, 2, 0, 1), (5, 4, 1, 0))
    return tuple(
        tuple(place - share if share <= place else count - 1 + share - place for share in range(count))
        for place in range(count)
    )


def lr_in_start_kernel(table, scalar_ref, gain_ref, *refs):
    count = len(table)
    *blocks, w_ref, total_ref, square_ref, scaled, held, total, sems, out_sems = refs
    tokens, width = blocks[0].shape
    parts, rows, columns = held.shape
    begin = jnp.where(scalar_ref[0] < count // 2, 0, width)
    copies = []
    for k in range(parts):
        p, first = divmod(k * columns, width)
        source = w_ref.at[p, pl.ds(pl.multiple_of(begin, width), rows), pl.ds(first, columns)]
        copies.append((pltpu.make_async_copy(source, held.at[k], sems.at[k]),))
    copies = Fetch(copies, 2)
    copies.begin()
    for place in range(count):
        shares = [share + (place >= count // 2) for share in range(count - 1)]
        sources = [blocks[table[place][share]] for share in shares]

        @pl.when(scalar_ref[0] == place)
        def _(shares=shares, sources=sources):
            @pl.loop(0, tokens // HALO)
            def _(block):
                where = pl.ds(pl.multiple_of(block * HALO, HALO), HALO)
                squares = jnp.zeros((HALO, LANES), F32)
                for k, source in enumerate(sources):
                    wide = source[where, :].astype(F32)
                    for lane in range(0, width, LANES):
                        squares = squares + wide[:, lane : lane + LANES] * wide[:, lane : lane + LANES]
                    gain = gain_ref[:, shares[k] * width : (shares[k] + 1) * width]
                    scaled[where, k * width : (k + 1) * width] = (wide * gain).astype(BF16)
                square_ref[where, :] = squares

    sent = []
    for k in range(parts):
        p, first = divmod(k * columns, width)
        copies.get(k)
        total[k] = jnp.dot(scaled[...], held[k], preferred_element_type=F32)
        sent.append(pltpu.make_async_copy(total.at[k], total_ref.at[k], out_sems.at[k]))
        sent[-1].start()
    for copy in sent:
        copy.wait()


def lr_in_start(place, gain, blocks, table, weight):
    count = len(table)
    tokens, width = blocks[0].shape
    rows = (count - 1) * width
    columns = min(512, width)
    parts = 3 * width // columns
    return pl.pallas_call(
        functools.partial(lr_in_start_kernel, table),
        out_shape=(
            jax.ShapeDtypeStruct((parts, tokens, columns), F32),
            jax.ShapeDtypeStruct((tokens, LANES), F32),
        ),
        in_specs=[pl.BlockSpec(memory_space=pltpu.SMEM), *vmem(1 + len(blocks)), *in_hbm(1)],
        out_specs=(*in_hbm(1), *vmem(1)),
        scratch_shapes=[
            pltpu.VMEM((tokens, rows), BF16),
            pltpu.VMEM((parts, rows, columns), BF16),
            pltpu.VMEM((parts, tokens, columns), F32),
            pltpu.SemaphoreType.DMA((parts,)),
            pltpu.SemaphoreType.DMA((parts,)),
        ],
        compiler_params=params(VMEM_MIB),
        cost_estimate=cost(6 * tokens * rows * width, 6 * rows * width),
        name="lr_in_start",
    )(place, gain, *blocks, weight)


SEGMENTS = 4


def lr_mix_kernel(table, scalar_ref, gain_ref, square_ref, short_ref, rate_ref, total_ref, *refs):
    count = len(table)
    blocks, w_ref, q_out, u_out, send_ref = refs[: len(refs) - 15], *refs[len(refs) - 15 : len(refs) - 11]
    source, scaled, scale, held, begun, raw, q_ref, u_ref, sems, begun_sems, out_sems = refs[len(refs) - 11 :]
    tokens, width = blocks[0].shape
    model = count * width
    parts, _, columns = held.shape
    lags = short_ref.shape[0]
    prior = lags - 1
    poles = rate_ref.shape[0]
    begin = jnp.where(scalar_ref[0] < count // 2, model - width, 0)
    for place in range(count):
        share = count - 1 if place < count // 2 else 0

        @pl.when(scalar_ref[0] == place)
        def _(block=blocks[table[place][share]]):
            pltpu.make_async_copy(block, source, out_sems.at[0, 0]).start()

    copies = []
    for k in range(parts):
        p, first = divmod(k * columns, width)
        weight = w_ref.at[p, pl.ds(pl.multiple_of(begin, width), width), pl.ds(first, columns)]
        both = (
            pltpu.make_async_copy(weight, held.at[k], sems.at[k]),
            pltpu.make_async_copy(total_ref.at[k], begun.at[k], begun_sems.at[k]),
        )
        copies.append(both)
    copies = Fetch(copies)
    copies.begin()
    pltpu.make_async_copy(blocks[0], source, out_sems.at[0, 0]).wait()

    @pl.loop(0, tokens // HALO)
    def _(block):
        where = pl.ds(pl.multiple_of(block * HALO, HALO), HALO)
        wide = source[where, :].astype(F32)
        squares = square_ref[where, :]
        for lane in range(0, width, LANES):
            squares = squares + wide[:, lane : lane + LANES] * wide[:, lane : lane + LANES]
        mean = jnp.sum(squares, axis=-1, keepdims=True) * (1.0 / model)
        scale[where, :] = jnp.broadcast_to(lax.rsqrt(mean + 1e-6), (HALO, LANES))
        gain = gain_ref[:, pl.ds(pl.multiple_of(begin, width), width)]
        scaled[where, :] = (wide * gain).astype(BF16)

    for k in range(parts):
        p, first = divmod(k * columns, width)
        copies.get(k)
        total = jnp.dot(scaled[...], held[k], preferred_element_type=F32)
        for lane in range(0, columns, LANES):
            whole = (total[:, lane : lane + LANES] + begun[k, :, lane : lane + LANES]) * scale[...]
            put_rows(raw.at[p], prior, tokens, (first + lane) // LANES, whole.astype(BF16).astype(F32))

    raw3 = raw.reshape(3, tokens + prior, SUB, LANES)
    for p in range(3):
        raw3[p, :prior] = jnp.zeros((prior, SUB, LANES), F32)
    decay = [jnp.exp(-rate_ref[n]) for n in range(poles)]

    def mix(p, first):
        total = short_ref[0, p] * raw3[p, pl.ds(first + prior, STEP)]
        for lag in range(1, lags):
            total = total + short_ref[lag, p] * raw3[p, pl.ds(first + prior - lag, STEP)]
        return total

    def block(index, states):
        first = index * STEP
        q_ref[pl.ds(first, STEP)] = mix(0, first)
        product = mix(1, first) * mix(2, first)
        u_ref[pl.ds(first, STEP)] = product
        states = list(states)
        for t in range(STEP):
            for n in range(poles):
                states[n] = decay[n] * states[n] + product[t]
        return tuple(states)

    rows = tokens // SEGMENTS

    def moved(segment):
        where = pl.ds(pl.multiple_of(segment * rows, rows), rows)
        return (
            pltpu.make_async_copy(q_ref.at[where], q_out.at[where], out_sems.at[0, segment]),
            pltpu.make_async_copy(u_ref.at[where], u_out.at[where], out_sems.at[1, segment]),
        )

    def segment(index, states):
        steps = rows // STEP
        states = lax.fori_loop(index * steps, (index + 1) * steps, block, states)
        for copy in moved(index):
            copy.start()
        return states

    nothing = jnp.zeros((SUB, LANES), F32)
    states = lax.fori_loop(0, SEGMENTS, segment, (nothing,) * poles)
    lines = [*states]
    lines += [raw3[p, prior + j] for p in (1, 2) for j in range(prior)]
    lines += [raw3[p, tokens + j] for p in range(3) for j in range(prior)]
    for n, line in enumerate(lines):
        send_ref[n] = line.astype(BF16)
    for n in range(len(lines), send_ref.shape[0]):
        send_ref[n] = jnp.zeros((SUB, LANES), BF16)
    for index in range(SEGMENTS):
        for copy in moved(index):
            copy.wait()


def lr_mix(place, gain, begun, blocks, table, weight, short_w, rate):
    tokens, width = blocks[0].shape
    columns = min(512, width)
    parts = 3 * width // columns
    poles = rate.shape[0]
    prior = short_w.shape[0] - 1
    lines = -(-(poles + 5 * prior) // HALO) * HALO
    total, squares = begun
    rows = jax.ShapeDtypeStruct((tokens, SUB, LANES), F32)
    return pl.pallas_call(
        functools.partial(lr_mix_kernel, table),
        out_shape=(rows, rows, jax.ShapeDtypeStruct((lines, SUB, LANES), BF16)),
        in_specs=[pl.BlockSpec(memory_space=pltpu.SMEM), *vmem(4), *in_hbm(2 + len(blocks))],
        out_specs=(*in_hbm(2), *vmem(1)),
        scratch_shapes=[
            pltpu.VMEM((tokens, width), BF16),
            pltpu.VMEM((tokens, width), BF16),
            pltpu.VMEM((tokens, LANES), F32),
            pltpu.VMEM((parts, width, columns), BF16),
            pltpu.VMEM((parts, tokens, columns), F32),
            pltpu.VMEM((3, (tokens + prior) * SUB, LANES), F32),
            pltpu.VMEM((tokens, SUB, LANES), F32),
            pltpu.VMEM((tokens, SUB, LANES), F32),
            pltpu.SemaphoreType.DMA((parts,)),
            pltpu.SemaphoreType.DMA((parts,)),
            pltpu.SemaphoreType.DMA((2, SEGMENTS)),
        ],
        compiler_params=params(VMEM_MIB),
        cost_estimate=cost(6 * tokens * width * width, 6 * width * width),
        name="lr_mix",
    )(place, gain, squares, short_w, rate, total, *blocks, weight)


def lr_modal_kernel(places, scalar_ref, sent_ref, short_ref, rate_ref, res_ref, skip_ref, q_in, u_in, *refs):
    blocks = len(places)
    weights, out_ref, zs, change, z_ref, result = refs[:blocks], *refs[blocks : blocks + 5]
    q_ref, u_ref, row_sems = refs[blocks + 5 : blocks + 8]
    held, in_sems, out_sems = refs[blocks + 8 : -2], refs[-2], refs[-1]
    rows = q_ref.shape[0] // SEGMENTS

    def moved(segment):
        where = pl.ds(pl.multiple_of(segment * rows, rows), rows)
        return (
            pltpu.make_async_copy(q_in.at[where], q_ref.at[where], row_sems.at[0, segment]),
            pltpu.make_async_copy(u_in.at[where], u_ref.at[where], row_sems.at[1, segment]),
        )

    for index in range(SEGMENTS):
        for copy in moved(index):
            copy.start()
    copies = Fetch(fetch(weights, held, in_sems).copies, blocks)
    tokens = q_ref.shape[0]
    width = z_ref.shape[1]
    lags = short_ref.shape[0]
    prior = lags - 1
    poles = rate_ref.shape[0]
    position = scalar_ref[0]
    zs3 = zs.reshape(tokens, SUB, LANES)

    def head(index, p, j):
        return sent_ref[index, poles + (p - 1) * prior + j].astype(F32)

    def tail(index, p, j):
        return sent_ref[index, poles + 2 * prior + p * prior + j].astype(F32)

    def missed(index, p, t):
        total = short_ref[t + 1, p] * tail(index - 1, p, prior - 1)
        for lag in range(t + 2, lags):
            total = total + short_ref[lag, p] * tail(index - 1, p, prior + t - lag)
        return total

    def had(index, p, t):
        total = short_ref[0, p] * head(index, p, t)
        for lag in range(1, t + 1):
            total = total + short_ref[lag, p] * head(index, p, t - lag)
        return total

    def change_of_u(index, t):
        key, value = had(index, 1, t), had(index, 2, t)
        more_key, more_value = missed(index, 1, t), missed(index, 2, t)
        return key * more_value + more_key * value + more_key * more_value

    nothing = jnp.zeros((SUB, LANES), F32)
    change[0] = jnp.zeros((prior, SUB, LANES), F32)

    @pl.loop(1, position + 1)
    def _(index):
        for t in range(prior):
            change[index, t] = change_of_u(index, t)

    decay, weight, enter = [], [], []
    for n in range(poles):
        rate = rate_ref[n]
        decay.append(jnp.exp(-rate))
        weight.append(res_ref[n] * jnp.sqrt(1.0 - jnp.exp(-2.0 * rate)))

        def arrive(index, total, n=n, rate=rate):
            distance = (position - 1 - index).astype(F32)
            end = sent_ref[index, n].astype(F32)
            for t in range(prior):
                end = end + jnp.exp(-rate * (tokens - 1 - t)) * change[index, t]
            return total + jnp.exp(-rate * tokens * distance) * end

        enter.append(lax.fori_loop(0, position, arrive, nothing))

    for copy in moved(0):
        copy.wait()
    copies.begin()
    first_u, first_q = [], []
    for t in range(prior):
        first_u.append(u_ref[t] + change[position, t])
        before = lax.max(position, 1)
        first_q.append(q_ref[t] + jnp.where(position > 0, missed(before, 0, t), 0.0))

    def row(states, value, query):
        total = skip_ref[...] * value
        for n in range(poles):
            states[n] = decay[n] * states[n] + value
            total = total + weight[n] * states[n]
        return query * total

    states = list(enter)
    for t in range(STEP):
        value, query = (first_u[t], first_q[t]) if t < prior else (u_ref[t], q_ref[t])
        zs3[t] = row(states, value, query)

    def block(index, states):
        first = index * STEP
        states = list(states)
        for t in range(STEP):
            zs3[first + t] = row(states, u_ref[first + t], q_ref[first + t])
        return tuple(states)

    steps = rows // STEP
    states = lax.fori_loop(1, steps, block, tuple(states))

    def segment(index, states):
        for copy in moved(index):
            copy.wait()
        return lax.fori_loop(index * steps, (index + 1) * steps, block, states)

    lax.fori_loop(1, SEGMENTS, segment, states)
    for tile in range(width // LANES):
        lanes = slice(tile * LANES, (tile + 1) * LANES)
        z_ref[:, lanes] = get_rows(zs, 0, tokens, tile).astype(BF16)
    place_blocks(places, position, z_ref[...], copies, held, result, out_ref, out_sems)


def lr_modal(position, q, u, sent, short_w, rate, res, skip, width, places, weights, shares):
    tokens = q.shape[0]
    prior = short_w.shape[0] - 1
    total = sum(w.shape[1] for w in weights)
    return pl.pallas_call(
        functools.partial(lr_modal_kernel, places),
        out_shape=jax.ShapeDtypeStruct((shares, tokens, total // shares), BF16),
        in_specs=[pl.BlockSpec(memory_space=pltpu.SMEM), *vmem(5), *in_hbm(2 + len(weights))],
        out_specs=in_hbm(1)[0],
        scratch_shapes=[
            pltpu.VMEM((tokens * SUB, LANES), F32),
            pltpu.VMEM((sent.shape[0], prior, SUB, LANES), F32),
            pltpu.VMEM((tokens, width), BF16),
            pltpu.VMEM((tokens, total), BF16),
            pltpu.VMEM((tokens, SUB, LANES), F32),
            pltpu.VMEM((tokens, SUB, LANES), F32),
            pltpu.SemaphoreType.DMA((2, SEGMENTS)),
            *[pltpu.VMEM(w.shape, w.dtype) for w in weights],
            pltpu.SemaphoreType.DMA((len(weights),)),
            pltpu.SemaphoreType.DMA((len(weights),)),
        ],
        compiler_params=params(VMEM_MIB),
        cost_estimate=cost(2 * tokens * width * total, 2 * total * (width + tokens)),
        name="lr_modal",
    )(position, sent, short_w, rate, res, skip, q, u, *weights)


def local(
    residual_in,
    mr_qkv,
    mr_short_w,
    mr_filter,
    mr_skip,
    mr_out_w,
    lr_gain,
    lr_in_w,
    lr_short_w,
    lr_rate,
    lr_res,
    lr_skip,
    lr_out_w,
):
    sequences, tokens, _, width = mr_qkv.shape
    taps = mr_filter.shape[0]
    prior = mr_short_w.shape[0] - 1
    ctx, tp = lax.axis_size("ctx"), lax.axis_size("tp")
    position = lax.axis_index("ctx").astype(jnp.int32).reshape(1)
    place = lax.axis_index("tp").astype(jnp.int32).reshape(1)
    onward = [(i, i + 1) for i in range(ctx - 1)]

    tail = mr_qkv[:, tokens - taps - prior :].astype(F32)
    mixed = sum(mr_short_w[lag, 1:] * tail[:, prior - lag : prior - lag + taps, 1:] for lag in range(prior + 1))
    tail_u = (mixed[:, :, 0] * mixed[:, :, 1]).astype(BF16)
    last = jnp.swapaxes(mr_qkv[:, tokens - prior :], 1, 2).reshape(sequences, 3 * prior, width)
    last = jnp.pad(last, ((0, 0), (0, HALO - 3 * prior), (0, 0)))
    halo = lax.ppermute(jnp.concatenate([tail_u, last], axis=1), "ctx", onward)

    x = jnp.swapaxes(mr_qkv, 1, 2)
    mr_short, lr_short = tiles(mr_short_w), tiles(lr_short_w)
    mr_taps, mr_direct = tiles(mr_filter), tiles(mr_skip)
    rate, res, lr_direct = tiles(lr_rate), tiles(lr_res), tiles(lr_skip)
    in_w = jnp.swapaxes(lr_in_w, 0, 1)
    gain = lr_gain.reshape(1, -1)

    def scattered(parts):
        return lax.psum_scatter(parts, "tp", scatter_dimension=0)

    def as_mid(s, *terms):
        total = residual_in[s].astype(F32)
        for term in terms:
            total = total + term.astype(F32)
        return lax.optimization_barrier(total.astype(BF16))

    table = line_table(tp)
    assert sequences == 2

    mr_w = SwapGather(mr_out_w, "ctx")
    mr_w.first()
    body, q, conv = mr_local(x, mr_short, mr_taps, mr_direct)
    mr_w.arrays, halo = together(mr_w.arrays, halo)

    early = list(mr_w.arrays)
    mr_w.second()
    early = [k for k in mr_w.arrays if k in early or (k[0] ^ 1, k[1]) in early]
    head = mr_finish(x, halo, q, conv, mr_short, mr_taps, mr_direct, 0, conv)
    z = head, body, 0
    first = project(z, position, mr_w.places(early), [mr_w.arrays[k] for k in early], tp)
    mr_w.arrays, first = together(mr_w.arrays, first)

    mr_w.third()
    late = [k for k in mr_w.arrays if k not in early]
    if late:
        first = project(z, position, mr_w.places(late), [mr_w.arrays[k] for k in late], tp, first)
    share = scattered(first)

    lr_w = SwapGather(after(lr_out_w, first), "ctx")
    lr_w.first()
    head = mr_finish(x, halo, q, conv, mr_short, mr_taps, mr_direct, 1, first)
    second = project((head, body, 1), position, mr_w.places(mr_w.arrays), list(mr_w.arrays.values()), tp)
    lr_w.arrays, second = together(lr_w.arrays, second)
    lr_w.second()
    lr_w.arrays, share = together(lr_w.arrays, share)

    def near(blocks):
        return blocks[:5] if tp == 4 else blocks

    def scatter_all(parts, steps, arrived):
        for step in steps:
            arrived = line_scatter(parts, "tp", step, arrived)
        return arrived

    mids = [as_mid(0, share)]
    blocks = line_gather(mids[0], "tp", 1, None)
    lr_w.third()
    blocks, second, lr_w.arrays = together(blocks, second, lr_w.arrays)
    blocks = line_gather(mids[0], "tp", 2, blocks)
    arrived = line_scatter(second, "tp", 1, None)
    blocks, arrived = together(blocks, arrived)
    blocks = line_gather(mids[0], "tp", 3, blocks)
    arrived = line_scatter(second, "tp", 2, arrived)
    begun = lr_in_start(place, gain, near(blocks), table, in_w)
    blocks, arrived, begun = together(blocks, arrived, begun)
    arrived = scatter_all(second, range(3, tp), arrived)
    q, u, send = lr_mix(place, gain, begun, blocks, table, in_w, lr_short, rate)
    arrived, q, u, send = together(arrived, q, u, send)
    mids.append(as_mid(1, line_part(second, "tp", lax.axis_index("tp")), *arrived))
    blocks = line_gather(mids[1], "tp", 1, None)
    sent = lax.all_gather(send, "ctx", axis=0)
    blocks, sent, q, u = together(blocks, sent, q, u)
    blocks = line_gather(mids[1], "tp", 2, blocks)
    lr_places, lr_weights = lr_w.places(lr_w.arrays), list(lr_w.arrays.values())
    modal_w = (lr_short, rate, res, lr_direct, width, lr_places, lr_weights, tp)
    first = lr_modal(position, q, u, sent, *modal_w)
    blocks, first = together(blocks, first)
    begun = lr_in_start(place, gain, near(blocks), table, in_w)
    blocks = line_gather(mids[1], "tp", 3, blocks)
    blocks, begun, first = together(blocks, begun, first)
    share = scattered(first)
    q, u, send = lr_mix(place, gain, begun, blocks, table, in_w, lr_short, rate)
    sent = lax.all_gather(send, "ctx", axis=0)
    second = lr_modal(position, q, u, sent, *modal_w)
    out = (mids[0].astype(F32) + share.astype(F32)).astype(BF16)
    out, second = together(jnp.stack([out, mids[1]]), second)
    last = (out[1].astype(F32) + scattered(second).astype(F32)).astype(BF16)
    return out.at[1].set(last)


def solution(mesh):
    in_specs = (
        P(None, "ctx", "tp"),
        P(None, "ctx", None, "tp"),
        P(None, None, "tp"),
        P(None, "tp"),
        P("tp"),
        P("tp", "ctx"),
        P(),
        P(None, None, "tp"),
        P(None, None, "tp"),
        P(None, "tp"),
        P(None, "tp"),
        P("tp"),
        P("tp", "ctx"),
    )
    out_specs = P(None, "ctx", "tp")
    return jax.shard_map(local, mesh=mesh, in_specs=in_specs, out_specs=out_specs, check_vma=False)
```

time: 384 us -> 341 us (0.89)
  waiting for transfers between devices: 196 us -> 114 us
  Pallas kernels: 93.6 us -> 116 us
  starting transfers between devices: 28.3 us -> 47.2 us
  other arithmetic: 9.9 us -> 15.9 us
  local copies, waits for them, and re-layouts: 17.4 us -> 11.4 us
    ppermute x10, waiting for transfers between devices: 104 us -> 28.1 us  [move(): return lax.ppermute(what, axis, pairs)]
    pallas_call x14 -> x10, Pallas kernels: 83.7 us -> 104 us  [the longest x1 23.6 us: mr_local(): pl.pallas_call(mr_local_kernel, grid=(sequences,), out_shape=(jax.ShapeDt...]
    ppermute x18 -> x23, waiting for transfers between devices: 49.8 us -> 29.7 us  [the longest x18 26.7 us: swap(): return lax.ppermute(value, self.axis, swap_pairs(self.axis, bit))]
    ppermute x18 -> x23, starting transfers between devices: 14.1 us -> 31.7 us  [the longest x18 12.3 us: swap(): return lax.ppermute(value, self.axis, swap_pairs(self.axis, bit))]
    reduce_scatter x4 -> x3, waiting for transfers between devices: 42.6 us -> 56 us  [scattered(): return lax.psum_scatter(parts, 'tp', scatter_dimension=0)]
    unnamed x89 -> x65, local copies, waits for them, and re-layouts: 15.1 us -> 7.13 us
    convert_element_type x2 -> x4, other arithmetic: 2.78 us -> 7.84 us  [the longest x2 5.05 us: add(): return (a.astype(F32) + b.astype(F32)).astype(BF16)]
  transfers between devices with their start and end apart: 33 -> 37, of which waited for: 15 -> 17; matrix products, arithmetic and copies ran while one was open for 2% -> 4% of each run, Pallas kernels for 21% -> 33%
where the time goes in v3:
time: 341 us; the launch traced here: 340 us
  Pallas kernels  116 us (34%)
  waiting for transfers between devices  114 us (33%)
  starting transfers between devices  47.2 us (14%)
  blocking collectives  21.6 us (6%)
  other arithmetic  15.9 us (5%)
  between operations  13.7 us (4%)
  local copies, waits for them, and re-layouts  11.4 us (3%)
    reduce_scatter x3, waiting for transfers between devices, scattered(): return lax.psum_scatter(parts, 'tp', scatter_dimension=0)  56 us
    ppermute x10, waiting for transfers between devices, move(): return lax.ppermute(what, axis, pairs)  28.1 us
    ppermute x18, waiting for transfers between devices, swap(): return lax.ppermute(value, self.axis, swap_pairs(self.axis, bit))  26.7 us
    pallas_call x1, Pallas kernels, mr_local(): pl.pallas_call(mr_local_kernel, grid=(sequences,), out_shape=(jax.ShapeDt...  23.6 us
    pallas_call x2, Pallas kernels, lr_in_start(): pl.pallas_call(functools.partial(lr_in_start_kernel, table), out_shape=(j...  23.3 us
    all_gather x2, blocking collectives, local(): sent = lax.all_gather(send, 'ctx', axis=0)  21.6 us
    pallas_call x2, Pallas kernels, lr_modal(): pl.pallas_call(functools.partial(lr_modal_kernel, places), out_shape=jax....  20.6 us
    pallas_call x2, Pallas kernels, lr_mix(): pl.pallas_call(functools.partial(lr_mix_kernel, table), out_shape=(rows,...  20.5 us
  transfers between devices with their start and end apart: 37, of which 17 were waited for; matrix products, arithmetic and copies ran while one was open for 4% of the time, Pallas kernels for 33%

profile of v3, /device:TPU:0, one launch (start us, length us, event | category | flops | bytes accessed | tf_op | source)
XLA Modules:
  0.0 340.0 jit_solution(11128583850267251723)
XLA Ops:
  7.0 2.5 collective-permute-start.1
  9.5 1.5 collective-permute-start.2
  11.0 1.9 copy_convert_fusion
  15.6 2.7 collective-permute-start.3
  19.9 23.6 %mr_local.1 = (bf16[2,256,1024]{2,1,0:T(8,128)(2,1)}, f32[2,144,8,128]{3,2,1,0:T(8,128)}, f32[2,144,8,128]{3,2,1,0:T(8,128)}) custom-call(bf16[2,3,256,1024]{3,2,1,0:T(8,128)(2,1)} %bitcast.62, f32[3,3,8,128]{3,2,1,0:T(8,128)} %reshape.85.short_ref, f32[128,8,128]{2,1,0:T(8,128)} %bitcast.65, f32[8,128]{1,0:T(8,128)} %bitcast.86), custom_call_target="tpu_custom_call" | custom-call | flops 1000000000 | bytes 1000000 | tf_op jit(solution)/shard_map/mr_local/pallas_call | solution.py:127
  45.2 6.1 %mr_finish.2.head_ref = bf16[144,1024]{1,0:T(8,128)(2,1)} custom-call(bf16[2,3,256,1024]{3,2,1,0:T(8,128)(2,1)} %bitcast.63, bf16[2,144,1024]{2,1,0:T(8,128)(2,1)} %collective-permute-done.3.halo_ref, f32[2,144,8,128]{3,2,1,0:T(8,128)} %get-tuple-element.119.q_ref, f32[2,144,8,128]{3,2,1,0:T(8,128)} %get-tuple-element.120.conv_ref.gate_ref, ...), custom_call_target="tpu_custom_call" | custom-call | flops 40000000000 | bytes 1000000 | tf_op jit(solution)/shard_map/mr_finish/pallas_call | solution.py:212
  52.8 5.3 %project.3.refs_4_ = bf16[4,256,1024]{2,1,0:T(8,128)(2,1)} custom-call(s32[1]{0:T(128)} %bitcast.1.scalar_ref, bf16[144,1024]{1,0:T(8,128)(2,1)} %mr_finish.2.head_ref, bf16[2,256,1024]{2,1,0:T(8,128)(2,1)} %get-tuple-element.121.body_ref, bf16[1024,512]{1,0:T(8,128)(2,1)} %refs_0_.1, bf16[1024,512]{1,0:T(8,128)(2,1)} %copy-done.9, ...), custom_call_target="tpu_custom_call" | custom-call | flops 1610612736 | bytes 7864320 | tf_op jit(solution)/shard_map/project/pallas_call | solution.py:300
  59.8 1.4 collective-permute-done.8.refs_2_.refs_8_
  62.8 3.8 %project.4.gate_ref = bf16[4,256,1024]{2,1,0:T(8,128)(2,1)} custom-call(s32[1]{0:T(128)} %bitcast.1.scalar_ref, bf16[144,1024]{1,0:T(8,128)(2,1)} %mr_finish.2.head_ref, bf16[2,256,1024]{2,1,0:T(8,128)(2,1)} %get-tuple-element.121.body_ref, bf16[1024,256]{1,0:T(8,128)(2,1)} %copy-done.19, ...), custom_call_target="tpu_custom_call", output_to_operand_aliasing={{}: (7, {})} | custom-call | flops 536870912 | bytes 2621440 | tf_op jit(solution)/shard_map/project/pallas_call | solution.py:300
  67.5 1.5 collective-permute-start.12
  69.1 6.1 %mr_finish.3.head_ref = bf16[144,1024]{1,0:T(8,128)(2,1)} custom-call(bf16[2,3,256,1024]{3,2,1,0:T(8,128)(2,1)} %bitcast.64, bf16[2,144,1024]{2,1,0:T(8,128)(2,1)} %collective-permute-done.3.halo_ref, f32[2,144,8,128]{3,2,1,0:T(8,128)} %get-tuple-element.119.q_ref, f32[2,144,8,128]{3,2,1,0:T(8,128)} %get-tuple-element.120.conv_ref.gate_ref, ...), custom_call_target="tpu_custom_call" | custom-call | flops 40000000000 | bytes 1000000 | tf_op jit(solution)/shard_map/mr_finish/pallas_call | solution.py:212
  75.2 7.1 %project.5 = bf16[4,256,1024]{2,1,0:T(8,128)(2,1)} custom-call(s32[1]{0:T(128)} %bitcast.1.scalar_ref, bf16[144,1024]{1,0:T(8,128)(2,1)} %mr_finish.3.head_ref, bf16[2,256,1024]{2,1,0:T(8,128)(2,1)} %get-tuple-element.121.body_ref, bf16[1024,512]{1,0:T(8,128)(2,1)} %refs_0_.1, bf16[1024,512]{1,0:T(8,128)(2,1)} %copy-done.9, bf16[1024,512]{1,0:T(8,128)(2,1)} %copy-done.6, ...), custom_call_target="tpu_custom_call" | custom-call | flops 2147483648 | bytes 10485760 | tf_op jit(solution)/shard_map/project/pallas_call | solution.py:300
  82.3 10.2 %collective-permute-done.11.refs_2_ = bf16[1024,512]{1,0:T(8,128)(2,1)S(1)} collective-permute-done((bf16[1024,512]{1,0:T(8,128)(2,1)}, bf16[1024,512]{1,0:T(8,128)(2,1)S(1)}, u32[]{:S(2)}, u32[]{:S(2)}) %collective-permute-start.11) | collective-permute-done | bytes 1048608 | tf_op jit(solution)/shard_map/ppermute | solution.py:340
  94.7 1.3 collective-permute-start.15
  97.0 11.6 %collective-permute-done.15.refs_6_ = bf16[1024,256]{1,0:T(8,128)(2,1)S(1)} collective-permute-done((bf16[1024,256]{1,0:T(8,128)(2,1)S(1)}, bf16[1024,256]{1,0:T(8,128)(2,1)S(1)}, u32[]{:S(2)}, u32[]{:S(2)}) %collective-permute-start.15) | collective-permute-done | bytes 524320 | tf_op jit(solution)/shard_map/ppermute | solution.py:340
  111.4 1.8 reduce-scatter.4.cloned.1.call-done
  113.2 1.4 fusion.9.refs_0_
  114.7 1.5 collective-permute-start.18
  116.7 11.5 %collective-permute-done.17.refs_1_ = bf16[256,1024]{1,0:T(8,128)(2,1)S(1)} collective-permute-done((bf16[256,1024]{1,0:T(8,128)(2,1)S(1)}, bf16[256,1024]{1,0:T(8,128)(2,1)S(1)}, u32[]{:S(2)}, u32[]{:S(2)}) %collective-permute-start.17) | collective-permute-done | bytes 524320 | tf_op jit(solution)/shard_map/ppermute | solution.py:405
  128.2 1.5 collective-permute-start.21
  129.7 1.3 collective-permute-start.22
  131.8 8.6 %collective-permute-start.23 = (bf16[256,1024]{1,0:T(8,128)(2,1)}, bf16[256,1024]{1,0:T(8,128)(2,1)}, u32[]{:S(2)}, u32[]{:S(2)}) collective-permute-start(bf16[256,1024]{1,0:T(8,128)(2,1)} %dynamic-slice_bitcast_fusion), channel_id=1, source_target_pairs={{0,1},{3,2},{4,5},{7,6},{8,9},{11,10},{12,13},{15,14},{16,17},{19,... | collective-permute-start | bytes 1572872 | tf_op jit(solution)/shard_map/ppermute | solution.py:394
  140.4 6.3 %collective-permute-done.22.refs_4_ = bf16[256,1024]{1,0:T(8,128)(2,1)} collective-permute-done((bf16[256,1024]{1,0:T(8,128)(2,1)}, bf16[256,1024]{1,0:T(8,128)(2,1)}, u32[]{:S(2)}, u32[]{:S(2)}) %collective-permute-start.22) | collective-permute-done | bytes 524320 | tf_op jit(solution)/shard_map/ppermute | solution.py:405
  146.7 2.8 collective-permute-done.23
  149.5 1.3 collective-permute-start.24
  150.8 2.6 fusion.6
  153.4 6.2 %collective-permute-start.25 = (bf16[256,1024]{1,0:T(8,128)(2,1)}, bf16[256,1024]{1,0:T(8,128)(2,1)}, u32[]{:S(2)}, u32[]{:S(2)}) collective-permute-start(bf16[256,1024]{1,0:T(8,128)(2,1)} %get-tuple-element.222), channel_id=1, source_target_pairs={{0,1},{1,2},{4,5},{5,6},{8,9},{9,10},{12,13},{13,14},{16,17},{17,1... | collective-permute-start | bytes 1572872 | tf_op jit(solution)/shard_map/ppermute | solution.py:398
  159.6 1.5 collective-permute-start.26
  161.1 11.6 %lr_in_start.2 = (f32[6,256,512]{2,1,0:T(8,128)}, f32[256,128]{1,0:T(8,128)}) custom-call(s32[1]{0:T(128)} %bitcast.16.scalar_ref, f32[1,4096]{1,0:T(1,128)} %bitcast.77, bf16[256,1024]{1,0:T(8,128)(2,1)} %copy-done.1, bf16[256,1024]{1,0:T(8,128)(2,1)} %copy-done.12, bf16[256,1024]{1,0:T(8,128)(2,1)} %collective-permute-done.18.refs_2_, ...), custom_call_target="tpu_custom_call" | custom-call | flops 4831838208 | bytes 18874368 | tf_op jit(solution)/shard_map/lr_in_start/pallas_call | solution.py:479
  172.8 2.4 fusion.5
  175.2 2.0 collective-permute-start.27
  177.2 1.3 collective-permute-start.28
  179.8 10.2 %lr_mix.2 = (f32[256,8,128]{2,1,0:T(8,128)}, f32[256,8,128]{2,1,0:T(8,128)}, bf16[32,8,128]{2,1,0:T(8,128)(2,1)}) custom-call(s32[1]{0:T(128)} %bitcast.16.scalar_ref, f32[1,4096]{1,0:T(1,128)} %bitcast.78, f32[256,128]{1,0:T(8,128)} %get-tuple-element.165.square_ref, f32[3,3,8,128]{3,2,1,0:T(8,128)} %reshape.89.short_ref, f32[16,8,128]{2,1,0:T(8,128)} %bitcast.70, ...), custom_call_target="tpu_custom_call" | custom-call | flops 1610612736 | bytes 6291456 | tf_op jit(solution)/shard_map/lr_mix/pallas_call | solution.py:615
  190.2 1.4 fusion.11.refs_0_
  191.6 3.2 collective-permute-start.29
  195.5 10.8 %all-gather = bf16[256,8,128]{2,1,0:T(8,128)(2,1)} all-gather(bf16[32,8,128]{2,1,0:T(8,128)(2,1)S(1)} %copy-done.27), channel_id=2, replica_groups=mesh['ctx'=8,'tp'=4] {'ctx'}, dimensions={0}, use_global_device_ids=true | all-gather | bytes 589824 | tf_op jit(solution)/shard_map/all_gather | solution.py:881
  207.0 1.3 collective-permute-start.32
  208.9 10.2 %lr_modal.2 = bf16[4,256,1024]{2,1,0:T(8,128)(2,1)} custom-call(s32[1]{0:T(128)} %bitcast.1.scalar_ref, bf16[8,32,8,128]{3,2,1,0:T(8,128)(2,1)} %bitcast.68, f32[3,3,8,128]{3,2,1,0:T(8,128)} %reshape.89.short_ref, f32[16,8,128]{2,1,0:T(8,128)} %bitcast.71, f32[16,8,128]{2,1,0:T(8,128)} %bitcast.74, f32[8,128]{1,0:T(8,128)} %bitcast.84, ...), custom_call_target="tpu_custom_call" | custom-call | flops 2147483648 | bytes 10485760 | tf_op jit(solution)/shard_map/lr_modal/pallas_call | solution.py:758
  219.2 7.7 %collective-permute-done.32.refs_4_ = bf16[256,1024]{1,0:T(8,128)(2,1)S(1)} collective-permute-done((bf16[256,1024]{1,0:T(8,128)(2,1)S(1)}, bf16[256,1024]{1,0:T(8,128)(2,1)S(1)}, u32[]{:S(2)}, u32[]{:S(2)}) %collective-permute-start.32) | collective-permute-done | bytes 524320 | tf_op jit(solution)/shard_map/ppermute | solution.py:405
  226.9 1.3 collective-permute-start.33
  228.2 11.6 %lr_in_start.3 = (f32[6,256,512]{2,1,0:T(8,128)}, f32[256,128]{1,0:T(8,128)}) custom-call(s32[1]{0:T(128)} %bitcast.16.scalar_ref, f32[1,4096]{1,0:T(1,128)} %bitcast.79, bf16[256,1024]{1,0:T(8,128)(2,1)} %copy-done.3, bf16[256,1024]{1,0:T(8,128)(2,1)} %copy-done.13, bf16[256,1024]{1,0:T(8,128)(2,1)} %copy-done.14, bf16[256,1024]{1,0:T(8,128)(2,1)} %copy-done.15, ...), custom_call_target="tpu_custom_call" | custom-call | flops 4831838208 | bytes 18874368 | tf_op jit(solution)/shard_map/lr_in_start/pallas_call | solution.py:479
  239.9 2.5 collective-permute-done.33.refs_5_
  243.2 10.3 %lr_mix.3 = (f32[256,8,128]{2,1,0:T(8,128)}, f32[256,8,128]{2,1,0:T(8,128)}, bf16[32,8,128]{2,1,0:T(8,128)(2,1)}) custom-call(s32[1]{0:T(128)} %bitcast.16.scalar_ref, f32[1,4096]{1,0:T(1,128)} %bitcast.80, f32[256,128]{1,0:T(8,128)} %get-tuple-element.206.square_ref, f32[3,3,8,128]{3,2,1,0:T(8,128)} %reshape.89.short_ref, f32[16,8,128]{2,1,0:T(8,128)} %bitcast.72, ...), custom_call_target="tpu_custom_call" | custom-call | flops 1610612736 | bytes 6291456 | tf_op jit(solution)/shard_map/lr_mix/pallas_call | solution.py:615
  253.6 10.8 %all-gather.1 = bf16[256,8,128]{2,1,0:T(8,128)(2,1)} all-gather(bf16[32,8,128]{2,1,0:T(8,128)(2,1)} %get-tuple-element.214), channel_id=3, replica_groups=mesh['ctx'=8,'tp'=4] {'ctx'}, dimensions={0}, use_global_device_ids=true | all-gather | bytes 589824 | tf_op jit(solution)/shard_map/all_gather | solution.py:893
  264.4 10.3 %lr_modal.3 = bf16[4,256,1024]{2,1,0:T(8,128)(2,1)} custom-call(s32[1]{0:T(128)} %bitcast.1.scalar_ref, bf16[8,32,8,128]{3,2,1,0:T(8,128)(2,1)} %bitcast.69, f32[3,3,8,128]{3,2,1,0:T(8,128)} %reshape.89.short_ref, f32[16,8,128]{2,1,0:T(8,128)} %bitcast.73, f32[16,8,128]{2,1,0:T(8,128)} %bitcast.75, f32[8,128]{1,0:T(8,128)} %bitcast.85, ...), custom_call_target="tpu_custom_call" | custom-call | flops 2147483648 | bytes 10485760 | tf_op jit(solution)/shard_map/lr_modal/pallas_call | solution.py:758
  274.7 10.7 %reduce-scatter.6.cloned.1.call-done = bf16[1,256,1024]{2,1,0:T(8,128)(2,1)} async-done(((bf16[4,256,1024]{2,1,0:T(8,128)(2,1)}), bf16[1,256,1024]{2,1,0:T(8,128)(2,1)}) %reduce-scatter.6.cloned.1.call-update) | async-done | bytes 524304 | tf_op jit(solution)/shard_map/reduce_scatter | solution.py:819
  287.7 43.5 %reduce-scatter.8.cloned.1.call-done = bf16[1,256,1024]{2,1,0:T(8,128)(2,1)} async-done(((bf16[4,256,1024]{2,1,0:T(8,128)(2,1)}), bf16[1,256,1024]{2,1,0:T(8,128)(2,1)}) %reduce-scatter.8.cloned.1.call-update) | async-done | bytes 524304 | tf_op jit(solution)/shard_map/reduce_scatter | solution.py:819
  331.2 2.2 fusion.13
  (131 shorter events, 26.1 us)
Async XLA Ops:
  6.5 106.6 %reduce-scatter.4.cloned.1.call-start = ((), (), s32[]{:S(2)}) async-start(), calls=%async_computation.3 | async-start | bytes 2621440 | tf_op jit(solution)/shard_map/reduce_scatter | solution.py:819
  6.5 37.0 %collective-permute-start = (bf16[1024,512]{1,0:T(8,128)(2,1)}, bf16[1024,512]{1,0:T(8,128)(2,1)S(1)}, u32[]{:S(2)}, u32[]{:S(2)}) collective-permute-start(bf16[1024,512]{1,0:T(8,128)(2,1)} %refs_0_.1), channel_id=1, source_target_pairs={{0,4},{4,0},{8,12},{12,8},{16,20},{20,16},{24,28},{28,24},{1,5},{5... | collective-permute-start | bytes 3145736 | tf_op jit(solution)/shard_map/ppermute | solution.py:340
  7.0 36.6 %collective-permute-start.1 = (bf16[1024,512]{1,0:T(8,128)(2,1)}, bf16[1024,512]{1,0:T(8,128)(2,1)S(1)}, u32[]{:S(2)}, u32[]{:S(2)}) collective-permute-start(bf16[1024,512]{1,0:T(8,128)(2,1)} %refs_0_.1), channel_id=1, source_target_pairs={{0,8},{4,12},{8,0},{12,4},{16,24},{20,28},{24,16},{28,20},{1,9},{5... | collective-permute-start | bytes 3145736 | tf_op jit(solution)/shard_map/ppermute | solution.py:340
  9.5 34.1 %collective-permute-start.2 = (bf16[1024,512]{1,0:T(8,128)(2,1)}, bf16[1024,512]{1,0:T(8,128)(2,1)S(1)}, u32[]{:S(2)}, u32[]{:S(2)}) collective-permute-start(bf16[1024,512]{1,0:T(8,128)(2,1)} %refs_0_.1), channel_id=1, source_target_pairs={{0,16},{4,20},{8,24},{12,28},{16,0},{20,4},{24,8},{28,12},{1,17},{... | collective-permute-start | bytes 3145736 | tf_op jit(solution)/shard_map/ppermute | solution.py:340
  15.6 27.9 %collective-permute-start.3 = (bf16[2,144,1024]{2,1,0:T(8,128)(2,1)}, bf16[2,144,1024]{2,1,0:T(8,128)(2,1)}, u32[]{:S(2)}, u32[]{:S(2)}) collective-permute-start(bf16[2,144,1024]{2,1,0:T(8,128)(2,1)} %fusion.12), channel_id=1, source_target_pairs={{0,4},{4,8},{8,12},{12,16},{16,20},{20,24},{24,28},{1,5},{5,9},{9,... | collective-permute-start | bytes 1769480 | tf_op jit(solution)/shard_map/ppermute | solution.py:809
  43.6 7.7 %collective-permute-start.5 = (bf16[1024,512]{1,0:T(8,128)(2,1)S(1)}, bf16[1024,512]{1,0:T(8,128)(2,1)S(1)}, u32[]{:S(2)}, u32[]{:S(2)}) collective-permute-start(bf16[1024,512]{1,0:T(8,128)(2,1)S(1)} %collective-permute-done.2.refs_3_.refs_4_), channel_id=1, source_target_pairs={{0,4},{4,0},{8,12},{12,8},{16,20},{20,16},{24,28},{28,24},{1,5},{5... | collective-permute-start | bytes 3145736 | tf_op jit(solution)/shard_map/ppermute | solution.py:340
  43.7 7.6 %collective-permute-start.4 = (bf16[1024,512]{1,0:T(8,128)(2,1)S(1)}, bf16[1024,512]{1,0:T(8,128)(2,1)S(1)}, u32[]{:S(2)}, u32[]{:S(2)}) collective-permute-start(bf16[1024,512]{1,0:T(8,128)(2,1)S(1)} %collective-permute-done.1.refs_2_), channel_id=1, source_target_pairs={{0,4},{4,0},{8,12},{12,8},{16,20},{20,16},{24,28},{28,24},{1,5},{5... | collective-permute-start | bytes 3145736 | tf_op jit(solution)/shard_map/ppermute | solution.py:340
  44.3 13.9 %collective-permute-start.6 = (bf16[1024,256]{1,0:T(8,128)(2,1)S(1)}, bf16[1024,256]{1,0:T(8,128)(2,1)S(1)}, u32[]{:S(2)}, u32[]{:S(2)}) collective-permute-start(bf16[1024,256]{1,0:T(8,128)(2,1)S(1)} %slice.82), channel_id=1, source_target_pairs={{0,8},{4,12},{8,0},{12,4},{16,24},{20,28},{24,16},{28,20},{1,9},{5... | collective-permute-start | bytes 1572872 | tf_op jit(solution)/shard_map/ppermute | solution.py:340
  45.2 14.0 %collective-permute-start.7 = (bf16[1024,256]{1,0:T(8,128)(2,1)S(1)}, bf16[1024,256]{1,0:T(8,128)(2,1)S(1)}, u32[]{:S(2)}, u32[]{:S(2)}) collective-permute-start(bf16[1024,256]{1,0:T(8,128)(2,1)S(1)} %slice.83), channel_id=1, source_target_pairs={{0,16},{4,20},{8,24},{12,28},{16,0},{20,4},{24,8},{28,12},{1,17},{... | collective-permute-start | bytes 1572872 | tf_op jit(solution)/shard_map/ppermute | solution.py:340
  59.2 1.9 collective-permute-start.8
  59.3 2.7 collective-permute-start.9
  66.6 15.6 %collective-permute-start.10 = (bf16[1024,512]{1,0:T(8,128)(2,1)}, bf16[1024,512]{1,0:T(8,128)(2,1)}, u32[]{:S(2)}, u32[]{:S(2)}) collective-permute-start(bf16[1024,512]{1,0:T(8,128)(2,1)} %refs_0_.3), channel_id=1, source_target_pairs={{0,4},{4,0},{8,12},{12,8},{16,20},{20,16},{24,28},{28,24},{1,5},{5... | collective-permute-start | bytes 3145736 | tf_op jit(solution)/shard_map/ppermute | solution.py:340
  66.8 25.6 %collective-permute-start.11 = (bf16[1024,512]{1,0:T(8,128)(2,1)}, bf16[1024,512]{1,0:T(8,128)(2,1)S(1)}, u32[]{:S(2)}, u32[]{:S(2)}) collective-permute-start(bf16[1024,512]{1,0:T(8,128)(2,1)} %refs_0_.3), channel_id=1, source_target_pairs={{0,8},{4,12},{8,0},{12,4},{16,24},{20,28},{24,16},{28,20},{1,9},{5... | collective-permute-start | bytes 3145736 | tf_op jit(solution)/shard_map/ppermute | solution.py:340
  67.5 25.5 %collective-permute-start.12 = (bf16[1024,512]{1,0:T(8,128)(2,1)}, bf16[1024,512]{1,0:T(8,128)(2,1)}, u32[]{:S(2)}, u32[]{:S(2)}) collective-permute-start(bf16[1024,512]{1,0:T(8,128)(2,1)} %refs_0_.3), channel_id=1, source_target_pairs={{0,16},{4,20},{8,24},{12,28},{16,0},{20,4},{24,8},{28,12},{1,17},{... | collective-permute-start | bytes 3145736 | tf_op jit(solution)/shard_map/ppermute | solution.py:340
  69.1 216.3 %reduce-scatter.6.cloned.1.call-start = ((), (), s32[]{:S(2)}) async-start(), calls=%async_computation.4 | async-start | bytes 2621440 | tf_op jit(solution)/shard_map/reduce_scatter | solution.py:819
  82.3 48.7 %copy-start = (bf16[4,256,1024]{2,1,0:T(8,128)(2,1)S(1)}, bf16[4,256,1024]{2,1,0:T(8,128)(2,1)}, u32[]{:S(2)}) copy-start(bf16[4,256,1024]{2,1,0:T(8,128)(2,1)} %project.5) | copy-start | bytes 6291460
  92.5 20.7 %copy-start.5 = (bf16[1024,512]{1,0:T(8,128)(2,1)}, bf16[1024,512]{1,0:T(8,128)(2,1)S(1)}, u32[]{:S(2)}) copy-start(bf16[1024,512]{1,0:T(8,128)(2,1)S(1)} %collective-permute-done.11.refs_2_) | copy-start | bytes 3145732
  93.1 16.5 %collective-permute-start.13 = (bf16[1024,512]{1,0:T(8,128)(2,1)S(1)}, bf16[1024,512]{1,0:T(8,128)(2,1)S(1)}, u32[]{:S(2)}, u32[]{:S(2)}) collective-permute-start(bf16[1024,512]{1,0:T(8,128)(2,1)S(1)} %collective-permute-done.11.refs_2_), channel_id=1, source_target_pairs={{0,4},{4,0},{8,12},{12,8},{16,20},{20,16},{24,28},{28,24},{1,5},{5... | collective-permute-start | bytes 3145736 | tf_op jit(solution)/shard_map/ppermute | solution.py:340
  93.1 18.3 %collective-permute-start.14 = (bf16[1024,512]{1,0:T(8,128)(2,1)}, bf16[1024,512]{1,0:T(8,128)(2,1)}, u32[]{:S(2)}, u32[]{:S(2)}) collective-permute-start(bf16[1024,512]{1,0:T(8,128)(2,1)} %collective-permute-done.12.refs_4_), channel_id=1, source_target_pairs={{0,4},{4,0},{8,12},{12,8},{16,20},{20,16},{24,28},{28,24},{1,5},{5... | collective-permute-start | bytes 3145736 | tf_op jit(solution)/shard_map/ppermute | solution.py:340
  94.7 13.9 %collective-permute-start.15 = (bf16[1024,256]{1,0:T(8,128)(2,1)S(1)}, bf16[1024,256]{1,0:T(8,128)(2,1)S(1)}, u32[]{:S(2)}, u32[]{:S(2)}) collective-permute-start(bf16[1024,256]{1,0:T(8,128)(2,1)S(1)} %slice.84), channel_id=1, source_target_pairs={{0,8},{4,12},{8,0},{12,4},{16,24},{20,28},{24,16},{28,20},{1,9},{5... | collective-permute-start | bytes 1572872 | tf_op jit(solution)/shard_map/ppermute | solution.py:340
  96.0 13.5 %collective-permute-start.16 = (bf16[1024,256]{1,0:T(8,128)(2,1)S(1)}, bf16[1024,256]{1,0:T(8,128)(2,1)S(1)}, u32[]{:S(2)}, u32[]{:S(2)}) collective-permute-start(bf16[1024,256]{1,0:T(8,128)(2,1)S(1)} %slice.85), channel_id=1, source_target_pairs={{0,16},{4,20},{8,24},{12,28},{16,0},{20,4},{24,8},{28,12},{1,17},{... | collective-permute-start | bytes 1572872 | tf_op jit(solution)/shard_map/ppermute | solution.py:340
  114.6 46.5 %copy-start.1 = (bf16[256,1024]{1,0:T(8,128)(2,1)}, bf16[256,1024]{1,0:T(8,128)(2,1)S(1)}, u32[]{:S(2)}) copy-start(bf16[256,1024]{1,0:T(8,128)(2,1)S(1)} %fusion.9.refs_0_) | copy-start | bytes 1572868
  114.6 13.6 %collective-permute-start.17 = (bf16[256,1024]{1,0:T(8,128)(2,1)S(1)}, bf16[256,1024]{1,0:T(8,128)(2,1)S(1)}, u32[]{:S(2)}, u32[]{:S(2)}) collective-permute-start(bf16[256,1024]{1,0:T(8,128)(2,1)S(1)} %fusion.9.refs_0_), channel_id=1, source_target_pairs={{0,1},{1,0},{2,3},{3,2},{4,5},{5,4},{6,7},{7,6},{8,9},{9,8},{10,11... | collective-permute-start | bytes 1572872 | tf_op jit(solution)/shard_map/ppermute | solution.py:405
  114.7 13.5 %collective-permute-start.18 = (bf16[256,1024]{1,0:T(8,128)(2,1)S(1)}, bf16[256,1024]{1,0:T(8,128)(2,1)}, u32[]{:S(2)}, u32[]{:S(2)}) collective-permute-start(bf16[256,1024]{1,0:T(8,128)(2,1)S(1)} %fusion.9.refs_0_), channel_id=1, source_target_pairs={{1,2},{2,1},{5,6},{6,5},{9,10},{10,9},{13,14},{14,13},{17,18},{18,... | collective-permute-start | bytes 1572872 | tf_op jit(solution)/shard_map/ppermute | solution.py:405
  116.1 12.0 %collective-permute-start.19 = (bf16[1024,256]{1,0:T(8,128)(2,1)}, bf16[1024,256]{1,0:T(8,128)(2,1)}, u32[]{:S(2)}, u32[]{:S(2)}) collective-permute-start(bf16[1024,256]{1,0:T(8,128)(2,1)} %copy-done.17), channel_id=1, source_target_pairs={{0,4},{4,0},{8,12},{12,8},{16,20},{20,16},{24,28},{28,24},{1,5},{5... | collective-permute-start | bytes 1572872 | tf_op jit(solution)/shard_map/ppermute | solution.py:340
  116.2 12.0 %collective-permute-start.20 = (bf16[1024,256]{1,0:T(8,128)(2,1)}, bf16[1024,256]{1,0:T(8,128)(2,1)}, u32[]{:S(2)}, u32[]{:S(2)}) collective-permute-start(bf16[1024,256]{1,0:T(8,128)(2,1)} %copy-done.18), channel_id=1, source_target_pairs={{0,4},{4,0},{8,12},{12,8},{16,20},{20,16},{24,28},{28,24},{1,5},{5... | collective-permute-start | bytes 1572872 | tf_op jit(solution)/shard_map/ppermute | solution.py:340
  128.2 32.9 %copy-start.12 = (bf16[256,1024]{1,0:T(8,128)(2,1)}, bf16[256,1024]{1,0:T(8,128)(2,1)S(1)}, u32[]{:S(2)}) copy-start(bf16[256,1024]{1,0:T(8,128)(2,1)S(1)} %collective-permute-done.17.refs_1_) | copy-start | bytes 1572868
  128.2 12.2 %collective-permute-start.21 = (bf16[256,1024]{1,0:T(8,128)(2,1)S(1)}, bf16[256,1024]{1,0:T(8,128)(2,1)}, u32[]{:S(2)}, u32[]{:S(2)}) collective-permute-start(bf16[256,1024]{1,0:T(8,128)(2,1)S(1)} %collective-permute-done.17.refs_1_), channel_id=1, source_target_pairs={{1,2},{2,1},{5,6},{6,5},{9,10},{10,9},{13,14},{14,13},{17,18},{18,... | collective-permute-start | bytes 1572872 | tf_op jit(solution)/shard_map/ppermute | solution.py:405
  129.7 17.1 %collective-permute-start.22 = (bf16[256,1024]{1,0:T(8,128)(2,1)}, bf16[256,1024]{1,0:T(8,128)(2,1)}, u32[]{:S(2)}, u32[]{:S(2)}) collective-permute-start(bf16[256,1024]{1,0:T(8,128)(2,1)} %collective-permute-done.18.refs_2_), channel_id=1, source_target_pairs={{1,0},{2,3},{5,4},{6,7},{9,8},{10,11},{13,12},{14,15},{17,16},{18,... | collective-permute-start | bytes 1572872 | tf_op jit(solution)/shard_map/ppermute | solution.py:405
  131.8 17.7 %collective-permute-start.23 = (bf16[256,1024]{1,0:T(8,128)(2,1)}, bf16[256,1024]{1,0:T(8,128)(2,1)}, u32[]{:S(2)}, u32[]{:S(2)}) collective-permute-start(bf16[256,1024]{1,0:T(8,128)(2,1)} %dynamic-slice_bitcast_fusion), channel_id=1, source_target_pairs={{0,1},{3,2},{4,5},{7,6},{8,9},{11,10},{12,13},{15,14},{16,17},{19,... | collective-permute-start | bytes 1572872 | tf_op jit(solution)/shard_map/ppermute | solution.py:394
  149.5 23.2 %collective-permute-start.24 = (bf16[256,1024]{1,0:T(8,128)(2,1)}, bf16[256,1024]{1,0:T(8,128)(2,1)}, u32[]{:S(2)}, u32[]{:S(2)}) collective-permute-start(bf16[256,1024]{1,0:T(8,128)(2,1)} %collective-permute-done.21.refs_3_), channel_id=1, source_target_pairs={{1,0},{2,3},{5,4},{6,7},{9,8},{10,11},{13,12},{14,15},{17,16},{18,... | collective-permute-start | bytes 1572872 | tf_op jit(solution)/shard_map/ppermute | solution.py:405
  153.4 19.3 %collective-permute-start.25 = (bf16[256,1024]{1,0:T(8,128)(2,1)}, bf16[256,1024]{1,0:T(8,128)(2,1)}, u32[]{:S(2)}, u32[]{:S(2)}) collective-permute-start(bf16[256,1024]{1,0:T(8,128)(2,1)} %get-tuple-element.222), channel_id=1, source_target_pairs={{0,1},{1,2},{4,5},{5,6},{8,9},{9,10},{12,13},{13,14},{16,17},{17,1... | collective-permute-start | bytes 1572872 | tf_op jit(solution)/shard_map/ppermute | solution.py:398
  159.6 13.2 %collective-permute-start.26 = (bf16[256,1024]{1,0:T(8,128)(2,1)}, bf16[256,1024]{1,0:T(8,128)(2,1)}, u32[]{:S(2)}, u32[]{:S(2)}) collective-permute-start(bf16[256,1024]{1,0:T(8,128)(2,1)} %get-tuple-element.221), channel_id=1, source_target_pairs={{2,1},{3,2},{6,5},{7,6},{10,9},{11,10},{14,13},{15,14},{18,17},{19... | collective-permute-start | bytes 1572872 | tf_op jit(solution)/shard_map/ppermute | solution.py:398
  175.2 14.8 %collective-permute-start.27 = (bf16[256,1024]{1,0:T(8,128)(2,1)}, bf16[256,1024]{1,0:T(8,128)(2,1)S(1)}, u32[]{:S(2)}, u32[]{:S(2)}) collective-permute-start(bf16[256,1024]{1,0:T(8,128)(2,1)} %get-tuple-element.220), channel_id=1, source_target_pairs={{0,1},{1,2},{2,3},{4,5},{5,6},{6,7},{8,9},{9,10},{10,11},{12,13},{... | collective-permute-start | bytes 1572872 | tf_op jit(solution)/shard_map/ppermute | solution.py:398
  177.2 13.0 %collective-permute-start.28 = (bf16[256,1024]{1,0:T(8,128)(2,1)S(1)}, bf16[256,1024]{1,0:T(8,128)(2,1)}, u32[]{:S(2)}, u32[]{:S(2)}) collective-permute-start(bf16[256,1024]{1,0:T(8,128)(2,1)S(1)} %get-tuple-element.219), channel_id=1, source_target_pairs={{1,0},{2,1},{3,2},{5,4},{6,5},{7,6},{9,8},{10,9},{11,10},{13,12},{... | collective-permute-start | bytes 1572872 | tf_op jit(solution)/shard_map/ppermute | solution.py:398
  179.8 10.4 %copy-start.23 = (bf16[2,256,1024]{2,1,0:T(8,128)(2,1)S(1)}, bf16[2,256,1024]{2,1,0:T(8,128)(2,1)}, u32[]{:S(2)}) copy-start(bf16[2,256,1024]{2,1,0:T(8,128)(2,1)} %param.15) | copy-start | bytes 3145732
  190.0 18.3 %copy-start.29 = (f32[16,1024]{1,0:T(8,128)S(1)}, f32[16,1024]{1,0:T(8,128)}, u32[]{:S(2)}) copy-start(f32[16,1024]{1,0:T(8,128)} %param.25) | copy-start | bytes 196612
  191.6 27.6 %copy-start.3 = (bf16[256,1024]{1,0:T(8,128)(2,1)}, bf16[256,1024]{1,0:T(8,128)(2,1)S(1)}, u32[]{:S(2)}) copy-start(bf16[256,1024]{1,0:T(8,128)(2,1)S(1)} %fusion.11.refs_0_) | copy-start | bytes 1572868
  191.6 14.7 %collective-permute-start.29 = (bf16[256,1024]{1,0:T(8,128)(2,1)S(1)}, bf16[256,1024]{1,0:T(8,128)(2,1)S(1)}, u32[]{:S(2)}, u32[]{:S(2)}) collective-permute-start(bf16[256,1024]{1,0:T(8,128)(2,1)S(1)} %fusion.11.refs_0_), channel_id=1, source_target_pairs={{0,1},{1,0},{2,3},{3,2},{4,5},{5,4},{6,7},{7,6},{8,9},{9,8},{10,11... | collective-permute-start | bytes 1572872 | tf_op jit(solution)/shard_map/ppermute | solution.py:405
  194.8 11.5 %collective-permute-start.30 = (bf16[256,1024]{1,0:T(8,128)(2,1)S(1)}, bf16[256,1024]{1,0:T(8,128)(2,1)S(1)}, u32[]{:S(2)}, u32[]{:S(2)}) collective-permute-start(bf16[256,1024]{1,0:T(8,128)(2,1)S(1)} %fusion.11.refs_0_), channel_id=1, source_target_pairs={{1,2},{2,1},{5,6},{6,5},{9,10},{10,9},{13,14},{14,13},{17,18},{18,... | collective-permute-start | bytes 1572872 | tf_op jit(solution)/shard_map/ppermute | solution.py:405
  206.3 12.9 %copy-start.13 = (bf16[256,1024]{1,0:T(8,128)(2,1)}, bf16[256,1024]{1,0:T(8,128)(2,1)S(1)}, u32[]{:S(2)}) copy-start(bf16[256,1024]{1,0:T(8,128)(2,1)S(1)} %collective-permute-done.29.refs_1_) | copy-start | bytes 1572868
  206.3 12.9 %copy-start.14 = (bf16[256,1024]{1,0:T(8,128)(2,1)}, bf16[256,1024]{1,0:T(8,128)(2,1)S(1)}, u32[]{:S(2)}) copy-start(bf16[256,1024]{1,0:T(8,128)(2,1)S(1)} %collective-permute-done.30.refs_2_) | copy-start | bytes 1572868
  206.3 12.9 %collective-permute-start.31 = (bf16[256,1024]{1,0:T(8,128)(2,1)S(1)}, bf16[256,1024]{1,0:T(8,128)(2,1)S(1)}, u32[]{:S(2)}, u32[]{:S(2)}) collective-permute-start(bf16[256,1024]{1,0:T(8,128)(2,1)S(1)} %collective-permute-done.29.refs_1_), channel_id=1, source_target_pairs={{1,2},{2,1},{5,6},{6,5},{9,10},{10,9},{13,14},{14,13},{17,18},{18,... | collective-permute-start | bytes 1572872 | tf_op jit(solution)/shard_map/ppermute | solution.py:405
  207.0 19.9 %collective-permute-start.32 = (bf16[256,1024]{1,0:T(8,128)(2,1)S(1)}, bf16[256,1024]{1,0:T(8,128)(2,1)S(1)}, u32[]{:S(2)}, u32[]{:S(2)}) collective-permute-start(bf16[256,1024]{1,0:T(8,128)(2,1)S(1)} %collective-permute-done.30.refs_2_), channel_id=1, source_target_pairs={{1,0},{2,3},{5,4},{6,7},{9,8},{10,11},{13,12},{14,15},{17,16},{18,... | collective-permute-start | bytes 1572872 | tf_op jit(solution)/shard_map/ppermute | solution.py:405
  226.9 15.5 %collective-permute-start.33 = (bf16[256,1024]{1,0:T(8,128)(2,1)S(1)}, bf16[256,1024]{1,0:T(8,128)(2,1)S(1)}, u32[]{:S(2)}, u32[]{:S(2)}) collective-permute-start(bf16[256,1024]{1,0:T(8,128)(2,1)S(1)} %collective-permute-done.31.refs_3_), channel_id=1, source_target_pairs={{1,0},{2,3},{5,4},{6,7},{9,8},{10,11},{13,12},{14,15},{17,16},{18,... | collective-permute-start | bytes 1572872 | tf_op jit(solution)/shard_map/ppermute | solution.py:405
  242.4 88.8 %reduce-scatter.8.cloned.1.call-start = ((), (), s32[]{:S(2)}) async-start(), calls=%async_computation.5 | async-start | bytes 2621440 | tf_op jit(solution)/shard_map/reduce_scatter | solution.py:819
  264.4 21.0 %copy-start.2 = (bf16[256,1024]{1,0:T(8,128)(2,1)S(1)}, bf16[256,1024]{1,0:T(8,128)(2,1)}, u32[]{:S(2)}) copy-start(bf16[256,1024]{1,0:T(8,128)(2,1)} %copy-done.1) | copy-start | bytes 1572868
  264.4 22.3 %copy-start.4 = (bf16[256,1024]{1,0:T(8,128)(2,1)S(1)}, bf16[256,1024]{1,0:T(8,128)(2,1)}, u32[]{:S(2)}) copy-start(bf16[256,1024]{1,0:T(8,128)(2,1)} %copy-done.3) | copy-start | bytes 1572868
  (20 other events, 77.0 us)
Sparse Core Ops, SparseCore 0:
  69.2 43.9 reduce-scatter.3
  242.6 42.7 reduce-scatter.5
  287.9 43.3 reduce-scatter.7

commit v4 on v3

--- a/solution.py
+++ b/solution.py
@@ -392,6 +392,11 @@
         if arrived:
             value = add(value, arrived[0])
         return [lax.ppermute(value, axis, up + down)] * 2
+    if step <= count - step:
+        value = line_part(parts, axis, jnp.where(place < step, up_share, down_share))
+        if arrived:
+            value = add(value, arrived[0] if arrived[0] is arrived[1] else jnp.where(place < step, *arrived))
+        return [lax.ppermute(value, axis, up), lax.ppermute(value, axis, down)]
     low, high = line_part(parts, axis, up_share), line_part(parts, axis, down_share)
     if arrived:
         low, high = add(low, arrived[0]), add(high, arrived[1])
@@ -639,8 +644,8 @@
 def lr_modal_kernel(places, scalar_ref, sent_ref, short_ref, rate_ref, res_ref, skip_ref, q_in, u_in, *refs):
     blocks = len(places)
     weights, out_ref, zs, change, z_ref, result = refs[:blocks], *refs[blocks : blocks + 5]
-    q_ref, u_ref, row_sems = refs[blocks + 5 : blocks + 8]
-    held, in_sems, out_sems = refs[blocks + 8 : -2], refs[-2], refs[-1]
+    q_ref, u_ref, row_sems, powers = refs[blocks + 5 : blocks + 9]
+    held, in_sems, out_sems = refs[blocks + 9 : -2], refs[-2], refs[-1]
     rows = q_ref.shape[0] // SEGMENTS
 
     def moved(segment):
@@ -693,20 +698,26 @@
         for t in range(prior):
             change[index, t] = change_of_u(index, t)
 
-    decay, weight, enter = [], [], []
+    decay, weight = [], []
     for n in range(poles):
         rate = rate_ref[n]
         decay.append(jnp.exp(-rate))
         weight.append(res_ref[n] * jnp.sqrt(1.0 - jnp.exp(-2.0 * rate)))
-
-        def arrive(index, total, n=n, rate=rate):
-            distance = (position - 1 - index).astype(F32)
+        powers[0, n] = jnp.exp(-rate * tokens)
+        for t in range(prior):
+            powers[1 + t, n] = jnp.exp(-rate * (tokens - 1 - t))
+
+    def arrive(index, totals):
+        totals = list(totals)
+        changes = [change[index, t] for t in range(prior)]
+        for n in range(poles):
             end = sent_ref[index, n].astype(F32)
             for t in range(prior):
-                end = end + jnp.exp(-rate * (tokens - 1 - t)) * change[index, t]
-            return total + jnp.exp(-rate * tokens * distance) * end
-
-        enter.append(lax.fori_loop(0, position, arrive, nothing))
+                end = end + powers[1 + t, n] * changes[t]
+            totals[n] = powers[0, n] * totals[n] + end
+        return tuple(totals)
+
+    enter = lax.fori_loop(0, position, arrive, (nothing,) * poles)
 
     for copy in moved(0):
         copy.wait()
@@ -768,6 +779,7 @@
             pltpu.VMEM((tokens, SUB, LANES), F32),
             pltpu.VMEM((tokens, SUB, LANES), F32),
             pltpu.SemaphoreType.DMA((2, SEGMENTS)),
+            pltpu.VMEM((1 + prior, *rate.shape), F32),
             *[pltpu.VMEM(w.shape, w.dtype) for w in weights],
             pltpu.SemaphoreType.DMA((len(weights),)),
             pltpu.SemaphoreType.DMA((len(weights),)),
@@ -863,17 +875,44 @@
         return arrived
 
     mids = [as_mid(0, share)]
-    blocks = line_gather(mids[0], "tp", 1, None)
-    lr_w.third()
-    blocks, second, lr_w.arrays = together(blocks, second, lr_w.arrays)
-    blocks = line_gather(mids[0], "tp", 2, blocks)
-    arrived = line_scatter(second, "tp", 1, None)
-    blocks, arrived = together(blocks, arrived)
-    blocks = line_gather(mids[0], "tp", 3, blocks)
-    arrived = line_scatter(second, "tp", 2, arrived)
-    begun = lr_in_start(place, gain, near(blocks), table, in_w)
-    blocks, arrived, begun = together(blocks, arrived, begun)
-    arrived = scatter_all(second, range(3, tp), arrived)
+    if tp == 4:
+        line = lax.axis_index("tp")
+        inside = (line == 1) | (line == 2)
+
+        def outer(value):
+            return lax.ppermute(value, "tp", [(0, 1), (1, 0), (2, 3), (3, 2)])
+
+        def inner(value):
+            return lax.ppermute(value, "tp", [(1, 2), (2, 1)])
+
+        def part(share):
+            return line_part(second, "tp", jnp.where(line < 2, share, 3 - share))
+
+        near_0, near_1 = outer(mids[0]), inner(mids[0])
+        lr_w.third()
+        near_0, near_1, second, lr_w.arrays = together(near_0, near_1, second, lr_w.arrays)
+        far_1 = outer(jnp.where(inside, near_1, part(3)))
+        far_0 = inner(near_0)
+        near_0, near_1, far_0, far_1 = together(near_0, near_1, far_0, far_1)
+        far_2 = outer(jnp.where(inside, far_0, part(2)))
+        sums_0 = inner(add(part(3), far_1))
+        begun = lr_in_start(place, gain, [mids[0], near_0, near_1, far_0, far_1], table, in_w)
+        begun, sums_0, far_0, far_1, far_2, near_0, near_1 = together(begun, sums_0, far_0, far_1, far_2, near_0, near_1)
+        blocks = [mids[0], near_0, near_1, far_0, far_1, far_2]
+        arrived = [outer(add(part(jnp.where(inside, 0, 1)), sums_0)), inner(add(part(2), far_2))]
+    else:
+        blocks = line_gather(mids[0], "tp", 1, None)
+        lr_w.third()
+        blocks, second, lr_w.arrays = together(blocks, second, lr_w.arrays)
+        blocks = line_gather(mids[0], "tp", 2, blocks)
+        arrived = line_scatter(second, "tp", 1, None)
+        blocks, arrived[:1] = together(blocks, arrived[:1])
+        arrived = arrived[:1] * 2 if tp == 4 else arrived
+        blocks = line_gather(mids[0], "tp", 3, blocks)
+        arrived = line_scatter(second, "tp", 2, arrived)
+        begun = lr_in_start(place, gain, near(blocks), table, in_w)
+        blocks, arrived, begun = together(blocks, arrived, begun)
+        arrived = scatter_all(second, range(3, tp), arrived)
     q, u, send = lr_mix(place, gain, begun, blocks, table, in_w, lr_short, rate)
     arrived, q, u, send = together(arrived, q, u, send)
     mids.append(as_mid(1, line_part(second, "tp", lax.axis_index("tp")), *arrived))

time: 341 us -> 329 us (0.965)
  starting transfers between devices: 47.2 us -> 35.9 us
    ppermute x10 -> x5, waiting for transfers between devices: 28.1 us -> 8 us  [move(): return lax.ppermute(what, axis, pairs)]
    ppermute x5 -> x8, waiting for transfers between devices: 2.97 us -> 21.7 us  [the longest x4 21.6 us: outer(): return lax.ppermute(value, 'tp', [(0, 1), (1, 0), (2, 3), (3, 2)])]
    ppermute x10 -> x5, starting transfers between devices: 12.7 us -> 6 us  [move(): return lax.ppermute(what, axis, pairs)]
    ppermute x5 -> x8, starting transfers between devices: 19.5 us -> 14.9 us  [the longest x4 9.8 us: outer(): return lax.ppermute(value, 'tp', [(0, 1), (1, 0), (2, 3), (3, 2)])]
    unnamed x65 -> x67, local copies, waits for them, and re-layouts: 7.13 us -> 7.85 us
  transfers between devices with their start and end apart: 37 -> 35, of which waited for: 17 -> 15; matrix products, arithmetic and copies ran while one was open for 4% -> 3% of each run, Pallas kernels for 33% -> 34%
where the time goes in v4:
time: 329 us; the launch traced here: 328 us
  Pallas kernels  116 us (35%)
  waiting for transfers between devices  112 us (34%)
  starting transfers between devices  35.9 us (11%)
  blocking collectives  21.8 us (7%)
  other arithmetic  16.1 us (5%)
  between operations  13.7 us (4%)
  local copies, waits for them, and re-layouts  12.1 us (4%)
    reduce_scatter x3, waiting for transfers between devices, scattered(): return lax.psum_scatter(parts, 'tp', scatter_dimension=0)  55.7 us
    ppermute x18, waiting for transfers between devices, swap(): return lax.ppermute(value, self.axis, swap_pairs(self.axis, bit))  26.8 us
    pallas_call x1, Pallas kernels, mr_local(): pl.pallas_call(mr_local_kernel, grid=(sequences,), out_shape=(jax.ShapeDt...  23.6 us
    pallas_call x2, Pallas kernels, lr_in_start(): pl.pallas_call(functools.partial(lr_in_start_kernel, table), out_shape=(j...  23.3 us
    all_gather x2, blocking collectives, local(): sent = lax.all_gather(send, 'ctx', axis=0)  21.8 us
    ppermute x4, waiting for transfers between devices, outer(): return lax.ppermute(value, 'tp', [(0, 1), (1, 0), (2, 3), (3, 2)])  21.6 us
    pallas_call x2, Pallas kernels, lr_modal(): pl.pallas_call(functools.partial(lr_modal_kernel, places), out_shape=jax....  20.6 us
    pallas_call x2, Pallas kernels, lr_mix(): pl.pallas_call(functools.partial(lr_mix_kernel, table), out_shape=(rows,...  20.5 us
  transfers between devices with their start and end apart: 35, of which 15 were waited for; matrix products, arithmetic and copies ran while one was open for 3% of the time, Pallas kernels for 34%

profile of v4, /device:TPU:0, one launch (start us, length us, event | category | flops | bytes accessed | tf_op | source)
XLA Modules:
  0.0 328.0 jit_solution(11840052135221648120)
XLA Ops:
  7.0 2.5 collective-permute-start.1
  9.5 1.5 collective-permute-start.2
  11.8 1.9 copy_convert_fusion
  16.4 2.7 collective-permute-start.3
  20.6 23.6 %mr_local.1 = (bf16[2,256,1024]{2,1,0:T(8,128)(2,1)}, f32[2,144,8,128]{3,2,1,0:T(8,128)}, f32[2,144,8,128]{3,2,1,0:T(8,128)}) custom-call(bf16[2,3,256,1024]{3,2,1,0:T(8,128)(2,1)} %bitcast.57, f32[3,3,8,128]{3,2,1,0:T(8,128)} %reshape.79.short_ref, f32[128,8,128]{2,1,0:T(8,128)} %bitcast.60, f32[8,128]{1,0:T(8,128)} %bitcast.81), custom_call_target="tpu_custom_call" | custom-call | flops 1000000000 | bytes 1000000 | tf_op jit(solution)/shard_map/mr_local/pallas_call | solution.py:127
  46.0 6.1 %mr_finish.2.head_ref = bf16[144,1024]{1,0:T(8,128)(2,1)} custom-call(bf16[2,3,256,1024]{3,2,1,0:T(8,128)(2,1)} %bitcast.58, bf16[2,144,1024]{2,1,0:T(8,128)(2,1)} %collective-permute-done.3.halo_ref, f32[2,144,8,128]{3,2,1,0:T(8,128)} %get-tuple-element.113.q_ref, f32[2,144,8,128]{3,2,1,0:T(8,128)} %get-tuple-element.114.conv_ref.gate_ref, ...), custom_call_target="tpu_custom_call" | custom-call | flops 40000000000 | bytes 1000000 | tf_op jit(solution)/shard_map/mr_finish/pallas_call | solution.py:212
  52.1 1.0 copy-done.13
  53.5 5.3 %project.3.refs_4_ = bf16[4,256,1024]{2,1,0:T(8,128)(2,1)} custom-call(s32[1]{0:T(128)} %bitcast.1.scalar_ref, bf16[144,1024]{1,0:T(8,128)(2,1)} %mr_finish.2.head_ref, bf16[2,256,1024]{2,1,0:T(8,128)(2,1)} %get-tuple-element.115.body_ref, bf16[1024,512]{1,0:T(8,128)(2,1)} %refs_0_.1, bf16[1024,512]{1,0:T(8,128)(2,1)} %copy-done.11, ...), custom_call_target="tpu_custom_call" | custom-call | flops 1610612736 | bytes 7864320 | tf_op jit(solution)/shard_map/project/pallas_call | solution.py:300
  59.0 1.0 collective-permute-done.7.refs_1_.refs_7_
  60.5 1.4 collective-permute-done.8.refs_2_.refs_8_
  63.6 3.8 %project.4.gate_ref = bf16[4,256,1024]{2,1,0:T(8,128)(2,1)} custom-call(s32[1]{0:T(128)} %bitcast.1.scalar_ref, bf16[144,1024]{1,0:T(8,128)(2,1)} %mr_finish.2.head_ref, bf16[2,256,1024]{2,1,0:T(8,128)(2,1)} %get-tuple-element.115.body_ref, bf16[1024,256]{1,0:T(8,128)(2,1)} %copy-done.20, ...), custom_call_target="tpu_custom_call", output_to_operand_aliasing={{}: (7, {})} | custom-call | flops 536870912 | bytes 2621440 | tf_op jit(solution)/shard_map/project/pallas_call | solution.py:300
  68.3 1.5 collective-permute-start.12
  69.8 6.1 %mr_finish.3.head_ref = bf16[144,1024]{1,0:T(8,128)(2,1)} custom-call(bf16[2,3,256,1024]{3,2,1,0:T(8,128)(2,1)} %bitcast.59, bf16[2,144,1024]{2,1,0:T(8,128)(2,1)} %collective-permute-done.3.halo_ref, f32[2,144,8,128]{3,2,1,0:T(8,128)} %get-tuple-element.113.q_ref, f32[2,144,8,128]{3,2,1,0:T(8,128)} %get-tuple-element.114.conv_ref.gate_ref, ...), custom_call_target="tpu_custom_call" | custom-call | flops 40000000000 | bytes 1000000 | tf_op jit(solution)/shard_map/mr_finish/pallas_call | solution.py:212
  75.9 7.1 %project.5 = bf16[4,256,1024]{2,1,0:T(8,128)(2,1)} custom-call(s32[1]{0:T(128)} %bitcast.1.scalar_ref, bf16[144,1024]{1,0:T(8,128)(2,1)} %mr_finish.3.head_ref, bf16[2,256,1024]{2,1,0:T(8,128)(2,1)} %get-tuple-element.115.body_ref, bf16[1024,512]{1,0:T(8,128)(2,1)} %refs_0_.1, bf16[1024,512]{1,0:T(8,128)(2,1)} %copy-done.11, bf16[1024,512]{1,0:T(8,128)(2,1)} %copy-done.6, ...), custom_call_target="tpu_custom_call" | custom-call | flops 2147483648 | bytes 10485760 | tf_op jit(solution)/shard_map/project/pallas_call | solution.py:300
  83.0 10.2 %collective-permute-done.11.refs_2_ = bf16[1024,512]{1,0:T(8,128)(2,1)S(1)} collective-permute-done((bf16[1024,512]{1,0:T(8,128)(2,1)}, bf16[1024,512]{1,0:T(8,128)(2,1)S(1)}, u32[]{:S(2)}, u32[]{:S(2)}) %collective-permute-start.11) | collective-permute-done | bytes 1048608 | tf_op jit(solution)/shard_map/ppermute | solution.py:340
  94.3 1.1 slice.84
  95.4 1.3 collective-permute-start.15
  97.7 11.6 %collective-permute-done.15.refs_6_ = bf16[1024,256]{1,0:T(8,128)(2,1)S(1)} collective-permute-done((bf16[1024,256]{1,0:T(8,128)(2,1)S(1)}, bf16[1024,256]{1,0:T(8,128)(2,1)S(1)}, u32[]{:S(2)}, u32[]{:S(2)}) %collective-permute-start.15) | collective-permute-done | bytes 524320 | tf_op jit(solution)/shard_map/ppermute | solution.py:340
  112.1 1.8 reduce-scatter.4.cloned.1.call-done
  113.9 1.4 fusion.6.refs_0_
  116.7 12.3 %collective-permute-done.17.refs_1_ = bf16[256,1024]{1,0:T(8,128)(2,1)} collective-permute-done((bf16[256,1024]{1,0:T(8,128)(2,1)S(1)}, bf16[256,1024]{1,0:T(8,128)(2,1)}, u32[]{:S(2)}, u32[]{:S(2)}) %collective-permute-start.17) | collective-permute-done | bytes 524320 | tf_op jit(solution)/shard_map/ppermute | solution.py:883
  130.7 3.5 %collective-permute-start.22 = (bf16[256,1024]{1,0:T(8,128)(2,1)}, bf16[256,1024]{1,0:T(8,128)(2,1)S(1)}, u32[]{:S(2)}, u32[]{:S(2)}) collective-permute-start(bf16[256,1024]{1,0:T(8,128)(2,1)} %bitcast_select_fusion.1), channel_id=1, source_target_pairs={{0,1},{1,0},{2,3},{3,2},{4,5},{5,4},{6,7},{7,6},{8,9},{9,8},{10,11... | collective-permute-start | bytes 1572872 | tf_op jit(solution)/shard_map/ppermute | solution.py:883
  134.2 1.5 collective-permute-start.21
  135.7 9.3 %collective-permute-done.22.refs_4_ = bf16[256,1024]{1,0:T(8,128)(2,1)S(1)} collective-permute-done((bf16[256,1024]{1,0:T(8,128)(2,1)}, bf16[256,1024]{1,0:T(8,128)(2,1)S(1)}, u32[]{:S(2)}, u32[]{:S(2)}) %collective-permute-start.22) | collective-permute-done | bytes 524320 | tf_op jit(solution)/shard_map/ppermute | solution.py:883
  145.9 4.7 %collective-permute-start.24 = (bf16[256,1024]{1,0:T(8,128)(2,1)}, bf16[256,1024]{1,0:T(8,128)(2,1)}, u32[]{:S(2)}, u32[]{:S(2)}) collective-permute-start(bf16[256,1024]{1,0:T(8,128)(2,1)} %bitcast_select_fusion), channel_id=1, source_target_pairs={{0,1},{1,0},{2,3},{3,2},{4,5},{5,4},{6,7},{7,6},{8,9},{9,8},{10,11... | collective-permute-start | bytes 1572872 | tf_op jit(solution)/shard_map/ppermute | solution.py:883
  151.6 1.5 collective-permute-start.23
  153.0 11.6 %lr_in_start.2 = (f32[6,256,512]{2,1,0:T(8,128)}, f32[256,128]{1,0:T(8,128)}) custom-call(s32[1]{0:T(128)} %bitcast.13.scalar_ref, f32[1,4096]{1,0:T(1,128)} %bitcast.72, bf16[256,1024]{1,0:T(8,128)(2,1)} %copy-done.1, bf16[256,1024]{1,0:T(8,128)(2,1)} %collective-permute-done.17.refs_1_, bf16[256,1024]{1,0:T(8,128)(2,1)} %copy-done.9, ...), custom_call_target="tpu_custom_call" | custom-call | flops 4831838208 | bytes 18874368 | tf_op jit(solution)/shard_map/lr_in_start/pallas_call | solution.py:484
  164.7 2.4 add_convert_fusion.1
  167.2 1.5 collective-permute-start.25
  168.7 1.5 collective-permute-start.26
  171.4 10.2 %lr_mix.2 = (f32[256,8,128]{2,1,0:T(8,128)}, f32[256,8,128]{2,1,0:T(8,128)}, bf16[32,8,128]{2,1,0:T(8,128)(2,1)}) custom-call(s32[1]{0:T(128)} %bitcast.13.scalar_ref, f32[1,4096]{1,0:T(1,128)} %bitcast.73, f32[256,128]{1,0:T(8,128)} %get-tuple-element.155.square_ref, f32[3,3,8,128]{3,2,1,0:T(8,128)} %reshape.83.short_ref, f32[16,8,128]{2,1,0:T(8,128)} %bitcast.65, ...), custom_call_target="tpu_custom_call" | custom-call | flops 1610612736 | bytes 6291456 | tf_op jit(solution)/shard_map/lr_mix/pallas_call | solution.py:620
  181.6 1.4 fusion.8.refs_0_
  183.1 2.1 collective-permute-start.27
  185.9 11.0 %all-gather = bf16[256,8,128]{2,1,0:T(8,128)(2,1)} all-gather(bf16[32,8,128]{2,1,0:T(8,128)(2,1)S(1)} %copy-done.28), channel_id=2, replica_groups=mesh['ctx'=8,'tp'=4] {'ctx'}, dimensions={0}, use_global_device_ids=true | all-gather | bytes 589824 | tf_op jit(solution)/shard_map/all_gather | solution.py:920
  197.6 1.3 collective-permute-start.30
  199.5 10.3 %lr_modal.2 = bf16[4,256,1024]{2,1,0:T(8,128)(2,1)} custom-call(s32[1]{0:T(128)} %bitcast.1.scalar_ref, bf16[8,32,8,128]{3,2,1,0:T(8,128)(2,1)} %bitcast.63, f32[3,3,8,128]{3,2,1,0:T(8,128)} %reshape.83.short_ref, f32[16,8,128]{2,1,0:T(8,128)} %bitcast.66, f32[16,8,128]{2,1,0:T(8,128)} %bitcast.69, f32[8,128]{1,0:T(8,128)} %bitcast.79, ...), custom_call_target="tpu_custom_call" | custom-call | flops 2147483648 | bytes 10485760 | tf_op jit(solution)/shard_map/lr_modal/pallas_call | solution.py:769
  209.8 5.7 %collective-permute-done.30.refs_4_ = bf16[256,1024]{1,0:T(8,128)(2,1)S(1)} collective-permute-done((bf16[256,1024]{1,0:T(8,128)(2,1)S(1)}, bf16[256,1024]{1,0:T(8,128)(2,1)S(1)}, u32[]{:S(2)}, u32[]{:S(2)}) %collective-permute-start.30) | collective-permute-done | bytes 524320 | tf_op jit(solution)/shard_map/ppermute | solution.py:410
  215.5 1.3 collective-permute-start.31
  216.8 11.6 %lr_in_start.3 = (f32[6,256,512]{2,1,0:T(8,128)}, f32[256,128]{1,0:T(8,128)}) custom-call(s32[1]{0:T(128)} %bitcast.13.scalar_ref, f32[1,4096]{1,0:T(1,128)} %bitcast.74, bf16[256,1024]{1,0:T(8,128)(2,1)} %copy-done.3, bf16[256,1024]{1,0:T(8,128)(2,1)} %copy-done.14, bf16[256,1024]{1,0:T(8,128)(2,1)} %copy-done.15, bf16[256,1024]{1,0:T(8,128)(2,1)} %copy-done.16, ...), custom_call_target="tpu_custom_call" | custom-call | flops 4831838208 | bytes 18874368 | tf_op jit(solution)/shard_map/lr_in_start/pallas_call | solution.py:484
  228.5 2.3 collective-permute-done.31.refs_5_
  231.6 10.3 %lr_mix.3 = (f32[256,8,128]{2,1,0:T(8,128)}, f32[256,8,128]{2,1,0:T(8,128)}, bf16[32,8,128]{2,1,0:T(8,128)(2,1)}) custom-call(s32[1]{0:T(128)} %bitcast.13.scalar_ref, f32[1,4096]{1,0:T(1,128)} %bitcast.75, f32[256,128]{1,0:T(8,128)} %get-tuple-element.194.square_ref, f32[3,3,8,128]{3,2,1,0:T(8,128)} %reshape.83.short_ref, f32[16,8,128]{2,1,0:T(8,128)} %bitcast.67, ...), custom_call_target="tpu_custom_call" | custom-call | flops 1610612736 | bytes 6291456 | tf_op jit(solution)/shard_map/lr_mix/pallas_call | solution.py:620
  241.9 10.8 %all-gather.1 = bf16[256,8,128]{2,1,0:T(8,128)(2,1)} all-gather(bf16[32,8,128]{2,1,0:T(8,128)(2,1)} %get-tuple-element.202), channel_id=3, replica_groups=mesh['ctx'=8,'tp'=4] {'ctx'}, dimensions={0}, use_global_device_ids=true | all-gather | bytes 589824 | tf_op jit(solution)/shard_map/all_gather | solution.py:932
  252.7 10.3 %lr_modal.3 = bf16[4,256,1024]{2,1,0:T(8,128)(2,1)} custom-call(s32[1]{0:T(128)} %bitcast.1.scalar_ref, bf16[8,32,8,128]{3,2,1,0:T(8,128)(2,1)} %bitcast.64, f32[3,3,8,128]{3,2,1,0:T(8,128)} %reshape.83.short_ref, f32[16,8,128]{2,1,0:T(8,128)} %bitcast.68, f32[16,8,128]{2,1,0:T(8,128)} %bitcast.70, f32[8,128]{1,0:T(8,128)} %bitcast.80, ...), custom_call_target="tpu_custom_call" | custom-call | flops 2147483648 | bytes 10485760 | tf_op jit(solution)/shard_map/lr_modal/pallas_call | solution.py:769
  263.0 10.7 %reduce-scatter.6.cloned.1.call-done = bf16[1,256,1024]{2,1,0:T(8,128)(2,1)} async-done(((bf16[4,256,1024]{2,1,0:T(8,128)(2,1)}), bf16[1,256,1024]{2,1,0:T(8,128)(2,1)}) %reduce-scatter.6.cloned.1.call-update) | async-done | bytes 524304 | tf_op jit(solution)/shard_map/reduce_scatter | solution.py:831
  273.8 1.2 fusion.11
  275.0 1.1 pad_maximum_fusion
  276.1 43.1 %reduce-scatter.8.cloned.1.call-done = bf16[1,256,1024]{2,1,0:T(8,128)(2,1)} async-done(((bf16[4,256,1024]{2,1,0:T(8,128)(2,1)}), bf16[1,256,1024]{2,1,0:T(8,128)(2,1)}) %reduce-scatter.8.cloned.1.call-update) | async-done | bytes 524304 | tf_op jit(solution)/shard_map/reduce_scatter | solution.py:831
  319.3 2.2 fusion.10
  (130 shorter events, 24.6 us)
Async XLA Ops:
  6.5 107.4 %reduce-scatter.4.cloned.1.call-start = ((), (), s32[]{:S(2)}) async-start(), calls=%async_computation.3 | async-start | bytes 2621440 | tf_op jit(solution)/shard_map/reduce_scatter | solution.py:831
  6.5 37.8 %collective-permute-start = (bf16[1024,512]{1,0:T(8,128)(2,1)}, bf16[1024,512]{1,0:T(8,128)(2,1)S(1)}, u32[]{:S(2)}, u32[]{:S(2)}) collective-permute-start(bf16[1024,512]{1,0:T(8,128)(2,1)} %refs_0_.1), channel_id=1, source_target_pairs={{0,4},{4,0},{8,12},{12,8},{16,20},{20,16},{24,28},{28,24},{1,5},{5... | collective-permute-start | bytes 3145736 | tf_op jit(solution)/shard_map/ppermute | solution.py:340
  7.0 37.3 %collective-permute-start.1 = (bf16[1024,512]{1,0:T(8,128)(2,1)}, bf16[1024,512]{1,0:T(8,128)(2,1)S(1)}, u32[]{:S(2)}, u32[]{:S(2)}) collective-permute-start(bf16[1024,512]{1,0:T(8,128)(2,1)} %refs_0_.1), channel_id=1, source_target_pairs={{0,8},{4,12},{8,0},{12,4},{16,24},{20,28},{24,16},{28,20},{1,9},{5... | collective-permute-start | bytes 3145736 | tf_op jit(solution)/shard_map/ppermute | solution.py:340
  9.5 34.9 %collective-permute-start.2 = (bf16[1024,512]{1,0:T(8,128)(2,1)}, bf16[1024,512]{1,0:T(8,128)(2,1)S(1)}, u32[]{:S(2)}, u32[]{:S(2)}) collective-permute-start(bf16[1024,512]{1,0:T(8,128)(2,1)} %refs_0_.1), channel_id=1, source_target_pairs={{0,16},{4,20},{8,24},{12,28},{16,0},{20,4},{24,8},{28,12},{1,17},{... | collective-permute-start | bytes 3145736 | tf_op jit(solution)/shard_map/ppermute | solution.py:340
  16.4 27.9 %collective-permute-start.3 = (bf16[2,144,1024]{2,1,0:T(8,128)(2,1)}, bf16[2,144,1024]{2,1,0:T(8,128)(2,1)}, u32[]{:S(2)}, u32[]{:S(2)}) collective-permute-start(bf16[2,144,1024]{2,1,0:T(8,128)(2,1)} %fusion.9), channel_id=1, source_target_pairs={{0,4},{4,8},{8,12},{12,16},{16,20},{20,24},{24,28},{1,5},{5,9},{9,... | collective-permute-start | bytes 1769480 | tf_op jit(solution)/shard_map/ppermute | solution.py:821
  44.3 7.7 %copy-start.11 = (bf16[1024,512]{1,0:T(8,128)(2,1)}, bf16[1024,512]{1,0:T(8,128)(2,1)S(1)}, u32[]{:S(2)}) copy-start(bf16[1024,512]{1,0:T(8,128)(2,1)S(1)} %collective-permute-done.refs_1_) | copy-start | bytes 3145732
  44.3 7.7 %copy-start.6 = (bf16[1024,512]{1,0:T(8,128)(2,1)}, bf16[1024,512]{1,0:T(8,128)(2,1)S(1)}, u32[]{:S(2)}) copy-start(bf16[1024,512]{1,0:T(8,128)(2,1)S(1)} %collective-permute-done.1.refs_2_) | copy-start | bytes 3145732
  44.3 7.7 %collective-permute-start.5 = (bf16[1024,512]{1,0:T(8,128)(2,1)S(1)}, bf16[1024,512]{1,0:T(8,128)(2,1)S(1)}, u32[]{:S(2)}, u32[]{:S(2)}) collective-permute-start(bf16[1024,512]{1,0:T(8,128)(2,1)S(1)} %collective-permute-done.2.refs_3_.refs_4_), channel_id=1, source_target_pairs={{0,4},{4,0},{8,12},{12,8},{16,20},{20,16},{24,28},{28,24},{1,5},{5... | collective-permute-start | bytes 3145736 | tf_op jit(solution)/shard_map/ppermute | solution.py:340
  44.5 7.6 %collective-permute-start.4 = (bf16[1024,512]{1,0:T(8,128)(2,1)S(1)}, bf16[1024,512]{1,0:T(8,128)(2,1)S(1)}, u32[]{:S(2)}, u32[]{:S(2)}) collective-permute-start(bf16[1024,512]{1,0:T(8,128)(2,1)S(1)} %collective-permute-done.1.refs_2_), channel_id=1, source_target_pairs={{0,4},{4,0},{8,12},{12,8},{16,20},{20,16},{24,28},{28,24},{1,5},{5... | collective-permute-start | bytes 3145736 | tf_op jit(solution)/shard_map/ppermute | solution.py:340
  45.1 13.9 %collective-permute-start.6 = (bf16[1024,256]{1,0:T(8,128)(2,1)S(1)}, bf16[1024,256]{1,0:T(8,128)(2,1)S(1)}, u32[]{:S(2)}, u32[]{:S(2)}) collective-permute-start(bf16[1024,256]{1,0:T(8,128)(2,1)S(1)} %slice.82), channel_id=1, source_target_pairs={{0,8},{4,12},{8,0},{12,4},{16,24},{20,28},{24,16},{28,20},{1,9},{5... | collective-permute-start | bytes 1572872 | tf_op jit(solution)/shard_map/ppermute | solution.py:340
  46.0 14.0 %collective-permute-start.7 = (bf16[1024,256]{1,0:T(8,128)(2,1)S(1)}, bf16[1024,256]{1,0:T(8,128)(2,1)S(1)}, u32[]{:S(2)}, u32[]{:S(2)}) collective-permute-start(bf16[1024,256]{1,0:T(8,128)(2,1)S(1)} %slice.83), channel_id=1, source_target_pairs={{0,16},{4,20},{8,24},{12,28},{16,0},{20,4},{24,8},{28,12},{1,17},{... | collective-permute-start | bytes 1572872 | tf_op jit(solution)/shard_map/ppermute | solution.py:340
  60.0 1.9 collective-permute-start.8
  60.0 2.7 collective-permute-start.9
  67.4 15.6 %collective-permute-start.10 = (bf16[1024,512]{1,0:T(8,128)(2,1)}, bf16[1024,512]{1,0:T(8,128)(2,1)}, u32[]{:S(2)}, u32[]{:S(2)}) collective-permute-start(bf16[1024,512]{1,0:T(8,128)(2,1)} %refs_0_.3), channel_id=1, source_target_pairs={{0,4},{4,0},{8,12},{12,8},{16,20},{20,16},{24,28},{28,24},{1,5},{5... | collective-permute-start | bytes 3145736 | tf_op jit(solution)/shard_map/ppermute | solution.py:340
  67.6 25.6 %collective-permute-start.11 = (bf16[1024,512]{1,0:T(8,128)(2,1)}, bf16[1024,512]{1,0:T(8,128)(2,1)S(1)}, u32[]{:S(2)}, u32[]{:S(2)}) collective-permute-start(bf16[1024,512]{1,0:T(8,128)(2,1)} %refs_0_.3), channel_id=1, source_target_pairs={{0,8},{4,12},{8,0},{12,4},{16,24},{20,28},{24,16},{28,20},{1,9},{5... | collective-permute-start | bytes 3145736 | tf_op jit(solution)/shard_map/ppermute | solution.py:340
  68.3 25.5 %collective-permute-start.12 = (bf16[1024,512]{1,0:T(8,128)(2,1)}, bf16[1024,512]{1,0:T(8,128)(2,1)}, u32[]{:S(2)}, u32[]{:S(2)}) collective-permute-start(bf16[1024,512]{1,0:T(8,128)(2,1)} %refs_0_.3), channel_id=1, source_target_pairs={{0,16},{4,20},{8,24},{12,28},{16,0},{20,4},{24,8},{28,12},{1,17},{... | collective-permute-start | bytes 3145736 | tf_op jit(solution)/shard_map/ppermute | solution.py:340
  69.8 204.0 %reduce-scatter.6.cloned.1.call-start = ((), (), s32[]{:S(2)}) async-start(), calls=%async_computation.4 | async-start | bytes 2621440 | tf_op jit(solution)/shard_map/reduce_scatter | solution.py:831
  83.0 46.8 %copy-start = (bf16[4,256,1024]{2,1,0:T(8,128)(2,1)S(1)}, bf16[4,256,1024]{2,1,0:T(8,128)(2,1)}, u32[]{:S(2)}) copy-start(bf16[4,256,1024]{2,1,0:T(8,128)(2,1)} %project.5) | copy-start | bytes 6291460
  93.2 20.7 %copy-start.5 = (bf16[1024,512]{1,0:T(8,128)(2,1)}, bf16[1024,512]{1,0:T(8,128)(2,1)S(1)}, u32[]{:S(2)}) copy-start(bf16[1024,512]{1,0:T(8,128)(2,1)S(1)} %collective-permute-done.11.refs_2_) | copy-start | bytes 3145732
  93.8 16.5 %collective-permute-start.13 = (bf16[1024,512]{1,0:T(8,128)(2,1)S(1)}, bf16[1024,512]{1,0:T(8,128)(2,1)S(1)}, u32[]{:S(2)}, u32[]{:S(2)}) collective-permute-start(bf16[1024,512]{1,0:T(8,128)(2,1)S(1)} %collective-permute-done.11.refs_2_), channel_id=1, source_target_pairs={{0,4},{4,0},{8,12},{12,8},{16,20},{20,16},{24,28},{28,24},{1,5},{5... | collective-permute-start | bytes 3145736 | tf_op jit(solution)/shard_map/ppermute | solution.py:340
  93.8 18.3 %collective-permute-start.14 = (bf16[1024,512]{1,0:T(8,128)(2,1)}, bf16[1024,512]{1,0:T(8,128)(2,1)}, u32[]{:S(2)}, u32[]{:S(2)}) collective-permute-start(bf16[1024,512]{1,0:T(8,128)(2,1)} %collective-permute-done.12.refs_4_), channel_id=1, source_target_pairs={{0,4},{4,0},{8,12},{12,8},{16,20},{20,16},{24,28},{28,24},{1,5},{5... | collective-permute-start | bytes 3145736 | tf_op jit(solution)/shard_map/ppermute | solution.py:340
  95.4 13.9 %collective-permute-start.15 = (bf16[1024,256]{1,0:T(8,128)(2,1)S(1)}, bf16[1024,256]{1,0:T(8,128)(2,1)S(1)}, u32[]{:S(2)}, u32[]{:S(2)}) collective-permute-start(bf16[1024,256]{1,0:T(8,128)(2,1)S(1)} %slice.84), channel_id=1, source_target_pairs={{0,8},{4,12},{8,0},{12,4},{16,24},{20,28},{24,16},{28,20},{1,9},{5... | collective-permute-start | bytes 1572872 | tf_op jit(solution)/shard_map/ppermute | solution.py:340
  96.8 13.5 %collective-permute-start.16 = (bf16[1024,256]{1,0:T(8,128)(2,1)S(1)}, bf16[1024,256]{1,0:T(8,128)(2,1)S(1)}, u32[]{:S(2)}, u32[]{:S(2)}) collective-permute-start(bf16[1024,256]{1,0:T(8,128)(2,1)S(1)} %slice.85), channel_id=1, source_target_pairs={{0,16},{4,20},{8,24},{12,28},{16,0},{20,4},{24,8},{28,12},{1,17},{... | collective-permute-start | bytes 1572872 | tf_op jit(solution)/shard_map/ppermute | solution.py:340
  115.3 36.3 %copy-start.1 = (bf16[256,1024]{1,0:T(8,128)(2,1)}, bf16[256,1024]{1,0:T(8,128)(2,1)S(1)}, u32[]{:S(2)}) copy-start(bf16[256,1024]{1,0:T(8,128)(2,1)S(1)} %fusion.6.refs_0_) | copy-start | bytes 1572868
  115.3 13.7 %collective-permute-start.17 = (bf16[256,1024]{1,0:T(8,128)(2,1)S(1)}, bf16[256,1024]{1,0:T(8,128)(2,1)}, u32[]{:S(2)}, u32[]{:S(2)}) collective-permute-start(bf16[256,1024]{1,0:T(8,128)(2,1)S(1)} %fusion.6.refs_0_), channel_id=1, source_target_pairs={{0,1},{1,0},{2,3},{3,2},{4,5},{5,4},{6,7},{7,6},{8,9},{9,8},{10,11... | collective-permute-start | bytes 1572872 | tf_op jit(solution)/shard_map/ppermute | solution.py:883
  115.4 13.6 %collective-permute-start.18 = (bf16[256,1024]{1,0:T(8,128)(2,1)S(1)}, bf16[256,1024]{1,0:T(8,128)(2,1)S(1)}, u32[]{:S(2)}, u32[]{:S(2)}) collective-permute-start(bf16[256,1024]{1,0:T(8,128)(2,1)S(1)} %fusion.6.refs_0_), channel_id=1, source_target_pairs={{1,2},{2,1},{5,6},{6,5},{9,10},{10,9},{13,14},{14,13},{17,18},{18,... | collective-permute-start | bytes 1572872 | tf_op jit(solution)/shard_map/ppermute | solution.py:886
  116.1 12.9 %collective-permute-start.19 = (bf16[1024,256]{1,0:T(8,128)(2,1)}, bf16[1024,256]{1,0:T(8,128)(2,1)}, u32[]{:S(2)}, u32[]{:S(2)}) collective-permute-start(bf16[1024,256]{1,0:T(8,128)(2,1)} %copy-done.18), channel_id=1, source_target_pairs={{0,4},{4,0},{8,12},{12,8},{16,20},{20,16},{24,28},{28,24},{1,5},{5... | collective-permute-start | bytes 1572872 | tf_op jit(solution)/shard_map/ppermute | solution.py:340
  116.2 12.8 %collective-permute-start.20 = (bf16[1024,256]{1,0:T(8,128)(2,1)}, bf16[1024,256]{1,0:T(8,128)(2,1)}, u32[]{:S(2)}, u32[]{:S(2)}) collective-permute-start(bf16[1024,256]{1,0:T(8,128)(2,1)} %copy-done.19), channel_id=1, source_target_pairs={{0,4},{4,0},{8,12},{12,8},{16,20},{20,16},{24,28},{28,24},{1,5},{5... | collective-permute-start | bytes 1572872 | tf_op jit(solution)/shard_map/ppermute | solution.py:340
  130.7 14.3 %collective-permute-start.22 = (bf16[256,1024]{1,0:T(8,128)(2,1)}, bf16[256,1024]{1,0:T(8,128)(2,1)S(1)}, u32[]{:S(2)}, u32[]{:S(2)}) collective-permute-start(bf16[256,1024]{1,0:T(8,128)(2,1)} %bitcast_select_fusion.1), channel_id=1, source_target_pairs={{0,1},{1,0},{2,3},{3,2},{4,5},{5,4},{6,7},{7,6},{8,9},{9,8},{10,11... | collective-permute-start | bytes 1572872 | tf_op jit(solution)/shard_map/ppermute | solution.py:883
  134.2 10.8 %collective-permute-start.21 = (bf16[256,1024]{1,0:T(8,128)(2,1)}, bf16[256,1024]{1,0:T(8,128)(2,1)}, u32[]{:S(2)}, u32[]{:S(2)}) collective-permute-start(bf16[256,1024]{1,0:T(8,128)(2,1)} %collective-permute-done.17.refs_1_), channel_id=1, source_target_pairs={{1,2},{2,1},{5,6},{6,5},{9,10},{10,9},{13,14},{14,13},{17,18},{18,... | collective-permute-start | bytes 1572872 | tf_op jit(solution)/shard_map/ppermute | solution.py:886
  145.0 8.1 %copy-start.8 = (bf16[256,1024]{1,0:T(8,128)(2,1)}, bf16[256,1024]{1,0:T(8,128)(2,1)S(1)}, u32[]{:S(2)}) copy-start(bf16[256,1024]{1,0:T(8,128)(2,1)S(1)} %collective-permute-done.22.refs_4_) | copy-start | bytes 1572868
  145.9 18.8 %collective-permute-start.24 = (bf16[256,1024]{1,0:T(8,128)(2,1)}, bf16[256,1024]{1,0:T(8,128)(2,1)}, u32[]{:S(2)}, u32[]{:S(2)}) collective-permute-start(bf16[256,1024]{1,0:T(8,128)(2,1)} %bitcast_select_fusion), channel_id=1, source_target_pairs={{0,1},{1,0},{2,3},{3,2},{4,5},{5,4},{6,7},{7,6},{8,9},{9,8},{10,11... | collective-permute-start | bytes 1572872 | tf_op jit(solution)/shard_map/ppermute | solution.py:883
  151.6 13.1 %collective-permute-start.23 = (bf16[256,1024]{1,0:T(8,128)(2,1)}, bf16[256,1024]{1,0:T(8,128)(2,1)}, u32[]{:S(2)}, u32[]{:S(2)}) collective-permute-start(bf16[256,1024]{1,0:T(8,128)(2,1)} %add_convert_fusion.2), channel_id=1, source_target_pairs={{1,2},{2,1},{5,6},{6,5},{9,10},{10,9},{13,14},{14,13},{17,18},{18,... | collective-permute-start | bytes 1572872 | tf_op jit(solution)/shard_map/ppermute | solution.py:886
  167.2 14.5 %collective-permute-start.25 = (bf16[256,1024]{1,0:T(8,128)(2,1)}, bf16[256,1024]{1,0:T(8,128)(2,1)S(1)}, u32[]{:S(2)}, u32[]{:S(2)}) collective-permute-start(bf16[256,1024]{1,0:T(8,128)(2,1)} %get-tuple-element.208), channel_id=1, source_target_pairs={{0,1},{1,0},{2,3},{3,2},{4,5},{5,4},{6,7},{7,6},{8,9},{9,8},{10,11... | collective-permute-start | bytes 1572872 | tf_op jit(solution)/shard_map/ppermute | solution.py:883
  168.7 12.9 %collective-permute-start.26 = (bf16[256,1024]{1,0:T(8,128)(2,1)S(1)}, bf16[256,1024]{1,0:T(8,128)(2,1)}, u32[]{:S(2)}, u32[]{:S(2)}) collective-permute-start(bf16[256,1024]{1,0:T(8,128)(2,1)S(1)} %get-tuple-element.207), channel_id=1, source_target_pairs={{1,2},{2,1},{5,6},{6,5},{9,10},{10,9},{13,14},{14,13},{17,18},{18,... | collective-permute-start | bytes 1572872 | tf_op jit(solution)/shard_map/ppermute | solution.py:886
  171.4 10.2 %copy-start.24 = (bf16[2,256,1024]{2,1,0:T(8,128)(2,1)S(1)}, bf16[2,256,1024]{2,1,0:T(8,128)(2,1)}, u32[]{:S(2)}) copy-start(bf16[2,256,1024]{2,1,0:T(8,128)(2,1)} %param.15) | copy-start | bytes 3145732
  181.6 17.3 %copy-start.30 = (f32[16,1024]{1,0:T(8,128)S(1)}, f32[16,1024]{1,0:T(8,128)}, u32[]{:S(2)}) copy-start(f32[16,1024]{1,0:T(8,128)} %param.25) | copy-start | bytes 196612
  183.1 26.7 %copy-start.3 = (bf16[256,1024]{1,0:T(8,128)(2,1)}, bf16[256,1024]{1,0:T(8,128)(2,1)S(1)}, u32[]{:S(2)}) copy-start(bf16[256,1024]{1,0:T(8,128)(2,1)S(1)} %fusion.8.refs_0_) | copy-start | bytes 1572868
  183.1 13.8 %collective-permute-start.27 = (bf16[256,1024]{1,0:T(8,128)(2,1)S(1)}, bf16[256,1024]{1,0:T(8,128)(2,1)S(1)}, u32[]{:S(2)}, u32[]{:S(2)}) collective-permute-start(bf16[256,1024]{1,0:T(8,128)(2,1)S(1)} %fusion.8.refs_0_), channel_id=1, source_target_pairs={{0,1},{1,0},{2,3},{3,2},{4,5},{5,4},{6,7},{7,6},{8,9},{9,8},{10,11... | collective-permute-start | bytes 1572872 | tf_op jit(solution)/shard_map/ppermute | solution.py:410
  185.2 11.7 %collective-permute-start.28 = (bf16[256,1024]{1,0:T(8,128)(2,1)S(1)}, bf16[256,1024]{1,0:T(8,128)(2,1)S(1)}, u32[]{:S(2)}, u32[]{:S(2)}) collective-permute-start(bf16[256,1024]{1,0:T(8,128)(2,1)S(1)} %fusion.8.refs_0_), channel_id=1, source_target_pairs={{1,2},{2,1},{5,6},{6,5},{9,10},{10,9},{13,14},{14,13},{17,18},{18,... | collective-permute-start | bytes 1572872 | tf_op jit(solution)/shard_map/ppermute | solution.py:410
  196.9 12.9 %copy-start.14 = (bf16[256,1024]{1,0:T(8,128)(2,1)}, bf16[256,1024]{1,0:T(8,128)(2,1)S(1)}, u32[]{:S(2)}) copy-start(bf16[256,1024]{1,0:T(8,128)(2,1)S(1)} %collective-permute-done.27.refs_1_) | copy-start | bytes 1572868
  196.9 12.9 %copy-start.15 = (bf16[256,1024]{1,0:T(8,128)(2,1)}, bf16[256,1024]{1,0:T(8,128)(2,1)S(1)}, u32[]{:S(2)}) copy-start(bf16[256,1024]{1,0:T(8,128)(2,1)S(1)} %collective-permute-done.28.refs_2_) | copy-start | bytes 1572868
  196.9 12.9 %collective-permute-start.29 = (bf16[256,1024]{1,0:T(8,128)(2,1)S(1)}, bf16[256,1024]{1,0:T(8,128)(2,1)S(1)}, u32[]{:S(2)}, u32[]{:S(2)}) collective-permute-start(bf16[256,1024]{1,0:T(8,128)(2,1)S(1)} %collective-permute-done.27.refs_1_), channel_id=1, source_target_pairs={{1,2},{2,1},{5,6},{6,5},{9,10},{10,9},{13,14},{14,13},{17,18},{18,... | collective-permute-start | bytes 1572872 | tf_op jit(solution)/shard_map/ppermute | solution.py:410
  197.6 17.9 %collective-permute-start.30 = (bf16[256,1024]{1,0:T(8,128)(2,1)S(1)}, bf16[256,1024]{1,0:T(8,128)(2,1)S(1)}, u32[]{:S(2)}, u32[]{:S(2)}) collective-permute-start(bf16[256,1024]{1,0:T(8,128)(2,1)S(1)} %collective-permute-done.28.refs_2_), channel_id=1, source_target_pairs={{1,0},{2,3},{5,4},{6,7},{9,8},{10,11},{13,12},{14,15},{17,16},{18,... | collective-permute-start | bytes 1572872 | tf_op jit(solution)/shard_map/ppermute | solution.py:410
  215.5 15.3 %collective-permute-start.31 = (bf16[256,1024]{1,0:T(8,128)(2,1)S(1)}, bf16[256,1024]{1,0:T(8,128)(2,1)S(1)}, u32[]{:S(2)}, u32[]{:S(2)}) collective-permute-start(bf16[256,1024]{1,0:T(8,128)(2,1)S(1)} %collective-permute-done.29.refs_3_), channel_id=1, source_target_pairs={{1,0},{2,3},{5,4},{6,7},{9,8},{10,11},{13,12},{14,15},{17,16},{18,... | collective-permute-start | bytes 1572872 | tf_op jit(solution)/shard_map/ppermute | solution.py:410
  230.8 88.4 %reduce-scatter.8.cloned.1.call-start = ((), (), s32[]{:S(2)}) async-start(), calls=%async_computation.5 | async-start | bytes 2621440 | tf_op jit(solution)/shard_map/reduce_scatter | solution.py:831
  252.7 21.1 %copy-start.2 = (bf16[256,1024]{1,0:T(8,128)(2,1)S(1)}, bf16[256,1024]{1,0:T(8,128)(2,1)}, u32[]{:S(2)}) copy-start(bf16[256,1024]{1,0:T(8,128)(2,1)} %copy-done.1) | copy-start | bytes 1572868
  252.7 22.3 %copy-start.4 = (bf16[256,1024]{1,0:T(8,128)(2,1)S(1)}, bf16[256,1024]{1,0:T(8,128)(2,1)}, u32[]{:S(2)}) copy-start(bf16[256,1024]{1,0:T(8,128)(2,1)} %copy-done.3) | copy-start | bytes 1572868
  (19 other events, 56.7 us)
Sparse Core Ops, SparseCore 0:
  69.9 43.9 reduce-scatter.3
  230.9 42.7 reduce-scatter.5
  276.2 42.9 reduce-scatter.7

commit v5 on v4

--- a/solution.py
+++ b/solution.py
@@ -62,7 +62,7 @@
     return lax.fori_loop(*chunks, chunk, tuple(totals))
 
 
-def mr_local_kernel(x_ref, short_ref, filter_ref, skip_ref, z_ref, q_ref, conv_ref, raw, u, zs):
+def mr_local_kernel(x_ref, short_ref, filter_ref, skip_ref, gate_ref, z_ref, q_ref, conv_ref, raw, u, zs):
     _, _, tokens, width = x_ref.shape
     head = q_ref.shape[1]
     taps = filter_ref.shape[0]
@@ -118,20 +118,20 @@
         z_ref[0, head:, lanes] = get_rows(zs, head, tokens - head, tile).astype(BF16)
 
 
-def mr_local(x, short_w, taps_w, skip):
-    sequences, _, tokens, width = x.shape
+def mr_local(x, short_w, taps_w, skip, seq, gate):
+    _, _, tokens, width = x.shape
     taps = taps_w.shape[0]
     prior = short_w.shape[0] - 1
     head = taps + HALO
-    rows = jax.ShapeDtypeStruct((sequences, head, SUB, LANES), F32)
+    rows = jax.ShapeDtypeStruct((1, head, SUB, LANES), F32)
     return pl.pallas_call(
         mr_local_kernel,
-        grid=(sequences,),
-        out_shape=(jax.ShapeDtypeStruct((sequences, tokens, width), BF16), rows, rows),
-        in_specs=[pl.BlockSpec((1, 3, tokens, width), lambda i: (i, 0, 0, 0)), *vmem(3)],
+        grid=(1,),
+        out_shape=(jax.ShapeDtypeStruct((1, tokens, width), BF16), rows, rows),
+        in_specs=[pl.BlockSpec((1, 3, tokens, width), lambda i: (seq, 0, 0, 0)), *vmem(3), *in_hbm(1)],
         out_specs=(
-            pl.BlockSpec((1, tokens, width), lambda i: (i, 0, 0)),
-            *(pl.BlockSpec((1, head, SUB, LANES), lambda i: (i, 0, 0, 0)),) * 2,
+            pl.BlockSpec((1, tokens, width), lambda i: (0, 0, 0)),
+            *(pl.BlockSpec((1, head, SUB, LANES), lambda i: (0, 0, 0, 0)),) * 2,
         ),
         scratch_shapes=[
             pltpu.VMEM((3, (tokens + prior) * SUB, LANES), F32),
@@ -141,7 +141,7 @@
         compiler_params=params(VMEM_MIB),
         cost_estimate=cost(1e9, 1e6),
         name="mr_local",
-    )(x, short_w, taps_w, skip)
+    )(x, short_w, taps_w, skip, gate)
 
 
 def mr_finish_kernel(x_ref, halo_ref, q_ref, conv_ref, short_ref, filter_ref, skip_ref, gate_ref, z_ref, raw, extra, zs):
@@ -208,7 +208,7 @@
     head = q.shape[1]
     taps = taps_w.shape[0]
     prior = short_w.shape[0] - 1
-    rows = pl.BlockSpec((1, head, SUB, LANES), lambda i: (seq, 0, 0, 0))
+    rows = pl.BlockSpec((1, head, SUB, LANES), lambda i: (0, 0, 0, 0))
     return pl.pallas_call(
         mr_finish_kernel,
         grid=(1,),
@@ -273,7 +273,7 @@
     return Fetch([(pltpu.make_async_copy(sources[k], held[k], sems.at[k]),) for k in range(len(held))])
 
 
-def project_kernel(places, seq, scalar_ref, head_ref, body_ref, *refs):
+def project_kernel(places, scalar_ref, head_ref, body_ref, *refs):
     count = len(places)
     weights = refs[:count]
     out_ref, z_ref, z_sems, result = refs[-6 - count], refs[-5 - count], refs[-4 - count], refs[-3 - count]
@@ -281,7 +281,7 @@
     head = head_ref.shape[0]
     rest = z_ref.shape[0] - head
     first = pltpu.make_async_copy(head_ref, z_ref.at[pl.ds(0, head)], z_sems.at[0])
-    second = pltpu.make_async_copy(body_ref.at[seq, pl.ds(head, rest)], z_ref.at[pl.ds(head, rest)], z_sems.at[1])
+    second = pltpu.make_async_copy(body_ref.at[0, pl.ds(head, rest)], z_ref.at[pl.ds(head, rest)], z_sems.at[1])
     first.start()
     second.start()
     copies = fetch(weights, held, in_sems)
@@ -292,13 +292,13 @@
 
 
 def project(z, position, places, weights, shares, given=None):
-    head, body, seq = z
+    head, body = z
     _, tokens, width = body.shape
     total = sum(w.shape[1] for w in weights)
     model = places[0][2] * lax.axis_size("ctx")
     extra = [] if given is None else [given]
     return pl.pallas_call(
-        functools.partial(project_kernel, places, seq),
+        functools.partial(project_kernel, places),
         out_shape=jax.ShapeDtypeStruct((shares, tokens, model // shares), BF16),
         in_specs=[pl.BlockSpec(memory_space=pltpu.SMEM), *in_hbm(2 + len(weights) + len(extra))],
         out_specs=in_hbm(1)[0],
@@ -335,6 +335,7 @@
         self.axis, self.whole = axis, block.shape[1]
         self.far = [1 << k for k in range(count.bit_length() - 1, 0, -1) if 1 << k < count]
         self.arrays = {(0, 0): block}
+        self.sent = []
 
     def swap(self, value, bit):
         return lax.ppermute(value, self.axis, swap_pairs(self.axis, bit))
@@ -355,6 +356,7 @@
         for piece in range(pieces if len(self.far) > 1 else 0):
             begin = piece * columns
             part = {bit: self.arrays[bit, 0][:, begin : begin + columns] for bit in self.far}
+            self.sent.append(part[self.far[piece]])
             order = self.far[piece:] + self.far[:piece]
             known = [order[0]]
             for bit in order[1:]:
@@ -433,9 +435,9 @@
     )
 
 
-def lr_in_start_kernel(table, scalar_ref, gain_ref, *refs):
+def lr_in_start_kernel(table, gates, scalar_ref, gain_ref, *refs):
     count = len(table)
-    *blocks, w_ref, total_ref, square_ref, scaled, held, total, sems, out_sems = refs
+    *blocks, w_ref, total_ref, square_ref, scaled, held, total, sems, out_sems = refs[gates:]
     tokens, width = blocks[0].shape
     parts, rows, columns = held.shape
     begin = jnp.where(scalar_ref[0] < count // 2, 0, width)
@@ -475,19 +477,19 @@
         copy.wait()
 
 
-def lr_in_start(place, gain, blocks, table, weight):
+def lr_in_start(place, gain, blocks, table, weight, gates=()):
     count = len(table)
     tokens, width = blocks[0].shape
     rows = (count - 1) * width
     columns = min(512, width)
     parts = 3 * width // columns
     return pl.pallas_call(
-        functools.partial(lr_in_start_kernel, table),
+        functools.partial(lr_in_start_kernel, table, len(gates)),
         out_shape=(
             jax.ShapeDtypeStruct((parts, tokens, columns), F32),
             jax.ShapeDtypeStruct((tokens, LANES), F32),
         ),
-        in_specs=[pl.BlockSpec(memory_space=pltpu.SMEM), *vmem(1 + len(blocks)), *in_hbm(1)],
+        in_specs=[pl.BlockSpec(memory_space=pltpu.SMEM), *vmem(1), *in_hbm(len(gates)), *vmem(len(blocks)), *in_hbm(1)],
         out_specs=(*in_hbm(1), *vmem(1)),
         scratch_shapes=[
             pltpu.VMEM((tokens, rows), BF16),
@@ -499,7 +501,7 @@
         compiler_params=params(VMEM_MIB),
         cost_estimate=cost(6 * tokens * rows * width, 6 * rows * width),
         name="lr_in_start",
-    )(place, gain, *blocks, weight)
+    )(place, gain, *gates, *blocks, weight)
 
 
 SEGMENTS = 4
@@ -790,6 +792,42 @@
     )(position, sent, short_w, rate, res, skip, q, u, *weights)
 
 
+def mid_kernel(seq, residual_ref, share_ref, *refs):
+    out_ref, residual, share, total, sems = refs[-5:]
+    copies = [
+        pltpu.make_async_copy(residual_ref.at[seq], residual, sems.at[0]),
+        pltpu.make_async_copy(share_ref, share, sems.at[1]),
+        pltpu.make_async_copy(total, out_ref, sems.at[2]),
+    ]
+    copies[0].start()
+    copies[1].start()
+    copies[0].wait()
+    copies[1].wait()
+
+    @pl.loop(0, total.shape[0] // HALO)
+    def _(block):
+        where = pl.ds(pl.multiple_of(block * HALO, HALO), HALO)
+        total[where, :] = (residual[where, :].astype(F32) + share[where, :].astype(F32)).astype(BF16)
+
+    copies[2].start()
+    copies[2].wait()
+
+
+def mid_sum(residual, share, seq, gates):
+    tokens, width = share.shape
+    rows = pltpu.VMEM((tokens, width), BF16)
+    return pl.pallas_call(
+        functools.partial(mid_kernel, seq),
+        out_shape=jax.ShapeDtypeStruct((tokens, width), BF16),
+        in_specs=in_hbm(2 + len(gates)),
+        out_specs=in_hbm(1)[0],
+        scratch_shapes=[rows, rows, rows, pltpu.SemaphoreType.DMA((3,))],
+        compiler_params=params(VMEM_MIB),
+        cost_estimate=cost(1e6, 1e6),
+        name="mid_sum",
+    )(residual, share, *gates)
+
+
 def local(
     residual_in,
     mr_qkv,
@@ -841,14 +879,14 @@
 
     mr_w = SwapGather(mr_out_w, "ctx")
     mr_w.first()
-    body, q, conv = mr_local(x, mr_short, mr_taps, mr_direct)
+    body, q, conv = mr_local(x, mr_short, mr_taps, mr_direct, 0, x)
     mr_w.arrays, halo = together(mr_w.arrays, halo)
 
     early = list(mr_w.arrays)
     mr_w.second()
     early = [k for k in mr_w.arrays if k in early or (k[0] ^ 1, k[1]) in early]
     head = mr_finish(x, halo, q, conv, mr_short, mr_taps, mr_direct, 0, conv)
-    z = head, body, 0
+    z = head, body
     first = project(z, position, mr_w.places(early), [mr_w.arrays[k] for k in early], tp)
     mr_w.arrays, first = together(mr_w.arrays, first)
 
@@ -860,11 +898,11 @@
 
     lr_w = SwapGather(after(lr_out_w, first), "ctx")
     lr_w.first()
+    body, q, conv = mr_local(x, mr_short, mr_taps, mr_direct, 1, first)
     head = mr_finish(x, halo, q, conv, mr_short, mr_taps, mr_direct, 1, first)
-    second = project((head, body, 1), position, mr_w.places(mr_w.arrays), list(mr_w.arrays.values()), tp)
+    second = project((head, body), position, mr_w.places(mr_w.arrays), list(mr_w.arrays.values()), tp)
     lr_w.arrays, second = together(lr_w.arrays, second)
     lr_w.second()
-    lr_w.arrays, share = together(lr_w.arrays, share)
 
     def near(blocks):
         return blocks[:5] if tp == 4 else blocks
@@ -874,7 +912,7 @@
             arrived = line_scatter(parts, "tp", step, arrived)
         return arrived
 
-    mids = [as_mid(0, share)]
+    mids = [mid_sum(residual_in, share, 0, [second, *lr_w.sent])]
     if tp == 4:
         line = lax.axis_index("tp")
         inside = (line == 1) | (line == 2)
@@ -889,14 +927,15 @@
             return line_part(second, "tp", jnp.where(line < 2, share, 3 - share))
 
         near_0, near_1 = outer(mids[0]), inner(mids[0])
-        lr_w.third()
-        near_0, near_1, second, lr_w.arrays = together(near_0, near_1, second, lr_w.arrays)
+        near_0, near_1, second = together(near_0, near_1, second)
         far_1 = outer(jnp.where(inside, near_1, part(3)))
         far_0 = inner(near_0)
+        lr_w.third()
+        arrived_w = list(lr_w.arrays.values())
         near_0, near_1, far_0, far_1 = together(near_0, near_1, far_0, far_1)
         far_2 = outer(jnp.where(inside, far_0, part(2)))
         sums_0 = inner(add(part(3), far_1))
-        begun = lr_in_start(place, gain, [mids[0], near_0, near_1, far_0, far_1], table, in_w)
+        begun = lr_in_start(place, gain, [mids[0], near_0, near_1, far_0, far_1], table, in_w, arrived_w)
         begun, sums_0, far_0, far_1, far_2, near_0, near_1 = together(begun, sums_0, far_0, far_1, far_2, near_0, near_1)
         blocks = [mids[0], near_0, near_1, far_0, far_1, far_2]
         arrived = [outer(add(part(jnp.where(inside, 0, 1)), sums_0)), inner(add(part(2), far_2))]
@@ -917,17 +956,22 @@
     arrived, q, u, send = together(arrived, q, u, send)
     mids.append(as_mid(1, line_part(second, "tp", lax.axis_index("tp")), *arrived))
     blocks = line_gather(mids[1], "tp", 1, None)
+    across = lax.ppermute(mids[1], "tp", [(0, 3), (3, 0)]) if tp == 4 else None
     sent = lax.all_gather(send, "ctx", axis=0)
-    blocks, sent, q, u = together(blocks, sent, q, u)
+    blocks, sent, q, u, across = together(blocks, sent, q, u, across)
     blocks = line_gather(mids[1], "tp", 2, blocks)
     lr_places, lr_weights = lr_w.places(lr_w.arrays), list(lr_w.arrays.values())
     modal_w = (lr_short, rate, res, lr_direct, width, lr_places, lr_weights, tp)
     first = lr_modal(position, q, u, sent, *modal_w)
     blocks, first = together(blocks, first)
-    begun = lr_in_start(place, gain, near(blocks), table, in_w)
-    blocks = line_gather(mids[1], "tp", 3, blocks)
-    blocks, begun, first = together(blocks, begun, first)
-    share = scattered(first)
+    if tp == 4:
+        blocks, across, first = together(blocks, across, first)
+        share = scattered(first)
+        begun = lr_in_start(place, gain, blocks, table, in_w)
+        blocks = [*blocks, across]
+    else:
+        share = scattered(first)
+        begun = lr_in_start(place, gain, blocks, table, in_w)
     q, u, send = lr_mix(place, gain, begun, blocks, table, in_w, lr_short, rate)
     sent = lax.all_gather(send, "ctx", axis=0)
     second = lr_modal(position, q, u, sent, *modal_w)

time: 329 us -> 324 us (0.985)
  waiting for transfers between devices: 112 us -> 94 us
  starting transfers between devices: 35.9 us -> 42.8 us
  Pallas kernels: 116 us -> 122 us
    ppermute x18, waiting for transfers between devices: 26.8 us -> 8.82 us  [swap(): return lax.ppermute(value, self.axis, swap_pairs(self.axis, bit))]
    ppermute x0 -> x1, waiting for transfers between devices: none -> 7.55 us  [local(): across = lax.ppermute(mids[1], 'tp', [(0, 3), (3, 0)]) if tp == 4 else None]
    ppermute x5 -> x4, waiting for transfers between devices: 8 us -> 2.46 us  [move(): return lax.ppermute(what, axis, pairs)]
    pallas_call x6 -> x8, Pallas kernels: 63.1 us -> 68.5 us  [the longest x2 26.3 us: mr_local(): pl.pallas_call(mr_local_kernel, grid=(1,), out_shape=(jax.ShapeDtypeStruc...]
    ppermute x0 -> x1, starting transfers between devices: none -> 3.79 us  [local(): across = lax.ppermute(mids[1], 'tp', [(0, 3), (3, 0)]) if tp == 4 else None]
    ppermute x4, waiting for transfers between devices: 21.6 us -> 18.2 us  [outer(): return lax.ppermute(value, 'tp', [(0, 1), (1, 0), (2, 3), (3, 2)])]
    unnamed x67 -> x61, local copies, waits for them, and re-layouts: 7.85 us -> 7.25 us
  transfers between devices with their start and end apart: 35 -> 35, of which waited for: 15 -> 10; matrix products, arithmetic and copies ran while one was open for 3% -> 4% of each run, Pallas kernels for 34% -> 36%
where the time goes in v5:
time: 324 us; the launch traced here: 322 us
  Pallas kernels  122 us (38%)
  waiting for transfers between devices  94 us (29%)
  starting transfers between devices  42.8 us (13%)
  blocking collectives  22.7 us (7%)
  other arithmetic  15.7 us (5%)
  between operations  13.7 us (4%)
  local copies, waits for them, and re-layouts  12 us (4%)
    reduce_scatter x3, waiting for transfers between devices, scattered(): return lax.psum_scatter(parts, 'tp', scatter_dimension=0)  56.9 us
    pallas_call x2, Pallas kernels, mr_local(): pl.pallas_call(mr_local_kernel, grid=(1,), out_shape=(jax.ShapeDtypeStruc...  26.3 us
    pallas_call x2, Pallas kernels, lr_in_start(): pl.pallas_call(functools.partial(lr_in_start_kernel, table, len(gates)),...  23.7 us
    all_gather x2, blocking collectives, local(): sent = lax.all_gather(send, 'ctx', axis=0)  22.7 us
    pallas_call x2, Pallas kernels, lr_modal(): pl.pallas_call(functools.partial(lr_modal_kernel, places), out_shape=jax....  20.5 us
    pallas_call x2, Pallas kernels, lr_mix(): pl.pallas_call(functools.partial(lr_mix_kernel, table), out_shape=(rows,...  20.3 us
    ppermute x4, waiting for transfers between devices, outer(): return lax.ppermute(value, 'tp', [(0, 1), (1, 0), (2, 3), (3, 2)])  18.2 us
    pallas_call x3, Pallas kernels, project(): pl.pallas_call(functools.partial(project_kernel, places), out_shape=jax.S...  16.1 us
  transfers between devices with their start and end apart: 35, of which 10 were waited for; matrix products, arithmetic and copies ran while one was open for 4% of the time, Pallas kernels for 36%

profile of v5, /device:TPU:0, one launch (start us, length us, event | category | flops | bytes accessed | tf_op | source)
XLA Modules:
  0.0 322.4 jit_solution(1445021526999662875)
XLA Ops:
  7.0 2.5 collective-permute-start.1
  9.5 1.5 collective-permute-start.2
  11.8 1.9 copy_convert_fusion
  16.4 2.7 collective-permute-start.3
  20.6 13.1 %mr_local.2 = (bf16[1,256,1024]{2,1,0:T(8,128)(2,1)}, f32[1,144,8,128]{3,2,1,0:T(8,128)}, f32[1,144,8,128]{3,2,1,0:T(8,128)}) custom-call(bf16[2,3,256,1024]{3,2,1,0:T(8,128)(2,1)} %bitcast.53, f32[3,3,8,128]{3,2,1,0:T(8,128)} %reshape.77.short_ref, f32[128,8,128]{2,1,0:T(8,128)} %bitcast.59, f32[8,128]{1,0:T(8,128)} %bitcast.81, ...), custom_call_target="tpu_custom_call" | custom-call | flops 1000000000 | bytes 1000000 | tf_op jit(solution)/shard_map/mr_local/pallas_call | solution.py:127
  33.8 6.6 %collective-permute-done.2.refs_3_.refs_4_ = bf16[1024,512]{1,0:T(8,128)(2,1)S(1)} collective-permute-done((bf16[1024,512]{1,0:T(8,128)(2,1)}, bf16[1024,512]{1,0:T(8,128)(2,1)S(1)}, u32[]{:S(2)}, u32[]{:S(2)}) %collective-permute-start.2) | collective-permute-done | bytes 1048608 | tf_op jit(solution)/shard_map/ppermute | solution.py:341
  41.1 1.4 collective-permute-start.6
  42.5 1.5 collective-permute-start.7
  44.0 6.1 %mr_finish.2.head_ref = bf16[144,1024]{1,0:T(8,128)(2,1)} custom-call(bf16[2,3,256,1024]{3,2,1,0:T(8,128)(2,1)} %bitcast.55, bf16[2,144,1024]{2,1,0:T(8,128)(2,1)} %collective-permute-done.3.halo_ref, f32[1,144,8,128]{3,2,1,0:T(8,128)} %get-tuple-element.96.q_ref, f32[1,144,8,128]{3,2,1,0:T(8,128)} %get-tuple-element.97.conv_ref.gate_ref, ...), custom_call_target="tpu_custom_call" | custom-call | flops 40000000000 | bytes 1000000 | tf_op jit(solution)/shard_map/mr_finish/pallas_call | solution.py:212
  51.5 5.3 %project.3.refs_4_ = bf16[4,256,1024]{2,1,0:T(8,128)(2,1)} custom-call(s32[1]{0:T(128)} %bitcast.scalar_ref, bf16[144,1024]{1,0:T(8,128)(2,1)} %mr_finish.2.head_ref, bf16[1,256,1024]{2,1,0:T(8,128)(2,1)} %get-tuple-element.98.body_ref, bf16[1024,512]{1,0:T(8,128)(2,1)} %refs_0_.1, bf16[1024,512]{1,0:T(8,128)(2,1)} %copy-done.10, ...), custom_call_target="tpu_custom_call" | custom-call | flops 1610612736 | bytes 7864320 | tf_op jit(solution)/shard_map/project/pallas_call | solution.py:300
  57.4 1.4 collective-permute-done.8.refs_2_.refs_8_
  60.4 3.8 %project.4.gate_ref = bf16[4,256,1024]{2,1,0:T(8,128)(2,1)} custom-call(s32[1]{0:T(128)} %bitcast.scalar_ref, bf16[144,1024]{1,0:T(8,128)(2,1)} %mr_finish.2.head_ref, bf16[1,256,1024]{2,1,0:T(8,128)(2,1)} %get-tuple-element.98.body_ref, bf16[1024,256]{1,0:T(8,128)(2,1)} %copy-done.18, bf16[1024,256]{1,0:T(8,128)(2,1)} %copy-done.19, ...), custom_call_target="tpu_custom_call", output_to_operand_aliasing={{}: (7, {})} | custom-call | flops 536870912 | bytes 2621440 | tf_op jit(solution)/shard_map/project/pallas_call | solution.py:300
  65.6 1.5 collective-permute-start.11
  67.8 13.2 %mr_local.3 = (bf16[1,256,1024]{2,1,0:T(8,128)(2,1)}, f32[1,144,8,128]{3,2,1,0:T(8,128)}, f32[1,144,8,128]{3,2,1,0:T(8,128)}) custom-call(bf16[2,3,256,1024]{3,2,1,0:T(8,128)(2,1)} %bitcast.56, f32[3,3,8,128]{3,2,1,0:T(8,128)} %reshape.77.short_ref, f32[128,8,128]{2,1,0:T(8,128)} %bitcast.61, f32[8,128]{1,0:T(8,128)} %bitcast.83, ...), custom_call_target="tpu_custom_call" | custom-call | flops 1000000000 | bytes 1000000 | tf_op jit(solution)/shard_map/mr_local/pallas_call | solution.py:127
  81.0 6.1 %mr_finish.3.head_ref = bf16[144,1024]{1,0:T(8,128)(2,1)} custom-call(bf16[2,3,256,1024]{3,2,1,0:T(8,128)(2,1)} %bitcast.57, bf16[2,144,1024]{2,1,0:T(8,128)(2,1)} %collective-permute-done.3.halo_ref, f32[1,144,8,128]{3,2,1,0:T(8,128)} %get-tuple-element.107.q_ref, f32[1,144,8,128]{3,2,1,0:T(8,128)} %get-tuple-element.108.conv_ref, ...), custom_call_target="tpu_custom_call" | custom-call | flops 40000000000 | bytes 1000000 | tf_op jit(solution)/shard_map/mr_finish/pallas_call | solution.py:212
  87.0 7.0 %project.5.refs_0_ = bf16[4,256,1024]{2,1,0:T(8,128)(2,1)} custom-call(s32[1]{0:T(128)} %bitcast.scalar_ref, bf16[144,1024]{1,0:T(8,128)(2,1)} %mr_finish.3.head_ref, bf16[1,256,1024]{2,1,0:T(8,128)(2,1)} %get-tuple-element.109.body_ref, bf16[1024,512]{1,0:T(8,128)(2,1)} %refs_0_.1, bf16[1024,512]{1,0:T(8,128)(2,1)} %copy-done.10, ...), custom_call_target="tpu_custom_call" | custom-call | flops 2147483648 | bytes 10485760 | tf_op jit(solution)/shard_map/project/pallas_call | solution.py:300
  96.8 11.9 %reduce-scatter.4.cloned.1.call-done = bf16[1,256,1024]{2,1,0:T(8,128)(2,1)} async-done(((bf16[4,256,1024]{2,1,0:T(8,128)(2,1)}), bf16[1,256,1024]{2,1,0:T(8,128)(2,1)}) %reduce-scatter.4.cloned.1.call-update) | async-done | bytes 524304 | tf_op jit(solution)/shard_map/reduce_scatter | solution.py:869
  108.8 2.4 mid_sum.1.refs_10_.refs_0_
  111.2 1.5 collective-permute-start.14
  112.7 1.5 collective-permute-start.15
  114.2 1.5 collective-permute-start.16
  115.7 9.4 %collective-permute-done.13.refs_11_.refs_1_ = bf16[256,1024]{1,0:T(8,128)(2,1)} collective-permute-done((bf16[256,1024]{1,0:T(8,128)(2,1)}, bf16[256,1024]{1,0:T(8,128)(2,1)}, u32[]{:S(2)}, u32[]{:S(2)}) %collective-permute-start.13) | collective-permute-done | bytes 524320 | tf_op jit(solution)/shard_map/ppermute | solution.py:921
  125.9 4.7 %collective-permute-start.22 = (bf16[256,1024]{1,0:T(8,128)(2,1)}, bf16[256,1024]{1,0:T(8,128)(2,1)}, u32[]{:S(2)}, u32[]{:S(2)}) collective-permute-start(bf16[256,1024]{1,0:T(8,128)(2,1)} %bitcast_select_fusion.1), channel_id=1, source_target_pairs={{0,1},{1,0},{2,3},{3,2},{4,5},{5,4},{6,7},{7,6},{8,9},{9,8},{10,11... | collective-permute-start | bytes 1572872 | tf_op jit(solution)/shard_map/ppermute | solution.py:921
  130.6 1.5 collective-permute-start.21
  132.6 8.8 %collective-permute-done.22.refs_14_.refs_4_ = bf16[256,1024]{1,0:T(8,128)(2,1)} collective-permute-done((bf16[256,1024]{1,0:T(8,128)(2,1)}, bf16[256,1024]{1,0:T(8,128)(2,1)}, u32[]{:S(2)}, u32[]{:S(2)}) %collective-permute-start.22) | collective-permute-done | bytes 524320 | tf_op jit(solution)/shard_map/ppermute | solution.py:921
  142.3 4.7 %collective-permute-start.24 = (bf16[256,1024]{1,0:T(8,128)(2,1)}, bf16[256,1024]{1,0:T(8,128)(2,1)}, u32[]{:S(2)}, u32[]{:S(2)}) collective-permute-start(bf16[256,1024]{1,0:T(8,128)(2,1)} %bitcast_select_fusion), channel_id=1, source_target_pairs={{0,1},{1,0},{2,3},{3,2},{4,5},{5,4},{6,7},{7,6},{8,9},{9,8},{10,11... | collective-permute-start | bytes 1572872 | tf_op jit(solution)/shard_map/ppermute | solution.py:921
  147.0 2.0 add_convert_fusion.2
  149.0 1.5 collective-permute-start.23
  150.4 11.7 %lr_in_start.2 = (f32[6,256,512]{2,1,0:T(8,128)}, f32[256,128]{1,0:T(8,128)}) custom-call(s32[1]{0:T(128)} %bitcast.12.scalar_ref, f32[1,4096]{1,0:T(1,128)} %bitcast.72, bf16[1024,512]{1,0:T(8,128)(2,1)} %refs_0_.4, bf16[1024,512]{1,0:T(8,128)(2,1)} %copy-done.4, bf16[1024,512]{1,0:T(8,128)(2,1)} %copy-done.1, bf16[1024,512]{1,0:T(8,128)(2,1)} %copy-done.2, ...), custom_call_target="tpu_custom_call" | custom-call | flops 4831838208 | bytes 18874368 | tf_op jit(solution)/shard_map/lr_in_start/pallas_call | solution.py:486
  162.2 2.4 add_convert_fusion.1
  164.6 1.8 collective-permute-start.25
  166.4 1.5 collective-permute-start.26
  169.1 10.2 %lr_mix.2 = (f32[256,8,128]{2,1,0:T(8,128)}, f32[256,8,128]{2,1,0:T(8,128)}, bf16[32,8,128]{2,1,0:T(8,128)(2,1)}) custom-call(s32[1]{0:T(128)} %bitcast.12.scalar_ref, f32[1,4096]{1,0:T(1,128)} %bitcast.73, f32[256,128]{1,0:T(8,128)} %get-tuple-element.132.square_ref, f32[3,3,8,128]{3,2,1,0:T(8,128)} %reshape.81.short_ref, f32[16,8,128]{2,1,0:T(8,128)} %bitcast.65, ...), custom_call_target="tpu_custom_call" | custom-call | flops 1610612736 | bytes 6291456 | tf_op jit(solution)/shard_map/lr_mix/pallas_call | solution.py:622
  179.4 1.4 fusion.7.refs_0_
  180.8 2.1 collective-permute-start.27
  183.6 3.8 %collective-permute-start.29 = (bf16[256,1024]{1,0:T(8,128)(2,1)S(1)}, bf16[256,1024]{1,0:T(8,128)(2,1)S(1)}, u32[]{:S(2)}, u32[]{:S(2)}) collective-permute-start(bf16[256,1024]{1,0:T(8,128)(2,1)S(1)} %fusion.7.refs_0_), channel_id=1, source_target_pairs={{0,3},{3,0},{4,7},{7,4},{8,11},{11,8},{12,15},{15,12},{16,19},{19,... | collective-permute-start | bytes 1572872 | tf_op jit(solution)/shard_map/ppermute | solution.py:959
  187.4 10.9 %all-gather = bf16[256,8,128]{2,1,0:T(8,128)(2,1)} all-gather(bf16[32,8,128]{2,1,0:T(8,128)(2,1)S(1)} %copy-done.25), channel_id=2, replica_groups=mesh['ctx'=8,'tp'=4] {'ctx'}, dimensions={0}, use_global_device_ids=true | all-gather | bytes 589824 | tf_op jit(solution)/shard_map/all_gather | solution.py:960
  198.2 7.6 %collective-permute-done.29.refs_5_ = bf16[256,1024]{1,0:T(8,128)(2,1)S(1)} collective-permute-done((bf16[256,1024]{1,0:T(8,128)(2,1)S(1)}, bf16[256,1024]{1,0:T(8,128)(2,1)S(1)}, u32[]{:S(2)}, u32[]{:S(2)}) %collective-permute-start.29) | collective-permute-done | bytes 524320 | tf_op jit(solution)/shard_map/ppermute | solution.py:959
  206.5 1.3 collective-permute-start.31
  208.4 10.2 %lr_modal.2 = bf16[4,256,1024]{2,1,0:T(8,128)(2,1)} custom-call(s32[1]{0:T(128)} %bitcast.scalar_ref, bf16[8,32,8,128]{3,2,1,0:T(8,128)(2,1)} %bitcast.63, f32[3,3,8,128]{3,2,1,0:T(8,128)} %reshape.81.short_ref, f32[16,8,128]{2,1,0:T(8,128)} %bitcast.66, f32[16,8,128]{2,1,0:T(8,128)} %bitcast.69, f32[8,128]{1,0:T(8,128)} %bitcast.79, ...), custom_call_target="tpu_custom_call" | custom-call | flops 2147483648 | bytes 10485760 | tf_op jit(solution)/shard_map/lr_modal/pallas_call | solution.py:771
  218.7 2.4 collective-permute-done.31.refs_4_
  222.0 12.0 %lr_in_start.3 = (f32[6,256,512]{2,1,0:T(8,128)}, f32[256,128]{1,0:T(8,128)}) custom-call(s32[1]{0:T(128)} %bitcast.12.scalar_ref, f32[1,4096]{1,0:T(1,128)} %bitcast.74, bf16[256,1024]{1,0:T(8,128)(2,1)} %copy-done.6, bf16[256,1024]{1,0:T(8,128)(2,1)} %copy-done.14, bf16[256,1024]{1,0:T(8,128)(2,1)} %copy-done.15, bf16[256,1024]{1,0:T(8,128)(2,1)} %copy-done.16, ...), custom_call_target="tpu_custom_call" | custom-call | flops 4831838208 | bytes 18874368 | tf_op jit(solution)/shard_map/lr_in_start/pallas_call | solution.py:486
  234.0 10.2 %lr_mix.3 = (f32[256,8,128]{2,1,0:T(8,128)}, f32[256,8,128]{2,1,0:T(8,128)}, bf16[32,8,128]{2,1,0:T(8,128)(2,1)}) custom-call(s32[1]{0:T(128)} %bitcast.12.scalar_ref, f32[1,4096]{1,0:T(1,128)} %bitcast.75, f32[256,128]{1,0:T(8,128)} %get-tuple-element.165.square_ref, f32[3,3,8,128]{3,2,1,0:T(8,128)} %reshape.81.short_ref, f32[16,8,128]{2,1,0:T(8,128)} %bitcast.67, ...), custom_call_target="tpu_custom_call" | custom-call | flops 1610612736 | bytes 6291456 | tf_op jit(solution)/shard_map/lr_mix/pallas_call | solution.py:622
  244.2 11.8 %all-gather.1 = bf16[256,8,128]{2,1,0:T(8,128)(2,1)} all-gather(bf16[32,8,128]{2,1,0:T(8,128)(2,1)} %get-tuple-element.168), channel_id=3, replica_groups=mesh['ctx'=8,'tp'=4] {'ctx'}, dimensions={0}, use_global_device_ids=true | all-gather | bytes 589824 | tf_op jit(solution)/shard_map/all_gather | solution.py:976
  256.0 10.3 %lr_modal.3 = bf16[4,256,1024]{2,1,0:T(8,128)(2,1)} custom-call(s32[1]{0:T(128)} %bitcast.scalar_ref, bf16[8,32,8,128]{3,2,1,0:T(8,128)(2,1)} %bitcast.64, f32[3,3,8,128]{3,2,1,0:T(8,128)} %reshape.81.short_ref, f32[16,8,128]{2,1,0:T(8,128)} %bitcast.68, f32[16,8,128]{2,1,0:T(8,128)} %bitcast.70, f32[8,128]{1,0:T(8,128)} %bitcast.80, ...), custom_call_target="tpu_custom_call" | custom-call | flops 2147483648 | bytes 10485760 | tf_op jit(solution)/shard_map/lr_modal/pallas_call | solution.py:771
  266.8 1.2 fusion.10
  269.1 44.5 %reduce-scatter.8.cloned.1.call-done = bf16[1,256,1024]{2,1,0:T(8,128)(2,1)} async-done(((bf16[4,256,1024]{2,1,0:T(8,128)(2,1)}), bf16[1,256,1024]{2,1,0:T(8,128)(2,1)}) %reduce-scatter.8.cloned.1.call-update) | async-done | bytes 524304 | tf_op jit(solution)/shard_map/reduce_scatter | solution.py:869
  313.6 2.2 fusion.9
  (125 shorter events, 22.4 us)
Async XLA Ops:
  6.5 102.2 %reduce-scatter.4.cloned.1.call-start = ((), (), s32[]{:S(2)}) async-start(), calls=%async_computation.3 | async-start | bytes 2621440 | tf_op jit(solution)/shard_map/reduce_scatter | solution.py:869
  6.5 27.2 %collective-permute-start = (bf16[1024,512]{1,0:T(8,128)(2,1)}, bf16[1024,512]{1,0:T(8,128)(2,1)S(1)}, u32[]{:S(2)}, u32[]{:S(2)}) collective-permute-start(bf16[1024,512]{1,0:T(8,128)(2,1)} %refs_0_.1), channel_id=1, source_target_pairs={{0,4},{4,0},{8,12},{12,8},{16,20},{20,16},{24,28},{28,24},{1,5},{5... | collective-permute-start | bytes 3145736 | tf_op jit(solution)/shard_map/ppermute | solution.py:341
  7.0 26.8 %collective-permute-start.1 = (bf16[1024,512]{1,0:T(8,128)(2,1)}, bf16[1024,512]{1,0:T(8,128)(2,1)S(1)}, u32[]{:S(2)}, u32[]{:S(2)}) collective-permute-start(bf16[1024,512]{1,0:T(8,128)(2,1)} %refs_0_.1), channel_id=1, source_target_pairs={{0,8},{4,12},{8,0},{12,4},{16,24},{20,28},{24,16},{28,20},{1,9},{5... | collective-permute-start | bytes 3145736 | tf_op jit(solution)/shard_map/ppermute | solution.py:341
  9.5 31.0 %collective-permute-start.2 = (bf16[1024,512]{1,0:T(8,128)(2,1)}, bf16[1024,512]{1,0:T(8,128)(2,1)S(1)}, u32[]{:S(2)}, u32[]{:S(2)}) collective-permute-start(bf16[1024,512]{1,0:T(8,128)(2,1)} %refs_0_.1), channel_id=1, source_target_pairs={{0,16},{4,20},{8,24},{12,28},{16,0},{20,4},{24,8},{28,12},{1,17},{... | collective-permute-start | bytes 3145736 | tf_op jit(solution)/shard_map/ppermute | solution.py:341
  16.4 17.4 %collective-permute-start.3 = (bf16[2,144,1024]{2,1,0:T(8,128)(2,1)}, bf16[2,144,1024]{2,1,0:T(8,128)(2,1)}, u32[]{:S(2)}, u32[]{:S(2)}) collective-permute-start(bf16[2,144,1024]{2,1,0:T(8,128)(2,1)} %fusion.8), channel_id=1, source_target_pairs={{0,4},{4,8},{8,12},{12,16},{16,20},{20,24},{24,28},{1,5},{5,9},{9,... | collective-permute-start | bytes 1769480 | tf_op jit(solution)/shard_map/ppermute | solution.py:859
  33.8 16.3 %copy-start.10 = (bf16[1024,512]{1,0:T(8,128)(2,1)}, bf16[1024,512]{1,0:T(8,128)(2,1)S(1)}, u32[]{:S(2)}) copy-start(bf16[1024,512]{1,0:T(8,128)(2,1)S(1)} %collective-permute-done.refs_1_) | copy-start | bytes 3145732
  33.8 16.3 %copy-start.8 = (bf16[1024,512]{1,0:T(8,128)(2,1)}, bf16[1024,512]{1,0:T(8,128)(2,1)S(1)}, u32[]{:S(2)}) copy-start(bf16[1024,512]{1,0:T(8,128)(2,1)S(1)} %collective-permute-done.1.refs_2_) | copy-start | bytes 3145732
  40.4 9.7 %collective-permute-start.5 = (bf16[1024,512]{1,0:T(8,128)(2,1)S(1)}, bf16[1024,512]{1,0:T(8,128)(2,1)S(1)}, u32[]{:S(2)}, u32[]{:S(2)}) collective-permute-start(bf16[1024,512]{1,0:T(8,128)(2,1)S(1)} %collective-permute-done.2.refs_3_.refs_4_), channel_id=1, source_target_pairs={{0,4},{4,0},{8,12},{12,8},{16,20},{20,16},{24,28},{28,24},{1,5},{5... | collective-permute-start | bytes 3145736 | tf_op jit(solution)/shard_map/ppermute | solution.py:341
  40.5 9.6 %collective-permute-start.4 = (bf16[1024,512]{1,0:T(8,128)(2,1)S(1)}, bf16[1024,512]{1,0:T(8,128)(2,1)S(1)}, u32[]{:S(2)}, u32[]{:S(2)}) collective-permute-start(bf16[1024,512]{1,0:T(8,128)(2,1)S(1)} %collective-permute-done.1.refs_2_), channel_id=1, source_target_pairs={{0,4},{4,0},{8,12},{12,8},{16,20},{20,16},{24,28},{28,24},{1,5},{5... | collective-permute-start | bytes 3145736 | tf_op jit(solution)/shard_map/ppermute | solution.py:341
  41.1 15.7 %collective-permute-start.6 = (bf16[1024,256]{1,0:T(8,128)(2,1)S(1)}, bf16[1024,256]{1,0:T(8,128)(2,1)S(1)}, u32[]{:S(2)}, u32[]{:S(2)}) collective-permute-start(bf16[1024,256]{1,0:T(8,128)(2,1)S(1)} %slice.78), channel_id=1, source_target_pairs={{0,8},{4,12},{8,0},{12,4},{16,24},{20,28},{24,16},{28,20},{1,9},{5... | collective-permute-start | bytes 1572872 | tf_op jit(solution)/shard_map/ppermute | solution.py:341
  42.5 14.3 %collective-permute-start.7 = (bf16[1024,256]{1,0:T(8,128)(2,1)S(1)}, bf16[1024,256]{1,0:T(8,128)(2,1)S(1)}, u32[]{:S(2)}, u32[]{:S(2)}) collective-permute-start(bf16[1024,256]{1,0:T(8,128)(2,1)S(1)} %slice.79), channel_id=1, source_target_pairs={{0,16},{4,20},{8,24},{12,28},{16,0},{20,4},{24,8},{28,12},{1,17},{... | collective-permute-start | bytes 1572872 | tf_op jit(solution)/shard_map/ppermute | solution.py:341
  56.8 2.0 collective-permute-start.8
  56.9 2.6 collective-permute-start.9
  64.2 202.5 %reduce-scatter.6.cloned.1.call-start = ((), (), s32[]{:S(2)}) async-start(), calls=%async_computation.4 | async-start | bytes 2621440 | tf_op jit(solution)/shard_map/reduce_scatter | solution.py:869
  65.4 28.7 %collective-permute-start.10 = (bf16[1024,512]{1,0:T(8,128)(2,1)S(1)}, bf16[1024,512]{1,0:T(8,128)(2,1)S(1)}, u32[]{:S(2)}, u32[]{:S(2)}) collective-permute-start(bf16[1024,512]{1,0:T(8,128)(2,1)S(1)} %copy-done.3), channel_id=1, source_target_pairs={{0,4},{4,0},{8,12},{12,8},{16,20},{20,16},{24,28},{28,24},{1,5},{5... | collective-permute-start | bytes 3145736 | tf_op jit(solution)/shard_map/ppermute | solution.py:341
  65.6 28.5 %collective-permute-start.11 = (bf16[1024,512]{1,0:T(8,128)(2,1)S(1)}, bf16[1024,512]{1,0:T(8,128)(2,1)S(1)}, u32[]{:S(2)}, u32[]{:S(2)}) collective-permute-start(bf16[1024,512]{1,0:T(8,128)(2,1)S(1)} %copy-done.3), channel_id=1, source_target_pairs={{0,8},{4,12},{8,0},{12,4},{16,24},{20,28},{24,16},{28,20},{1,9},{5... | collective-permute-start | bytes 3145736 | tf_op jit(solution)/shard_map/ppermute | solution.py:341
  67.1 27.0 %collective-permute-start.12 = (bf16[1024,512]{1,0:T(8,128)(2,1)S(1)}, bf16[1024,512]{1,0:T(8,128)(2,1)S(1)}, u32[]{:S(2)}, u32[]{:S(2)}) collective-permute-start(bf16[1024,512]{1,0:T(8,128)(2,1)S(1)} %copy-done.3), channel_id=1, source_target_pairs={{0,16},{4,20},{8,24},{12,28},{16,0},{20,4},{24,8},{28,12},{1,17},{... | collective-permute-start | bytes 3145736 | tf_op jit(solution)/shard_map/ppermute | solution.py:341
  94.1 14.7 %copy-start.4 = (bf16[1024,512]{1,0:T(8,128)(2,1)}, bf16[1024,512]{1,0:T(8,128)(2,1)S(1)}, u32[]{:S(2)}) copy-start(bf16[1024,512]{1,0:T(8,128)(2,1)S(1)} %collective-permute-done.10.refs_1_) | copy-start | bytes 3145732
  94.1 37.9 %copy-start.1 = (bf16[1024,512]{1,0:T(8,128)(2,1)}, bf16[1024,512]{1,0:T(8,128)(2,1)S(1)}, u32[]{:S(2)}) copy-start(bf16[1024,512]{1,0:T(8,128)(2,1)S(1)} %collective-permute-done.11.refs_2_) | copy-start | bytes 3145732
  108.7 16.3 %copy-start = (bf16[4,256,1024]{2,1,0:T(8,128)(2,1)S(1)}, bf16[4,256,1024]{2,1,0:T(8,128)(2,1)}, u32[]{:S(2)}) copy-start(bf16[4,256,1024]{2,1,0:T(8,128)(2,1)} %project.5.refs_0_) | copy-start | bytes 6291460
  111.2 13.9 %collective-permute-start.13 = (bf16[256,1024]{1,0:T(8,128)(2,1)}, bf16[256,1024]{1,0:T(8,128)(2,1)}, u32[]{:S(2)}, u32[]{:S(2)}) collective-permute-start(bf16[256,1024]{1,0:T(8,128)(2,1)} %mid_sum.1.refs_10_.refs_0_), channel_id=1, source_target_pairs={{0,1},{1,0},{2,3},{3,2},{4,5},{5,4},{6,7},{7,6},{8,9},{9,8},{10,11... | collective-permute-start | bytes 1572872 | tf_op jit(solution)/shard_map/ppermute | solution.py:921
  111.2 13.8 %collective-permute-start.14 = (bf16[256,1024]{1,0:T(8,128)(2,1)}, bf16[256,1024]{1,0:T(8,128)(2,1)}, u32[]{:S(2)}, u32[]{:S(2)}) collective-permute-start(bf16[256,1024]{1,0:T(8,128)(2,1)} %mid_sum.1.refs_10_.refs_0_), channel_id=1, source_target_pairs={{1,2},{2,1},{5,6},{6,5},{9,10},{10,9},{13,14},{14,13},{17,18},{18,... | collective-permute-start | bytes 1572872 | tf_op jit(solution)/shard_map/ppermute | solution.py:924
  112.7 19.3 %collective-permute-start.15 = (bf16[1024,256]{1,0:T(8,128)(2,1)}, bf16[1024,256]{1,0:T(8,128)(2,1)}, u32[]{:S(2)}, u32[]{:S(2)}) collective-permute-start(bf16[1024,256]{1,0:T(8,128)(2,1)} %slice.80.refs_1_), channel_id=1, source_target_pairs={{0,8},{4,12},{8,0},{12,4},{16,24},{20,28},{24,16},{28,20},{1,9},{5... | collective-permute-start | bytes 1572872 | tf_op jit(solution)/shard_map/ppermute | solution.py:341
  114.2 18.4 %collective-permute-start.16 = (bf16[1024,256]{1,0:T(8,128)(2,1)}, bf16[1024,256]{1,0:T(8,128)(2,1)}, u32[]{:S(2)}, u32[]{:S(2)}) collective-permute-start(bf16[1024,256]{1,0:T(8,128)(2,1)} %slice.81.refs_2_), channel_id=1, source_target_pairs={{0,16},{4,20},{8,24},{12,28},{16,0},{20,4},{24,8},{28,12},{1,17},{... | collective-permute-start | bytes 1572872 | tf_op jit(solution)/shard_map/ppermute | solution.py:341
  125.9 15.5 %collective-permute-start.22 = (bf16[256,1024]{1,0:T(8,128)(2,1)}, bf16[256,1024]{1,0:T(8,128)(2,1)}, u32[]{:S(2)}, u32[]{:S(2)}) collective-permute-start(bf16[256,1024]{1,0:T(8,128)(2,1)} %bitcast_select_fusion.1), channel_id=1, source_target_pairs={{0,1},{1,0},{2,3},{3,2},{4,5},{5,4},{6,7},{7,6},{8,9},{9,8},{10,11... | collective-permute-start | bytes 1572872 | tf_op jit(solution)/shard_map/ppermute | solution.py:921
  130.6 10.9 %collective-permute-start.21 = (bf16[256,1024]{1,0:T(8,128)(2,1)}, bf16[256,1024]{1,0:T(8,128)(2,1)}, u32[]{:S(2)}, u32[]{:S(2)}) collective-permute-start(bf16[256,1024]{1,0:T(8,128)(2,1)} %collective-permute-done.13.refs_11_.refs_1_), channel_id=1, source_target_pairs={{1,2},{2,1},{5,6},{6,5},{9,10},{10,9},{13,14},{14,13},{17,18},{18,... | collective-permute-start | bytes 1572872 | tf_op jit(solution)/shard_map/ppermute | solution.py:924
  132.0 18.4 %collective-permute-start.17 = (bf16[1024,512]{1,0:T(8,128)(2,1)}, bf16[1024,512]{1,0:T(8,128)(2,1)}, u32[]{:S(2)}, u32[]{:S(2)}) collective-permute-start(bf16[1024,512]{1,0:T(8,128)(2,1)} %copy-done.2), channel_id=1, source_target_pairs={{0,4},{4,0},{8,12},{12,8},{16,20},{20,16},{24,28},{28,24},{1,5},{5... | collective-permute-start | bytes 3145736 | tf_op jit(solution)/shard_map/ppermute | solution.py:341
  132.0 18.4 %collective-permute-start.18 = (bf16[1024,512]{1,0:T(8,128)(2,1)S(1)}, bf16[1024,512]{1,0:T(8,128)(2,1)}, u32[]{:S(2)}, u32[]{:S(2)}) collective-permute-start(bf16[1024,512]{1,0:T(8,128)(2,1)S(1)} %collective-permute-done.11.refs_2_), channel_id=1, source_target_pairs={{0,4},{4,0},{8,12},{12,8},{16,20},{20,16},{24,28},{28,24},{1,5},{5... | collective-permute-start | bytes 3145736 | tf_op jit(solution)/shard_map/ppermute | solution.py:341
  132.5 16.4 %collective-permute-start.19 = (bf16[1024,256]{1,0:T(8,128)(2,1)}, bf16[1024,256]{1,0:T(8,128)(2,1)}, u32[]{:S(2)}, u32[]{:S(2)}) collective-permute-start(bf16[1024,256]{1,0:T(8,128)(2,1)} %collective-permute-done.15.refs_4_), channel_id=1, source_target_pairs={{0,4},{4,0},{8,12},{12,8},{16,20},{20,16},{24,28},{28,24},{1,5},{5... | collective-permute-start | bytes 1572872 | tf_op jit(solution)/shard_map/ppermute | solution.py:341
  141.4 9.0 %collective-permute-start.20 = (bf16[1024,256]{1,0:T(8,128)(2,1)}, bf16[1024,256]{1,0:T(8,128)(2,1)}, u32[]{:S(2)}, u32[]{:S(2)}) collective-permute-start(bf16[1024,256]{1,0:T(8,128)(2,1)} %collective-permute-done.16.refs_5_), channel_id=1, source_target_pairs={{0,4},{4,0},{8,12},{12,8},{16,20},{20,16},{24,28},{28,24},{1,5},{5... | collective-permute-start | bytes 1572872 | tf_op jit(solution)/shard_map/ppermute | solution.py:341
  142.3 19.8 %collective-permute-start.24 = (bf16[256,1024]{1,0:T(8,128)(2,1)}, bf16[256,1024]{1,0:T(8,128)(2,1)}, u32[]{:S(2)}, u32[]{:S(2)}) collective-permute-start(bf16[256,1024]{1,0:T(8,128)(2,1)} %bitcast_select_fusion), channel_id=1, source_target_pairs={{0,1},{1,0},{2,3},{3,2},{4,5},{5,4},{6,7},{7,6},{8,9},{9,8},{10,11... | collective-permute-start | bytes 1572872 | tf_op jit(solution)/shard_map/ppermute | solution.py:921
  149.0 13.2 %collective-permute-start.23 = (bf16[256,1024]{1,0:T(8,128)(2,1)}, bf16[256,1024]{1,0:T(8,128)(2,1)}, u32[]{:S(2)}, u32[]{:S(2)}) collective-permute-start(bf16[256,1024]{1,0:T(8,128)(2,1)} %add_convert_fusion.2), channel_id=1, source_target_pairs={{1,2},{2,1},{5,6},{6,5},{9,10},{10,9},{13,14},{14,13},{17,18},{18,... | collective-permute-start | bytes 1572872 | tf_op jit(solution)/shard_map/ppermute | solution.py:924
  164.6 14.8 %collective-permute-start.25 = (bf16[256,1024]{1,0:T(8,128)(2,1)}, bf16[256,1024]{1,0:T(8,128)(2,1)S(1)}, u32[]{:S(2)}, u32[]{:S(2)}) collective-permute-start(bf16[256,1024]{1,0:T(8,128)(2,1)} %get-tuple-element.174), channel_id=1, source_target_pairs={{0,1},{1,0},{2,3},{3,2},{4,5},{5,4},{6,7},{7,6},{8,9},{9,8},{10,11... | collective-permute-start | bytes 1572872 | tf_op jit(solution)/shard_map/ppermute | solution.py:921
  166.4 13.0 %collective-permute-start.26 = (bf16[256,1024]{1,0:T(8,128)(2,1)S(1)}, bf16[256,1024]{1,0:T(8,128)(2,1)}, u32[]{:S(2)}, u32[]{:S(2)}) collective-permute-start(bf16[256,1024]{1,0:T(8,128)(2,1)S(1)} %get-tuple-element.173), channel_id=1, source_target_pairs={{1,2},{2,1},{5,6},{6,5},{9,10},{10,9},{13,14},{14,13},{17,18},{18,... | collective-permute-start | bytes 1572872 | tf_op jit(solution)/shard_map/ppermute | solution.py:924
  169.1 10.2 %copy-start.13 = (bf16[2,256,1024]{2,1,0:T(8,128)(2,1)S(1)}, bf16[2,256,1024]{2,1,0:T(8,128)(2,1)}, u32[]{:S(2)}) copy-start(bf16[2,256,1024]{2,1,0:T(8,128)(2,1)} %residual_ref.1) | copy-start | bytes 3145732
  179.3 28.5 %copy-start.27 = (f32[16,1024]{1,0:T(8,128)S(1)}, f32[16,1024]{1,0:T(8,128)}, u32[]{:S(2)}) copy-start(f32[16,1024]{1,0:T(8,128)} %param.25) | copy-start | bytes 196612
  180.8 37.9 %copy-start.6 = (bf16[256,1024]{1,0:T(8,128)(2,1)}, bf16[256,1024]{1,0:T(8,128)(2,1)S(1)}, u32[]{:S(2)}) copy-start(bf16[256,1024]{1,0:T(8,128)(2,1)S(1)} %fusion.7.refs_0_) | copy-start | bytes 1572868
  180.8 17.4 %collective-permute-start.27 = (bf16[256,1024]{1,0:T(8,128)(2,1)S(1)}, bf16[256,1024]{1,0:T(8,128)(2,1)S(1)}, u32[]{:S(2)}, u32[]{:S(2)}) collective-permute-start(bf16[256,1024]{1,0:T(8,128)(2,1)S(1)} %fusion.7.refs_0_), channel_id=1, source_target_pairs={{0,1},{1,0},{2,3},{3,2},{4,5},{5,4},{6,7},{7,6},{8,9},{9,8},{10,11... | collective-permute-start | bytes 1572872 | tf_op jit(solution)/shard_map/ppermute | solution.py:412
  182.9 15.4 %collective-permute-start.28 = (bf16[256,1024]{1,0:T(8,128)(2,1)S(1)}, bf16[256,1024]{1,0:T(8,128)(2,1)S(1)}, u32[]{:S(2)}, u32[]{:S(2)}) collective-permute-start(bf16[256,1024]{1,0:T(8,128)(2,1)S(1)} %fusion.7.refs_0_), channel_id=1, source_target_pairs={{1,2},{2,1},{5,6},{6,5},{9,10},{10,9},{13,14},{14,13},{17,18},{18,... | collective-permute-start | bytes 1572872 | tf_op jit(solution)/shard_map/ppermute | solution.py:412
  183.6 22.2 %collective-permute-start.29 = (bf16[256,1024]{1,0:T(8,128)(2,1)S(1)}, bf16[256,1024]{1,0:T(8,128)(2,1)S(1)}, u32[]{:S(2)}, u32[]{:S(2)}) collective-permute-start(bf16[256,1024]{1,0:T(8,128)(2,1)S(1)} %fusion.7.refs_0_), channel_id=1, source_target_pairs={{0,3},{3,0},{4,7},{7,4},{8,11},{11,8},{12,15},{15,12},{16,19},{19,... | collective-permute-start | bytes 1572872 | tf_op jit(solution)/shard_map/ppermute | solution.py:959
  198.2 20.5 %copy-start.14 = (bf16[256,1024]{1,0:T(8,128)(2,1)}, bf16[256,1024]{1,0:T(8,128)(2,1)S(1)}, u32[]{:S(2)}) copy-start(bf16[256,1024]{1,0:T(8,128)(2,1)S(1)} %collective-permute-done.27.refs_1_) | copy-start | bytes 1572868
  198.2 20.5 %copy-start.15 = (bf16[256,1024]{1,0:T(8,128)(2,1)}, bf16[256,1024]{1,0:T(8,128)(2,1)S(1)}, u32[]{:S(2)}) copy-start(bf16[256,1024]{1,0:T(8,128)(2,1)S(1)} %collective-permute-done.28.refs_2_) | copy-start | bytes 1572868
  205.8 12.9 %copy-start.22 = (bf16[256,1024]{1,0:T(8,128)(2,1)}, bf16[256,1024]{1,0:T(8,128)(2,1)S(1)}, u32[]{:S(2)}) copy-start(bf16[256,1024]{1,0:T(8,128)(2,1)S(1)} %collective-permute-done.29.refs_5_) | copy-start | bytes 1572868
  205.8 12.9 %collective-permute-start.30 = (bf16[256,1024]{1,0:T(8,128)(2,1)S(1)}, bf16[256,1024]{1,0:T(8,128)(2,1)S(1)}, u32[]{:S(2)}, u32[]{:S(2)}) collective-permute-start(bf16[256,1024]{1,0:T(8,128)(2,1)S(1)} %collective-permute-done.27.refs_1_), channel_id=1, source_target_pairs={{1,2},{2,1},{5,6},{6,5},{9,10},{10,9},{13,14},{14,13},{17,18},{18,... | collective-permute-start | bytes 1572872 | tf_op jit(solution)/shard_map/ppermute | solution.py:412
  206.5 14.7 %collective-permute-start.31 = (bf16[256,1024]{1,0:T(8,128)(2,1)S(1)}, bf16[256,1024]{1,0:T(8,128)(2,1)S(1)}, u32[]{:S(2)}, u32[]{:S(2)}) collective-permute-start(bf16[256,1024]{1,0:T(8,128)(2,1)S(1)} %collective-permute-done.28.refs_2_), channel_id=1, source_target_pairs={{1,0},{2,3},{5,4},{6,7},{9,8},{10,11},{13,12},{14,15},{17,16},{18,... | collective-permute-start | bytes 1572872 | tf_op jit(solution)/shard_map/ppermute | solution.py:412
  221.2 92.4 %reduce-scatter.8.cloned.1.call-start = ((), (), s32[]{:S(2)}) async-start(), calls=%async_computation.5 | async-start | bytes 2621440 | tf_op jit(solution)/shard_map/reduce_scatter | solution.py:869
  256.0 10.8 %copy-start.5 = (bf16[256,1024]{1,0:T(8,128)(2,1)S(1)}, bf16[256,1024]{1,0:T(8,128)(2,1)}, u32[]{:S(2)}) copy-start(bf16[256,1024]{1,0:T(8,128)(2,1)} %mid_sum.1.refs_10_.refs_0_) | copy-start | bytes 1572868
  256.0 12.0 %copy-start.7 = (bf16[256,1024]{1,0:T(8,128)(2,1)S(1)}, bf16[256,1024]{1,0:T(8,128)(2,1)}, u32[]{:S(2)}) copy-start(bf16[256,1024]{1,0:T(8,128)(2,1)} %copy-done.6) | copy-start | bytes 1572868
  (16 other events, 55.0 us)
Sparse Core Ops, SparseCore 0:
  64.4 44.3 reduce-scatter.3
  221.3 45.3 reduce-scatter.5
  269.2 44.3 reduce-scatter.7

commit v6 on v5

--- a/solution.py
+++ b/solution.py
@@ -446,7 +446,7 @@
         p, first = divmod(k * columns, width)
         source = w_ref.at[p, pl.ds(pl.multiple_of(begin, width), rows), pl.ds(first, columns)]
         copies.append((pltpu.make_async_copy(source, held.at[k], sems.at[k]),))
-    copies = Fetch(copies, 2)
+    copies = Fetch(copies, 3)
     copies.begin()
     for place in range(count):
         shares = [share + (place >= count // 2) for share in range(count - 1)]

time: 324 us -> 323 us (level)
  no operation moved by 1% of the time
where the time goes in v6:
time: 323 us; the launch traced here: 322 us
  Pallas kernels  121 us (37%)
  waiting for transfers between devices  93.7 us (29%)
  starting transfers between devices  42.8 us (13%)
  blocking collectives  22.7 us (7%)
  other arithmetic  15.7 us (5%)
  between operations  13.7 us (4%)
  local copies, waits for them, and re-layouts  12 us (4%)
    reduce_scatter x3, waiting for transfers between devices, scattered(): return lax.psum_scatter(parts, 'tp', scatter_dimension=0)  56.6 us
    pallas_call x2, Pallas kernels, mr_local(): pl.pallas_call(mr_local_kernel, grid=(1,), out_shape=(jax.ShapeDtypeStruc...  26.3 us
    pallas_call x2, Pallas kernels, lr_in_start(): pl.pallas_call(functools.partial(lr_in_start_kernel, table, len(gates)),...  23.4 us
    all_gather x2, blocking collectives, local(): sent = lax.all_gather(send, 'ctx', axis=0)  22.7 us
    pallas_call x2, Pallas kernels, lr_modal(): pl.pallas_call(functools.partial(lr_modal_kernel, places), out_shape=jax....  20.6 us
    pallas_call x2, Pallas kernels, lr_mix(): pl.pallas_call(functools.partial(lr_mix_kernel, table), out_shape=(rows,...  20.3 us
    ppermute x4, waiting for transfers between devices, outer(): return lax.ppermute(value, 'tp', [(0, 1), (1, 0), (2, 3), (3, 2)])  18.2 us
    pallas_call x3, Pallas kernels, project(): pl.pallas_call(functools.partial(project_kernel, places), out_shape=jax.S...  16.1 us
  transfers between devices with their start and end apart: 35, of which 10 were waited for; matrix products, arithmetic and copies ran while one was open for 4% of the time, Pallas kernels for 36%

profile of v6, /device:TPU:0, one launch (start us, length us, event | category | flops | bytes accessed | tf_op | source)
XLA Modules:
  0.0 321.8 jit_solution(14806262069656730953)
XLA Ops:
  7.0 2.5 collective-permute-start.1
  9.5 1.5 collective-permute-start.2
  11.8 1.9 copy_convert_fusion
  16.4 2.7 collective-permute-start.3
  20.6 13.1 %mr_local.2 = (bf16[1,256,1024]{2,1,0:T(8,128)(2,1)}, f32[1,144,8,128]{3,2,1,0:T(8,128)}, f32[1,144,8,128]{3,2,1,0:T(8,128)}) custom-call(bf16[2,3,256,1024]{3,2,1,0:T(8,128)(2,1)} %bitcast.53, f32[3,3,8,128]{3,2,1,0:T(8,128)} %reshape.77.short_ref, f32[128,8,128]{2,1,0:T(8,128)} %bitcast.59, f32[8,128]{1,0:T(8,128)} %bitcast.81, ...), custom_call_target="tpu_custom_call" | custom-call | flops 1000000000 | bytes 1000000 | tf_op jit(solution)/shard_map/mr_local/pallas_call | solution.py:127
  33.8 6.6 %collective-permute-done.2.refs_3_.refs_4_ = bf16[1024,512]{1,0:T(8,128)(2,1)S(1)} collective-permute-done((bf16[1024,512]{1,0:T(8,128)(2,1)}, bf16[1024,512]{1,0:T(8,128)(2,1)S(1)}, u32[]{:S(2)}, u32[]{:S(2)}) %collective-permute-start.2) | collective-permute-done | bytes 1048608 | tf_op jit(solution)/shard_map/ppermute | solution.py:341
  41.1 1.4 collective-permute-start.6
  42.5 1.5 collective-permute-start.7
  44.0 6.1 %mr_finish.2.head_ref = bf16[144,1024]{1,0:T(8,128)(2,1)} custom-call(bf16[2,3,256,1024]{3,2,1,0:T(8,128)(2,1)} %bitcast.55, bf16[2,144,1024]{2,1,0:T(8,128)(2,1)} %collective-permute-done.3.halo_ref, f32[1,144,8,128]{3,2,1,0:T(8,128)} %get-tuple-element.96.q_ref, f32[1,144,8,128]{3,2,1,0:T(8,128)} %get-tuple-element.97.conv_ref.gate_ref, ...), custom_call_target="tpu_custom_call" | custom-call | flops 40000000000 | bytes 1000000 | tf_op jit(solution)/shard_map/mr_finish/pallas_call | solution.py:212
  51.5 5.3 %project.3.refs_4_ = bf16[4,256,1024]{2,1,0:T(8,128)(2,1)} custom-call(s32[1]{0:T(128)} %bitcast.scalar_ref, bf16[144,1024]{1,0:T(8,128)(2,1)} %mr_finish.2.head_ref, bf16[1,256,1024]{2,1,0:T(8,128)(2,1)} %get-tuple-element.98.body_ref, bf16[1024,512]{1,0:T(8,128)(2,1)} %refs_0_.1, bf16[1024,512]{1,0:T(8,128)(2,1)} %copy-done.10, ...), custom_call_target="tpu_custom_call" | custom-call | flops 1610612736 | bytes 7864320 | tf_op jit(solution)/shard_map/project/pallas_call | solution.py:300
  57.4 1.4 collective-permute-done.8.refs_2_.refs_8_
  60.4 3.8 %project.4.gate_ref = bf16[4,256,1024]{2,1,0:T(8,128)(2,1)} custom-call(s32[1]{0:T(128)} %bitcast.scalar_ref, bf16[144,1024]{1,0:T(8,128)(2,1)} %mr_finish.2.head_ref, bf16[1,256,1024]{2,1,0:T(8,128)(2,1)} %get-tuple-element.98.body_ref, bf16[1024,256]{1,0:T(8,128)(2,1)} %copy-done.18, bf16[1024,256]{1,0:T(8,128)(2,1)} %copy-done.19, ...), custom_call_target="tpu_custom_call", output_to_operand_aliasing={{}: (7, {})} | custom-call | flops 536870912 | bytes 2621440 | tf_op jit(solution)/shard_map/project/pallas_call | solution.py:300
  65.6 1.5 collective-permute-start.11
  67.8 13.2 %mr_local.3 = (bf16[1,256,1024]{2,1,0:T(8,128)(2,1)}, f32[1,144,8,128]{3,2,1,0:T(8,128)}, f32[1,144,8,128]{3,2,1,0:T(8,128)}) custom-call(bf16[2,3,256,1024]{3,2,1,0:T(8,128)(2,1)} %bitcast.56, f32[3,3,8,128]{3,2,1,0:T(8,128)} %reshape.77.short_ref, f32[128,8,128]{2,1,0:T(8,128)} %bitcast.61, f32[8,128]{1,0:T(8,128)} %bitcast.83, ...), custom_call_target="tpu_custom_call" | custom-call | flops 1000000000 | bytes 1000000 | tf_op jit(solution)/shard_map/mr_local/pallas_call | solution.py:127
  81.0 6.1 %mr_finish.3.head_ref = bf16[144,1024]{1,0:T(8,128)(2,1)} custom-call(bf16[2,3,256,1024]{3,2,1,0:T(8,128)(2,1)} %bitcast.57, bf16[2,144,1024]{2,1,0:T(8,128)(2,1)} %collective-permute-done.3.halo_ref, f32[1,144,8,128]{3,2,1,0:T(8,128)} %get-tuple-element.107.q_ref, f32[1,144,8,128]{3,2,1,0:T(8,128)} %get-tuple-element.108.conv_ref, ...), custom_call_target="tpu_custom_call" | custom-call | flops 40000000000 | bytes 1000000 | tf_op jit(solution)/shard_map/mr_finish/pallas_call | solution.py:212
  87.0 7.0 %project.5.refs_0_ = bf16[4,256,1024]{2,1,0:T(8,128)(2,1)} custom-call(s32[1]{0:T(128)} %bitcast.scalar_ref, bf16[144,1024]{1,0:T(8,128)(2,1)} %mr_finish.3.head_ref, bf16[1,256,1024]{2,1,0:T(8,128)(2,1)} %get-tuple-element.109.body_ref, bf16[1024,512]{1,0:T(8,128)(2,1)} %refs_0_.1, bf16[1024,512]{1,0:T(8,128)(2,1)} %copy-done.10, ...), custom_call_target="tpu_custom_call" | custom-call | flops 2147483648 | bytes 10485760 | tf_op jit(solution)/shard_map/project/pallas_call | solution.py:300
  96.8 11.9 %reduce-scatter.4.cloned.1.call-done = bf16[1,256,1024]{2,1,0:T(8,128)(2,1)} async-done(((bf16[4,256,1024]{2,1,0:T(8,128)(2,1)}), bf16[1,256,1024]{2,1,0:T(8,128)(2,1)}) %reduce-scatter.4.cloned.1.call-update) | async-done | bytes 524304 | tf_op jit(solution)/shard_map/reduce_scatter | solution.py:869
  108.8 2.4 mid_sum.1.refs_10_.refs_0_
  111.2 1.5 collective-permute-start.14
  112.7 1.5 collective-permute-start.15
  114.2 1.5 collective-permute-start.16
  115.7 9.4 %collective-permute-done.13.refs_11_.refs_1_ = bf16[256,1024]{1,0:T(8,128)(2,1)} collective-permute-done((bf16[256,1024]{1,0:T(8,128)(2,1)}, bf16[256,1024]{1,0:T(8,128)(2,1)}, u32[]{:S(2)}, u32[]{:S(2)}) %collective-permute-start.13) | collective-permute-done | bytes 524320 | tf_op jit(solution)/shard_map/ppermute | solution.py:921
  125.9 4.7 %collective-permute-start.22 = (bf16[256,1024]{1,0:T(8,128)(2,1)}, bf16[256,1024]{1,0:T(8,128)(2,1)}, u32[]{:S(2)}, u32[]{:S(2)}) collective-permute-start(bf16[256,1024]{1,0:T(8,128)(2,1)} %bitcast_select_fusion.1), channel_id=1, source_target_pairs={{0,1},{1,0},{2,3},{3,2},{4,5},{5,4},{6,7},{7,6},{8,9},{9,8},{10,11... | collective-permute-start | bytes 1572872 | tf_op jit(solution)/shard_map/ppermute | solution.py:921
  130.6 1.5 collective-permute-start.21
  132.6 8.8 %collective-permute-done.22.refs_14_.refs_4_ = bf16[256,1024]{1,0:T(8,128)(2,1)} collective-permute-done((bf16[256,1024]{1,0:T(8,128)(2,1)}, bf16[256,1024]{1,0:T(8,128)(2,1)}, u32[]{:S(2)}, u32[]{:S(2)}) %collective-permute-start.22) | collective-permute-done | bytes 524320 | tf_op jit(solution)/shard_map/ppermute | solution.py:921
  142.3 4.7 %collective-permute-start.24 = (bf16[256,1024]{1,0:T(8,128)(2,1)}, bf16[256,1024]{1,0:T(8,128)(2,1)}, u32[]{:S(2)}, u32[]{:S(2)}) collective-permute-start(bf16[256,1024]{1,0:T(8,128)(2,1)} %bitcast_select_fusion), channel_id=1, source_target_pairs={{0,1},{1,0},{2,3},{3,2},{4,5},{5,4},{6,7},{7,6},{8,9},{9,8},{10,11... | collective-permute-start | bytes 1572872 | tf_op jit(solution)/shard_map/ppermute | solution.py:921
  147.0 2.0 add_convert_fusion.2
  149.0 1.5 collective-permute-start.23
  150.4 11.5 %lr_in_start.2 = (f32[6,256,512]{2,1,0:T(8,128)}, f32[256,128]{1,0:T(8,128)}) custom-call(s32[1]{0:T(128)} %bitcast.12.scalar_ref, f32[1,4096]{1,0:T(1,128)} %bitcast.72, bf16[1024,512]{1,0:T(8,128)(2,1)} %refs_0_.4, bf16[1024,512]{1,0:T(8,128)(2,1)} %copy-done.4, bf16[1024,512]{1,0:T(8,128)(2,1)} %copy-done.1, bf16[1024,512]{1,0:T(8,128)(2,1)} %copy-done.2, ...), custom_call_target="tpu_custom_call" | custom-call | flops 4831838208 | bytes 18874368 | tf_op jit(solution)/shard_map/lr_in_start/pallas_call | solution.py:486
  162.0 2.4 add_convert_fusion.1
  164.4 1.8 collective-permute-start.25
  166.3 1.5 collective-permute-start.26
  169.0 10.2 %lr_mix.2 = (f32[256,8,128]{2,1,0:T(8,128)}, f32[256,8,128]{2,1,0:T(8,128)}, bf16[32,8,128]{2,1,0:T(8,128)(2,1)}) custom-call(s32[1]{0:T(128)} %bitcast.12.scalar_ref, f32[1,4096]{1,0:T(1,128)} %bitcast.73, f32[256,128]{1,0:T(8,128)} %get-tuple-element.132.square_ref, f32[3,3,8,128]{3,2,1,0:T(8,128)} %reshape.81.short_ref, f32[16,8,128]{2,1,0:T(8,128)} %bitcast.65, ...), custom_call_target="tpu_custom_call" | custom-call | flops 1610612736 | bytes 6291456 | tf_op jit(solution)/shard_map/lr_mix/pallas_call | solution.py:622
  179.2 1.4 fusion.7.refs_0_
  180.7 2.1 collective-permute-start.27
  183.4 3.8 %collective-permute-start.29 = (bf16[256,1024]{1,0:T(8,128)(2,1)S(1)}, bf16[256,1024]{1,0:T(8,128)(2,1)S(1)}, u32[]{:S(2)}, u32[]{:S(2)}) collective-permute-start(bf16[256,1024]{1,0:T(8,128)(2,1)S(1)} %fusion.7.refs_0_), channel_id=1, source_target_pairs={{0,3},{3,0},{4,7},{7,4},{8,11},{11,8},{12,15},{15,12},{16,19},{19,... | collective-permute-start | bytes 1572872 | tf_op jit(solution)/shard_map/ppermute | solution.py:959
  187.2 10.9 %all-gather = bf16[256,8,128]{2,1,0:T(8,128)(2,1)} all-gather(bf16[32,8,128]{2,1,0:T(8,128)(2,1)S(1)} %copy-done.25), channel_id=2, replica_groups=mesh['ctx'=8,'tp'=4] {'ctx'}, dimensions={0}, use_global_device_ids=true | all-gather | bytes 589824 | tf_op jit(solution)/shard_map/all_gather | solution.py:960
  198.1 7.6 %collective-permute-done.29.refs_5_ = bf16[256,1024]{1,0:T(8,128)(2,1)S(1)} collective-permute-done((bf16[256,1024]{1,0:T(8,128)(2,1)S(1)}, bf16[256,1024]{1,0:T(8,128)(2,1)S(1)}, u32[]{:S(2)}, u32[]{:S(2)}) %collective-permute-start.29) | collective-permute-done | bytes 524320 | tf_op jit(solution)/shard_map/ppermute | solution.py:959
  206.4 1.3 collective-permute-start.31
  208.3 10.2 %lr_modal.2 = bf16[4,256,1024]{2,1,0:T(8,128)(2,1)} custom-call(s32[1]{0:T(128)} %bitcast.scalar_ref, bf16[8,32,8,128]{3,2,1,0:T(8,128)(2,1)} %bitcast.63, f32[3,3,8,128]{3,2,1,0:T(8,128)} %reshape.81.short_ref, f32[16,8,128]{2,1,0:T(8,128)} %bitcast.66, f32[16,8,128]{2,1,0:T(8,128)} %bitcast.69, f32[8,128]{1,0:T(8,128)} %bitcast.79, ...), custom_call_target="tpu_custom_call" | custom-call | flops 2147483648 | bytes 10485760 | tf_op jit(solution)/shard_map/lr_modal/pallas_call | solution.py:771
  218.6 2.5 collective-permute-done.31.refs_4_
  221.9 11.9 %lr_in_start.3 = (f32[6,256,512]{2,1,0:T(8,128)}, f32[256,128]{1,0:T(8,128)}) custom-call(s32[1]{0:T(128)} %bitcast.12.scalar_ref, f32[1,4096]{1,0:T(1,128)} %bitcast.74, bf16[256,1024]{1,0:T(8,128)(2,1)} %copy-done.6, bf16[256,1024]{1,0:T(8,128)(2,1)} %copy-done.14, bf16[256,1024]{1,0:T(8,128)(2,1)} %copy-done.15, bf16[256,1024]{1,0:T(8,128)(2,1)} %copy-done.16, ...), custom_call_target="tpu_custom_call" | custom-call | flops 4831838208 | bytes 18874368 | tf_op jit(solution)/shard_map/lr_in_start/pallas_call | solution.py:486
  233.7 10.2 %lr_mix.3 = (f32[256,8,128]{2,1,0:T(8,128)}, f32[256,8,128]{2,1,0:T(8,128)}, bf16[32,8,128]{2,1,0:T(8,128)(2,1)}) custom-call(s32[1]{0:T(128)} %bitcast.12.scalar_ref, f32[1,4096]{1,0:T(1,128)} %bitcast.75, f32[256,128]{1,0:T(8,128)} %get-tuple-element.165.square_ref, f32[3,3,8,128]{3,2,1,0:T(8,128)} %reshape.81.short_ref, f32[16,8,128]{2,1,0:T(8,128)} %bitcast.67, ...), custom_call_target="tpu_custom_call" | custom-call | flops 1610612736 | bytes 6291456 | tf_op jit(solution)/shard_map/lr_mix/pallas_call | solution.py:622
  243.9 11.8 %all-gather.1 = bf16[256,8,128]{2,1,0:T(8,128)(2,1)} all-gather(bf16[32,8,128]{2,1,0:T(8,128)(2,1)} %get-tuple-element.168), channel_id=3, replica_groups=mesh['ctx'=8,'tp'=4] {'ctx'}, dimensions={0}, use_global_device_ids=true | all-gather | bytes 589824 | tf_op jit(solution)/shard_map/all_gather | solution.py:976
  255.7 10.3 %lr_modal.3 = bf16[4,256,1024]{2,1,0:T(8,128)(2,1)} custom-call(s32[1]{0:T(128)} %bitcast.scalar_ref, bf16[8,32,8,128]{3,2,1,0:T(8,128)(2,1)} %bitcast.64, f32[3,3,8,128]{3,2,1,0:T(8,128)} %reshape.81.short_ref, f32[16,8,128]{2,1,0:T(8,128)} %bitcast.68, f32[16,8,128]{2,1,0:T(8,128)} %bitcast.70, f32[8,128]{1,0:T(8,128)} %bitcast.80, ...), custom_call_target="tpu_custom_call" | custom-call | flops 2147483648 | bytes 10485760 | tf_op jit(solution)/shard_map/lr_modal/pallas_call | solution.py:771
  266.6 1.2 fusion.10
  269.0 44.1 %reduce-scatter.8.cloned.1.call-done = bf16[1,256,1024]{2,1,0:T(8,128)(2,1)} async-done(((bf16[4,256,1024]{2,1,0:T(8,128)(2,1)}), bf16[1,256,1024]{2,1,0:T(8,128)(2,1)}) %reduce-scatter.8.cloned.1.call-update) | async-done | bytes 524304 | tf_op jit(solution)/shard_map/reduce_scatter | solution.py:869
  313.1 2.2 fusion.9
  (125 shorter events, 22.5 us)
Async XLA Ops:
  6.5 102.2 %reduce-scatter.4.cloned.1.call-start = ((), (), s32[]{:S(2)}) async-start(), calls=%async_computation.3 | async-start | bytes 2621440 | tf_op jit(solution)/shard_map/reduce_scatter | solution.py:869
  6.5 27.2 %collective-permute-start = (bf16[1024,512]{1,0:T(8,128)(2,1)}, bf16[1024,512]{1,0:T(8,128)(2,1)S(1)}, u32[]{:S(2)}, u32[]{:S(2)}) collective-permute-start(bf16[1024,512]{1,0:T(8,128)(2,1)} %refs_0_.1), channel_id=1, source_target_pairs={{0,4},{4,0},{8,12},{12,8},{16,20},{20,16},{24,28},{28,24},{1,5},{5... | collective-permute-start | bytes 3145736 | tf_op jit(solution)/shard_map/ppermute | solution.py:341
  7.0 26.8 %collective-permute-start.1 = (bf16[1024,512]{1,0:T(8,128)(2,1)}, bf16[1024,512]{1,0:T(8,128)(2,1)S(1)}, u32[]{:S(2)}, u32[]{:S(2)}) collective-permute-start(bf16[1024,512]{1,0:T(8,128)(2,1)} %refs_0_.1), channel_id=1, source_target_pairs={{0,8},{4,12},{8,0},{12,4},{16,24},{20,28},{24,16},{28,20},{1,9},{5... | collective-permute-start | bytes 3145736 | tf_op jit(solution)/shard_map/ppermute | solution.py:341
  9.5 31.0 %collective-permute-start.2 = (bf16[1024,512]{1,0:T(8,128)(2,1)}, bf16[1024,512]{1,0:T(8,128)(2,1)S(1)}, u32[]{:S(2)}, u32[]{:S(2)}) collective-permute-start(bf16[1024,512]{1,0:T(8,128)(2,1)} %refs_0_.1), channel_id=1, source_target_pairs={{0,16},{4,20},{8,24},{12,28},{16,0},{20,4},{24,8},{28,12},{1,17},{... | collective-permute-start | bytes 3145736 | tf_op jit(solution)/shard_map/ppermute | solution.py:341
  16.4 17.4 %collective-permute-start.3 = (bf16[2,144,1024]{2,1,0:T(8,128)(2,1)}, bf16[2,144,1024]{2,1,0:T(8,128)(2,1)}, u32[]{:S(2)}, u32[]{:S(2)}) collective-permute-start(bf16[2,144,1024]{2,1,0:T(8,128)(2,1)} %fusion.8), channel_id=1, source_target_pairs={{0,4},{4,8},{8,12},{12,16},{16,20},{20,24},{24,28},{1,5},{5,9},{9,... | collective-permute-start | bytes 1769480 | tf_op jit(solution)/shard_map/ppermute | solution.py:859
  33.8 16.3 %copy-start.10 = (bf16[1024,512]{1,0:T(8,128)(2,1)}, bf16[1024,512]{1,0:T(8,128)(2,1)S(1)}, u32[]{:S(2)}) copy-start(bf16[1024,512]{1,0:T(8,128)(2,1)S(1)} %collective-permute-done.refs_1_) | copy-start | bytes 3145732
  33.8 16.3 %copy-start.8 = (bf16[1024,512]{1,0:T(8,128)(2,1)}, bf16[1024,512]{1,0:T(8,128)(2,1)S(1)}, u32[]{:S(2)}) copy-start(bf16[1024,512]{1,0:T(8,128)(2,1)S(1)} %collective-permute-done.1.refs_2_) | copy-start | bytes 3145732
  40.4 9.7 %collective-permute-start.5 = (bf16[1024,512]{1,0:T(8,128)(2,1)S(1)}, bf16[1024,512]{1,0:T(8,128)(2,1)S(1)}, u32[]{:S(2)}, u32[]{:S(2)}) collective-permute-start(bf16[1024,512]{1,0:T(8,128)(2,1)S(1)} %collective-permute-done.2.refs_3_.refs_4_), channel_id=1, source_target_pairs={{0,4},{4,0},{8,12},{12,8},{16,20},{20,16},{24,28},{28,24},{1,5},{5... | collective-permute-start | bytes 3145736 | tf_op jit(solution)/shard_map/ppermute | solution.py:341
  40.5 9.6 %collective-permute-start.4 = (bf16[1024,512]{1,0:T(8,128)(2,1)S(1)}, bf16[1024,512]{1,0:T(8,128)(2,1)S(1)}, u32[]{:S(2)}, u32[]{:S(2)}) collective-permute-start(bf16[1024,512]{1,0:T(8,128)(2,1)S(1)} %collective-permute-done.1.refs_2_), channel_id=1, source_target_pairs={{0,4},{4,0},{8,12},{12,8},{16,20},{20,16},{24,28},{28,24},{1,5},{5... | collective-permute-start | bytes 3145736 | tf_op jit(solution)/shard_map/ppermute | solution.py:341
  41.1 15.7 %collective-permute-start.6 = (bf16[1024,256]{1,0:T(8,128)(2,1)S(1)}, bf16[1024,256]{1,0:T(8,128)(2,1)S(1)}, u32[]{:S(2)}, u32[]{:S(2)}) collective-permute-start(bf16[1024,256]{1,0:T(8,128)(2,1)S(1)} %slice.78), channel_id=1, source_target_pairs={{0,8},{4,12},{8,0},{12,4},{16,24},{20,28},{24,16},{28,20},{1,9},{5... | collective-permute-start | bytes 1572872 | tf_op jit(solution)/shard_map/ppermute | solution.py:341
  42.5 14.3 %collective-permute-start.7 = (bf16[1024,256]{1,0:T(8,128)(2,1)S(1)}, bf16[1024,256]{1,0:T(8,128)(2,1)S(1)}, u32[]{:S(2)}, u32[]{:S(2)}) collective-permute-start(bf16[1024,256]{1,0:T(8,128)(2,1)S(1)} %slice.79), channel_id=1, source_target_pairs={{0,16},{4,20},{8,24},{12,28},{16,0},{20,4},{24,8},{28,12},{1,17},{... | collective-permute-start | bytes 1572872 | tf_op jit(solution)/shard_map/ppermute | solution.py:341
  56.8 2.0 collective-permute-start.8
  56.9 2.6 collective-permute-start.9
  64.2 202.4 %reduce-scatter.6.cloned.1.call-start = ((), (), s32[]{:S(2)}) async-start(), calls=%async_computation.4 | async-start | bytes 2621440 | tf_op jit(solution)/shard_map/reduce_scatter | solution.py:869
  65.4 28.7 %collective-permute-start.10 = (bf16[1024,512]{1,0:T(8,128)(2,1)S(1)}, bf16[1024,512]{1,0:T(8,128)(2,1)S(1)}, u32[]{:S(2)}, u32[]{:S(2)}) collective-permute-start(bf16[1024,512]{1,0:T(8,128)(2,1)S(1)} %copy-done.3), channel_id=1, source_target_pairs={{0,4},{4,0},{8,12},{12,8},{16,20},{20,16},{24,28},{28,24},{1,5},{5... | collective-permute-start | bytes 3145736 | tf_op jit(solution)/shard_map/ppermute | solution.py:341
  65.6 28.5 %collective-permute-start.11 = (bf16[1024,512]{1,0:T(8,128)(2,1)S(1)}, bf16[1024,512]{1,0:T(8,128)(2,1)S(1)}, u32[]{:S(2)}, u32[]{:S(2)}) collective-permute-start(bf16[1024,512]{1,0:T(8,128)(2,1)S(1)} %copy-done.3), channel_id=1, source_target_pairs={{0,8},{4,12},{8,0},{12,4},{16,24},{20,28},{24,16},{28,20},{1,9},{5... | collective-permute-start | bytes 3145736 | tf_op jit(solution)/shard_map/ppermute | solution.py:341
  67.1 27.0 %collective-permute-start.12 = (bf16[1024,512]{1,0:T(8,128)(2,1)S(1)}, bf16[1024,512]{1,0:T(8,128)(2,1)S(1)}, u32[]{:S(2)}, u32[]{:S(2)}) collective-permute-start(bf16[1024,512]{1,0:T(8,128)(2,1)S(1)} %copy-done.3), channel_id=1, source_target_pairs={{0,16},{4,20},{8,24},{12,28},{16,0},{20,4},{24,8},{28,12},{1,17},{... | collective-permute-start | bytes 3145736 | tf_op jit(solution)/shard_map/ppermute | solution.py:341
  94.1 14.7 %copy-start.4 = (bf16[1024,512]{1,0:T(8,128)(2,1)}, bf16[1024,512]{1,0:T(8,128)(2,1)S(1)}, u32[]{:S(2)}) copy-start(bf16[1024,512]{1,0:T(8,128)(2,1)S(1)} %collective-permute-done.10.refs_1_) | copy-start | bytes 3145732
  94.1 37.9 %copy-start.1 = (bf16[1024,512]{1,0:T(8,128)(2,1)}, bf16[1024,512]{1,0:T(8,128)(2,1)S(1)}, u32[]{:S(2)}) copy-start(bf16[1024,512]{1,0:T(8,128)(2,1)S(1)} %collective-permute-done.11.refs_2_) | copy-start | bytes 3145732
  108.7 16.3 %copy-start = (bf16[4,256,1024]{2,1,0:T(8,128)(2,1)S(1)}, bf16[4,256,1024]{2,1,0:T(8,128)(2,1)}, u32[]{:S(2)}) copy-start(bf16[4,256,1024]{2,1,0:T(8,128)(2,1)} %project.5.refs_0_) | copy-start | bytes 6291460
  111.2 13.9 %collective-permute-start.13 = (bf16[256,1024]{1,0:T(8,128)(2,1)}, bf16[256,1024]{1,0:T(8,128)(2,1)}, u32[]{:S(2)}, u32[]{:S(2)}) collective-permute-start(bf16[256,1024]{1,0:T(8,128)(2,1)} %mid_sum.1.refs_10_.refs_0_), channel_id=1, source_target_pairs={{0,1},{1,0},{2,3},{3,2},{4,5},{5,4},{6,7},{7,6},{8,9},{9,8},{10,11... | collective-permute-start | bytes 1572872 | tf_op jit(solution)/shard_map/ppermute | solution.py:921
  111.2 13.8 %collective-permute-start.14 = (bf16[256,1024]{1,0:T(8,128)(2,1)}, bf16[256,1024]{1,0:T(8,128)(2,1)}, u32[]{:S(2)}, u32[]{:S(2)}) collective-permute-start(bf16[256,1024]{1,0:T(8,128)(2,1)} %mid_sum.1.refs_10_.refs_0_), channel_id=1, source_target_pairs={{1,2},{2,1},{5,6},{6,5},{9,10},{10,9},{13,14},{14,13},{17,18},{18,... | collective-permute-start | bytes 1572872 | tf_op jit(solution)/shard_map/ppermute | solution.py:924
  112.7 19.3 %collective-permute-start.15 = (bf16[1024,256]{1,0:T(8,128)(2,1)}, bf16[1024,256]{1,0:T(8,128)(2,1)}, u32[]{:S(2)}, u32[]{:S(2)}) collective-permute-start(bf16[1024,256]{1,0:T(8,128)(2,1)} %slice.80.refs_1_), channel_id=1, source_target_pairs={{0,8},{4,12},{8,0},{12,4},{16,24},{20,28},{24,16},{28,20},{1,9},{5... | collective-permute-start | bytes 1572872 | tf_op jit(solution)/shard_map/ppermute | solution.py:341
  114.2 18.4 %collective-permute-start.16 = (bf16[1024,256]{1,0:T(8,128)(2,1)}, bf16[1024,256]{1,0:T(8,128)(2,1)}, u32[]{:S(2)}, u32[]{:S(2)}) collective-permute-start(bf16[1024,256]{1,0:T(8,128)(2,1)} %slice.81.refs_2_), channel_id=1, source_target_pairs={{0,16},{4,20},{8,24},{12,28},{16,0},{20,4},{24,8},{28,12},{1,17},{... | collective-permute-start | bytes 1572872 | tf_op jit(solution)/shard_map/ppermute | solution.py:341
  125.9 15.5 %collective-permute-start.22 = (bf16[256,1024]{1,0:T(8,128)(2,1)}, bf16[256,1024]{1,0:T(8,128)(2,1)}, u32[]{:S(2)}, u32[]{:S(2)}) collective-permute-start(bf16[256,1024]{1,0:T(8,128)(2,1)} %bitcast_select_fusion.1), channel_id=1, source_target_pairs={{0,1},{1,0},{2,3},{3,2},{4,5},{5,4},{6,7},{7,6},{8,9},{9,8},{10,11... | collective-permute-start | bytes 1572872 | tf_op jit(solution)/shard_map/ppermute | solution.py:921
  130.6 10.9 %collective-permute-start.21 = (bf16[256,1024]{1,0:T(8,128)(2,1)}, bf16[256,1024]{1,0:T(8,128)(2,1)}, u32[]{:S(2)}, u32[]{:S(2)}) collective-permute-start(bf16[256,1024]{1,0:T(8,128)(2,1)} %collective-permute-done.13.refs_11_.refs_1_), channel_id=1, source_target_pairs={{1,2},{2,1},{5,6},{6,5},{9,10},{10,9},{13,14},{14,13},{17,18},{18,... | collective-permute-start | bytes 1572872 | tf_op jit(solution)/shard_map/ppermute | solution.py:924
  132.0 18.4 %collective-permute-start.17 = (bf16[1024,512]{1,0:T(8,128)(2,1)}, bf16[1024,512]{1,0:T(8,128)(2,1)}, u32[]{:S(2)}, u32[]{:S(2)}) collective-permute-start(bf16[1024,512]{1,0:T(8,128)(2,1)} %copy-done.2), channel_id=1, source_target_pairs={{0,4},{4,0},{8,12},{12,8},{16,20},{20,16},{24,28},{28,24},{1,5},{5... | collective-permute-start | bytes 3145736 | tf_op jit(solution)/shard_map/ppermute | solution.py:341
  132.0 18.4 %collective-permute-start.18 = (bf16[1024,512]{1,0:T(8,128)(2,1)S(1)}, bf16[1024,512]{1,0:T(8,128)(2,1)}, u32[]{:S(2)}, u32[]{:S(2)}) collective-permute-start(bf16[1024,512]{1,0:T(8,128)(2,1)S(1)} %collective-permute-done.11.refs_2_), channel_id=1, source_target_pairs={{0,4},{4,0},{8,12},{12,8},{16,20},{20,16},{24,28},{28,24},{1,5},{5... | collective-permute-start | bytes 3145736 | tf_op jit(solution)/shard_map/ppermute | solution.py:341
  132.5 16.4 %collective-permute-start.19 = (bf16[1024,256]{1,0:T(8,128)(2,1)}, bf16[1024,256]{1,0:T(8,128)(2,1)}, u32[]{:S(2)}, u32[]{:S(2)}) collective-permute-start(bf16[1024,256]{1,0:T(8,128)(2,1)} %collective-permute-done.15.refs_4_), channel_id=1, source_target_pairs={{0,4},{4,0},{8,12},{12,8},{16,20},{20,16},{24,28},{28,24},{1,5},{5... | collective-permute-start | bytes 1572872 | tf_op jit(solution)/shard_map/ppermute | solution.py:341
  141.4 9.0 %collective-permute-start.20 = (bf16[1024,256]{1,0:T(8,128)(2,1)}, bf16[1024,256]{1,0:T(8,128)(2,1)}, u32[]{:S(2)}, u32[]{:S(2)}) collective-permute-start(bf16[1024,256]{1,0:T(8,128)(2,1)} %collective-permute-done.16.refs_5_), channel_id=1, source_target_pairs={{0,4},{4,0},{8,12},{12,8},{16,20},{20,16},{24,28},{28,24},{1,5},{5... | collective-permute-start | bytes 1572872 | tf_op jit(solution)/shard_map/ppermute | solution.py:341
  142.3 19.7 %collective-permute-start.24 = (bf16[256,1024]{1,0:T(8,128)(2,1)}, bf16[256,1024]{1,0:T(8,128)(2,1)}, u32[]{:S(2)}, u32[]{:S(2)}) collective-permute-start(bf16[256,1024]{1,0:T(8,128)(2,1)} %bitcast_select_fusion), channel_id=1, source_target_pairs={{0,1},{1,0},{2,3},{3,2},{4,5},{5,4},{6,7},{7,6},{8,9},{9,8},{10,11... | collective-permute-start | bytes 1572872 | tf_op jit(solution)/shard_map/ppermute | solution.py:921
  149.0 13.0 %collective-permute-start.23 = (bf16[256,1024]{1,0:T(8,128)(2,1)}, bf16[256,1024]{1,0:T(8,128)(2,1)}, u32[]{:S(2)}, u32[]{:S(2)}) collective-permute-start(bf16[256,1024]{1,0:T(8,128)(2,1)} %add_convert_fusion.2), channel_id=1, source_target_pairs={{1,2},{2,1},{5,6},{6,5},{9,10},{10,9},{13,14},{14,13},{17,18},{18,... | collective-permute-start | bytes 1572872 | tf_op jit(solution)/shard_map/ppermute | solution.py:924
  164.4 14.8 %collective-permute-start.25 = (bf16[256,1024]{1,0:T(8,128)(2,1)}, bf16[256,1024]{1,0:T(8,128)(2,1)S(1)}, u32[]{:S(2)}, u32[]{:S(2)}) collective-permute-start(bf16[256,1024]{1,0:T(8,128)(2,1)} %get-tuple-element.174), channel_id=1, source_target_pairs={{0,1},{1,0},{2,3},{3,2},{4,5},{5,4},{6,7},{7,6},{8,9},{9,8},{10,11... | collective-permute-start | bytes 1572872 | tf_op jit(solution)/shard_map/ppermute | solution.py:921
  166.3 13.0 %collective-permute-start.26 = (bf16[256,1024]{1,0:T(8,128)(2,1)S(1)}, bf16[256,1024]{1,0:T(8,128)(2,1)}, u32[]{:S(2)}, u32[]{:S(2)}) collective-permute-start(bf16[256,1024]{1,0:T(8,128)(2,1)S(1)} %get-tuple-element.173), channel_id=1, source_target_pairs={{1,2},{2,1},{5,6},{6,5},{9,10},{10,9},{13,14},{14,13},{17,18},{18,... | collective-permute-start | bytes 1572872 | tf_op jit(solution)/shard_map/ppermute | solution.py:924
  169.0 10.2 %copy-start.13 = (bf16[2,256,1024]{2,1,0:T(8,128)(2,1)S(1)}, bf16[2,256,1024]{2,1,0:T(8,128)(2,1)}, u32[]{:S(2)}) copy-start(bf16[2,256,1024]{2,1,0:T(8,128)(2,1)} %residual_ref.1) | copy-start | bytes 3145732
  179.2 28.5 %copy-start.27 = (f32[16,1024]{1,0:T(8,128)S(1)}, f32[16,1024]{1,0:T(8,128)}, u32[]{:S(2)}) copy-start(f32[16,1024]{1,0:T(8,128)} %param.25) | copy-start | bytes 196612
  180.7 37.9 %copy-start.6 = (bf16[256,1024]{1,0:T(8,128)(2,1)}, bf16[256,1024]{1,0:T(8,128)(2,1)S(1)}, u32[]{:S(2)}) copy-start(bf16[256,1024]{1,0:T(8,128)(2,1)S(1)} %fusion.7.refs_0_) | copy-start | bytes 1572868
  180.7 17.4 %collective-permute-start.27 = (bf16[256,1024]{1,0:T(8,128)(2,1)S(1)}, bf16[256,1024]{1,0:T(8,128)(2,1)S(1)}, u32[]{:S(2)}, u32[]{:S(2)}) collective-permute-start(bf16[256,1024]{1,0:T(8,128)(2,1)S(1)} %fusion.7.refs_0_), channel_id=1, source_target_pairs={{0,1},{1,0},{2,3},{3,2},{4,5},{5,4},{6,7},{7,6},{8,9},{9,8},{10,11... | collective-permute-start | bytes 1572872 | tf_op jit(solution)/shard_map/ppermute | solution.py:412
  182.7 15.4 %collective-permute-start.28 = (bf16[256,1024]{1,0:T(8,128)(2,1)S(1)}, bf16[256,1024]{1,0:T(8,128)(2,1)S(1)}, u32[]{:S(2)}, u32[]{:S(2)}) collective-permute-start(bf16[256,1024]{1,0:T(8,128)(2,1)S(1)} %fusion.7.refs_0_), channel_id=1, source_target_pairs={{1,2},{2,1},{5,6},{6,5},{9,10},{10,9},{13,14},{14,13},{17,18},{18,... | collective-permute-start | bytes 1572872 | tf_op jit(solution)/shard_map/ppermute | solution.py:412
  183.4 22.2 %collective-permute-start.29 = (bf16[256,1024]{1,0:T(8,128)(2,1)S(1)}, bf16[256,1024]{1,0:T(8,128)(2,1)S(1)}, u32[]{:S(2)}, u32[]{:S(2)}) collective-permute-start(bf16[256,1024]{1,0:T(8,128)(2,1)S(1)} %fusion.7.refs_0_), channel_id=1, source_target_pairs={{0,3},{3,0},{4,7},{7,4},{8,11},{11,8},{12,15},{15,12},{16,19},{19,... | collective-permute-start | bytes 1572872 | tf_op jit(solution)/shard_map/ppermute | solution.py:959
  198.1 20.5 %copy-start.14 = (bf16[256,1024]{1,0:T(8,128)(2,1)}, bf16[256,1024]{1,0:T(8,128)(2,1)S(1)}, u32[]{:S(2)}) copy-start(bf16[256,1024]{1,0:T(8,128)(2,1)S(1)} %collective-permute-done.27.refs_1_) | copy-start | bytes 1572868
  198.1 20.5 %copy-start.15 = (bf16[256,1024]{1,0:T(8,128)(2,1)}, bf16[256,1024]{1,0:T(8,128)(2,1)S(1)}, u32[]{:S(2)}) copy-start(bf16[256,1024]{1,0:T(8,128)(2,1)S(1)} %collective-permute-done.28.refs_2_) | copy-start | bytes 1572868
  205.7 12.9 %copy-start.22 = (bf16[256,1024]{1,0:T(8,128)(2,1)}, bf16[256,1024]{1,0:T(8,128)(2,1)S(1)}, u32[]{:S(2)}) copy-start(bf16[256,1024]{1,0:T(8,128)(2,1)S(1)} %collective-permute-done.29.refs_5_) | copy-start | bytes 1572868
  205.7 12.9 %collective-permute-start.30 = (bf16[256,1024]{1,0:T(8,128)(2,1)S(1)}, bf16[256,1024]{1,0:T(8,128)(2,1)S(1)}, u32[]{:S(2)}, u32[]{:S(2)}) collective-permute-start(bf16[256,1024]{1,0:T(8,128)(2,1)S(1)} %collective-permute-done.27.refs_1_), channel_id=1, source_target_pairs={{1,2},{2,1},{5,6},{6,5},{9,10},{10,9},{13,14},{14,13},{17,18},{18,... | collective-permute-start | bytes 1572872 | tf_op jit(solution)/shard_map/ppermute | solution.py:412
  206.4 14.7 %collective-permute-start.31 = (bf16[256,1024]{1,0:T(8,128)(2,1)S(1)}, bf16[256,1024]{1,0:T(8,128)(2,1)S(1)}, u32[]{:S(2)}, u32[]{:S(2)}) collective-permute-start(bf16[256,1024]{1,0:T(8,128)(2,1)S(1)} %collective-permute-done.28.refs_2_), channel_id=1, source_target_pairs={{1,0},{2,3},{5,4},{6,7},{9,8},{10,11},{13,12},{14,15},{17,16},{18,... | collective-permute-start | bytes 1572872 | tf_op jit(solution)/shard_map/ppermute | solution.py:412
  221.1 92.0 %reduce-scatter.8.cloned.1.call-start = ((), (), s32[]{:S(2)}) async-start(), calls=%async_computation.5 | async-start | bytes 2621440 | tf_op jit(solution)/shard_map/reduce_scatter | solution.py:869
  255.7 10.9 %copy-start.5 = (bf16[256,1024]{1,0:T(8,128)(2,1)S(1)}, bf16[256,1024]{1,0:T(8,128)(2,1)}, u32[]{:S(2)}) copy-start(bf16[256,1024]{1,0:T(8,128)(2,1)} %mid_sum.1.refs_10_.refs_0_) | copy-start | bytes 1572868
  255.7 12.1 %copy-start.7 = (bf16[256,1024]{1,0:T(8,128)(2,1)S(1)}, bf16[256,1024]{1,0:T(8,128)(2,1)}, u32[]{:S(2)}) copy-start(bf16[256,1024]{1,0:T(8,128)(2,1)} %copy-done.6) | copy-start | bytes 1572868
  (16 other events, 55.0 us)
Sparse Core Ops, SparseCore 0:
  64.4 44.3 reduce-scatter.3
  221.2 45.3 reduce-scatter.5
  269.1 43.9 reduce-scatter.7
